TPU v7x, 32 devices: a whole 2x2x4 slice. The times are simulated.
32 devices in a mesh: groups: 2 (over y), dp: 8 (over z, x), tensor: 2 (over core).
Axes of the slice: x: 2, y: 2, z: 4, core: 2. Of those that a mesh axis runs over, the one named last changes fastest.
Arguments:
- saved_input: bfloat16 [2048, 5120], P(('groups', 'dp'), 'tensor'), parts along dimension 0, may hold values from -6 to 6
- saved_pre: bfloat16 [2048, 10240], P(('groups', 'dp'), 'tensor'), parts along dimension 0, may hold values from -8 to 8
- grad_act: bfloat16 [2048, 10240], P(('groups', 'dp'), 'tensor'), parts along dimension 0, may hold values from -6 to 6
Outputs:
- a_factor: float32 [2, 5120, 128], P('tensor', ('groups', 'dp')), parts along dimension 1
- g_factor: float32 [2, 10240, 128], P('tensor', ('groups', 'dp')), parts along dimension 1
There are 2 independent parts, one for each index of `groups`. A program takes and returns all parts, laid end to end along the dimension named above; each array names one. Nothing has to cross between parts.
All inputs are finite; a program needn't handle non-finite values.
Results may differ from a plain program's by a relative error of at most 0.001.
The roundings to bfloat16 on the way count: a program that leaves them out, or rounds other values in their place, can miss the bound.
Values sent between devices are 32-bit elements; how exact they have to be, the bound alone decides.
No kernel may reach another device: no remote copies, remote signals or barrier semaphores. Data moves between devices by JAX's collectives and lax.ppermute only.
A program may use at most 64 MiB of HBM per device.

v0:
```python
import jax
import jax.numpy as jnp
from jax import lax
from jax.sharding import PartitionSpec as P

D = 5120
FFW = 10240
B = 128


def gelu_slope(value):
    return (
        0.5 * (1.0 + lax.erf(value * 0.7071067811865476))
        + value * jnp.exp(-0.5 * value * value) * 0.3989422804014327
    )


def local_blocks(matrix, block, total):
    tokens, width = matrix.shape
    pieces = matrix.reshape(tokens, width // block, block)
    cov = jnp.einsum("tkb,tkc->kbc", pieces, pieces, preferred_element_type=jnp.float32)
    return cov.reshape(width, block) / total


def owned_unit(owned, block):
    count = owned.shape[0]
    rows = lax.axis_index("dp") * count + jnp.arange(count, dtype=jnp.int32)
    cols = jnp.arange(block, dtype=jnp.int32)
    return (cols[None, :] == (rows % block)[:, None]).astype(jnp.float32)


def on_device(saved_input, saved_pre, grad_act):
    block = B
    owners = lax.axis_size("dp")
    total = jnp.float32(saved_input.shape[0] * owners)
    slope = gelu_slope(saved_pre.astype(jnp.float32))
    grad_pre = (grad_act.astype(jnp.float32) * slope).astype(jnp.bfloat16)
    terms_a = local_blocks(saved_input, block, total)
    terms_g = local_blocks(grad_pre, block, total)
    owned_a = lax.psum_scatter(terms_a, "dp", scatter_dimension=0, tiled=True)
    owned_g = lax.psum_scatter(terms_g, "dp", scatter_dimension=0, tiled=True)
    unit_a = owned_unit(owned_a, block)
    unit_g = owned_unit(owned_g, block)
    trace_a, trace_g = lax.psum(
        (jnp.sum(owned_a * unit_a), jnp.sum(owned_g * unit_g)), ("dp", "tensor")
    )
    ratio = jnp.sqrt(trace_a / D / (trace_g / FFW))
    damp = jnp.sqrt(jnp.float32(0.1))
    a_factor = (owned_a + ratio * damp * unit_a)[None]
    g_factor = (owned_g + damp / ratio * unit_g)[None]
    return (a_factor, g_factor)


def solution(mesh):
    in_specs = (
        P(("groups", "dp"), "tensor"),
        P(("groups", "dp"), "tensor"),
        P(("groups", "dp"), "tensor"),
    )
    out_specs = (P("tensor", ("groups", "dp"), None), P("tensor", ("groups", "dp"), None))
    return jax.shard_map(
        on_device, mesh=mesh, in_specs=in_specs, out_specs=out_specs, check_vma=False
    )
```

profile of v0, /device:TPU:0, one launch (start us, length us, event | category | flops | bytes accessed | tf_op | source)
XLA Modules:
  0.0 196.1 jit_solution(3264476164811163197)
XLA Ops:
  7.2 0.0 copy-start
  7.2 0.0 copy-start.1
  7.2 0.0 reduce-scatter.3.cloned.1.call-start
  7.2 1.6 copy.9
  8.8 1.7 convolution_multiply_fusion.1
  10.5 0.0 reduce-scatter.3.cloned.1.call-update
  10.5 0.0 reduce-scatter.5.cloned.1.call-start
  10.5 0.0 copy-done
  10.5 0.0 copy-done.1
  10.6 4.1 %convolution_multiply_fusion = f32[40,128,128]{2,1,0:T(8,128)} fusion(bf16[128,5120]{1,0:T(8,128)(2,1)S(1)} %copy-done, bf16[128,5120]{1,0:T(8,128)(2,1)S(1)} %copy-done.1), kind=kOutput, calls=%fused_computation.12 | convolution fusion | flops 176291840 | bytes 5242880 | tf_op jit(solution)/shard_map/tkb,tkc->kbc/dot_general | solution.py:21
  14.6 0.0 reduce-scatter.5.cloned.1.call-update
  14.7 63.7 %reduce-scatter.3.cloned.1.call-done = f32[320,128]{1,0:T(8,128)} async-done(((f32[2560,128]{1,0:T(8,128)}), f32[320,128]{1,0:T(8,128)}) %reduce-scatter.3.cloned.1.call-update) | async-done | bytes 163856 | tf_op jit(solution)/shard_map/reduce_scatter | solution.py:40
  78.4 1.6 select_reduce_fusion.1
  80.1 71.2 %reduce-scatter.5.cloned.1.call-done = f32[640,128]{1,0:T(8,128)} async-done(((f32[5120,128]{1,0:T(8,128)}), f32[640,128]{1,0:T(8,128)}) %reduce-scatter.5.cloned.1.call-update) | async-done | bytes 327696 | tf_op jit(solution)/shard_map/reduce_scatter | solution.py:41
  151.3 1.7 select_reduce_fusion
  153.0 31.3 %all-reduce = (f32[]{:T(128)}, f32[]{:T(128)}) all-reduce(f32[]{:T(128)} %select_reduce_fusion.1, f32[]{:T(128)} %select_reduce_fusion), channel_id=1, replica_groups=mesh['groups'=2,'dp'=8,'tensor'=2] {'dp','tensor'}, use_global_device_ids=true, to_apply=%region_2.3 | all-reduce | flops 2 | bytes 16 | tf_op jit(solution)/shard_map/psum | solution.py:44
  185.7 1.9 add_bitcast_fusion
  187.6 1.7 add_bitcast_fusion.1
  (2 shorter events, 0.0 us)
Async XLA Ops:
  7.2 3.4 %copy-start = (bf16[128,5120]{1,0:T(8,128)(2,1)S(1)}, bf16[128,5120]{1,0:T(8,128)(2,1)}, u32[]{:S(2)}) copy-start(bf16[128,5120]{1,0:T(8,128)(2,1)} %param.4) | copy-start | bytes 3932164
  7.2 3.4 %copy-start.1 = (bf16[128,5120]{1,0:T(8,128)(2,1)S(1)}, bf16[128,5120]{1,0:T(8,128)(2,1)}, u32[]{:S(2)}) copy-start(bf16[128,5120]{1,0:T(8,128)(2,1)} %param.5) | copy-start | bytes 3932164
  7.2 71.2 %reduce-scatter.3.cloned.1.call-start = ((), (), s32[]{:S(2)}) async-start(), calls=%async_computation.2 | async-start | bytes 1474560 | tf_op jit(solution)/shard_map/reduce_scatter | solution.py:40
  10.5 140.8 %reduce-scatter.5.cloned.1.call-start = ((), (), s32[]{:S(2)}) async-start(), calls=%async_computation.3 | async-start | bytes 2949120 | tf_op jit(solution)/shard_map/reduce_scatter | solution.py:41
Sparse Core Ops, SparseCore 0:
  11.4 66.9 reduce-scatter.2
  81.9 69.2 reduce-scatter.4
where the time goes:
time: 196 us
  waiting for transfers between devices  135 us (69%)
  blocking collectives  31.3 us (16%)
  between operations  15.5 us (8%)
  other arithmetic  6.92 us (4%)
  matrix products  5.75 us (3%)
    reduce_scatter x1, waiting for transfers between devices, on_device(): owned_g = lax.psum_scatter(terms_g, 'dp', scatter_dimension=0, tiled=True)  71.2 us
    reduce_scatter x1, waiting for transfers between devices, on_device(): owned_a = lax.psum_scatter(terms_a, 'dp', scatter_dimension=0, tiled=True)  63.7 us
    psum x1, blocking collectives, on_device(): lax.psum((jnp.sum(owned_a * unit_a), jnp.sum(owned_g * unit_g)), ('dp', '...  31.3 us
    dot_general x2, matrix products, local_blocks(): jnp.einsum('tkb,tkc->kbc', pieces, pieces, preferred_element_type=jnp.flo...  5.75 us
  transfers between devices with their start and end apart: 2, of which 2 were waited for; matrix products, arithmetic and copies ran while one was open for 3% of the time, Pallas kernels for 0%

commit v1 on v0

v1 whole, which is shorter than its diff:
```python
import functools

import jax
import jax.numpy as jnp
from jax import lax
from jax.experimental import pallas as pl
from jax.experimental.pallas import tpu as pltpu
from jax.sharding import PartitionSpec as P

D = 5120
FFW = 10240
B = 128
H = B // 2
EDGE = 8


def gelu_slope(value):
    return (
        0.5 * (1.0 + lax.erf(value * 0.7071067811865476))
        + value * jnp.exp(-0.5 * value * value) * 0.3989422804014327
    )


def local_blocks(matrix, block, total):
    tokens, width = matrix.shape
    pieces = matrix.reshape(tokens, width // block, block)
    cov = jnp.einsum("tkb,tkc->kbc", pieces, pieces, preferred_element_type=jnp.float32)
    return cov.reshape(width, block) / total


def owned_unit(owned, block):
    count = owned.shape[0]
    rows = lax.axis_index("dp") * count + jnp.arange(count, dtype=jnp.int32)
    cols = jnp.arange(block, dtype=jnp.int32)
    return (cols[None, :] == (rows % block)[:, None]).astype(jnp.float32)


def plain(saved_input, saved_pre, grad_act):
    total = jnp.float32(saved_input.shape[0] * lax.axis_size("dp"))
    slope = gelu_slope(saved_pre.astype(jnp.float32))
    grad_pre = (grad_act.astype(jnp.float32) * slope).astype(jnp.bfloat16)
    terms_a = local_blocks(saved_input, B, total)
    terms_g = local_blocks(grad_pre, B, total)
    owned_a = lax.psum_scatter(terms_a, "dp", scatter_dimension=0, tiled=True)
    owned_g = lax.psum_scatter(terms_g, "dp", scatter_dimension=0, tiled=True)
    unit_a = owned_unit(owned_a, B)
    unit_g = owned_unit(owned_g, B)
    trace_a, trace_g = lax.psum(
        (jnp.sum(owned_a * unit_a), jnp.sum(owned_g * unit_g)), ("dp", "tensor")
    )
    ratio = jnp.sqrt(trace_a / D / (trace_g / FFW))
    damp = jnp.sqrt(jnp.float32(0.1))
    return (
        (owned_a + ratio * damp * unit_a)[None],
        (owned_g + damp / ratio * unit_g)[None],
    )


def split_rows(count):
    return count // B, (count % B) // H


def chunk_rows(count):
    full, half = split_rows(count)
    return (full + half) * H + EDGE


def iotas():
    shape = (H, B)
    return lax.broadcasted_iota(jnp.int32, shape, 0), lax.broadcasted_iota(jnp.int32, shape, 1)


def slot_mask(slot, order):
    bits = len(order)
    mask = 0
    for place, bit in enumerate(order):
        mask = mask + (((slot >> (bits - 1 - place)) & 1) << bit)
    return mask


def pack_chunk(read_block, odd, full, half, out_ref):
    row, col = iotas()
    low = col < row
    diag_low = col == row
    diag_high = col == row + H
    zero = jnp.zeros((H, B), jnp.float32)
    trace = zero

    def cov(block):
        piece = read_block(block)
        return lax.dot_general(
            piece, piece, (((0,), (0,)), ((), ())), preferred_element_type=jnp.float32
        )

    for i in range(full):
        block = cov((half * odd) * ((full + half)) + i if half else i)
        top, bottom = block[:H], block[H:]
        out_ref[0, i * H : (i + 1) * H, :] = jnp.where(low, pltpu.roll(bottom, H, 1), top)
        corner = jnp.where(diag_high, bottom, zero)
        out_ref[0, (full + half) * H + i : (full + half) * H + i + 1, :] = jnp.sum(
            corner, axis=0, keepdims=True
        )
        trace = trace + corner + jnp.where(diag_low, top, zero)
    if half:
        block = cov(full)
        piece = jnp.where(odd == 1, block[H:], block[:H])
        out_ref[0, full * H : (full + 1) * H, :] = piece
        trace = trace + jnp.where(col == row + odd * H, piece, zero)
    out_ref[0, (full + half) * H + full :, :] = jnp.zeros((EDGE - full, B), jnp.float32)
    return jnp.sum(trace, axis=0, keepdims=True)


def pack_body(order, first, full, half, slope, row_out, n_in, *refs):
    ins, (trace_in, out_ref, trace_ref) = refs[:n_in], refs[n_in:]
    step = pl.program_id(0)
    owner = lax.axis_index("dp") ^ slot_mask(first + step, order)
    odd = owner & 1

    def read_block(block):
        start = block * B
        if not isinstance(start, int):
            start = pl.multiple_of(start, B)
        part = pl.ds(start, B)
        if slope:
            value = ins[0][:, part].astype(jnp.float32)
            grad = ins[1][:, part].astype(jnp.float32)
            return (grad * gelu_slope(value)).astype(jnp.bfloat16)
        return ins[0][:, part]

    line = pack_chunk(read_block, odd, full, half, out_ref)

    @pl.when(step == 0)
    def _():
        trace_ref[...] = trace_in[...]

    trace_ref[row_out : row_out + 1, :] += line


def pack(arrays, order, first, slots, count, trace, row_out):
    full, half = split_rows(count)
    tokens = arrays[0].shape[0]
    span = (2 * full + 1) * B if half else full * B

    def in_map(step):
        owner = lax.axis_index("dp") ^ slot_mask(first + step, order)
        return 0, owner >> half

    rows = chunk_rows(count)
    n = len(arrays)
    return pl.pallas_call(
        functools.partial(pack_body, order, first, full, half, n == 2, row_out, n),
        grid=(slots,),
        in_specs=[pl.BlockSpec((tokens, span), in_map) for _ in arrays]
        + [pl.BlockSpec((EDGE, B), lambda step: (0, 0))],
        out_specs=[
            pl.BlockSpec((1, rows, B), lambda step: (step, 0, 0)),
            pl.BlockSpec((EDGE, B), lambda step: (0, 0)),
        ],
        out_shape=[
            jax.ShapeDtypeStruct((slots, rows, B), jnp.float32),
            jax.ShapeDtypeStruct((EDGE, B), jnp.float32),
        ],
        compiler_params=pltpu.CompilerParams(vmem_limit_bytes=32 * 2**20),
        cost_estimate=pl.CostEstimate(
            flops=slots * count * B * tokens * 2,
            bytes_accessed=slots * rows * B * 4 + n * slots * count * tokens * 2,
            transcendentals=0,
        ),
    )(*arrays, trace)


def unfold(own, recv, count, odd, shift, total, out_ref):
    full, half = split_rows(count)
    row, col = iotas()
    edge = (full + half) * H
    unit_low = jnp.where(col == row, shift, 0.0)
    unit_high = jnp.where(col == row + H, shift, 0.0)
    for i in range(full):
        part = slice(i * H, (i + 1) * H)
        folded = (own[0, part, :] + recv[0, part, :]) / total
        corner = (own[0, edge + i : edge + i + 1, :] + recv[0, edge + i : edge + i + 1, :]) / total
        turned = jnp.concatenate([folded, folded], axis=0).T
        top = jnp.where(col < row, turned[:H], folded) + unit_low
        last = pltpu.roll(jnp.where(col < row, folded, turned[:H]), H, 1)
        bottom = jnp.where(col < H, turned[H:], jnp.where(col == row + H, corner, last)) + unit_high
        start = i * B + odd * H if half else i * B
        if half:
            start = pl.multiple_of(start, H)
        out_ref[pl.ds(start, H), :] = top
        out_ref[pl.ds(start + H, H), :] = bottom
    if half:
        part = slice(full * H, (full + 1) * H)
        piece = (own[0, part, :] + recv[0, part, :]) / total
        start = pl.multiple_of((1 - odd) * full * B, H)
        out_ref[pl.ds(start, H), :] = piece + jnp.where(col == row + odd * H, shift, 0.0)


def finish_body(count_a, count_g, total, n_traces, *refs):
    traces, (own_a, recv_a, own_g, recv_g, a_ref, g_ref) = refs[:n_traces], refs[n_traces:]
    odd = lax.axis_index("dp") & 1
    tile = traces[0][...]
    for other in traces[1:]:
        tile = tile + other[...]
    sums = jnp.sum(tile, axis=1, keepdims=True) / total
    ratio = jnp.sqrt(sums[0:1] / D / (sums[1:2] / FFW))
    damp = jnp.sqrt(jnp.full((1, 1), 0.1, jnp.float32))
    unfold(own_a, recv_a, count_a, odd, ratio * damp, total, a_ref)
    unfold(own_g, recv_g, count_g, odd, damp / ratio, total, g_ref)


def finish(traces, own_a, recv_a, own_g, recv_g, count_a, count_g, total):
    args = (*traces, own_a, recv_a, own_g, recv_g)
    return pl.pallas_call(
        functools.partial(finish_body, count_a, count_g, total, len(traces)),
        in_specs=[pl.BlockSpec(memory_space=pltpu.VMEM)] * len(args),
        out_specs=[pl.BlockSpec(memory_space=pltpu.VMEM)] * 2,
        out_shape=[
            jax.ShapeDtypeStruct((count_a, B), jnp.float32),
            jax.ShapeDtypeStruct((count_g, B), jnp.float32),
        ],
        compiler_params=pltpu.CompilerParams(vmem_limit_bytes=32 * 2**20),
    )(*args)


def swap(value, mask):
    dp, tensor = lax.axis_size("dp"), lax.axis_size("tensor")
    dp_mask, tensor_mask = mask
    if tensor_mask == 0:
        return lax.ppermute(value, "dp", [(i, i ^ dp_mask) for i in range(dp)])
    pairs = [
        (i * tensor + j, (i ^ dp_mask) * tensor + (j ^ tensor_mask))
        for i in range(dp)
        for j in range(tensor)
    ]
    return lax.ppermute(value, ("dp", "tensor"), pairs)


def halve(keep, got):
    half = keep.shape[0] // 2
    return keep[:half] + got[:half], keep[half:] + got[half:]


def packed(saved_input, saved_pre, grad_act):
    dp = lax.axis_size("dp")
    total = float(saved_input.shape[0] * dp)
    count_a = saved_input.shape[1] // dp
    count_g = saved_pre.shape[1] // dp
    order_a, order_g = (0, 1, 2), (1, 0, 2)
    half = dp // 2
    blank = jnp.zeros((EDGE, B), jnp.float32)

    send_a, trace = pack((saved_input,), order_a, half, half, count_a, blank, 0)
    got_a = swap(send_a, (1 << order_a[0], 0))
    send_g, trace = pack((saved_pre, grad_act), order_g, half, half, count_g, trace, 1)
    got_g = swap(send_g, (1 << order_g[0], 0))
    keep_a, trace = pack((saved_input,), order_a, 0, half, count_a, trace, 0)
    keep_g, trace = pack((saved_pre, grad_act), order_g, 0, half, count_g, trace, 1)

    keep_a, send_a = halve(keep_a, got_a)
    got_a = swap(send_a, (1 << order_a[1], 0))
    keep_g, send_g = halve(keep_g, got_g)
    got_g = swap(send_g, (1 << order_g[1], 0))
    trace = trace + swap(trace, (1, 0)) + swap(trace, (0, 1)) + swap(trace, (1, 1))

    keep_a, send_a = halve(keep_a, got_a)
    got_a = swap(send_a, (1 << order_a[2], 0))
    keep_g, send_g = halve(keep_g, got_g)
    got_g = swap(send_g, (1 << order_g[2], 0))
    traces = (trace, swap(trace, (2, 0)), swap(trace, (4, 0)), swap(trace, (6, 0)))

    a_factor, g_factor = finish(traces, keep_a, got_a, keep_g, got_g, count_a, count_g, total)
    return a_factor[None], g_factor[None]


def fits(count):
    return count % H == 0 and count // B <= EDGE


def on_device(saved_input, saved_pre, grad_act):
    dp = lax.axis_size("dp")
    count_a = saved_input.shape[1] // dp
    count_g = saved_pre.shape[1] // dp
    if dp == 8 and lax.axis_size("tensor") == 2 and fits(count_a) and fits(count_g):
        return packed(saved_input, saved_pre, grad_act)
    return plain(saved_input, saved_pre, grad_act)


def solution(mesh):
    spec = P(("groups", "dp"), "tensor")
    out = P("tensor", ("groups", "dp"), None)
    return jax.shard_map(
        on_device, mesh=mesh, in_specs=(spec, spec, spec), out_specs=(out, out), check_vma=False
    )
```

time: 196 us -> 47.6 us (0.24)
  waiting for transfers between devices: 135 us -> 16 us
  blocking collectives: 31.3 us -> 0 us
  starting transfers between devices: 0.08 us -> 18.8 us
  between operations: 15.5 us -> 0.74 us
  Pallas kernels: 0 us -> 7.97 us
  other arithmetic: 6.92 us -> 0.19 us
  matrix products: 5.75 us -> 0 us
  local copies, waits for them, and re-layouts: 1.57 us -> 3.72 us
    reduce_scatter x2 -> x0, waiting for transfers between devices: 135 us -> none  [the longest x1 71.2 us: on_device(): owned_g = lax.psum_scatter(terms_g, 'dp', scatter_dimension=0, tiled=True)]
    psum x1 -> x0, blocking collectives: 31.3 us -> none  [on_device(): lax.psum((jnp.sum(owned_a * unit_a), jnp.sum(owned_g * unit_g)), ('dp', '...]
    ppermute x0 -> x12, starting transfers between devices: none -> 18.8 us  [the longest x10 18.6 us: swap(): return lax.ppermute(value, 'dp', [(i, i ^ dp_mask) for i in range(dp)])]
    ppermute x0 -> x12, waiting for transfers between devices: none -> 16 us  [the longest x10 16 us: swap(): return lax.ppermute(value, 'dp', [(i, i ^ dp_mask) for i in range(dp)])]
    pallas_call x0 -> x5, Pallas kernels: none -> 7.97 us  [the longest x4 6.9 us: pack(): pl.pallas_call(functools.partial(pack_body, order, first, full, half, n =...]
    dot_general x2 -> x0, matrix products: 5.75 us -> none  [local_blocks(): jnp.einsum('tkb,tkc->kbc', pieces, pieces, preferred_element_type=jnp.flo...]
    broadcast_in_dim x2 -> x0, other arithmetic: 3.54 us -> none  [the longest x1 1.85 us: on_device(): g_factor = (owned_g + damp / ratio * unit_g)[None]]
    reduce_sum x2 -> x0, other arithmetic: 3.36 us -> none  [the longest x1 1.73 us: on_device(): jnp.sum(owned_g * unit_g)]
  transfers between devices with their start and end apart: 2 -> 12, of which waited for: 2 -> 5; matrix products, arithmetic and copies ran while one was open for 3% -> 0% of each run, Pallas kernels for 0% -> 7%
where the time goes in v1:
time: 47.6 us; the launch traced here: 47.4 us
  starting transfers between devices  18.8 us (39%)
  waiting for transfers between devices  16 us (34%)
  Pallas kernels  7.97 us (17%)
  local copies, waits for them, and re-layouts  3.72 us (8%)
  between operations  0.74 us (2%)
    ppermute x10, starting transfers between devices, swap(): return lax.ppermute(value, 'dp', [(i, i ^ dp_mask) for i in range(dp)])  18.6 us
    ppermute x10, waiting for transfers between devices, swap(): return lax.ppermute(value, 'dp', [(i, i ^ dp_mask) for i in range(dp)])  16 us
    pallas_call x4, Pallas kernels, pack(): pl.pallas_call(functools.partial(pack_body, order, first, full, half, n =...  6.9 us
    unnamed x12, local copies, waits for them, and re-layouts  3.72 us
    pallas_call x1, Pallas kernels, finish(): pl.pallas_call(functools.partial(finish_body, count_a, count_g, total, le...  1.07 us
  transfers between devices with their start and end apart: 12, of which 5 were waited for; matrix products, arithmetic and copies ran while one was open for 0% of the time, Pallas kernels for 7%

profile of v1, /device:TPU:0, one launch (start us, length us, event | category | flops | bytes accessed | tf_op | source)
XLA Modules:
  0.0 47.4 jit_solution(9916710904954639148)
XLA Ops:
  0.7 1.1 %copy-done.4 = bf16[128,2560]{1,0:T(8,128)(2,1)S(1)} copy-done((bf16[128,2560]{1,0:T(8,128)(2,1)S(1)}, bf16[128,2560]{1,0:T(8,128)(2,1)}, u32[]{:S(2)}) %copy-start.4) | copy-done | bytes 655384
  1.7 1.4 %shard_map.50 = (f32[4,200,128]{2,1,0:T(8,128)S(1)}, f32[8,128]{1,0:T(8,128)S(1)}) custom-call(bf16[128,2560]{1,0:T(8,128)(2,1)S(1)} %copy-done.4, f32[8,128]{1,0:T(8,128)S(1)} %broadcast_in_dim.9.refs_1_), custom_call_target="tpu_custom_call" | custom-call | flops 41943040 | bytes 737280 | tf_op jit(solution)/shard_map/pallas_call | solution.py:150
  3.1 1.3 %copy-done = bf16[128,5120]{1,0:T(8,128)(2,1)S(1)} copy-done((bf16[128,5120]{1,0:T(8,128)(2,1)S(1)}, bf16[128,5120]{1,0:T(8,128)(2,1)}, u32[]{:S(2)}) %copy-start) | copy-done | bytes 1310744
  4.4 1.3 %copy-done.2 = bf16[128,5120]{1,0:T(8,128)(2,1)S(1)} copy-done((bf16[128,5120]{1,0:T(8,128)(2,1)S(1)}, bf16[128,5120]{1,0:T(8,128)(2,1)}, u32[]{:S(2)}) %copy-start.2) | copy-done | bytes 1310744
  5.8 2.1 %shard_map.51 = (f32[4,328,128]{2,1,0:T(8,128)S(1)}, f32[8,128]{1,0:T(8,128)S(1)}) custom-call(bf16[128,5120]{1,0:T(8,128)(2,1)S(1)} %copy-done, bf16[128,5120]{1,0:T(8,128)(2,1)S(1)} %copy-done.2, f32[8,128]{1,0:T(8,128)S(1)} %get-tuple-element.12.refs_2_), custom_call_target="tpu_custom_call" | custom-call | flops 83886080 | bytes 1982464 | tf_op jit(solution)/shard_map/pallas_call | solution.py:150
  7.8 3.1 %collective-permute-start.9 = (f32[4,328,128]{2,1,0:T(8,128)S(1)}, f32[4,328,128]{2,1,0:T(8,128)S(1)}, u32[]{:S(2)}, u32[]{:S(2)}) collective-permute-start(f32[4,328,128]{2,1,0:T(8,128)S(1)} %get-tuple-element.19), channel_id=1, source_target_pairs={{0,4},{2,6},{4,0},{6,2},{8,12},{10,14},{12,8},{14,10},{1,5},{3,7},... | collective-permute-start | bytes 2015240 | tf_op jit(solution)/shard_map/ppermute | solution.py:229
  10.9 1.5 %collective-permute-start.6 = (f32[4,200,128]{2,1,0:T(8,128)S(1)}, f32[4,200,128]{2,1,0:T(8,128)S(1)}, u32[]{:S(2)}, u32[]{:S(2)}) collective-permute-start(f32[4,200,128]{2,1,0:T(8,128)S(1)} %get-tuple-element.17), channel_id=1, source_target_pairs={{0,2},{2,0},{4,6},{6,4},{8,10},{10,8},{12,14},{14,12},{1,3},{3,1},... | collective-permute-start | bytes 1228808 | tf_op jit(solution)/shard_map/ppermute | solution.py:229
  12.4 1.4 %shard_map.52 = (f32[4,200,128]{2,1,0:T(8,128)S(1)}, f32[8,128]{1,0:T(8,128)S(1)}) custom-call(bf16[128,2560]{1,0:T(8,128)(2,1)S(1)} %copy-done.5, f32[8,128]{1,0:T(8,128)S(1)} %get-tuple-element.13.refs_1_), custom_call_target="tpu_custom_call" | custom-call | flops 41943040 | bytes 737280 | tf_op jit(solution)/shard_map/pallas_call | solution.py:150
  13.8 2.1 %shard_map.53 = (f32[4,328,128]{2,1,0:T(8,128)S(1)}, f32[8,128]{1,0:T(8,128)S(1)}) custom-call(bf16[128,5120]{1,0:T(8,128)(2,1)S(1)} %copy-done.1, bf16[128,5120]{1,0:T(8,128)(2,1)S(1)} %copy-done.3, f32[8,128]{1,0:T(8,128)S(1)} %get-tuple-element.14.refs_2_), custom_call_target="tpu_custom_call" | custom-call | flops 83886080 | bytes 1982464 | tf_op jit(solution)/shard_map/pallas_call | solution.py:150
  15.9 5.9 %collective-permute-done.6 = f32[4,200,128]{2,1,0:T(8,128)S(1)} collective-permute-done((f32[4,200,128]{2,1,0:T(8,128)S(1)}, f32[4,200,128]{2,1,0:T(8,128)S(1)}, u32[]{:S(2)}, u32[]{:S(2)}) %collective-permute-start.6) | collective-permute-done | bytes 409632 | tf_op jit(solution)/shard_map/ppermute | solution.py:229
  21.9 0.4 collective-permute-start.7
  22.3 4.5 %collective-permute-done.9 = f32[4,328,128]{2,1,0:T(8,128)S(1)} collective-permute-done((f32[4,328,128]{2,1,0:T(8,128)S(1)}, f32[4,328,128]{2,1,0:T(8,128)S(1)}, u32[]{:S(2)}, u32[]{:S(2)}) %collective-permute-start.9) | collective-permute-done | bytes 671776 | tf_op jit(solution)/shard_map/ppermute | solution.py:229
  26.9 2.0 %collective-permute-start.10 = (f32[2,328,128]{2,1,0:T(8,128)S(1)}, f32[2,328,128]{2,1,0:T(8,128)S(1)}, u32[]{:S(2)}, u32[]{:S(2)}) collective-permute-start(f32[2,328,128]{2,1,0:T(8,128)S(1)} %get-tuple-element.23), channel_id=1, source_target_pairs={{0,2},{2,0},{4,6},{6,4},{8,10},{10,8},{12,14},{14,12},{1,3},{3,1},... | collective-permute-start | bytes 1007624 | tf_op jit(solution)/shard_map/ppermute | solution.py:229
  28.9 0.2 collective-permute-start.1
  29.1 1.9 %collective-permute-start = (f32[8,128]{1,0:T(8,128)S(1)}, f32[8,128]{1,0:T(8,128)S(1)}, u32[]{:S(2)}, u32[]{:S(2)}) collective-permute-start(f32[8,128]{1,0:T(8,128)S(1)} %get-tuple-element.15), channel_id=1, source_target_pairs={{0,2},{2,0},{4,6},{6,4},{8,10},{10,8},{12,14},{14,12},{1,3},{3,1},... | collective-permute-start | bytes 12296 | tf_op jit(solution)/shard_map/ppermute | solution.py:229
  31.1 2.7 %collective-permute-start.8 = (f32[1,200,128]{2,1,0:T(8,128)S(1)}, f32[1,200,128]{2,1,0:T(8,128)S(1)}, u32[]{:S(2)}, u32[]{:S(2)}) collective-permute-start(f32[1,200,128]{2,1,0:T(8,128)S(1)} %get-tuple-element.28), channel_id=1, source_target_pairs={{0,8},{2,10},{4,12},{6,14},{8,0},{10,2},{12,4},{14,6},{1,9},{3,11}... | collective-permute-start | bytes 307208 | tf_op jit(solution)/shard_map/ppermute | solution.py:229
  33.8 1.5 %collective-permute-done.10 = f32[2,328,128]{2,1,0:T(8,128)S(1)} collective-permute-done((f32[2,328,128]{2,1,0:T(8,128)S(1)}, f32[2,328,128]{2,1,0:T(8,128)S(1)}, u32[]{:S(2)}, u32[]{:S(2)}) %collective-permute-start.10) | collective-permute-done | bytes 335904 | tf_op jit(solution)/shard_map/ppermute | solution.py:229
  35.3 2.5 %collective-permute-start.11 = (f32[1,328,128]{2,1,0:T(8,128)S(1)}, f32[1,328,128]{2,1,0:T(8,128)S(1)}, u32[]{:S(2)}, u32[]{:S(2)}) collective-permute-start(f32[1,328,128]{2,1,0:T(8,128)S(1)} %get-tuple-element.26), channel_id=1, source_target_pairs={{0,8},{2,10},{4,12},{6,14},{8,0},{10,2},{12,4},{14,6},{1,9},{3,11}... | collective-permute-start | bytes 503816 | tf_op jit(solution)/shard_map/ppermute | solution.py:229
  37.9 1.4 %collective-permute-start.5 = (f32[8,128]{1,0:T(8,128)S(1)}, f32[8,128]{1,0:T(8,128)S(1)}, u32[]{:S(2)}, u32[]{:S(2)}) collective-permute-start(f32[8,128]{1,0:T(8,128)S(1)} %add_add_fusion.refs_0_), channel_id=1, source_target_pairs={{0,12},{2,14},{4,8},{6,10},{8,4},{10,6},{12,0},{14,2},{1,13},{3,15... | collective-permute-start | bytes 12296 | tf_op jit(solution)/shard_map/ppermute | solution.py:229
  39.3 1.7 %collective-permute-start.4 = (f32[8,128]{1,0:T(8,128)S(1)}, f32[8,128]{1,0:T(8,128)S(1)}, u32[]{:S(2)}, u32[]{:S(2)}) collective-permute-start(f32[8,128]{1,0:T(8,128)S(1)} %add_add_fusion.refs_0_), channel_id=1, source_target_pairs={{0,8},{2,10},{4,12},{6,14},{8,0},{10,2},{12,4},{14,6},{1,9},{3,11}... | collective-permute-start | bytes 12296 | tf_op jit(solution)/shard_map/ppermute | solution.py:229
  41.0 1.3 %collective-permute-start.3 = (f32[8,128]{1,0:T(8,128)S(1)}, f32[8,128]{1,0:T(8,128)S(1)}, u32[]{:S(2)}, u32[]{:S(2)}) collective-permute-start(f32[8,128]{1,0:T(8,128)S(1)} %add_add_fusion.refs_0_), channel_id=1, source_target_pairs={{0,4},{2,6},{4,0},{6,2},{8,12},{10,14},{12,8},{14,10},{1,5},{3,7},... | collective-permute-start | bytes 12296 | tf_op jit(solution)/shard_map/ppermute | solution.py:229
  42.3 1.1 %collective-permute-done.5.refs_3_ = f32[8,128]{1,0:T(8,128)S(1)} collective-permute-done((f32[8,128]{1,0:T(8,128)S(1)}, f32[8,128]{1,0:T(8,128)S(1)}, u32[]{:S(2)}, u32[]{:S(2)}) %collective-permute-start.5) | collective-permute-done | bytes 4128 | tf_op jit(solution)/shard_map/ppermute | solution.py:229
  43.4 2.9 %collective-permute-done.4.refs_2_ = f32[8,128]{1,0:T(8,128)S(1)} collective-permute-done((f32[8,128]{1,0:T(8,128)S(1)}, f32[8,128]{1,0:T(8,128)S(1)}, u32[]{:S(2)}, u32[]{:S(2)}) %collective-permute-start.4) | collective-permute-done | bytes 4128 | tf_op jit(solution)/shard_map/ppermute | solution.py:229
  46.3 1.1 %shard_map.54 = (f32[320,128]{1,0:T(8,128)}, f32[640,128]{1,0:T(8,128)}) custom-call(f32[8,128]{1,0:T(8,128)S(1)} %add_add_fusion.refs_0_, f32[8,128]{1,0:T(8,128)S(1)} %collective-permute-done.3.refs_1_, f32[8,128]{1,0:T(8,128)S(1)} %collective-permute-done.4.refs_2_, f32[8,128]{1,0:T(8,128)S(1)} %collective-permute-done.5.refs_3_, ...), custom_call_target="tpu_custom_call" | custom-call | tf_op jit(solution)/shard_map/pallas_call | solution.py:213
  (23 shorter events, 0.2 us)
Async XLA Ops:
  0.6 1.1 %copy-start.4 = (bf16[128,2560]{1,0:T(8,128)(2,1)S(1)}, bf16[128,2560]{1,0:T(8,128)(2,1)}, u32[]{:S(2)}) copy-start(bf16[128,2560]{1,0:T(8,128)(2,1)} %refs_0_.6) | copy-start | bytes 1966084
  1.7 10.7 %copy-start.5 = (bf16[128,2560]{1,0:T(8,128)(2,1)S(1)}, bf16[128,2560]{1,0:T(8,128)(2,1)}, u32[]{:S(2)}) copy-start(bf16[128,2560]{1,0:T(8,128)(2,1)} %refs_0_.6) | copy-start | bytes 1966084
  3.1 1.3 %copy-start = (bf16[128,5120]{1,0:T(8,128)(2,1)S(1)}, bf16[128,5120]{1,0:T(8,128)(2,1)}, u32[]{:S(2)}) copy-start(bf16[128,5120]{1,0:T(8,128)(2,1)} %refs_0_.7) | copy-start | bytes 3932164
  4.4 1.3 %copy-start.2 = (bf16[128,5120]{1,0:T(8,128)(2,1)S(1)}, bf16[128,5120]{1,0:T(8,128)(2,1)}, u32[]{:S(2)}) copy-start(bf16[128,5120]{1,0:T(8,128)(2,1)} %refs_1_.3) | copy-start | bytes 3932164
  5.8 8.0 %copy-start.1 = (bf16[128,5120]{1,0:T(8,128)(2,1)S(1)}, bf16[128,5120]{1,0:T(8,128)(2,1)}, u32[]{:S(2)}) copy-start(bf16[128,5120]{1,0:T(8,128)(2,1)} %refs_0_.7) | copy-start | bytes 3932164
  5.8 8.1 %copy-start.3 = (bf16[128,5120]{1,0:T(8,128)(2,1)S(1)}, bf16[128,5120]{1,0:T(8,128)(2,1)}, u32[]{:S(2)}) copy-start(bf16[128,5120]{1,0:T(8,128)(2,1)} %refs_1_.3) | copy-start | bytes 3932164
  7.8 19.0 %collective-permute-start.9 = (f32[4,328,128]{2,1,0:T(8,128)S(1)}, f32[4,328,128]{2,1,0:T(8,128)S(1)}, u32[]{:S(2)}, u32[]{:S(2)}) collective-permute-start(f32[4,328,128]{2,1,0:T(8,128)S(1)} %get-tuple-element.19), channel_id=1, source_target_pairs={{0,4},{2,6},{4,0},{6,2},{8,12},{10,14},{12,8},{14,10},{1,5},{3,7},... | collective-permute-start | bytes 2015240 | tf_op jit(solution)/shard_map/ppermute | solution.py:229
  10.9 10.9 %collective-permute-start.6 = (f32[4,200,128]{2,1,0:T(8,128)S(1)}, f32[4,200,128]{2,1,0:T(8,128)S(1)}, u32[]{:S(2)}, u32[]{:S(2)}) collective-permute-start(f32[4,200,128]{2,1,0:T(8,128)S(1)} %get-tuple-element.17), channel_id=1, source_target_pairs={{0,2},{2,0},{4,6},{6,4},{8,10},{10,8},{12,14},{14,12},{1,3},{3,1},... | collective-permute-start | bytes 1228808 | tf_op jit(solution)/shard_map/ppermute | solution.py:229
  21.9 9.2 %collective-permute-start.7 = (f32[2,200,128]{2,1,0:T(8,128)S(1)}, f32[2,200,128]{2,1,0:T(8,128)S(1)}, u32[]{:S(2)}, u32[]{:S(2)}) collective-permute-start(f32[2,200,128]{2,1,0:T(8,128)S(1)} %get-tuple-element.25), channel_id=1, source_target_pairs={{0,4},{2,6},{4,0},{6,2},{8,12},{10,14},{12,8},{14,10},{1,5},{3,7},... | collective-permute-start | bytes 614408 | tf_op jit(solution)/shard_map/ppermute | solution.py:229
  26.9 8.4 %collective-permute-start.10 = (f32[2,328,128]{2,1,0:T(8,128)S(1)}, f32[2,328,128]{2,1,0:T(8,128)S(1)}, u32[]{:S(2)}, u32[]{:S(2)}) collective-permute-start(f32[2,328,128]{2,1,0:T(8,128)S(1)} %get-tuple-element.23), channel_id=1, source_target_pairs={{0,2},{2,0},{4,6},{6,4},{8,10},{10,8},{12,14},{14,12},{1,3},{3,1},... | collective-permute-start | bytes 1007624 | tf_op jit(solution)/shard_map/ppermute | solution.py:229
  28.9 8.9 %collective-permute-start.2 = (f32[8,128]{1,0:T(8,128)S(1)}, f32[8,128]{1,0:T(8,128)S(1)}, u32[]{:S(2)}, u32[]{:S(2)}) collective-permute-start(f32[8,128]{1,0:T(8,128)S(1)} %get-tuple-element.15), channel_id=1, source_target_pairs={{0,3},{1,2},{2,1},{3,0},{4,7},{5,6},{6,5},{7,4},{8,11},{9,10},{10,... | collective-permute-start | bytes 12296 | tf_op jit(solution)/shard_map/ppermute | solution.py:235
  28.9 8.9 %collective-permute-start.1 = (f32[8,128]{1,0:T(8,128)S(1)}, f32[8,128]{1,0:T(8,128)S(1)}, u32[]{:S(2)}, u32[]{:S(2)}) collective-permute-start(f32[8,128]{1,0:T(8,128)S(1)} %get-tuple-element.15), channel_id=1, source_target_pairs={{0,1},{1,0},{2,3},{3,2},{4,5},{5,4},{6,7},{7,6},{8,9},{9,8},{10,11... | collective-permute-start | bytes 12296 | tf_op jit(solution)/shard_map/ppermute | solution.py:235
  29.1 8.7 %collective-permute-start = (f32[8,128]{1,0:T(8,128)S(1)}, f32[8,128]{1,0:T(8,128)S(1)}, u32[]{:S(2)}, u32[]{:S(2)}) collective-permute-start(f32[8,128]{1,0:T(8,128)S(1)} %get-tuple-element.15), channel_id=1, source_target_pairs={{0,2},{2,0},{4,6},{6,4},{8,10},{10,8},{12,14},{14,12},{1,3},{3,1},... | collective-permute-start | bytes 12296 | tf_op jit(solution)/shard_map/ppermute | solution.py:229
  31.1 15.2 %collective-permute-start.8 = (f32[1,200,128]{2,1,0:T(8,128)S(1)}, f32[1,200,128]{2,1,0:T(8,128)S(1)}, u32[]{:S(2)}, u32[]{:S(2)}) collective-permute-start(f32[1,200,128]{2,1,0:T(8,128)S(1)} %get-tuple-element.28), channel_id=1, source_target_pairs={{0,8},{2,10},{4,12},{6,14},{8,0},{10,2},{12,4},{14,6},{1,9},{3,11}... | collective-permute-start | bytes 307208 | tf_op jit(solution)/shard_map/ppermute | solution.py:229
  35.3 11.0 %collective-permute-start.11 = (f32[1,328,128]{2,1,0:T(8,128)S(1)}, f32[1,328,128]{2,1,0:T(8,128)S(1)}, u32[]{:S(2)}, u32[]{:S(2)}) collective-permute-start(f32[1,328,128]{2,1,0:T(8,128)S(1)} %get-tuple-element.26), channel_id=1, source_target_pairs={{0,8},{2,10},{4,12},{6,14},{8,0},{10,2},{12,4},{14,6},{1,9},{3,11}... | collective-permute-start | bytes 503816 | tf_op jit(solution)/shard_map/ppermute | solution.py:229
  37.9 5.6 %collective-permute-start.5 = (f32[8,128]{1,0:T(8,128)S(1)}, f32[8,128]{1,0:T(8,128)S(1)}, u32[]{:S(2)}, u32[]{:S(2)}) collective-permute-start(f32[8,128]{1,0:T(8,128)S(1)} %add_add_fusion.refs_0_), channel_id=1, source_target_pairs={{0,12},{2,14},{4,8},{6,10},{8,4},{10,6},{12,0},{14,2},{1,13},{3,15... | collective-permute-start | bytes 12296 | tf_op jit(solution)/shard_map/ppermute | solution.py:229
  39.3 7.0 %collective-permute-start.4 = (f32[8,128]{1,0:T(8,128)S(1)}, f32[8,128]{1,0:T(8,128)S(1)}, u32[]{:S(2)}, u32[]{:S(2)}) collective-permute-start(f32[8,128]{1,0:T(8,128)S(1)} %add_add_fusion.refs_0_), channel_id=1, source_target_pairs={{0,8},{2,10},{4,12},{6,14},{8,0},{10,2},{12,4},{14,6},{1,9},{3,11}... | collective-permute-start | bytes 12296 | tf_op jit(solution)/shard_map/ppermute | solution.py:229
  41.0 5.4 %collective-permute-start.3 = (f32[8,128]{1,0:T(8,128)S(1)}, f32[8,128]{1,0:T(8,128)S(1)}, u32[]{:S(2)}, u32[]{:S(2)}) collective-permute-start(f32[8,128]{1,0:T(8,128)S(1)} %add_add_fusion.refs_0_), channel_id=1, source_target_pairs={{0,4},{2,6},{4,0},{6,2},{8,12},{10,14},{12,8},{14,10},{1,5},{3,7},... | collective-permute-start | bytes 12296 | tf_op jit(solution)/shard_map/ppermute | solution.py:229

commit v2 on v0

v2 whole, which is shorter than its diff:
```python
import functools

import jax
import jax.numpy as jnp
from jax import lax
from jax.experimental import pallas as pl
from jax.experimental.pallas import tpu as pltpu
from jax.sharding import PartitionSpec as P

D = 5120
FFW = 10240
B = 128
H = B // 2
EDGE = 8


def gelu_slope(value):
    return (
        0.5 * (1.0 + lax.erf(value * 0.7071067811865476))
        + value * jnp.exp(-0.5 * value * value) * 0.3989422804014327
    )


def local_blocks(matrix, block, total):
    tokens, width = matrix.shape
    pieces = matrix.reshape(tokens, width // block, block)
    cov = jnp.einsum("tkb,tkc->kbc", pieces, pieces, preferred_element_type=jnp.float32)
    return cov.reshape(width, block) / total


def owned_unit(owned, block):
    count = owned.shape[0]
    rows = lax.axis_index("dp") * count + jnp.arange(count, dtype=jnp.int32)
    cols = jnp.arange(block, dtype=jnp.int32)
    return (cols[None, :] == (rows % block)[:, None]).astype(jnp.float32)


def plain(saved_input, saved_pre, grad_act):
    total = jnp.float32(saved_input.shape[0] * lax.axis_size("dp"))
    slope = gelu_slope(saved_pre.astype(jnp.float32))
    grad_pre = (grad_act.astype(jnp.float32) * slope).astype(jnp.bfloat16)
    terms_a = local_blocks(saved_input, B, total)
    terms_g = local_blocks(grad_pre, B, total)
    owned_a = lax.psum_scatter(terms_a, "dp", scatter_dimension=0, tiled=True)
    owned_g = lax.psum_scatter(terms_g, "dp", scatter_dimension=0, tiled=True)
    unit_a = owned_unit(owned_a, B)
    unit_g = owned_unit(owned_g, B)
    trace_a, trace_g = lax.psum(
        (jnp.sum(owned_a * unit_a), jnp.sum(owned_g * unit_g)), ("dp", "tensor")
    )
    ratio = jnp.sqrt(trace_a / D / (trace_g / FFW))
    damp = jnp.sqrt(jnp.float32(0.1))
    return (
        (owned_a + ratio * damp * unit_a)[None],
        (owned_g + damp / ratio * unit_g)[None],
    )


def split_rows(count):
    return count // B, (count % B) // H


def piece_rows(piece):
    a_blocks, a_half, g_blocks, _ = piece
    return (len(a_blocks) + a_half + len(g_blocks)) * H + EDGE


def iotas():
    shape = (H, B)
    return lax.broadcasted_iota(jnp.int32, shape, 0), lax.broadcasted_iota(jnp.int32, shape, 1)


def slot_owner(slot, turn):
    flip = lax.axis_index("tensor") ^ turn
    high, middle, low = (slot >> 2) & 1, (slot >> 1) & 1, slot & 1
    mask = (high << flip) | (middle << (1 - flip)) | (low << 2)
    return lax.axis_index("dp") ^ mask


def lanes(start, size):
    return pl.ds(start if isinstance(start, int) else pl.multiple_of(start, B), size)


def pack_body(pieces, first, slots, count_a, count_g, *refs):
    n = len(pieces)
    a_hbm, pre_hbm, grad_hbm, trace_in = refs[:4]
    outs, trace_ref = refs[4 : 4 + n], refs[4 + n]
    buffers, sems = refs[5 + n : 5 + 4 * n], refs[5 + 4 * n]
    full, half = split_rows(count_a)
    row, col = iotas()
    low = col < row
    diag_low, diag_high = col == row, col == row + H
    zero = jnp.zeros((H, B), jnp.float32)

    def copies(i, slot):
        a_blocks, a_half, g_blocks, turn = pieces[i]
        a_buf, pre_buf, grad_buf = buffers[3 * i : 3 * i + 3]
        owner = slot_owner(first + slot, turn)
        found = []
        if a_blocks:
            start = owner * full * B if not half else (owner >> 1) * (2 * full + 1) * B + (owner & 1) * full * B
            found.append(
                pltpu.make_async_copy(
                    a_hbm.at[:, lanes(start, a_buf.shape[2])], a_buf.at[slot], sems.at[i, slot, 0]
                )
            )
        if g_blocks:
            start = owner * count_g + g_blocks[0] * B
            size = len(g_blocks) * B
            for k, (src, dst) in enumerate(((pre_hbm, pre_buf), (grad_hbm, grad_buf))):
                found.append(
                    pltpu.make_async_copy(
                        src.at[:, lanes(start, size)], dst.at[slot], sems.at[i, slot, 1 + k]
                    )
                )
        return found

    def cov(part):
        return lax.dot_general(
            part, part, (((0,), (0,)), ((), ())), preferred_element_type=jnp.float32
        )

    places = [(i, slot) for i in range(n) for slot in range(slots)]
    for place in places:
        for copy in copies(*place):
            copy.start()

    trace_a, trace_g = zero, zero
    for i, slot in places:
        a_blocks, a_half, g_blocks, turn = pieces[i]
        a_buf, pre_buf, grad_buf = buffers[3 * i : 3 * i + 3]
        out = outs[i]
        odd = slot_owner(first + slot, turn) & 1
        edge = piece_rows(pieces[i]) - EDGE
        for copy in copies(i, slot):
            copy.wait()
        at = 0
        corners = 0

        def fold(block):
            nonlocal at, corners
            top, bottom = block[:H], block[H:]
            out[slot, at * H : (at + 1) * H, :] = jnp.where(low, pltpu.roll(bottom, H, 1), top)
            corner = jnp.where(diag_high, bottom, zero)
            out[slot, edge + corners : edge + corners + 1, :] = jnp.sum(
                corner, axis=0, keepdims=True
            )
            at, corners = at + 1, corners + 1
            return corner + jnp.where(diag_low, top, zero)

        for b in a_blocks:
            place = (b + odd * half) * B
            trace_a = trace_a + fold(cov(a_buf[slot, :, lanes(place, B)]))
        if a_half:
            place = (1 - odd) * full * B
            block = cov(a_buf[slot, :, lanes(place, B)])
            part = jnp.where(odd == 1, block[H:], block[:H])
            out[slot, at * H : (at + 1) * H, :] = part
            trace_a = trace_a + jnp.where(col == row + odd * H, part, zero)
            at = at + 1
        for k in range(len(g_blocks)):
            here = slice(k * B, (k + 1) * B)
            value = pre_buf[slot, :, here].astype(jnp.float32)
            grad = grad_buf[slot, :, here].astype(jnp.float32)
            trace_g = trace_g + fold(cov((grad * gelu_slope(value)).astype(jnp.bfloat16)))
        out[slot, edge + corners :, :] = jnp.zeros((EDGE - corners, B), jnp.float32)

    trace_ref[...] = trace_in[...]
    trace_ref[0:1, :] += jnp.sum(trace_a, axis=0, keepdims=True)
    trace_ref[1:2, :] += jnp.sum(trace_g, axis=0, keepdims=True)


def pack(arrays, pieces, first, slots, count_a, count_g, trace):
    full, half = split_rows(count_a)
    tokens = arrays[0].shape[0]
    dtype = arrays[0].dtype
    scratch = []
    for a_blocks, _, g_blocks, _ in pieces:
        scratch.append(pltpu.VMEM((slots, tokens, (full + half) * B if a_blocks else B), dtype))
        for _ in range(2):
            scratch.append(pltpu.VMEM((slots, tokens, max(len(g_blocks), 1) * B), dtype))
    *chunks, trace = pl.pallas_call(
        functools.partial(pack_body, pieces, first, slots, count_a, count_g),
        in_specs=[pl.BlockSpec(memory_space=pltpu.HBM)] * 3
        + [pl.BlockSpec(memory_space=pltpu.VMEM)],
        out_specs=[pl.BlockSpec(memory_space=pltpu.VMEM)] * (len(pieces) + 1),
        out_shape=[
            jax.ShapeDtypeStruct((slots, piece_rows(piece), B), jnp.float32) for piece in pieces
        ]
        + [jax.ShapeDtypeStruct((EDGE, B), jnp.float32)],
        scratch_shapes=scratch + [pltpu.SemaphoreType.DMA((len(pieces), slots, 3))],
        compiler_params=pltpu.CompilerParams(vmem_limit_bytes=32 * 2**20),
        cost_estimate=pl.CostEstimate(flops=1, bytes_accessed=1, transcendentals=0),
    )(*arrays, trace)
    return chunks, trace


def finish_body(pieces, count_a, total, *refs):
    n = len(pieces)
    trace_ref, owns, gots = refs[0], refs[1 : 1 + n], refs[1 + n : 1 + 2 * n]
    a_ref, g_ref = refs[1 + 2 * n :]
    full, half = split_rows(count_a)
    odd = lax.axis_index("dp") & 1
    row, col = iotas()

    sums = trace_ref[...] + gots[-1][0, -2:, :]
    sums = jnp.sum(sums, axis=1, keepdims=True) / total
    ratio = jnp.sqrt(sums[0:1] / D / (sums[1:2] / FFW))
    damp = jnp.sqrt(jnp.full((1, 1), 0.1, jnp.float32))
    shift_a, shift_g = ratio * damp, damp / ratio

    def unfold(own, got, at, corner_row, shift, out, start):
        part = slice(at * H, (at + 1) * H)
        here = slice(corner_row, corner_row + 1)
        folded = (own[0, part, :] + got[0, part, :]) / total
        corner = (own[0, here, :] + got[0, here, :]) / total
        turned = jnp.concatenate([folded, folded], axis=0).T
        top = jnp.where(col < row, turned[:H], folded)
        last = pltpu.roll(jnp.where(col < row, folded, turned[:H]), H, 1)
        bottom = jnp.where(col < H, turned[H:], jnp.where(col == row + H, corner, last))
        out[pl.ds(start, H), :] = top + jnp.where(col == row, shift, 0.0)
        out[pl.ds(start + H, H), :] = bottom + jnp.where(col == row + H, shift, 0.0)

    for piece, own, got in zip(pieces, owns, gots):
        a_blocks, a_half, g_blocks, _ = piece
        at, corner = 0, piece_rows(piece) - EDGE
        for b in a_blocks:
            start = pl.multiple_of(b * B + odd * H, H) if half else b * B
            unfold(own, got, at, corner, shift_a, a_ref, start)
            at, corner = at + 1, corner + 1
        if a_half:
            part = slice(at * H, (at + 1) * H)
            value = (own[0, part, :] + got[0, part, :]) / total
            start = pl.multiple_of((1 - odd) * full * B, H)
            a_ref[pl.ds(start, H), :] = value + jnp.where(col == row + odd * H, shift_a, 0.0)
            at = at + 1
        for b in g_blocks:
            unfold(own, got, at, corner, shift_g, g_ref, b * B)
            at, corner = at + 1, corner + 1


def finish(pieces, trace, owns, gots, count_a, count_g, total):
    args = (trace, *owns, *gots)
    return pl.pallas_call(
        functools.partial(finish_body, pieces, count_a, total),
        in_specs=[pl.BlockSpec(memory_space=pltpu.VMEM)] * len(args),
        out_specs=[pl.BlockSpec(memory_space=pltpu.VMEM)] * 2,
        out_shape=[
            jax.ShapeDtypeStruct((count_a, B), jnp.float32),
            jax.ShapeDtypeStruct((count_g, B), jnp.float32),
        ],
        compiler_params=pltpu.CompilerParams(vmem_limit_bytes=32 * 2**20),
    )(*args)


def swap(value, partner):
    dp, tensor = lax.axis_size("dp"), lax.axis_size("tensor")
    pairs = []
    for i in range(dp):
        for j in range(tensor):
            other = partner(i, j)
            pairs.append((i * tensor + j, other[0] * tensor + other[1]))
    return lax.ppermute(value, ("dp", "tensor"), pairs)


def along(stage, turn):
    if stage == 2:
        return lambda i, j: (i ^ 4, j)
    return lambda i, j: (i ^ (1 << (j ^ turn ^ stage)), j)


def halve(keep, got):
    half = keep.shape[0] // 2
    return keep[:half] + got[:half], keep[half:] + got[half:]


def with_trace(send, trace):
    return lax.dynamic_update_slice(send, trace[None], (0, send.shape[1] - 2, 0))


def packed(saved_input, saved_pre, grad_act):
    dp = lax.axis_size("dp")
    total = float(saved_input.shape[0] * dp)
    count_a = saved_input.shape[1] // dp
    count_g = saved_pre.shape[1] // dp
    arrays = tuple(
        pltpu.with_memory_space_constraint(array, pltpu.HBM)
        for array in (saved_input, saved_pre, grad_act)
    )
    full_a, half_a = split_rows(count_a)
    full_g, _ = split_rows(count_g)
    pieces = (
        (tuple(range(full_a)), half_a, (0,), 0),
        ((), 0, tuple(range(1, full_g)), 1),
    )
    half = dp // 2
    blank = jnp.zeros((EDGE, B), jnp.float32)

    (send_p,), trace = pack(arrays, pieces[:1], half, half, count_a, count_g, blank)
    got_p = swap(send_p, along(0, 0))
    (send_q,), trace = pack(arrays, pieces[1:], half, half, count_a, count_g, trace)
    got_q = swap(send_q, along(0, 1))
    (keep_p, keep_q), trace = pack(arrays, pieces, 0, half, count_a, count_g, trace)
    trace = trace[:2] + swap(trace, lambda i, j: (i, j ^ 1))[:2]

    keep_p, send_p = halve(keep_p, got_p)
    got_p = swap(with_trace(send_p, trace), along(1, 0))
    trace = trace + got_p[0, -2:, :]
    keep_q, send_q = halve(keep_q, got_q)
    got_q = swap(with_trace(send_q, trace), along(1, 1))
    trace = trace + got_q[0, -2:, :]

    keep_p, send_p = halve(keep_p, got_p)
    got_p = swap(send_p, along(2, 0))
    keep_q, send_q = halve(keep_q, got_q)
    got_q = swap(with_trace(send_q, trace), along(2, 1))

    a_factor, g_factor = finish(
        pieces, trace, (keep_p, keep_q), (got_p, got_q), count_a, count_g, total
    )
    return a_factor[None], g_factor[None]


def fits(count_a, count_g):
    return count_a % H == 0 and 0 < count_a // B <= EDGE - 3 and count_g % B == 0 and 1 < count_g // B <= EDGE - 1


def on_device(saved_input, saved_pre, grad_act):
    dp = lax.axis_size("dp")
    count_a = saved_input.shape[1] // dp
    count_g = saved_pre.shape[1] // dp
    if dp == 8 and lax.axis_size("tensor") == 2 and fits(count_a, count_g):
        return packed(saved_input, saved_pre, grad_act)
    return plain(saved_input, saved_pre, grad_act)


def solution(mesh):
    spec = P(("groups", "dp"), "tensor")
    out = P("tensor", ("groups", "dp"), None)
    return jax.shard_map(
        on_device, mesh=mesh, in_specs=(spec, spec, spec), out_specs=(out, out), check_vma=False
    )
```

time: 196 us -> 41.3 us (0.21)
  waiting for transfers between devices: 135 us -> 15.1 us
  blocking collectives: 31.3 us -> 0 us
  starting transfers between devices: 0.08 us -> 15.1 us
  between operations: 15.5 us -> 0.69 us
  Pallas kernels: 0 us -> 9.91 us
  other arithmetic: 6.92 us -> 0.28 us
  matrix products: 5.75 us -> 0 us
    reduce_scatter x2 -> x0, waiting for transfers between devices: 135 us -> none  [the longest x1 71.2 us: on_device(): owned_g = lax.psum_scatter(terms_g, 'dp', scatter_dimension=0, tiled=True)]
    psum x1 -> x0, blocking collectives: 31.3 us -> none  [on_device(): lax.psum((jnp.sum(owned_a * unit_a), jnp.sum(owned_g * unit_g)), ('dp', '...]
    ppermute x0 -> x7, waiting for transfers between devices: none -> 15.1 us  [swap(): return lax.ppermute(value, ('dp', 'tensor'), pairs)]
    ppermute x0 -> x7, starting transfers between devices: none -> 15.1 us  [swap(): return lax.ppermute(value, ('dp', 'tensor'), pairs)]
    pallas_call x0 -> x4, Pallas kernels: none -> 9.91 us  [the longest x3 8.84 us: pack(): pl.pallas_call(functools.partial(pack_body, pieces, first, slots, count_a...]
    dot_general x2 -> x0, matrix products: 5.75 us -> none  [local_blocks(): jnp.einsum('tkb,tkc->kbc', pieces, pieces, preferred_element_type=jnp.flo...]
    broadcast_in_dim x2 -> x0, other arithmetic: 3.54 us -> none  [the longest x1 1.85 us: on_device(): g_factor = (owned_g + damp / ratio * unit_g)[None]]
    reduce_sum x2 -> x0, other arithmetic: 3.36 us -> none  [the longest x1 1.73 us: on_device(): jnp.sum(owned_g * unit_g)]
  transfers between devices with their start and end apart: 2 -> 7, of which waited for: 2 -> 5; matrix products, arithmetic and copies ran while one was open for 3% -> 1% of each run, Pallas kernels for 0% -> 16%
where the time goes in v2:
time: 41.3 us; the launch traced here: 41.1 us
  starting transfers between devices  15.1 us (37%)
  waiting for transfers between devices  15.1 us (37%)
  Pallas kernels  9.91 us (24%)
  between operations  0.69 us (2%)
    ppermute x7, waiting for transfers between devices, swap(): return lax.ppermute(value, ('dp', 'tensor'), pairs)  15.1 us
    ppermute x7, starting transfers between devices, swap(): return lax.ppermute(value, ('dp', 'tensor'), pairs)  15.1 us
    pallas_call x3, Pallas kernels, pack(): pl.pallas_call(functools.partial(pack_body, pieces, first, slots, count_a...  8.84 us
    pallas_call x1, Pallas kernels, finish(): pl.pallas_call(functools.partial(finish_body, pieces, count_a, total), in...  1.07 us
  transfers between devices with their start and end apart: 7, of which 5 were waited for; matrix products, arithmetic and copies ran while one was open for 1% of the time, Pallas kernels for 16%

profile of v2, /device:TPU:0, one launch (start us, length us, event | category | flops | bytes accessed | tf_op | source)
XLA Modules:
  0.0 41.1 jit_solution(3131830100792655259)
XLA Ops:
  0.6 2.2 %shard_map.50 = (f32[4,264,128]{2,1,0:T(8,128)S(1)}, f32[8,128]{1,0:T(8,128)S(1)}) custom-call(bf16[128,2560]{1,0:T(8,128)(2,1)} %refs_0_.5, bf16[128,5120]{1,0:T(8,128)(2,1)} %refs_1_.5, bf16[128,5120]{1,0:T(8,128)(2,1)} %refs_2_.5, f32[8,128]{1,0:T(8,128)S(1)} %broadcast_in_dim.18.refs_3_), custom_call_target="tpu_custom_call" | custom-call | flops 1 | bytes 1 | tf_op jit(solution)/shard_map/pallas_call | solution.py:182
  2.9 3.0 %collective-permute-start.1 = (f32[4,264,128]{2,1,0:T(8,128)S(1)}, f32[4,264,128]{2,1,0:T(8,128)S(1)}, u32[]{:S(2)}, u32[]{:S(2)}) collective-permute-start(f32[4,264,128]{2,1,0:T(8,128)S(1)} %get-tuple-element.15), channel_id=1, source_target_pairs={{0,2},{1,5},{2,0},{3,7},{4,6},{5,1},{6,4},{7,3},{8,10},{9,13},{10,... | collective-permute-start | bytes 1622024 | tf_op jit(solution)/shard_map/ppermute | solution.py:263
  5.9 2.7 %shard_map.51 = (f32[4,264,128]{2,1,0:T(8,128)S(1)}, f32[8,128]{1,0:T(8,128)S(1)}) custom-call(bf16[128,2560]{1,0:T(8,128)(2,1)} %refs_0_.5, bf16[128,5120]{1,0:T(8,128)(2,1)} %refs_1_.5, bf16[128,5120]{1,0:T(8,128)(2,1)} %refs_2_.5, f32[8,128]{1,0:T(8,128)S(1)} %get-tuple-element.11.refs_3_), custom_call_target="tpu_custom_call" | custom-call | flops 1 | bytes 1 | tf_op jit(solution)/shard_map/pallas_call | solution.py:182
  8.6 1.6 %collective-permute-start.3 = (f32[4,264,128]{2,1,0:T(8,128)S(1)}, f32[4,264,128]{2,1,0:T(8,128)S(1)}, u32[]{:S(2)}, u32[]{:S(2)}) collective-permute-start(f32[4,264,128]{2,1,0:T(8,128)S(1)} %get-tuple-element.17), channel_id=1, source_target_pairs={{0,4},{1,3},{2,6},{3,1},{4,0},{5,7},{6,2},{7,5},{8,12},{9,11},{10,... | collective-permute-start | bytes 1622024 | tf_op jit(solution)/shard_map/ppermute | solution.py:263
  10.2 3.9 %shard_map.52 = (f32[4,264,128]{2,1,0:T(8,128)S(1)}, f32[4,264,128]{2,1,0:T(8,128)S(1)}, f32[8,128]{1,0:T(8,128)S(1)}) custom-call(bf16[128,2560]{1,0:T(8,128)(2,1)} %refs_0_.5, bf16[128,5120]{1,0:T(8,128)(2,1)} %refs_1_.5, bf16[128,5120]{1,0:T(8,128)(2,1)} %refs_2_.5, f32[8,128]{1,0:T(8,128)S(1)} %get-tuple-element.12.refs_3_), custom_call_target="tpu_custom_call" | custom-call | flops 1 | bytes 1 | tf_op jit(solution)/shard_map/pallas_call | solution.py:182
  14.2 0.1 collective-permute-start
  14.2 1.3 %collective-permute-done.1 = f32[4,264,128]{2,1,0:T(8,128)S(1)} collective-permute-done((f32[4,264,128]{2,1,0:T(8,128)S(1)}, f32[4,264,128]{2,1,0:T(8,128)S(1)}, u32[]{:S(2)}, u32[]{:S(2)}) %collective-permute-start.1) | collective-permute-done | bytes 540704 | tf_op jit(solution)/shard_map/ppermute | solution.py:263
  15.6 0.1 slice_add_fusion.1
  15.6 0.0 collective-permute-done
  15.7 3.9 %collective-permute-start.2 = (f32[2,264,128]{2,1,0:T(8,128)S(1)}, f32[2,264,128]{2,1,0:T(8,128)S(1)}, u32[]{:S(2)}, u32[]{:S(2)}) collective-permute-start(f32[2,264,128]{2,1,0:T(8,128)S(1)} %bitcast_dynamic-update-slice_fusion.2), channel_id=1, source_target_pairs={{0,4},{1,3},{2,6},{3,1},{4,0},{5,7},{6,2},{7,5},{8,12},{9,11},{10,... | collective-permute-start | bytes 811016 | tf_op jit(solution)/shard_map/ppermute | solution.py:263
  19.6 0.0 collective-permute-done.3
  19.6 0.1 slice_add_fusion
  19.7 4.3 %collective-permute-done.2 = f32[2,264,128]{2,1,0:T(8,128)S(1)} collective-permute-done((f32[2,264,128]{2,1,0:T(8,128)S(1)}, f32[2,264,128]{2,1,0:T(8,128)S(1)}, u32[]{:S(2)}, u32[]{:S(2)}) %collective-permute-start.2) | collective-permute-done | bytes 270368 | tf_op jit(solution)/shard_map/ppermute | solution.py:263
  24.0 1.4 %collective-permute-start.4 = (f32[2,264,128]{2,1,0:T(8,128)S(1)}, f32[2,264,128]{2,1,0:T(8,128)S(1)}, u32[]{:S(2)}, u32[]{:S(2)}) collective-permute-start(f32[2,264,128]{2,1,0:T(8,128)S(1)} %bitcast_dynamic-update-slice_fusion.1), channel_id=1, source_target_pairs={{0,2},{1,5},{2,0},{3,7},{4,6},{5,1},{6,4},{7,3},{8,10},{9,13},{10,... | collective-permute-start | bytes 811016 | tf_op jit(solution)/shard_map/ppermute | solution.py:263
  25.4 2.6 %collective-permute-start.5 = (f32[1,264,128]{2,1,0:T(8,128)S(1)}, f32[1,264,128]{2,1,0:T(8,128)S(1)}, u32[]{:S(2)}, u32[]{:S(2)}) collective-permute-start(f32[1,264,128]{2,1,0:T(8,128)S(1)} %get-tuple-element.26), channel_id=1, source_target_pairs={{0,8},{1,9},{2,10},{3,11},{4,12},{5,13},{6,14},{7,15},{8,0},{9,1},... | collective-permute-start | bytes 405512 | tf_op jit(solution)/shard_map/ppermute | solution.py:263
  28.1 2.4 %collective-permute-done.4 = f32[2,264,128]{2,1,0:T(8,128)S(1)} collective-permute-done((f32[2,264,128]{2,1,0:T(8,128)S(1)}, f32[2,264,128]{2,1,0:T(8,128)S(1)}, u32[]{:S(2)}, u32[]{:S(2)}) %collective-permute-start.4) | collective-permute-done | bytes 270368 | tf_op jit(solution)/shard_map/ppermute | solution.py:263
  30.5 2.5 %collective-permute-start.6 = (f32[1,264,128]{2,1,0:T(8,128)S(1)}, f32[1,264,128]{2,1,0:T(8,128)S(1)}, u32[]{:S(2)}, u32[]{:S(2)}) collective-permute-start(f32[1,264,128]{2,1,0:T(8,128)S(1)} %get-tuple-element.20), channel_id=1, source_target_pairs={{0,8},{1,9},{2,10},{3,11},{4,12},{5,13},{6,14},{7,15},{8,0},{9,1},... | collective-permute-start | bytes 405512 | tf_op jit(solution)/shard_map/ppermute | solution.py:263
  33.0 5.3 %collective-permute-done.5.refs_3_ = f32[1,264,128]{2,1,0:T(8,128)S(1)} collective-permute-done((f32[1,264,128]{2,1,0:T(8,128)S(1)}, f32[1,264,128]{2,1,0:T(8,128)S(1)}, u32[]{:S(2)}, u32[]{:S(2)}) %collective-permute-start.5) | collective-permute-done | bytes 135200 | tf_op jit(solution)/shard_map/ppermute | solution.py:263
  38.4 1.7 %collective-permute-done.6.refs_4_ = f32[1,264,128]{2,1,0:T(8,128)S(1)} collective-permute-done((f32[1,264,128]{2,1,0:T(8,128)S(1)}, f32[1,264,128]{2,1,0:T(8,128)S(1)}, u32[]{:S(2)}, u32[]{:S(2)}) %collective-permute-start.6) | collective-permute-done | bytes 135200 | tf_op jit(solution)/shard_map/ppermute | solution.py:263
  40.1 1.1 %shard_map.53 = (f32[320,128]{1,0:T(8,128)}, f32[640,128]{1,0:T(8,128)}) custom-call(f32[2,128]{1,0:T(2,128)S(1)} %get-tuple-element.21.refs_0_, f32[1,264,128]{2,1,0:T(8,128)S(1)} %get-tuple-element.27.refs_1_, f32[1,264,128]{2,1,0:T(8,128)S(1)} %get-tuple-element.28.refs_2_, f32[1,264,128]{2,1,0:T(8,128)S(1)} %collective-permute-done.5.refs_3_, ...), custom_call_target="tpu_custom_call" | custom-call | tf_op jit(solution)/shard_map/pallas_call | solution.py:244
  (6 shorter events, 0.1 us)
Async XLA Ops:
  2.9 12.7 %collective-permute-start.1 = (f32[4,264,128]{2,1,0:T(8,128)S(1)}, f32[4,264,128]{2,1,0:T(8,128)S(1)}, u32[]{:S(2)}, u32[]{:S(2)}) collective-permute-start(f32[4,264,128]{2,1,0:T(8,128)S(1)} %get-tuple-element.15), channel_id=1, source_target_pairs={{0,2},{1,5},{2,0},{3,7},{4,6},{5,1},{6,4},{7,3},{8,10},{9,13},{10,... | collective-permute-start | bytes 1622024 | tf_op jit(solution)/shard_map/ppermute | solution.py:263
  8.6 11.0 %collective-permute-start.3 = (f32[4,264,128]{2,1,0:T(8,128)S(1)}, f32[4,264,128]{2,1,0:T(8,128)S(1)}, u32[]{:S(2)}, u32[]{:S(2)}) collective-permute-start(f32[4,264,128]{2,1,0:T(8,128)S(1)} %get-tuple-element.17), channel_id=1, source_target_pairs={{0,4},{1,3},{2,6},{3,1},{4,0},{5,7},{6,2},{7,5},{8,12},{9,11},{10,... | collective-permute-start | bytes 1622024 | tf_op jit(solution)/shard_map/ppermute | solution.py:263
  14.2 1.5 %collective-permute-start = (f32[8,128]{1,0:T(8,128)S(1)}, f32[8,128]{1,0:T(8,128)S(1)}, u32[]{:S(2)}, u32[]{:S(2)}) collective-permute-start(f32[8,128]{1,0:T(8,128)S(1)} %get-tuple-element.13), channel_id=1, source_target_pairs={{0,1},{1,0},{2,3},{3,2},{4,5},{5,4},{6,7},{7,6},{8,9},{9,8},{10,11... | collective-permute-start | bytes 12296 | tf_op jit(solution)/shard_map/ppermute | solution.py:263
  15.7 8.3 %collective-permute-start.2 = (f32[2,264,128]{2,1,0:T(8,128)S(1)}, f32[2,264,128]{2,1,0:T(8,128)S(1)}, u32[]{:S(2)}, u32[]{:S(2)}) collective-permute-start(f32[2,264,128]{2,1,0:T(8,128)S(1)} %bitcast_dynamic-update-slice_fusion.2), channel_id=1, source_target_pairs={{0,4},{1,3},{2,6},{3,1},{4,0},{5,7},{6,2},{7,5},{8,12},{9,11},{10,... | collective-permute-start | bytes 811016 | tf_op jit(solution)/shard_map/ppermute | solution.py:263
  24.0 6.5 %collective-permute-start.4 = (f32[2,264,128]{2,1,0:T(8,128)S(1)}, f32[2,264,128]{2,1,0:T(8,128)S(1)}, u32[]{:S(2)}, u32[]{:S(2)}) collective-permute-start(f32[2,264,128]{2,1,0:T(8,128)S(1)} %bitcast_dynamic-update-slice_fusion.1), channel_id=1, source_target_pairs={{0,2},{1,5},{2,0},{3,7},{4,6},{5,1},{6,4},{7,3},{8,10},{9,13},{10,... | collective-permute-start | bytes 811016 | tf_op jit(solution)/shard_map/ppermute | solution.py:263
  25.4 13.0 %collective-permute-start.5 = (f32[1,264,128]{2,1,0:T(8,128)S(1)}, f32[1,264,128]{2,1,0:T(8,128)S(1)}, u32[]{:S(2)}, u32[]{:S(2)}) collective-permute-start(f32[1,264,128]{2,1,0:T(8,128)S(1)} %get-tuple-element.26), channel_id=1, source_target_pairs={{0,8},{1,9},{2,10},{3,11},{4,12},{5,13},{6,14},{7,15},{8,0},{9,1},... | collective-permute-start | bytes 405512 | tf_op jit(solution)/shard_map/ppermute | solution.py:263
  30.5 9.5 %collective-permute-start.6 = (f32[1,264,128]{2,1,0:T(8,128)S(1)}, f32[1,264,128]{2,1,0:T(8,128)S(1)}, u32[]{:S(2)}, u32[]{:S(2)}) collective-permute-start(f32[1,264,128]{2,1,0:T(8,128)S(1)} %get-tuple-element.20), channel_id=1, source_target_pairs={{0,8},{1,9},{2,10},{3,11},{4,12},{5,13},{6,14},{7,15},{8,0},{9,1},... | collective-permute-start | bytes 405512 | tf_op jit(solution)/shard_map/ppermute | solution.py:263

commit v3 on v2

--- a/solution.py
+++ b/solution.py
@@ -62,7 +62,8 @@
 
 def piece_rows(piece):
     a_blocks, a_half, g_blocks, _ = piece
-    return (len(a_blocks) + a_half + len(g_blocks)) * H + EDGE
+    edge = (len(a_blocks) + a_half + len(g_blocks)) * H
+    return edge + (EDGE if a_blocks or a_half else len(g_blocks) + 2), edge
 
 
 def iotas():
@@ -70,10 +71,11 @@
     return lax.broadcasted_iota(jnp.int32, shape, 0), lax.broadcasted_iota(jnp.int32, shape, 1)
 
 
-def slot_owner(slot, turn):
-    flip = lax.axis_index("tensor") ^ turn
-    high, middle, low = (slot >> 2) & 1, (slot >> 1) & 1, slot & 1
-    mask = (high << flip) | (middle << (1 - flip)) | (low << 2)
+def slot_owner(slot, orders):
+    core = lax.axis_index("tensor")
+    mask = 0
+    for stage, (one, other) in enumerate(zip(*orders)):
+        mask = mask | (((slot >> (2 - stage)) & 1) << (one + core * (other - one)))
     return lax.axis_index("dp") ^ mask
 
 
@@ -85,7 +87,7 @@
     n = len(pieces)
     a_hbm, pre_hbm, grad_hbm, trace_in = refs[:4]
     outs, trace_ref = refs[4 : 4 + n], refs[4 + n]
-    buffers, sems = refs[5 + n : 5 + 4 * n], refs[5 + 4 * n]
+    buffers, sems = refs[5 + n : 5 + 5 * n], refs[5 + 5 * n]
     full, half = split_rows(count_a)
     row, col = iotas()
     low = col < row
@@ -93,27 +95,26 @@
     zero = jnp.zeros((H, B), jnp.float32)
 
     def copies(i, slot):
-        a_blocks, a_half, g_blocks, turn = pieces[i]
-        a_buf, pre_buf, grad_buf = buffers[3 * i : 3 * i + 3]
-        owner = slot_owner(first + slot, turn)
-        found = []
+        a_blocks, a_half, g_blocks, orders = pieces[i]
+        a_buf, half_buf, pre_buf, grad_buf = buffers[4 * i : 4 * i + 4]
+        owner = slot_owner(first + slot, orders)
+        odd = owner & half
+        base = (owner >> half) * (full * (1 + half) + half) * B
+        moves = []
         if a_blocks:
-            start = owner * full * B if not half else (owner >> 1) * (2 * full + 1) * B + (owner & 1) * full * B
-            found.append(
-                pltpu.make_async_copy(
-                    a_hbm.at[:, lanes(start, a_buf.shape[2])], a_buf.at[slot], sems.at[i, slot, 0]
-                )
-            )
+            start = base + odd * (full + 1) * B + a_blocks[0] * B
+            moves.append((a_hbm, start, a_buf))
+        if a_half:
+            moves.append((a_hbm, base + full * B, half_buf))
         if g_blocks:
             start = owner * count_g + g_blocks[0] * B
-            size = len(g_blocks) * B
-            for k, (src, dst) in enumerate(((pre_hbm, pre_buf), (grad_hbm, grad_buf))):
-                found.append(
-                    pltpu.make_async_copy(
-                        src.at[:, lanes(start, size)], dst.at[slot], sems.at[i, slot, 1 + k]
-                    )
-                )
-        return found
+            moves += [(pre_hbm, start, pre_buf), (grad_hbm, start, grad_buf)]
+        return [
+            pltpu.make_async_copy(
+                src.at[:, lanes(start, dst.shape[2])], dst.at[slot], sems.at[i, slot, k]
+            )
+            for k, (src, start, dst) in enumerate(moves)
+        ]
 
     def cov(part):
         return lax.dot_general(
@@ -127,11 +128,11 @@
 
     trace_a, trace_g = zero, zero
     for i, slot in places:
-        a_blocks, a_half, g_blocks, turn = pieces[i]
-        a_buf, pre_buf, grad_buf = buffers[3 * i : 3 * i + 3]
+        a_blocks, a_half, g_blocks, orders = pieces[i]
+        a_buf, half_buf, pre_buf, grad_buf = buffers[4 * i : 4 * i + 4]
         out = outs[i]
-        odd = slot_owner(first + slot, turn) & 1
-        edge = piece_rows(pieces[i]) - EDGE
+        odd = slot_owner(first + slot, orders) & half
+        rows, edge = piece_rows(pieces[i])
         for copy in copies(i, slot):
             copy.wait()
         at = 0
@@ -148,12 +149,10 @@
             at, corners = at + 1, corners + 1
             return corner + jnp.where(diag_low, top, zero)
 
-        for b in a_blocks:
-            place = (b + odd * half) * B
-            trace_a = trace_a + fold(cov(a_buf[slot, :, lanes(place, B)]))
+        for k in range(len(a_blocks)):
+            trace_a = trace_a + fold(cov(a_buf[slot, :, k * B : (k + 1) * B]))
         if a_half:
-            place = (1 - odd) * full * B
-            block = cov(a_buf[slot, :, lanes(place, B)])
+            block = cov(half_buf[slot])
             part = jnp.where(odd == 1, block[H:], block[:H])
             out[slot, at * H : (at + 1) * H, :] = part
             trace_a = trace_a + jnp.where(col == row + odd * H, part, zero)
@@ -163,7 +162,7 @@
             value = pre_buf[slot, :, here].astype(jnp.float32)
             grad = grad_buf[slot, :, here].astype(jnp.float32)
             trace_g = trace_g + fold(cov((grad * gelu_slope(value)).astype(jnp.bfloat16)))
-        out[slot, edge + corners :, :] = jnp.zeros((EDGE - corners, B), jnp.float32)
+        out[slot, edge + corners :, :] = jnp.zeros((rows - edge - corners, B), jnp.float32)
 
     trace_ref[...] = trace_in[...]
     trace_ref[0:1, :] += jnp.sum(trace_a, axis=0, keepdims=True)
@@ -171,39 +170,37 @@
 
 
 def pack(arrays, pieces, first, slots, count_a, count_g, trace):
-    full, half = split_rows(count_a)
-    tokens = arrays[0].shape[0]
-    dtype = arrays[0].dtype
-    scratch = []
-    for a_blocks, _, g_blocks, _ in pieces:
-        scratch.append(pltpu.VMEM((slots, tokens, (full + half) * B if a_blocks else B), dtype))
-        for _ in range(2):
-            scratch.append(pltpu.VMEM((slots, tokens, max(len(g_blocks), 1) * B), dtype))
+    tokens, dtype = arrays[0].shape[0], arrays[0].dtype
+    scratch = [
+        pltpu.VMEM((slots, tokens, max(size, 1) * B), dtype)
+        for a_blocks, _, g_blocks, _ in pieces
+        for size in (len(a_blocks), 1, len(g_blocks), len(g_blocks))
+    ]
     *chunks, trace = pl.pallas_call(
         functools.partial(pack_body, pieces, first, slots, count_a, count_g),
         in_specs=[pl.BlockSpec(memory_space=pltpu.HBM)] * 3
         + [pl.BlockSpec(memory_space=pltpu.VMEM)],
         out_specs=[pl.BlockSpec(memory_space=pltpu.VMEM)] * (len(pieces) + 1),
         out_shape=[
-            jax.ShapeDtypeStruct((slots, piece_rows(piece), B), jnp.float32) for piece in pieces
+            jax.ShapeDtypeStruct((slots, piece_rows(piece)[0], B), jnp.float32) for piece in pieces
         ]
         + [jax.ShapeDtypeStruct((EDGE, B), jnp.float32)],
-        scratch_shapes=scratch + [pltpu.SemaphoreType.DMA((len(pieces), slots, 3))],
+        scratch_shapes=scratch + [pltpu.SemaphoreType.DMA((len(pieces), slots, 4))],
         compiler_params=pltpu.CompilerParams(vmem_limit_bytes=32 * 2**20),
         cost_estimate=pl.CostEstimate(flops=1, bytes_accessed=1, transcendentals=0),
     )(*arrays, trace)
     return chunks, trace
 
 
-def finish_body(pieces, count_a, total, *refs):
+def finish_body(pieces, n_traces, count_a, total, *refs):
     n = len(pieces)
-    trace_ref, owns, gots = refs[0], refs[1 : 1 + n], refs[1 + n : 1 + 2 * n]
-    a_ref, g_ref = refs[1 + 2 * n :]
+    traces, refs = refs[:n_traces], refs[n_traces:]
+    owns, gots, (a_ref, g_ref) = refs[:n], refs[n : 2 * n], refs[2 * n :]
     full, half = split_rows(count_a)
-    odd = lax.axis_index("dp") & 1
+    odd = lax.axis_index("dp") & half
     row, col = iotas()
 
-    sums = trace_ref[...] + gots[-1][0, -2:, :]
+    sums = sum((trace[...] for trace in traces[1:]), traces[0][...])
     sums = jnp.sum(sums, axis=1, keepdims=True) / total
     ratio = jnp.sqrt(sums[0:1] / D / (sums[1:2] / FFW))
     damp = jnp.sqrt(jnp.full((1, 1), 0.1, jnp.float32))
@@ -223,7 +220,7 @@
 
     for piece, own, got in zip(pieces, owns, gots):
         a_blocks, a_half, g_blocks, _ = piece
-        at, corner = 0, piece_rows(piece) - EDGE
+        at, corner = 0, piece_rows(piece)[1]
         for b in a_blocks:
             start = pl.multiple_of(b * B + odd * H, H) if half else b * B
             unfold(own, got, at, corner, shift_a, a_ref, start)
@@ -239,10 +236,10 @@
             at, corner = at + 1, corner + 1
 
 
-def finish(pieces, trace, owns, gots, count_a, count_g, total):
-    args = (trace, *owns, *gots)
+def finish(pieces, traces, owns, gots, count_a, count_g, total):
+    args = (*traces, *owns, *gots)
     return pl.pallas_call(
-        functools.partial(finish_body, pieces, count_a, total),
+        functools.partial(finish_body, pieces, len(traces), count_a, total),
         in_specs=[pl.BlockSpec(memory_space=pltpu.VMEM)] * len(args),
         out_specs=[pl.BlockSpec(memory_space=pltpu.VMEM)] * 2,
         out_shape=[
@@ -263,10 +260,8 @@
     return lax.ppermute(value, ("dp", "tensor"), pairs)
 
 
-def along(stage, turn):
-    if stage == 2:
-        return lambda i, j: (i ^ 4, j)
-    return lambda i, j: (i ^ (1 << (j ^ turn ^ stage)), j)
+def along(stage, orders):
+    return lambda i, j: (i ^ (1 << orders[j][stage]), j)
 
 
 def halve(keep, got):
@@ -276,6 +271,18 @@
 
 def with_trace(send, trace):
     return lax.dynamic_update_slice(send, trace[None], (0, send.shape[1] - 2, 0))
+
+
+def cut(count_a, count_g):
+    full_a, half_a = split_rows(count_a)
+    full_g, _ = split_rows(count_g)
+    some = full_g // 2
+    x, near, far = 0, 1, 2
+    return (
+        (tuple(range(full_a)), 0, (), ((near, x, far), (far, x, near))),
+        ((), half_a, tuple(range(some)), ((x, near, far), (x, far, near))),
+        ((), 0, tuple(range(some, full_g)), ((far, x, near), (near, x, far))),
+    )
 
 
 def packed(saved_input, saved_pre, grad_act):
@@ -287,42 +294,38 @@
         pltpu.with_memory_space_constraint(array, pltpu.HBM)
         for array in (saved_input, saved_pre, grad_act)
     )
-    full_a, half_a = split_rows(count_a)
-    full_g, _ = split_rows(count_g)
-    pieces = (
-        (tuple(range(full_a)), half_a, (0,), 0),
-        ((), 0, tuple(range(1, full_g)), 1),
-    )
     half = dp // 2
-    blank = jnp.zeros((EDGE, B), jnp.float32)
-
-    (send_p,), trace = pack(arrays, pieces[:1], half, half, count_a, count_g, blank)
-    got_p = swap(send_p, along(0, 0))
-    (send_q,), trace = pack(arrays, pieces[1:], half, half, count_a, count_g, trace)
-    got_q = swap(send_q, along(0, 1))
-    (keep_p, keep_q), trace = pack(arrays, pieces, 0, half, count_a, count_g, trace)
+    pieces = cut(count_a, count_g)
+    chunks = range(len(pieces))
+
+    trace = jnp.zeros((EDGE, B), jnp.float32)
+    gots = []
+    for part in (pieces[:1], pieces[1:]):
+        sends, trace = pack(arrays, part, half, half, count_a, count_g, trace)
+        gots += [swap(send, along(0, piece[3])) for send, piece in zip(sends, part)]
+    keeps, trace = pack(arrays, pieces, 0, half, count_a, count_g, trace)
+
     trace = trace[:2] + swap(trace, lambda i, j: (i, j ^ 1))[:2]
-
-    keep_p, send_p = halve(keep_p, got_p)
-    got_p = swap(with_trace(send_p, trace), along(1, 0))
-    trace = trace + got_p[0, -2:, :]
-    keep_q, send_q = halve(keep_q, got_q)
-    got_q = swap(with_trace(send_q, trace), along(1, 1))
-    trace = trace + got_q[0, -2:, :]
-
-    keep_p, send_p = halve(keep_p, got_p)
-    got_p = swap(send_p, along(2, 0))
-    keep_q, send_q = halve(keep_q, got_q)
-    got_q = swap(with_trace(send_q, trace), along(2, 1))
-
-    a_factor, g_factor = finish(
-        pieces, trace, (keep_p, keep_q), (got_p, got_q), count_a, count_g, total
-    )
+    last = len(pieces) - 1
+    carriers = ((0, 1), (0, 2), (last, 2))
+    for stage in (1, 2):
+        for k in chunks:
+            keeps[k], send = halve(keeps[k], gots[k])
+            if (k, stage) in carriers:
+                if (k, stage) != carriers[0]:
+                    trace = trace + news
+                send = with_trace(send, trace)
+            gots[k] = swap(send, along(stage, pieces[k][3]))
+            if (k, stage) in carriers:
+                news = gots[k][0, -2:, :]
+
+    a_factor, g_factor = finish(pieces, (trace, news), keeps, gots, count_a, count_g, total)
     return a_factor[None], g_factor[None]
 
 
 def fits(count_a, count_g):
-    return count_a % H == 0 and 0 < count_a // B <= EDGE - 3 and count_g % B == 0 and 1 < count_g // B <= EDGE - 1
+    whole_a, whole_g = count_a // B, count_g // B
+    return count_a % H == 0 and 0 < whole_a < EDGE - 1 and count_g % B == 0 and 1 < whole_g < EDGE
 
 
 def on_device(saved_input, saved_pre, grad_act):

time: 41.3 us -> 43.1 us (1.044)
  starting transfers between devices: 15.1 us -> 11.4 us
  waiting for transfers between devices: 15.1 us -> 18.1 us
  Pallas kernels: 9.91 us -> 12.2 us
    ppermute x7 -> x10, starting transfers between devices: 15.1 us -> 11.4 us  [swap(): return lax.ppermute(value, ('dp', 'tensor'), pairs)]
    ppermute x7 -> x10, waiting for transfers between devices: 15.1 us -> 18.1 us  [swap(): return lax.ppermute(value, ('dp', 'tensor'), pairs)]
    pallas_call x3, Pallas kernels: 8.84 us -> 11.1 us  [pack(): pl.pallas_call(functools.partial(pack_body, pieces, first, slots, count_a...]
  transfers between devices with their start and end apart: 7 -> 10, of which waited for: 5 -> 5; matrix products, arithmetic and copies ran while one was open for 1% -> 1% of each run, Pallas kernels for 16% -> 21%
where the time goes in v3:
time: 43.1 us; the launch traced here: 42.9 us
  waiting for transfers between devices  18.1 us (42%)
  Pallas kernels  12.2 us (28%)
  starting transfers between devices  11.4 us (26%)
  between operations  0.75 us (2%)
    ppermute x10, waiting for transfers between devices, swap(): return lax.ppermute(value, ('dp', 'tensor'), pairs)  18.1 us
    ppermute x10, starting transfers between devices, swap(): return lax.ppermute(value, ('dp', 'tensor'), pairs)  11.4 us
    pallas_call x3, Pallas kernels, pack(): pl.pallas_call(functools.partial(pack_body, pieces, first, slots, count_a...  11.1 us
    pallas_call x1, Pallas kernels, finish(): pl.pallas_call(functools.partial(finish_body, pieces, len(traces), count_...  1.07 us
  transfers between devices with their start and end apart: 10, of which 5 were waited for; matrix products, arithmetic and copies ran while one was open for 1% of the time, Pallas kernels for 21%

profile of v3, /device:TPU:0, one launch (start us, length us, event | category | flops | bytes accessed | tf_op | source)
XLA Modules:
  0.0 42.9 jit_solution(17238174775310974837)
XLA Ops:
  0.6 2.1 %shard_map.50 = (f32[4,136,128]{2,1,0:T(8,128)S(1)}, f32[8,128]{1,0:T(8,128)S(1)}) custom-call(bf16[128,2560]{1,0:T(8,128)(2,1)} %refs_0_.5, bf16[128,5120]{1,0:T(8,128)(2,1)} %refs_1_.5, bf16[128,5120]{1,0:T(8,128)(2,1)} %refs_2_.5, f32[8,128]{1,0:T(8,128)S(1)} %broadcast_in_dim.18.refs_3_), custom_call_target="tpu_custom_call" | custom-call | flops 1 | bytes 1 | tf_op jit(solution)/shard_map/pallas_call | solution.py:179
  2.8 3.1 %collective-permute-start.1 = (f32[4,136,128]{2,1,0:T(8,128)S(1)}, f32[4,136,128]{2,1,0:T(8,128)S(1)}, u32[]{:S(2)}, u32[]{:S(2)}) collective-permute-start(f32[4,136,128]{2,1,0:T(8,128)S(1)} %get-tuple-element.17), channel_id=1, source_target_pairs={{0,4},{1,9},{2,6},{3,11},{4,0},{5,13},{6,2},{7,15},{8,12},{9,1},{1... | collective-permute-start | bytes 835592 | tf_op jit(solution)/shard_map/ppermute | solution.py:260
  5.8 3.9 %shard_map.51 = (f32[4,200,128]{2,1,0:T(8,128)S(1)}, f32[4,197,128]{2,1,0:T(8,128)S(1)}, f32[8,128]{1,0:T(8,128)S(1)}) custom-call(bf16[128,2560]{1,0:T(8,128)(2,1)} %refs_0_.5, bf16[128,5120]{1,0:T(8,128)(2,1)} %refs_1_.5, bf16[128,5120]{1,0:T(8,128)(2,1)} %refs_2_.5, f32[8,128]{1,0:T(8,128)S(1)} %get-tuple-element.13.refs_3_), custom_call_target="tpu_custom_call" | custom-call | flops 1 | bytes 1 | tf_op jit(solution)/shard_map/pallas_call | solution.py:179
  9.8 2.7 %collective-permute-start.4 = (f32[4,197,128]{2,1,0:T(8,128)S(1)}, f32[4,197,128]{2,1,0:T(8,128)S(1)}, u32[]{:S(2)}, u32[]{:S(2)}) collective-permute-start(f32[4,197,128]{2,1,0:T(8,128)S(1)} %get-tuple-element.19), channel_id=1, source_target_pairs={{0,8},{1,5},{2,10},{3,7},{4,12},{5,1},{6,14},{7,3},{8,0},{9,13},{1... | collective-permute-start | bytes 1210376 | tf_op jit(solution)/shard_map/ppermute | solution.py:260
  12.4 1.5 %collective-permute-start.7 = (f32[4,200,128]{2,1,0:T(8,128)S(1)}, f32[4,200,128]{2,1,0:T(8,128)S(1)}, u32[]{:S(2)}, u32[]{:S(2)}) collective-permute-start(f32[4,200,128]{2,1,0:T(8,128)S(1)} %get-tuple-element.21), channel_id=1, source_target_pairs={{0,2},{1,3},{2,0},{3,1},{4,6},{5,7},{6,4},{7,5},{8,10},{9,11},{10,... | collective-permute-start | bytes 1228808 | tf_op jit(solution)/shard_map/ppermute | solution.py:260
  13.9 5.1 %shard_map.52 = (f32[4,136,128]{2,1,0:T(8,128)S(1)}, f32[4,200,128]{2,1,0:T(8,128)S(1)}, f32[4,197,128]{2,1,0:T(8,128)S(1)}, f32[8,128]{1,0:T(8,128)S(1)}) custom-call(bf16[128,2560]{1,0:T(8,128)(2,1)} %refs_0_.5, bf16[128,5120]{1,0:T(8,128)(2,1)} %refs_1_.5, bf16[128,5120]{1,0:T(8,128)(2,1)} %refs_2_.5, f32[8,128]{1,0:T(8,128)S(1)} %get-tuple-element.14.refs_3_), custom_call_target="tpu_custom_call" | custom-call | flops 1 | bytes 1 | tf_op jit(solution)/shard_map/pallas_call | solution.py:179
  19.0 0.1 collective-permute-start
  19.2 1.1 %collective-permute-done = f32[8,128]{1,0:T(8,128)S(1)} collective-permute-done((f32[8,128]{1,0:T(8,128)S(1)}, f32[8,128]{1,0:T(8,128)S(1)}, u32[]{:S(2)}, u32[]{:S(2)}) %collective-permute-start) | collective-permute-done | bytes 4128 | tf_op jit(solution)/shard_map/ppermute | solution.py:260
  20.3 0.5 %collective-permute-start.2 = (f32[2,136,128]{2,1,0:T(8,128)S(1)}, f32[2,136,128]{2,1,0:T(8,128)S(1)}, u32[]{:S(2)}, u32[]{:S(2)}) collective-permute-start(f32[2,136,128]{2,1,0:T(8,128)S(1)} %bitcast_dynamic-update-slice_fusion.1), channel_id=1, source_target_pairs={{0,2},{1,3},{2,0},{3,1},{4,6},{5,7},{6,4},{7,5},{8,10},{9,11},{10,... | collective-permute-start | bytes 417800 | tf_op jit(solution)/shard_map/ppermute | solution.py:260
  20.8 0.8 %collective-permute-done.4 = f32[4,197,128]{2,1,0:T(8,128)S(1)} collective-permute-done((f32[4,197,128]{2,1,0:T(8,128)S(1)}, f32[4,197,128]{2,1,0:T(8,128)S(1)}, u32[]{:S(2)}, u32[]{:S(2)}) %collective-permute-start.4) | collective-permute-done | bytes 403488 | tf_op jit(solution)/shard_map/ppermute | solution.py:260
  21.6 0.1 slice_add_fusion.3
  21.7 1.6 %collective-permute-start.5 = (f32[2,197,128]{2,1,0:T(8,128)S(1)}, f32[2,197,128]{2,1,0:T(8,128)S(1)}, u32[]{:S(2)}, u32[]{:S(2)}) collective-permute-start(f32[2,197,128]{2,1,0:T(8,128)S(1)} %get-tuple-element.27), channel_id=1, source_target_pairs={{0,2},{1,3},{2,0},{3,1},{4,6},{5,7},{6,4},{7,5},{8,10},{9,11},{10,... | collective-permute-start | bytes 605192 | tf_op jit(solution)/shard_map/ppermute | solution.py:260
  23.2 3.6 %collective-permute-done.2 = f32[2,136,128]{2,1,0:T(8,128)S(1)} collective-permute-done((f32[2,136,128]{2,1,0:T(8,128)S(1)}, f32[2,136,128]{2,1,0:T(8,128)S(1)}, u32[]{:S(2)}, u32[]{:S(2)}) %collective-permute-start.2) | collective-permute-done | bytes 139296 | tf_op jit(solution)/shard_map/ppermute | solution.py:260
  26.8 0.1 collective-permute-start.3
  26.9 0.1 slice_add_fusion.1
  27.0 0.4 %collective-permute-start.8 = (f32[2,200,128]{2,1,0:T(8,128)S(1)}, f32[2,200,128]{2,1,0:T(8,128)S(1)}, u32[]{:S(2)}, u32[]{:S(2)}) collective-permute-start(f32[2,200,128]{2,1,0:T(8,128)S(1)} %get-tuple-element.25), channel_id=1, source_target_pairs={{0,4},{1,9},{2,6},{3,11},{4,0},{5,13},{6,2},{7,15},{8,12},{9,1},{1... | collective-permute-start | bytes 614408 | tf_op jit(solution)/shard_map/ppermute | solution.py:260
  27.4 8.1 %collective-permute-done.3.refs_5_ = f32[1,136,128]{2,1,0:T(8,128)S(1)} collective-permute-done((f32[1,136,128]{2,1,0:T(8,128)S(1)}, f32[1,136,128]{2,1,0:T(8,128)S(1)}, u32[]{:S(2)}, u32[]{:S(2)}) %collective-permute-start.3) | collective-permute-done | bytes 69664 | tf_op jit(solution)/shard_map/ppermute | solution.py:260
  35.6 0.1 dynamic_update_slice.11
  35.7 0.1 collective-permute-start.6
  35.8 0.0 collective-permute-done.8
  35.8 1.4 %collective-permute-start.9 = (f32[1,200,128]{2,1,0:T(8,128)S(1)}, f32[1,200,128]{2,1,0:T(8,128)S(1)}, u32[]{:S(2)}, u32[]{:S(2)}) collective-permute-start(f32[1,200,128]{2,1,0:T(8,128)S(1)} %get-tuple-element.30), channel_id=1, source_target_pairs={{0,8},{1,5},{2,10},{3,7},{4,12},{5,1},{6,14},{7,3},{8,0},{9,13},{1... | collective-permute-start | bytes 307208 | tf_op jit(solution)/shard_map/ppermute | solution.py:260
  37.3 4.6 %collective-permute-done.6.refs_7_ = f32[1,197,128]{2,1,0:T(8,128)S(1)} collective-permute-done((f32[1,197,128]{2,1,0:T(8,128)S(1)}, f32[1,197,128]{2,1,0:T(8,128)S(1)}, u32[]{:S(2)}, u32[]{:S(2)}) %collective-permute-start.6) | collective-permute-done | bytes 100896 | tf_op jit(solution)/shard_map/ppermute | solution.py:260
  41.8 0.0 collective-permute-done.9.refs_6_
  41.8 1.1 %shard_map.53 = (f32[320,128]{1,0:T(8,128)}, f32[640,128]{1,0:T(8,128)}) custom-call(f32[2,128]{1,0:T(2,128)S(1)} %fusion.refs_0_, f32[2,128]{1,0:T(2,128)S(1)} %slice_bitcast_fusion.refs_1_, f32[1,136,128]{2,1,0:T(8,128)S(1)} %get-tuple-element.34.refs_2_, f32[1,200,128]{2,1,0:T(8,128)S(1)} %get-tuple-element.31.refs_3_, ...), custom_call_target="tpu_custom_call" | custom-call | tf_op jit(solution)/shard_map/pallas_call | solution.py:241
  (12 shorter events, 0.2 us)
Async XLA Ops:
  2.8 16.4 %collective-permute-start.1 = (f32[4,136,128]{2,1,0:T(8,128)S(1)}, f32[4,136,128]{2,1,0:T(8,128)S(1)}, u32[]{:S(2)}, u32[]{:S(2)}) collective-permute-start(f32[4,136,128]{2,1,0:T(8,128)S(1)} %get-tuple-element.17), channel_id=1, source_target_pairs={{0,4},{1,9},{2,6},{3,11},{4,0},{5,13},{6,2},{7,15},{8,12},{9,1},{1... | collective-permute-start | bytes 835592 | tf_op jit(solution)/shard_map/ppermute | solution.py:260
  9.8 11.8 %collective-permute-start.4 = (f32[4,197,128]{2,1,0:T(8,128)S(1)}, f32[4,197,128]{2,1,0:T(8,128)S(1)}, u32[]{:S(2)}, u32[]{:S(2)}) collective-permute-start(f32[4,197,128]{2,1,0:T(8,128)S(1)} %get-tuple-element.19), channel_id=1, source_target_pairs={{0,8},{1,5},{2,10},{3,7},{4,12},{5,1},{6,14},{7,3},{8,0},{9,13},{1... | collective-permute-start | bytes 1210376 | tf_op jit(solution)/shard_map/ppermute | solution.py:260
  12.4 14.5 %collective-permute-start.7 = (f32[4,200,128]{2,1,0:T(8,128)S(1)}, f32[4,200,128]{2,1,0:T(8,128)S(1)}, u32[]{:S(2)}, u32[]{:S(2)}) collective-permute-start(f32[4,200,128]{2,1,0:T(8,128)S(1)} %get-tuple-element.21), channel_id=1, source_target_pairs={{0,2},{1,3},{2,0},{3,1},{4,6},{5,7},{6,4},{7,5},{8,10},{9,11},{10,... | collective-permute-start | bytes 1228808 | tf_op jit(solution)/shard_map/ppermute | solution.py:260
  19.0 1.2 %collective-permute-start = (f32[8,128]{1,0:T(8,128)S(1)}, f32[8,128]{1,0:T(8,128)S(1)}, u32[]{:S(2)}, u32[]{:S(2)}) collective-permute-start(f32[8,128]{1,0:T(8,128)S(1)} %get-tuple-element.15), channel_id=1, source_target_pairs={{0,1},{1,0},{2,3},{3,2},{4,5},{5,4},{6,7},{7,6},{8,9},{9,8},{10,11... | collective-permute-start | bytes 12296 | tf_op jit(solution)/shard_map/ppermute | solution.py:260
  20.3 6.5 %collective-permute-start.2 = (f32[2,136,128]{2,1,0:T(8,128)S(1)}, f32[2,136,128]{2,1,0:T(8,128)S(1)}, u32[]{:S(2)}, u32[]{:S(2)}) collective-permute-start(f32[2,136,128]{2,1,0:T(8,128)S(1)} %bitcast_dynamic-update-slice_fusion.1), channel_id=1, source_target_pairs={{0,2},{1,3},{2,0},{3,1},{4,6},{5,7},{6,4},{7,5},{8,10},{9,11},{10,... | collective-permute-start | bytes 417800 | tf_op jit(solution)/shard_map/ppermute | solution.py:260
  21.7 13.9 %collective-permute-start.5 = (f32[2,197,128]{2,1,0:T(8,128)S(1)}, f32[2,197,128]{2,1,0:T(8,128)S(1)}, u32[]{:S(2)}, u32[]{:S(2)}) collective-permute-start(f32[2,197,128]{2,1,0:T(8,128)S(1)} %get-tuple-element.27), channel_id=1, source_target_pairs={{0,2},{1,3},{2,0},{3,1},{4,6},{5,7},{6,4},{7,5},{8,10},{9,11},{10,... | collective-permute-start | bytes 605192 | tf_op jit(solution)/shard_map/ppermute | solution.py:260
  26.8 8.7 %collective-permute-start.3 = (f32[1,136,128]{2,1,0:T(8,128)S(1)}, f32[1,136,128]{2,1,0:T(8,128)S(1)}, u32[]{:S(2)}, u32[]{:S(2)}) collective-permute-start(f32[1,136,128]{2,1,0:T(8,128)S(1)} %bitcast_dynamic-update-slice_fusion), channel_id=1, source_target_pairs={{0,8},{1,5},{2,10},{3,7},{4,12},{5,1},{6,14},{7,3},{8,0},{9,13},{1... | collective-permute-start | bytes 208904 | tf_op jit(solution)/shard_map/ppermute | solution.py:260
  27.0 8.8 %collective-permute-start.8 = (f32[2,200,128]{2,1,0:T(8,128)S(1)}, f32[2,200,128]{2,1,0:T(8,128)S(1)}, u32[]{:S(2)}, u32[]{:S(2)}) collective-permute-start(f32[2,200,128]{2,1,0:T(8,128)S(1)} %get-tuple-element.25), channel_id=1, source_target_pairs={{0,4},{1,9},{2,6},{3,11},{4,0},{5,13},{6,2},{7,15},{8,12},{9,1},{1... | collective-permute-start | bytes 614408 | tf_op jit(solution)/shard_map/ppermute | solution.py:260
  35.7 6.1 %collective-permute-start.6 = (f32[1,197,128]{2,1,0:T(8,128)S(1)}, f32[1,197,128]{2,1,0:T(8,128)S(1)}, u32[]{:S(2)}, u32[]{:S(2)}) collective-permute-start(f32[1,197,128]{2,1,0:T(8,128)S(1)} %dynamic_update_slice.11), channel_id=1, source_target_pairs={{0,4},{1,9},{2,6},{3,11},{4,0},{5,13},{6,2},{7,15},{8,12},{9,1},{1... | collective-permute-start | bytes 302600 | tf_op jit(solution)/shard_map/ppermute | solution.py:260
  35.8 6.0 %collective-permute-start.9 = (f32[1,200,128]{2,1,0:T(8,128)S(1)}, f32[1,200,128]{2,1,0:T(8,128)S(1)}, u32[]{:S(2)}, u32[]{:S(2)}) collective-permute-start(f32[1,200,128]{2,1,0:T(8,128)S(1)} %get-tuple-element.30), channel_id=1, source_target_pairs={{0,8},{1,5},{2,10},{3,7},{4,12},{5,1},{6,14},{7,3},{8,0},{9,13},{1... | collective-permute-start | bytes 307208 | tf_op jit(solution)/shard_map/ppermute | solution.py:260

commit v4 on v3

--- a/solution.py
+++ b/solution.py
@@ -63,7 +63,7 @@
 def piece_rows(piece):
     a_blocks, a_half, g_blocks, _ = piece
     edge = (len(a_blocks) + a_half + len(g_blocks)) * H
-    return edge + (EDGE if a_blocks or a_half else len(g_blocks) + 2), edge
+    return edge + EDGE, edge
 
 
 def iotas():
@@ -133,8 +133,10 @@
         out = outs[i]
         odd = slot_owner(first + slot, orders) & half
         rows, edge = piece_rows(pieces[i])
-        for copy in copies(i, slot):
-            copy.wait()
+        if slot == 0:
+            for other in range(slots):
+                for copy in copies(i, other):
+                    copy.wait()
         at = 0
         corners = 0
 
@@ -192,16 +194,14 @@
     return chunks, trace
 
 
-def finish_body(pieces, n_traces, count_a, total, *refs):
+def finish_body(pieces, count_a, total, *refs):
     n = len(pieces)
-    traces, refs = refs[:n_traces], refs[n_traces:]
-    owns, gots, (a_ref, g_ref) = refs[:n], refs[n : 2 * n], refs[2 * n :]
+    trace_ref, owns, gots, (a_ref, g_ref) = refs[0], refs[1 : n + 1], refs[n + 1 : 2 * n + 1], refs[2 * n + 1 :]
     full, half = split_rows(count_a)
     odd = lax.axis_index("dp") & half
     row, col = iotas()
 
-    sums = sum((trace[...] for trace in traces[1:]), traces[0][...])
-    sums = jnp.sum(sums, axis=1, keepdims=True) / total
+    sums = jnp.sum(trace_ref[...] + gots[-1][0, -2:, :], axis=1, keepdims=True) / total
     ratio = jnp.sqrt(sums[0:1] / D / (sums[1:2] / FFW))
     damp = jnp.sqrt(jnp.full((1, 1), 0.1, jnp.float32))
     shift_a, shift_g = ratio * damp, damp / ratio
@@ -236,10 +236,10 @@
             at, corner = at + 1, corner + 1
 
 
-def finish(pieces, traces, owns, gots, count_a, count_g, total):
-    args = (*traces, *owns, *gots)
+def finish(pieces, trace, owns, gots, count_a, count_g, total):
+    args = (trace, *owns, *gots)
     return pl.pallas_call(
-        functools.partial(finish_body, pieces, len(traces), count_a, total),
+        functools.partial(finish_body, pieces, count_a, total),
         in_specs=[pl.BlockSpec(memory_space=pltpu.VMEM)] * len(args),
         out_specs=[pl.BlockSpec(memory_space=pltpu.VMEM)] * 2,
         out_shape=[
@@ -276,12 +276,15 @@
 def cut(count_a, count_g):
     full_a, half_a = split_rows(count_a)
     full_g, _ = split_rows(count_g)
-    some = full_g // 2
+    some = 1 + (full_g - 1) // 2
     x, near, far = 0, 1, 2
+    one = ((x, near, far), (near, x, far))
+    other = one[::-1]
     return (
-        (tuple(range(full_a)), 0, (), ((near, x, far), (far, x, near))),
-        ((), half_a, tuple(range(some)), ((x, near, far), (x, far, near))),
-        ((), 0, tuple(range(some, full_g)), ((far, x, near), (near, x, far))),
+        (tuple(range(full_a)), 0, (), one),
+        ((), 0, tuple(range(1, some)), one),
+        ((), half_a, (0,), other),
+        ((), 0, tuple(range(some, full_g)), other),
     )
 
 
@@ -299,33 +302,36 @@
     chunks = range(len(pieces))
 
     trace = jnp.zeros((EDGE, B), jnp.float32)
-    gots = []
-    for part in (pieces[:1], pieces[1:]):
-        sends, trace = pack(arrays, part, half, half, count_a, count_g, trace)
-        gots += [swap(send, along(0, piece[3])) for send, piece in zip(sends, part)]
+    gots = [None] * len(pieces)
+    for part in ((0, 2), (1, 3)):
+        sends, trace = pack(
+            arrays, tuple(pieces[k] for k in part), half, half, count_a, count_g, trace
+        )
+        for k, send in zip(part, sends):
+            gots[k] = swap(send, along(0, pieces[k][3]))
     keeps, trace = pack(arrays, pieces, 0, half, count_a, count_g, trace)
 
     trace = trace[:2] + swap(trace, lambda i, j: (i, j ^ 1))[:2]
     last = len(pieces) - 1
-    carriers = ((0, 1), (0, 2), (last, 2))
+    carriers = ((0, 1), (last, 1), (last, 2))
     for stage in (1, 2):
         for k in chunks:
             keeps[k], send = halve(keeps[k], gots[k])
             if (k, stage) in carriers:
                 if (k, stage) != carriers[0]:
-                    trace = trace + news
+                    trace = trace + news[0, -2:, :]
                 send = with_trace(send, trace)
             gots[k] = swap(send, along(stage, pieces[k][3]))
             if (k, stage) in carriers:
-                news = gots[k][0, -2:, :]
-
-    a_factor, g_factor = finish(pieces, (trace, news), keeps, gots, count_a, count_g, total)
+                news = gots[k]
+
+    a_factor, g_factor = finish(pieces, trace, keeps, gots, count_a, count_g, total)
     return a_factor[None], g_factor[None]
 
 
 def fits(count_a, count_g):
     whole_a, whole_g = count_a // B, count_g // B
-    return count_a % H == 0 and 0 < whole_a < EDGE - 1 and count_g % B == 0 and 1 < whole_g < EDGE
+    return count_a % H == 0 and 0 < whole_a < EDGE - 1 and count_g % B == 0 and 2 < whole_g < 2 * EDGE - 4
 
 
 def on_device(saved_input, saved_pre, grad_act):

time: 43.1 us -> 39.3 us (0.912)
  waiting for transfers between devices: 18.1 us -> 11.3 us
  starting transfers between devices: 11.4 us -> 17.9 us
  Pallas kernels: 12.2 us -> 8.84 us
    ppermute x10 -> x13, waiting for transfers between devices: 18.1 us -> 11.3 us  [swap(): return lax.ppermute(value, ('dp', 'tensor'), pairs)]
    ppermute x10 -> x13, starting transfers between devices: 11.4 us -> 17.9 us  [swap(): return lax.ppermute(value, ('dp', 'tensor'), pairs)]
    pallas_call x3, Pallas kernels: 11.1 us -> 7.76 us  [pack(): pl.pallas_call(functools.partial(pack_body, pieces, first, slots, count_a...]
  transfers between devices with their start and end apart: 10 -> 13, of which waited for: 5 -> 6; matrix products, arithmetic and copies ran while one was open for 1% -> 1% of each run, Pallas kernels for 21% -> 15%
where the time goes in v4:
time: 39.3 us; the launch traced here: 39 us
  starting transfers between devices  17.9 us (46%)
  waiting for transfers between devices  11.3 us (29%)
  Pallas kernels  8.84 us (22%)
  between operations  0.72 us (2%)
    ppermute x13, starting transfers between devices, swap(): return lax.ppermute(value, ('dp', 'tensor'), pairs)  17.9 us
    ppermute x13, waiting for transfers between devices, swap(): return lax.ppermute(value, ('dp', 'tensor'), pairs)  11.3 us
    pallas_call x3, Pallas kernels, pack(): pl.pallas_call(functools.partial(pack_body, pieces, first, slots, count_a...  7.76 us
    pallas_call x1, Pallas kernels, finish(): pl.pallas_call(functools.partial(finish_body, pieces, count_a, total), in...  1.07 us
  transfers between devices with their start and end apart: 13, of which 6 were waited for; matrix products, arithmetic and copies ran while one was open for 1% of the time, Pallas kernels for 15%

profile of v4, /device:TPU:0, one launch (start us, length us, event | category | flops | bytes accessed | tf_op | source)
XLA Modules:
  0.0 39.0 jit_solution(10157227663187018593)
XLA Ops:
  0.6 2.0 %shard_map.50 = (f32[4,136,128]{2,1,0:T(8,128)S(1)}, f32[4,136,128]{2,1,0:T(8,128)S(1)}, f32[8,128]{1,0:T(8,128)S(1)}) custom-call(bf16[128,2560]{1,0:T(8,128)(2,1)} %refs_0_.5, bf16[128,5120]{1,0:T(8,128)(2,1)} %refs_1_.5, bf16[128,5120]{1,0:T(8,128)(2,1)} %refs_2_.5, f32[8,128]{1,0:T(8,128)S(1)} %broadcast_in_dim.18.refs_3_), custom_call_target="tpu_custom_call" | custom-call | flops 1 | bytes 1 | tf_op jit(solution)/shard_map/pallas_call | solution.py:181
  2.6 3.0 %collective-permute-start.1 = (f32[4,136,128]{2,1,0:T(8,128)S(1)}, f32[4,136,128]{2,1,0:T(8,128)S(1)}, u32[]{:S(2)}, u32[]{:S(2)}) collective-permute-start(f32[4,136,128]{2,1,0:T(8,128)S(1)} %get-tuple-element.19), channel_id=1, source_target_pairs={{0,2},{1,5},{2,0},{3,7},{4,6},{5,1},{6,4},{7,3},{8,10},{9,13},{10,... | collective-permute-start | bytes 835592 | tf_op jit(solution)/shard_map/ppermute | solution.py:260
  5.6 1.6 %collective-permute-start.7 = (f32[4,136,128]{2,1,0:T(8,128)S(1)}, f32[4,136,128]{2,1,0:T(8,128)S(1)}, u32[]{:S(2)}, u32[]{:S(2)}) collective-permute-start(f32[4,136,128]{2,1,0:T(8,128)S(1)} %get-tuple-element.25), channel_id=1, source_target_pairs={{0,4},{1,3},{2,6},{3,1},{4,0},{5,7},{6,2},{7,5},{8,12},{9,11},{10,... | collective-permute-start | bytes 835592 | tf_op jit(solution)/shard_map/ppermute | solution.py:260
  7.2 2.4 %shard_map.51 = (f32[4,136,128]{2,1,0:T(8,128)S(1)}, f32[4,136,128]{2,1,0:T(8,128)S(1)}, f32[8,128]{1,0:T(8,128)S(1)}) custom-call(bf16[128,2560]{1,0:T(8,128)(2,1)} %refs_0_.5, bf16[128,5120]{1,0:T(8,128)(2,1)} %refs_1_.5, bf16[128,5120]{1,0:T(8,128)(2,1)} %refs_2_.5, f32[8,128]{1,0:T(8,128)S(1)} %get-tuple-element.15.refs_3_), custom_call_target="tpu_custom_call" | custom-call | flops 1 | bytes 1 | tf_op jit(solution)/shard_map/pallas_call | solution.py:181
  9.7 0.5 %collective-permute-start.3 = (f32[4,136,128]{2,1,0:T(8,128)S(1)}, f32[4,136,128]{2,1,0:T(8,128)S(1)}, u32[]{:S(2)}, u32[]{:S(2)}) collective-permute-start(f32[4,136,128]{2,1,0:T(8,128)S(1)} %get-tuple-element.21), channel_id=1, source_target_pairs={{0,4},{1,3},{2,6},{3,1},{4,0},{5,7},{6,2},{7,5},{8,12},{9,11},{10,... | collective-permute-start | bytes 835592 | tf_op jit(solution)/shard_map/ppermute | solution.py:260
  10.2 0.2 collective-permute-start.5
  10.3 3.3 %shard_map.52 = (f32[4,136,128]{2,1,0:T(8,128)S(1)}, f32[4,136,128]{2,1,0:T(8,128)S(1)}, f32[4,136,128]{2,1,0:T(8,128)S(1)}, f32[4,136,128]{2,1,0:T(8,128)S(1)}, f32[8,128]{1,0:T(8,128)S(1)}) custom-call(bf16[128,2560]{1,0:T(8,128)(2,1)} %refs_0_.5, bf16[128,5120]{1,0:T(8,128)(2,1)} %refs_1_.5, bf16[128,5120]{1,0:T(8,128)(2,1)} %refs_2_.5, ...), custom_call_target="tpu_custom_call" | custom-call | flops 1 | bytes 1 | tf_op jit(solution)/shard_map/pallas_call | solution.py:181
  13.7 0.1 collective-permute-start
  13.8 0.0 collective-permute-done.1
  13.8 1.1 %collective-permute-done = f32[8,128]{1,0:T(8,128)S(1)} collective-permute-done((f32[8,128]{1,0:T(8,128)S(1)}, f32[8,128]{1,0:T(8,128)S(1)}, u32[]{:S(2)}, u32[]{:S(2)}) %collective-permute-start) | collective-permute-done | bytes 4128 | tf_op jit(solution)/shard_map/ppermute | solution.py:260
  14.9 1.9 %collective-permute-start.2 = (f32[2,136,128]{2,1,0:T(8,128)S(1)}, f32[2,136,128]{2,1,0:T(8,128)S(1)}, u32[]{:S(2)}, u32[]{:S(2)}) collective-permute-start(f32[2,136,128]{2,1,0:T(8,128)S(1)} %bitcast_dynamic-update-slice_fusion.2), channel_id=1, source_target_pairs={{0,4},{1,3},{2,6},{3,1},{4,0},{5,7},{6,2},{7,5},{8,12},{9,11},{10,... | collective-permute-start | bytes 417800 | tf_op jit(solution)/shard_map/ppermute | solution.py:260
  16.9 1.6 %collective-permute-start.8 = (f32[2,136,128]{2,1,0:T(8,128)S(1)}, f32[2,136,128]{2,1,0:T(8,128)S(1)}, u32[]{:S(2)}, u32[]{:S(2)}) collective-permute-start(f32[2,136,128]{2,1,0:T(8,128)S(1)} %get-tuple-element.31), channel_id=1, source_target_pairs={{0,2},{1,5},{2,0},{3,7},{4,6},{5,1},{6,4},{7,3},{8,10},{9,13},{10,... | collective-permute-start | bytes 417800 | tf_op jit(solution)/shard_map/ppermute | solution.py:260
  18.5 1.3 %collective-permute-done.5 = f32[4,136,128]{2,1,0:T(8,128)S(1)} collective-permute-done((f32[4,136,128]{2,1,0:T(8,128)S(1)}, f32[4,136,128]{2,1,0:T(8,128)S(1)}, u32[]{:S(2)}, u32[]{:S(2)}) %collective-permute-start.5) | collective-permute-done | bytes 278560 | tf_op jit(solution)/shard_map/ppermute | solution.py:260
  19.8 0.9 %collective-permute-start.6 = (f32[2,136,128]{2,1,0:T(8,128)S(1)}, f32[2,136,128]{2,1,0:T(8,128)S(1)}, u32[]{:S(2)}, u32[]{:S(2)}) collective-permute-start(f32[2,136,128]{2,1,0:T(8,128)S(1)} %get-tuple-element.33), channel_id=1, source_target_pairs={{0,4},{1,3},{2,6},{3,1},{4,0},{5,7},{6,2},{7,5},{8,12},{9,11},{10,... | collective-permute-start | bytes 417800 | tf_op jit(solution)/shard_map/ppermute | solution.py:260
  20.8 3.3 %collective-permute-start.9 = (f32[1,136,128]{2,1,0:T(8,128)S(1)}, f32[1,136,128]{2,1,0:T(8,128)S(1)}, u32[]{:S(2)}, u32[]{:S(2)}) collective-permute-start(f32[1,136,128]{2,1,0:T(8,128)S(1)} %get-tuple-element.42), channel_id=1, source_target_pairs={{0,8},{1,9},{2,10},{3,11},{4,12},{5,13},{6,14},{7,15},{8,0},{9,1},... | collective-permute-start | bytes 208904 | tf_op jit(solution)/shard_map/ppermute | solution.py:260
  24.1 1.6 %collective-permute-start.4 = (f32[2,136,128]{2,1,0:T(8,128)S(1)}, f32[2,136,128]{2,1,0:T(8,128)S(1)}, u32[]{:S(2)}, u32[]{:S(2)}) collective-permute-start(f32[2,136,128]{2,1,0:T(8,128)S(1)} %bitcast_dynamic-update-slice_fusion.1), channel_id=1, source_target_pairs={{0,2},{1,5},{2,0},{3,7},{4,6},{5,1},{6,4},{7,3},{8,10},{9,13},{10,... | collective-permute-start | bytes 417800 | tf_op jit(solution)/shard_map/ppermute | solution.py:260
  25.7 0.6 %collective-permute-start.11 = (f32[1,136,128]{2,1,0:T(8,128)S(1)}, f32[1,136,128]{2,1,0:T(8,128)S(1)}, u32[]{:S(2)}, u32[]{:S(2)}) collective-permute-start(f32[1,136,128]{2,1,0:T(8,128)S(1)} %get-tuple-element.38), channel_id=1, source_target_pairs={{0,8},{1,9},{2,10},{3,11},{4,12},{5,13},{6,14},{7,15},{8,0},{9,1},... | collective-permute-start | bytes 208904 | tf_op jit(solution)/shard_map/ppermute | solution.py:260
  26.3 2.5 %collective-permute-start.10 = (f32[1,136,128]{2,1,0:T(8,128)S(1)}, f32[1,136,128]{2,1,0:T(8,128)S(1)}, u32[]{:S(2)}, u32[]{:S(2)}) collective-permute-start(f32[1,136,128]{2,1,0:T(8,128)S(1)} %get-tuple-element.40), channel_id=1, source_target_pairs={{0,8},{1,9},{2,10},{3,11},{4,12},{5,13},{6,14},{7,15},{8,0},{9,1},... | collective-permute-start | bytes 208904 | tf_op jit(solution)/shard_map/ppermute | solution.py:260
  28.8 0.3 collective-permute-done.4
  29.2 0.2 collective-permute-start.12
  29.4 6.7 %collective-permute-done.11.refs_7_ = f32[1,136,128]{2,1,0:T(8,128)S(1)} collective-permute-done((f32[1,136,128]{2,1,0:T(8,128)S(1)}, f32[1,136,128]{2,1,0:T(8,128)S(1)}, u32[]{:S(2)}, u32[]{:S(2)}) %collective-permute-start.11) | collective-permute-done | bytes 69664 | tf_op jit(solution)/shard_map/ppermute | solution.py:260
  36.1 1.1 %collective-permute-done.10.refs_6_ = f32[1,136,128]{2,1,0:T(8,128)S(1)} collective-permute-done((f32[1,136,128]{2,1,0:T(8,128)S(1)}, f32[1,136,128]{2,1,0:T(8,128)S(1)}, u32[]{:S(2)}, u32[]{:S(2)}) %collective-permute-start.10) | collective-permute-done | bytes 69664 | tf_op jit(solution)/shard_map/ppermute | solution.py:260
  37.2 0.7 %collective-permute-done.12.refs_8_ = f32[1,136,128]{2,1,0:T(8,128)S(1)} collective-permute-done((f32[1,136,128]{2,1,0:T(8,128)S(1)}, f32[1,136,128]{2,1,0:T(8,128)S(1)}, u32[]{:S(2)}, u32[]{:S(2)}) %collective-permute-start.12) | collective-permute-done | bytes 69664 | tf_op jit(solution)/shard_map/ppermute | solution.py:260
  37.9 1.1 %shard_map.53 = (f32[320,128]{1,0:T(8,128)}, f32[640,128]{1,0:T(8,128)}) custom-call(f32[2,128]{1,0:T(2,128)S(1)} %get-tuple-element.29.refs_0_, f32[1,136,128]{2,1,0:T(8,128)S(1)} %get-tuple-element.43.refs_1_, f32[1,136,128]{2,1,0:T(8,128)S(1)} %get-tuple-element.41.refs_2_, f32[1,136,128]{2,1,0:T(8,128)S(1)} %get-tuple-element.39.refs_3_, ...), custom_call_target="tpu_custom_call" | custom-call | tf_op jit(solution)/shard_map/pallas_call | solution.py:241
  (18 shorter events, 0.3 us)
Async XLA Ops:
  2.6 11.1 %collective-permute-start.1 = (f32[4,136,128]{2,1,0:T(8,128)S(1)}, f32[4,136,128]{2,1,0:T(8,128)S(1)}, u32[]{:S(2)}, u32[]{:S(2)}) collective-permute-start(f32[4,136,128]{2,1,0:T(8,128)S(1)} %get-tuple-element.19), channel_id=1, source_target_pairs={{0,2},{1,5},{2,0},{3,7},{4,6},{5,1},{6,4},{7,3},{8,10},{9,13},{10,... | collective-permute-start | bytes 835592 | tf_op jit(solution)/shard_map/ppermute | solution.py:260
  5.6 11.2 %collective-permute-start.7 = (f32[4,136,128]{2,1,0:T(8,128)S(1)}, f32[4,136,128]{2,1,0:T(8,128)S(1)}, u32[]{:S(2)}, u32[]{:S(2)}) collective-permute-start(f32[4,136,128]{2,1,0:T(8,128)S(1)} %get-tuple-element.25), channel_id=1, source_target_pairs={{0,4},{1,3},{2,6},{3,1},{4,0},{5,7},{6,2},{7,5},{8,12},{9,11},{10,... | collective-permute-start | bytes 835592 | tf_op jit(solution)/shard_map/ppermute | solution.py:260
  9.7 11.1 %collective-permute-start.3 = (f32[4,136,128]{2,1,0:T(8,128)S(1)}, f32[4,136,128]{2,1,0:T(8,128)S(1)}, u32[]{:S(2)}, u32[]{:S(2)}) collective-permute-start(f32[4,136,128]{2,1,0:T(8,128)S(1)} %get-tuple-element.21), channel_id=1, source_target_pairs={{0,4},{1,3},{2,6},{3,1},{4,0},{5,7},{6,2},{7,5},{8,12},{9,11},{10,... | collective-permute-start | bytes 835592 | tf_op jit(solution)/shard_map/ppermute | solution.py:260
  10.2 9.6 %collective-permute-start.5 = (f32[4,136,128]{2,1,0:T(8,128)S(1)}, f32[4,136,128]{2,1,0:T(8,128)S(1)}, u32[]{:S(2)}, u32[]{:S(2)}) collective-permute-start(f32[4,136,128]{2,1,0:T(8,128)S(1)} %get-tuple-element.23), channel_id=1, source_target_pairs={{0,2},{1,5},{2,0},{3,7},{4,6},{5,1},{6,4},{7,3},{8,10},{9,13},{10,... | collective-permute-start | bytes 835592 | tf_op jit(solution)/shard_map/ppermute | solution.py:260
  13.7 1.2 %collective-permute-start = (f32[8,128]{1,0:T(8,128)S(1)}, f32[8,128]{1,0:T(8,128)S(1)}, u32[]{:S(2)}, u32[]{:S(2)}) collective-permute-start(f32[8,128]{1,0:T(8,128)S(1)} %get-tuple-element.17), channel_id=1, source_target_pairs={{0,1},{1,0},{2,3},{3,2},{4,5},{5,4},{6,7},{7,6},{8,9},{9,8},{10,11... | collective-permute-start | bytes 12296 | tf_op jit(solution)/shard_map/ppermute | solution.py:260
  14.9 5.8 %collective-permute-start.2 = (f32[2,136,128]{2,1,0:T(8,128)S(1)}, f32[2,136,128]{2,1,0:T(8,128)S(1)}, u32[]{:S(2)}, u32[]{:S(2)}) collective-permute-start(f32[2,136,128]{2,1,0:T(8,128)S(1)} %bitcast_dynamic-update-slice_fusion.2), channel_id=1, source_target_pairs={{0,4},{1,3},{2,6},{3,1},{4,0},{5,7},{6,2},{7,5},{8,12},{9,11},{10,... | collective-permute-start | bytes 417800 | tf_op jit(solution)/shard_map/ppermute | solution.py:260
  16.9 8.7 %collective-permute-start.8 = (f32[2,136,128]{2,1,0:T(8,128)S(1)}, f32[2,136,128]{2,1,0:T(8,128)S(1)}, u32[]{:S(2)}, u32[]{:S(2)}) collective-permute-start(f32[2,136,128]{2,1,0:T(8,128)S(1)} %get-tuple-element.31), channel_id=1, source_target_pairs={{0,2},{1,5},{2,0},{3,7},{4,6},{5,1},{6,4},{7,3},{8,10},{9,13},{10,... | collective-permute-start | bytes 417800 | tf_op jit(solution)/shard_map/ppermute | solution.py:260
  19.8 6.5 %collective-permute-start.6 = (f32[2,136,128]{2,1,0:T(8,128)S(1)}, f32[2,136,128]{2,1,0:T(8,128)S(1)}, u32[]{:S(2)}, u32[]{:S(2)}) collective-permute-start(f32[2,136,128]{2,1,0:T(8,128)S(1)} %get-tuple-element.33), channel_id=1, source_target_pairs={{0,4},{1,3},{2,6},{3,1},{4,0},{5,7},{6,2},{7,5},{8,12},{9,11},{10,... | collective-permute-start | bytes 417800 | tf_op jit(solution)/shard_map/ppermute | solution.py:260
  20.8 8.6 %collective-permute-start.9 = (f32[1,136,128]{2,1,0:T(8,128)S(1)}, f32[1,136,128]{2,1,0:T(8,128)S(1)}, u32[]{:S(2)}, u32[]{:S(2)}) collective-permute-start(f32[1,136,128]{2,1,0:T(8,128)S(1)} %get-tuple-element.42), channel_id=1, source_target_pairs={{0,8},{1,9},{2,10},{3,11},{4,12},{5,13},{6,14},{7,15},{8,0},{9,1},... | collective-permute-start | bytes 208904 | tf_op jit(solution)/shard_map/ppermute | solution.py:260
  24.1 5.1 %collective-permute-start.4 = (f32[2,136,128]{2,1,0:T(8,128)S(1)}, f32[2,136,128]{2,1,0:T(8,128)S(1)}, u32[]{:S(2)}, u32[]{:S(2)}) collective-permute-start(f32[2,136,128]{2,1,0:T(8,128)S(1)} %bitcast_dynamic-update-slice_fusion.1), channel_id=1, source_target_pairs={{0,2},{1,5},{2,0},{3,7},{4,6},{5,1},{6,4},{7,3},{8,10},{9,13},{10,... | collective-permute-start | bytes 417800 | tf_op jit(solution)/shard_map/ppermute | solution.py:260
  25.7 10.4 %collective-permute-start.11 = (f32[1,136,128]{2,1,0:T(8,128)S(1)}, f32[1,136,128]{2,1,0:T(8,128)S(1)}, u32[]{:S(2)}, u32[]{:S(2)}) collective-permute-start(f32[1,136,128]{2,1,0:T(8,128)S(1)} %get-tuple-element.38), channel_id=1, source_target_pairs={{0,8},{1,9},{2,10},{3,11},{4,12},{5,13},{6,14},{7,15},{8,0},{9,1},... | collective-permute-start | bytes 208904 | tf_op jit(solution)/shard_map/ppermute | solution.py:260
  26.3 10.9 %collective-permute-start.10 = (f32[1,136,128]{2,1,0:T(8,128)S(1)}, f32[1,136,128]{2,1,0:T(8,128)S(1)}, u32[]{:S(2)}, u32[]{:S(2)}) collective-permute-start(f32[1,136,128]{2,1,0:T(8,128)S(1)} %get-tuple-element.40), channel_id=1, source_target_pairs={{0,8},{1,9},{2,10},{3,11},{4,12},{5,13},{6,14},{7,15},{8,0},{9,1},... | collective-permute-start | bytes 208904 | tf_op jit(solution)/shard_map/ppermute | solution.py:260
  29.2 8.7 %collective-permute-start.12 = (f32[1,136,128]{2,1,0:T(8,128)S(1)}, f32[1,136,128]{2,1,0:T(8,128)S(1)}, u32[]{:S(2)}, u32[]{:S(2)}) collective-permute-start(f32[1,136,128]{2,1,0:T(8,128)S(1)} %get-tuple-element.28), channel_id=1, source_target_pairs={{0,8},{1,9},{2,10},{3,11},{4,12},{5,13},{6,14},{7,15},{8,0},{9,1},... | collective-permute-start | bytes 208904 | tf_op jit(solution)/shard_map/ppermute | solution.py:260

commit v5 on v4

v5 whole, which is shorter than its diff:
```python
import functools
import math

import jax
import jax.numpy as jnp
from jax import lax
from jax.experimental import pallas as pl
from jax.experimental.pallas import tpu as pltpu
from jax.sharding import PartitionSpec as P

D = 5120
FFW = 10240
B = 128
H = B // 2


def gelu_slope(value):
    return (
        0.5 * (1.0 + lax.erf(value * 0.7071067811865476))
        + value * jnp.exp(-0.5 * value * value) * 0.3989422804014327
    )


def local_blocks(matrix, block, total):
    tokens, width = matrix.shape
    pieces = matrix.reshape(tokens, width // block, block)
    cov = jnp.einsum("tkb,tkc->kbc", pieces, pieces, preferred_element_type=jnp.float32)
    return cov.reshape(width, block) / total


def owned_unit(owned, block):
    count = owned.shape[0]
    rows = lax.axis_index("dp") * count + jnp.arange(count, dtype=jnp.int32)
    cols = jnp.arange(block, dtype=jnp.int32)
    return (cols[None, :] == (rows % block)[:, None]).astype(jnp.float32)


def plain(saved_input, saved_pre, grad_act):
    total = jnp.float32(saved_input.shape[0] * lax.axis_size("dp"))
    slope = gelu_slope(saved_pre.astype(jnp.float32))
    grad_pre = (grad_act.astype(jnp.float32) * slope).astype(jnp.bfloat16)
    terms_a = local_blocks(saved_input, B, total)
    terms_g = local_blocks(grad_pre, B, total)
    owned_a = lax.psum_scatter(terms_a, "dp", scatter_dimension=0, tiled=True)
    owned_g = lax.psum_scatter(terms_g, "dp", scatter_dimension=0, tiled=True)
    unit_a = owned_unit(owned_a, B)
    unit_g = owned_unit(owned_g, B)
    trace_a, trace_g = lax.psum(
        (jnp.sum(owned_a * unit_a), jnp.sum(owned_g * unit_g)), ("dp", "tensor")
    )
    ratio = jnp.sqrt(trace_a / D / (trace_g / FFW))
    damp = jnp.sqrt(jnp.float32(0.1))
    return (
        (owned_a + ratio * damp * unit_a)[None],
        (owned_g + damp / ratio * unit_g)[None],
    )


EDGE = 8
SLOTS = 8
X, NEAR, FAR = 0, 1, 2
KINDS = (((X, NEAR, FAR), (NEAR, X, FAR)), ((NEAR, X, FAR), (X, NEAR, FAR)))
NOTES = len(KINDS) * SLOTS


def split_rows(count):
    return count // B, (count % B) // H


def has_edge(pieces, k):
    return all(later[3] != pieces[k][3] for later in pieces[k + 1 :])


def piece_rows(pieces, k):
    a_blocks, a_half, g_blocks, _ = pieces[k]
    rows = (len(a_blocks) + len(g_blocks)) * H + a_half * (H * 3 // 4)
    return rows + (EDGE if has_edge(pieces, k) else 0)


def corner_indices(pieces, k):
    parts = [len(a) + a_half + len(g) if kind == pieces[k][3] else 0 for a, a_half, g, kind in pieces]
    return iter(range(sum(parts[:k]), sum(parts[: k + 1])))


def iotas(rows):
    shape = (rows, B)
    return lax.broadcasted_iota(jnp.int32, shape, 0), lax.broadcasted_iota(jnp.int32, shape, 1)


def slot_owner(slot, orders):
    core = lax.axis_index("tensor")
    mask = 0
    for stage, (one, other) in enumerate(zip(*orders)):
        mask = mask | (((slot >> (2 - stage)) & 1) << (one + core * (other - one)))
    return lax.axis_index("dp") ^ mask


def lanes(start, size):
    return pl.ds(start if isinstance(start, int) else pl.multiple_of(start, B), size)


def pack_body(pieces, items, count_a, count_g, fresh, *refs):
    a_hbm, pre_hbm, grad_hbm = refs[:3]
    notes_in = None if fresh else refs[3]
    refs = refs[3 if fresh else 4 :]
    n = len(items)
    outs, notes = refs[:n], refs[n]
    buffers, sems = refs[n + 1 : 5 * n + 1], refs[5 * n + 1]
    full, half = split_rows(count_a)
    slots = SLOTS // 2

    def copies(i, slot):
        k, first = items[i]
        a_blocks, a_half, g_blocks, kind = pieces[k]
        a_buf, half_buf, pre_buf, grad_buf = buffers[4 * i : 4 * i + 4]
        owner = slot_owner(first + slot, KINDS[kind])
        odd = owner & half
        base = (owner >> half) * (full * (1 + half) + half) * B
        moves = []
        if a_blocks:
            start = base + odd * (full + 1) * B + a_blocks[0] * B
            moves.append((a_hbm, start, a_buf))
        if a_half:
            moves.append((a_hbm, base + full * B, half_buf))
        if g_blocks:
            start = owner * count_g + g_blocks[0] * B
            moves += [(pre_hbm, start, pre_buf), (grad_hbm, start, grad_buf)]
        return [
            pltpu.make_async_copy(
                src.at[:, lanes(start, dst.shape[2])], dst.at[slot], sems.at[i, slot, m]
            )
            for m, (src, start, dst) in enumerate(moves)
        ]

    for i in range(n):
        for slot in range(slots):
            for copy in copies(i, slot):
                copy.start()

    row, col = iotas(H)
    low = col < row
    diag_low, diag_high = col == row, col == row + H
    quarter = H // 2
    row_q, col_q = row[:quarter], col[:quarter]
    note_row, _ = iotas(EDGE)
    zero = jnp.zeros((H, B), jnp.float32)
    traces = [zero, zero]
    tiles = {}

    def cov(part):
        return lax.dot_general(
            part, part, (((0,), (0,)), ((), ())), preferred_element_type=jnp.float32
        )

    def note(slot, index, corner, natural):
        line = jnp.sum(corner, axis=0, keepdims=True)
        if index % 2 != natural:
            line = pltpu.roll(line, H, 1)
        tiles[slot] = tiles[slot] + jnp.where(note_row == index // 2, line, 0.0)

    def fold(block, slot, index, which):
        top, bottom = block[:H], block[H:]
        corner = jnp.where(diag_high, bottom, zero)
        note(slot, index, corner, 0)
        traces[which] = traces[which] + corner + jnp.where(diag_low, top, zero)
        return jnp.where(low, pltpu.roll(bottom, H, 1), top)

    def fold_half(block, odd, slot, index):
        part = jnp.where(odd == 1, pltpu.roll(block[H:], H, 1), block[:H])
        traces[0] = traces[0] + jnp.where(diag_low, part, zero)
        upper, lower = part[:quarter], part[quarter:]
        corner = jnp.where(col_q == row_q + quarter, lower, 0.0)
        note(slot, index, corner, 1)
        square = jnp.where(col_q < row_q, pltpu.roll(lower, B - quarter, 1), upper)
        rest = lower.reshape(2, quarter // 2, B)
        rest = jnp.where(col[: quarter // 2] < H, pltpu.roll(rest[1], H, 1), rest[0])
        return square, rest

    for i, (k, first) in enumerate(items):
        a_blocks, a_half, g_blocks, kind = pieces[k]
        a_buf, half_buf, pre_buf, grad_buf = buffers[4 * i : 4 * i + 4]
        out = outs[i]
        for slot in range(slots):
            for copy in copies(i, slot):
                copy.wait()
        for slot in range(slots):
            here = kind * SLOTS + first + slot
            if here not in tiles:
                tiles[here] = jnp.zeros((EDGE, B), jnp.float32) if fresh else notes_in[here]
            index = corner_indices(pieces, k)
            at = 0
            for b in range(len(a_blocks)):
                block = cov(a_buf[slot, :, b * B : (b + 1) * B])
                out[slot, at : at + H, :] = fold(block, here, next(index), 0)
                at = at + H
            if a_half:
                odd = slot_owner(first + slot, KINDS[kind]) & 1
                square, rest = fold_half(cov(half_buf[slot]), odd, here, next(index))
                out[slot, at : at + quarter, :] = square
                out[slot, at + quarter : at + quarter * 3 // 2, :] = rest
                at = at + quarter * 3 // 2
            for b in range(len(g_blocks)):
                part = slice(b * B, (b + 1) * B)
                value = pre_buf[slot, :, part].astype(jnp.float32)
                grad = grad_buf[slot, :, part].astype(jnp.float32)
                block = cov((grad * gelu_slope(value)).astype(jnp.bfloat16))
                out[slot, at : at + H, :] = fold(block, here, next(index), 1)
                at = at + H
            if has_edge(pieces, k):
                out[slot, at:, :] = tiles[here]

    for slot in range(NOTES):
        if slot in tiles:
            notes[slot] = tiles[slot]
        else:
            notes[slot] = jnp.zeros((EDGE, B), jnp.float32) if fresh else notes_in[slot]
    lines = [jnp.sum(trace, axis=0, keepdims=True) for trace in traces]
    tile = jnp.where(note_row == 0, lines[0], jnp.where(note_row == 1, lines[1], 0.0))
    notes[NOTES] = tile if fresh else notes_in[NOTES] + tile


def pack(arrays, pieces, items, count_a, count_g, notes):
    tokens, dtype = arrays[0].shape[0], arrays[0].dtype
    slots = SLOTS // 2
    scratch = []
    for k, _ in items:
        a_blocks, _, g_blocks, _ = pieces[k]
        for size in (len(a_blocks), 1, len(g_blocks), len(g_blocks)):
            scratch.append(pltpu.VMEM((slots, tokens, max(size, 1) * B), dtype))
    fresh = notes is None
    *chunks, notes = pl.pallas_call(
        functools.partial(pack_body, pieces, items, count_a, count_g, fresh),
        in_specs=[pl.BlockSpec(memory_space=pltpu.HBM)] * 3
        + [pl.BlockSpec(memory_space=pltpu.VMEM)] * (not fresh),
        out_specs=[pl.BlockSpec(memory_space=pltpu.VMEM)] * (len(items) + 1),
        out_shape=[
            jax.ShapeDtypeStruct((slots, piece_rows(pieces, k), B), jnp.float32)
            for k, _ in items
        ]
        + [jax.ShapeDtypeStruct((NOTES + 1, EDGE, B), jnp.float32)],
        scratch_shapes=scratch + [pltpu.SemaphoreType.DMA((len(items), slots, 4))],
        compiler_params=pltpu.CompilerParams(vmem_limit_bytes=32 * 2**20),
        cost_estimate=pl.CostEstimate(flops=1, bytes_accessed=1, transcendentals=0),
    )(*arrays, *([] if fresh else [notes]))
    return chunks, notes


def finish_body(pieces, count_a, total, *refs):
    n = len(pieces)
    trace_ref, owns, gots = refs[0], refs[1 : n + 1], refs[n + 1 : 2 * n + 1]
    a_ref, g_ref = refs[2 * n + 1 :]
    full, half = split_rows(count_a)
    odd = lax.axis_index("dp") & half
    row, col = iotas(H)
    quarter = H // 2
    row_q, col_q = row[:quarter], col[:quarter]

    def mean(value):
        return value * (1.0 / total) if math.frexp(total)[0] == 0.5 else value / total

    sums = mean(jnp.sum(trace_ref[...] + gots[-1][0, -2:, :], axis=1, keepdims=True))
    ratio = jnp.sqrt(sums[0:1] / D / (sums[1:2] / FFW))
    damp = jnp.sqrt(jnp.full((1, 1), 0.1, jnp.float32))
    shift_a, shift_g = ratio * damp, damp / ratio

    edges = {}
    for k in range(n):
        if has_edge(pieces, k):
            edge = mean(owns[k][0, -EDGE:, :] + gots[k][0, -EDGE:, :])
            edges[pieces[k][3]] = (edge, pltpu.roll(edge, H, 1))

    def corner(kind, index, natural):
        line = index // 2
        return edges[kind][0 if index % 2 == natural else 1][line : line + 1]

    def turn(folded):
        return jnp.concatenate([folded] * (B // folded.shape[0]), axis=0).T

    def unfold(folded, kind, index, shift, out, start):
        turned = turn(folded)
        top = jnp.where(col < row, turned[:H], folded)
        last = pltpu.roll(jnp.where(col < row, folded, turned[:H]), H, 1)
        bottom = jnp.where(
            col < H, turned[H:], jnp.where(col == row + H, corner(kind, index, 0), last)
        )
        out[pl.ds(start, H), :] = top + jnp.where(col == row, shift, 0.0)
        out[pl.ds(start + H, H), :] = bottom + jnp.where(col == row + H, shift, 0.0)

    def unfold_half(square, rest, kind, index, shift, out, start):
        turned = turn(square)
        upper = jnp.where(col_q < row_q, turned[:quarter], square)
        last = pltpu.roll(jnp.where(col_q < row_q, square, turned[:quarter]), quarter, 1)
        last = jnp.where(col_q == row_q + quarter, corner(kind, index, 1), last)
        lower = jnp.where(col_q < quarter, turned[quarter:H], last)
        rest = jnp.concatenate([rest, pltpu.roll(rest, H, 1)], axis=0)
        lower = jnp.where(col_q < H, lower, rest)
        part = jnp.concatenate([upper, lower], axis=0) + jnp.where(col == row, shift, 0.0)
        out[pl.ds(start, H), :] = jnp.where(odd == 1, pltpu.roll(part, H, 1), part)

    for k, (own, got) in enumerate(zip(owns, gots)):
        a_blocks, a_half, g_blocks, kind = pieces[k]
        index = corner_indices(pieces, k)
        at = 0

        def take(rows):
            nonlocal at
            at = at + rows
            return mean(own[0, at - rows : at, :] + got[0, at - rows : at, :])

        for b in a_blocks:
            start = pl.multiple_of(b * B + odd * H, H) if half else b * B
            unfold(take(H), kind, next(index), shift_a, a_ref, start)
        if a_half:
            square, rest = take(quarter), take(quarter // 2)
            start = pl.multiple_of((1 - odd) * full * B, H)
            unfold_half(square, rest, kind, next(index), shift_a, a_ref, start)
        for b in g_blocks:
            unfold(take(H), kind, next(index), shift_g, g_ref, b * B)


def finish(pieces, trace, owns, gots, count_a, count_g, total):
    args = (trace, *owns, *gots)
    return pl.pallas_call(
        functools.partial(finish_body, pieces, count_a, total),
        in_specs=[pl.BlockSpec(memory_space=pltpu.VMEM)] * len(args),
        out_specs=[pl.BlockSpec(memory_space=pltpu.VMEM)] * 2,
        out_shape=[
            jax.ShapeDtypeStruct((count_a, B), jnp.float32),
            jax.ShapeDtypeStruct((count_g, B), jnp.float32),
        ],
        compiler_params=pltpu.CompilerParams(vmem_limit_bytes=32 * 2**20),
    )(*args)


def swap(value, partner):
    dp, tensor = lax.axis_size("dp"), lax.axis_size("tensor")
    pairs = []
    for i in range(dp):
        for j in range(tensor):
            other = partner(i, j)
            pairs.append((i * tensor + j, other[0] * tensor + other[1]))
    return lax.ppermute(value, ("dp", "tensor"), pairs)


def along(stage, kind):
    return lambda i, j: (i ^ (1 << KINDS[kind][j][stage]), j)


def halve(keep, got):
    half = keep.shape[0] // 2
    return keep[:half] + got[:half], keep[half:] + got[half:]


def with_trace(send, trace):
    return lax.dynamic_update_slice(send, trace[None], (0, send.shape[1] - 2, 0))


def packed(saved_input, saved_pre, grad_act):
    dp = lax.axis_size("dp")
    total = float(saved_input.shape[0] * dp)
    count_a = saved_input.shape[1] // dp
    count_g = saved_pre.shape[1] // dp
    full_a, half_a = split_rows(count_a)
    full_g, _ = split_rows(count_g)
    some = 1 + (full_g - 1) // 2
    pieces = (
        (tuple(range(full_a)), 0, (), 0),
        ((), 0, tuple(range(1, some)), 0),
        ((), half_a, (0,), 1),
        ((), 0, tuple(range(some, full_g)), 1),
    )
    arrays = tuple(
        pltpu.with_memory_space_constraint(array, pltpu.HBM)
        for array in (saved_input, saved_pre, grad_act)
    )
    chunks = range(len(pieces))
    last = len(pieces) - 1
    keep, send = 0, SLOTS // 2

    keeps, gots, notes = {}, {}, None
    calls = (
        ((0, send), (2, send)),
        ((1, send), (3, send)),
        ((0, keep), (2, keep), (1, keep), (3, keep)),
    )
    for items in calls:
        parts, notes = pack(arrays, pieces, items, count_a, count_g, notes)
        for (k, first), part in zip(items, parts):
            if first == send:
                gots[k] = swap(part, along(0, pieces[k][3]))
            else:
                keeps[k] = part

    trace = notes[NOTES, :2, :]
    trace = trace + swap(trace, lambda i, j: (i, j ^ 1))
    carriers = ((1, 1), (last, 1), (last, 2))
    for stage in (1, 2):
        for k in chunks:
            keeps[k], part = halve(keeps[k], gots[k])
            if (k, stage) in carriers:
                if (k, stage) != carriers[0]:
                    trace = trace + news[0, -2:, :]
                part = with_trace(part, trace)
            gots[k] = swap(part, along(stage, pieces[k][3]))
            if (k, stage) in carriers:
                news = gots[k]

    a_factor, g_factor = finish(
        pieces, trace, [keeps[k] for k in chunks], [gots[k] for k in chunks], count_a, count_g, total
    )
    return a_factor[None], g_factor[None]


def fits(count_a, count_g):
    (full_a, half_a), full_g = split_rows(count_a), count_g // B
    if count_a % H or count_g % B or full_a < 1 or full_g < 3:
        return False
    return full_a + half_a + full_g <= 2 * (EDGE - 2)


def on_device(saved_input, saved_pre, grad_act):
    dp = lax.axis_size("dp")
    count_a = saved_input.shape[1] // dp
    count_g = saved_pre.shape[1] // dp
    if dp == SLOTS and lax.axis_size("tensor") == 2 and fits(count_a, count_g):
        return packed(saved_input, saved_pre, grad_act)
    return plain(saved_input, saved_pre, grad_act)


def solution(mesh):
    spec = P(("groups", "dp"), "tensor")
    out = P("tensor", ("groups", "dp"), None)
    return jax.shard_map(
        on_device, mesh=mesh, in_specs=(spec, spec, spec), out_specs=(out, out), check_vma=False
    )
```

time: 39.3 us -> 39.3 us (level)
  waiting for transfers between devices: 11.3 us -> 9.1 us
  starting transfers between devices: 17.9 us -> 19.8 us
    ppermute x13, waiting for transfers between devices: 11.3 us -> 9.1 us  [swap(): return lax.ppermute(value, ('dp', 'tensor'), pairs)]
    ppermute x13, starting transfers between devices: 17.9 us -> 19.8 us  [swap(): return lax.ppermute(value, ('dp', 'tensor'), pairs)]
  transfers between devices with their start and end apart: 13 -> 13, of which waited for: 6 -> 4; matrix products, arithmetic and copies ran while one was open for 1% -> 1% of each run, Pallas kernels for 15% -> 15%
where the time goes in v5:
time: 39.3 us; the launch traced here: 39 us
  starting transfers between devices  19.8 us (50%)
  waiting for transfers between devices  9.1 us (23%)
  Pallas kernels  9.07 us (23%)
  between operations  0.72 us (2%)
    ppermute x13, starting transfers between devices, swap(): return lax.ppermute(value, ('dp', 'tensor'), pairs)  19.8 us
    ppermute x13, waiting for transfers between devices, swap(): return lax.ppermute(value, ('dp', 'tensor'), pairs)  9.1 us
    pallas_call x3, Pallas kernels, pack(): pl.pallas_call(functools.partial(pack_body, pieces, items, count_a, count...  7.92 us
    pallas_call x1, Pallas kernels, finish(): pl.pallas_call(functools.partial(finish_body, pieces, count_a, total), in...  1.15 us
  transfers between devices with their start and end apart: 13, of which 4 were waited for; matrix products, arithmetic and copies ran while one was open for 1% of the time, Pallas kernels for 15%

profile of v5, /device:TPU:0, one launch (start us, length us, event | category | flops | bytes accessed | tf_op | source)
XLA Modules:
  0.0 39.0 jit_solution(1328676996960474651)
XLA Ops:
  0.6 2.0 %shard_map.50 = (f32[4,128,128]{2,1,0:T(8,128)S(1)}, f32[4,112,128]{2,1,0:T(8,128)S(1)}, f32[17,8,128]{2,1,0:T(8,128)S(1)}) custom-call(bf16[128,2560]{1,0:T(8,128)(2,1)} %refs_0_.5, bf16[128,5120]{1,0:T(8,128)(2,1)} %refs_1_.5, bf16[128,5120]{1,0:T(8,128)(2,1)} %refs_2_.5), custom_call_target="tpu_custom_call" | custom-call | flops 1 | bytes 1 | tf_op jit(solution)/shard_map/pallas_call | solution.py:231
  2.7 3.1 %collective-permute-start.7 = (f32[4,112,128]{2,1,0:T(8,128)S(1)}, f32[4,112,128]{2,1,0:T(8,128)S(1)}, u32[]{:S(2)}, u32[]{:S(2)}) collective-permute-start(f32[4,112,128]{2,1,0:T(8,128)S(1)} %get-tuple-element.25), channel_id=1, source_target_pairs={{0,4},{1,3},{2,6},{3,1},{4,0},{5,7},{6,2},{7,5},{8,12},{9,11},{10,... | collective-permute-start | bytes 688136 | tf_op jit(solution)/shard_map/ppermute | solution.py:342
  5.8 1.5 %collective-permute-start.5 = (f32[4,128,128]{2,1,0:T(8,128)S(1)}, f32[4,128,128]{2,1,0:T(8,128)S(1)}, u32[]{:S(2)}, u32[]{:S(2)}) collective-permute-start(f32[4,128,128]{2,1,0:T(8,128)S(1)} %get-tuple-element.23), channel_id=1, source_target_pairs={{0,2},{1,5},{2,0},{3,7},{4,6},{5,1},{6,4},{7,3},{8,10},{9,13},{10,... | collective-permute-start | bytes 786440 | tf_op jit(solution)/shard_map/ppermute | solution.py:342
  7.3 2.4 %shard_map.51 = (f32[4,136,128]{2,1,0:T(8,128)S(1)}, f32[4,136,128]{2,1,0:T(8,128)S(1)}, f32[17,8,128]{2,1,0:T(8,128)S(1)}) custom-call(bf16[128,2560]{1,0:T(8,128)(2,1)} %refs_0_.5, bf16[128,5120]{1,0:T(8,128)(2,1)} %refs_1_.5, bf16[128,5120]{1,0:T(8,128)(2,1)} %refs_2_.5, f32[17,8,128]{2,1,0:T(8,128)S(1)} %get-tuple-element.15.refs_3_), custom_call_target="tpu_custom_call" | custom-call | flops 1 | bytes 1 | tf_op jit(solution)/shard_map/pallas_call | solution.py:231
  9.7 0.6 %collective-permute-start.1 = (f32[4,136,128]{2,1,0:T(8,128)S(1)}, f32[4,136,128]{2,1,0:T(8,128)S(1)}, u32[]{:S(2)}, u32[]{:S(2)}) collective-permute-start(f32[4,136,128]{2,1,0:T(8,128)S(1)} %get-tuple-element.19), channel_id=1, source_target_pairs={{0,2},{1,5},{2,0},{3,7},{4,6},{5,1},{6,4},{7,3},{8,10},{9,13},{10,... | collective-permute-start | bytes 835592 | tf_op jit(solution)/shard_map/ppermute | solution.py:342
  10.3 0.1 collective-permute-start.3
  10.4 3.4 %shard_map.52 = (f32[4,128,128]{2,1,0:T(8,128)S(1)}, f32[4,112,128]{2,1,0:T(8,128)S(1)}, f32[4,136,128]{2,1,0:T(8,128)S(1)}, f32[4,136,128]{2,1,0:T(8,128)S(1)}, f32[17,8,128]{2,1,0:T(8,128)S(1)}) custom-call(bf16[128,2560]{1,0:T(8,128)(2,1)} %refs_0_.5, bf16[128,5120]{1,0:T(8,128)(2,1)} %refs_1_.5, bf16[128,5120]{1,0:T(8,128)(2,1)} %refs_2_.5, ...), custom_call_target="tpu_custom_call" | custom-call | flops 1 | bytes 1 | tf_op jit(solution)/shard_map/pallas_call | solution.py:231
  13.8 0.1 collective-permute-start
  13.9 0.0 collective-permute-done.7
  14.0 1.9 %collective-permute-start.8 = (f32[2,112,128]{2,1,0:T(8,128)S(1)}, f32[2,112,128]{2,1,0:T(8,128)S(1)}, u32[]{:S(2)}, u32[]{:S(2)}) collective-permute-start(f32[2,112,128]{2,1,0:T(8,128)S(1)} %get-tuple-element.37), channel_id=1, source_target_pairs={{0,2},{1,5},{2,0},{3,7},{4,6},{5,1},{6,4},{7,3},{8,10},{9,13},{10,... | collective-permute-start | bytes 344072 | tf_op jit(solution)/shard_map/ppermute | solution.py:342
  15.9 1.6 %collective-permute-start.6 = (f32[2,128,128]{2,1,0:T(8,128)S(1)}, f32[2,128,128]{2,1,0:T(8,128)S(1)}, u32[]{:S(2)}, u32[]{:S(2)}) collective-permute-start(f32[2,128,128]{2,1,0:T(8,128)S(1)} %get-tuple-element.35), channel_id=1, source_target_pairs={{0,4},{1,3},{2,6},{3,1},{4,0},{5,7},{6,2},{7,5},{8,12},{9,11},{10,... | collective-permute-start | bytes 393224 | tf_op jit(solution)/shard_map/ppermute | solution.py:342
  17.6 0.5 %collective-permute-done.1 = f32[4,136,128]{2,1,0:T(8,128)S(1)} collective-permute-done((f32[4,136,128]{2,1,0:T(8,128)S(1)}, f32[4,136,128]{2,1,0:T(8,128)S(1)}, u32[]{:S(2)}, u32[]{:S(2)}) %collective-permute-start.1) | collective-permute-done | bytes 278560 | tf_op jit(solution)/shard_map/ppermute | solution.py:342
  18.2 1.6 %collective-permute-start.2 = (f32[2,136,128]{2,1,0:T(8,128)S(1)}, f32[2,136,128]{2,1,0:T(8,128)S(1)}, u32[]{:S(2)}, u32[]{:S(2)}) collective-permute-start(f32[2,136,128]{2,1,0:T(8,128)S(1)} %bitcast_dynamic-update-slice_fusion.2), channel_id=1, source_target_pairs={{0,4},{1,3},{2,6},{3,1},{4,0},{5,7},{6,2},{7,5},{8,12},{9,11},{10,... | collective-permute-start | bytes 417800 | tf_op jit(solution)/shard_map/ppermute | solution.py:342
  19.7 0.0 collective-permute-done.3
  19.8 1.4 %collective-permute-done.6 = f32[2,128,128]{2,1,0:T(8,128)S(1)} collective-permute-done((f32[2,128,128]{2,1,0:T(8,128)S(1)}, f32[2,128,128]{2,1,0:T(8,128)S(1)}, u32[]{:S(2)}, u32[]{:S(2)}) %collective-permute-start.6) | collective-permute-done | bytes 131104 | tf_op jit(solution)/shard_map/ppermute | solution.py:342
  21.2 3.1 %collective-permute-start.9 = (f32[1,128,128]{2,1,0:T(8,128)S(1)}, f32[1,128,128]{2,1,0:T(8,128)S(1)}, u32[]{:S(2)}, u32[]{:S(2)}) collective-permute-start(f32[1,128,128]{2,1,0:T(8,128)S(1)} %get-tuple-element.42), channel_id=1, source_target_pairs={{0,8},{1,9},{2,10},{3,11},{4,12},{5,13},{6,14},{7,15},{8,0},{9,1},... | collective-permute-start | bytes 196616 | tf_op jit(solution)/shard_map/ppermute | solution.py:342
  24.3 0.7 %collective-permute-start.4 = (f32[2,136,128]{2,1,0:T(8,128)S(1)}, f32[2,136,128]{2,1,0:T(8,128)S(1)}, u32[]{:S(2)}, u32[]{:S(2)}) collective-permute-start(f32[2,136,128]{2,1,0:T(8,128)S(1)} %bitcast_dynamic-update-slice_fusion.1), channel_id=1, source_target_pairs={{0,2},{1,5},{2,0},{3,7},{4,6},{5,1},{6,4},{7,3},{8,10},{9,13},{10,... | collective-permute-start | bytes 417800 | tf_op jit(solution)/shard_map/ppermute | solution.py:342
  25.0 2.5 %collective-permute-start.10 = (f32[1,136,128]{2,1,0:T(8,128)S(1)}, f32[1,136,128]{2,1,0:T(8,128)S(1)}, u32[]{:S(2)}, u32[]{:S(2)}) collective-permute-start(f32[1,136,128]{2,1,0:T(8,128)S(1)} %get-tuple-element.38), channel_id=1, source_target_pairs={{0,8},{1,9},{2,10},{3,11},{4,12},{5,13},{6,14},{7,15},{8,0},{9,1},... | collective-permute-start | bytes 208904 | tf_op jit(solution)/shard_map/ppermute | solution.py:342
  27.6 1.9 %collective-permute-done.4 = f32[2,136,128]{2,1,0:T(8,128)S(1)} collective-permute-done((f32[2,136,128]{2,1,0:T(8,128)S(1)}, f32[2,136,128]{2,1,0:T(8,128)S(1)}, u32[]{:S(2)}, u32[]{:S(2)}) %collective-permute-start.4) | collective-permute-done | bytes 139296 | tf_op jit(solution)/shard_map/ppermute | solution.py:342
  29.5 1.7 %collective-permute-start.12 = (f32[1,136,128]{2,1,0:T(8,128)S(1)}, f32[1,136,128]{2,1,0:T(8,128)S(1)}, u32[]{:S(2)}, u32[]{:S(2)}) collective-permute-start(f32[1,136,128]{2,1,0:T(8,128)S(1)} %get-tuple-element.28), channel_id=1, source_target_pairs={{0,8},{1,9},{2,10},{3,11},{4,12},{5,13},{6,14},{7,15},{8,0},{9,1},... | collective-permute-start | bytes 208904 | tf_op jit(solution)/shard_map/ppermute | solution.py:342
  31.1 0.0 collective-permute-done.8
  31.2 1.4 %collective-permute-start.11 = (f32[1,112,128]{2,1,0:T(8,128)S(1)}, f32[1,112,128]{2,1,0:T(8,128)S(1)}, u32[]{:S(2)}, u32[]{:S(2)}) collective-permute-start(f32[1,112,128]{2,1,0:T(8,128)S(1)} %get-tuple-element.44), channel_id=1, source_target_pairs={{0,8},{1,9},{2,10},{3,11},{4,12},{5,13},{6,14},{7,15},{8,0},{9,1},... | collective-permute-start | bytes 172040 | tf_op jit(solution)/shard_map/ppermute | solution.py:342
  32.6 5.3 %collective-permute-done.11.refs_7_ = f32[1,112,128]{2,1,0:T(8,128)S(1)} collective-permute-done((f32[1,112,128]{2,1,0:T(8,128)S(1)}, f32[1,112,128]{2,1,0:T(8,128)S(1)}, u32[]{:S(2)}, u32[]{:S(2)}) %collective-permute-start.11) | collective-permute-done | bytes 57376 | tf_op jit(solution)/shard_map/ppermute | solution.py:342
  37.8 1.1 %shard_map.53 = (f32[320,128]{1,0:T(8,128)}, f32[640,128]{1,0:T(8,128)}) custom-call(f32[2,128]{1,0:T(2,128)S(1)} %get-tuple-element.29.refs_0_, f32[1,128,128]{2,1,0:T(8,128)S(1)} %get-tuple-element.43.refs_1_, f32[1,136,128]{2,1,0:T(8,128)S(1)} %get-tuple-element.39.refs_2_, f32[1,112,128]{2,1,0:T(8,128)S(1)} %get-tuple-element.45.refs_3_, ...), custom_call_target="tpu_custom_call" | custom-call | tf_op jit(solution)/shard_map/pallas_call | solution.py:323
  (18 shorter events, 0.3 us)
Async XLA Ops:
  2.7 11.2 %collective-permute-start.7 = (f32[4,112,128]{2,1,0:T(8,128)S(1)}, f32[4,112,128]{2,1,0:T(8,128)S(1)}, u32[]{:S(2)}, u32[]{:S(2)}) collective-permute-start(f32[4,112,128]{2,1,0:T(8,128)S(1)} %get-tuple-element.25), channel_id=1, source_target_pairs={{0,4},{1,3},{2,6},{3,1},{4,0},{5,7},{6,2},{7,5},{8,12},{9,11},{10,... | collective-permute-start | bytes 688136 | tf_op jit(solution)/shard_map/ppermute | solution.py:342
  5.8 10.1 %collective-permute-start.5 = (f32[4,128,128]{2,1,0:T(8,128)S(1)}, f32[4,128,128]{2,1,0:T(8,128)S(1)}, u32[]{:S(2)}, u32[]{:S(2)}) collective-permute-start(f32[4,128,128]{2,1,0:T(8,128)S(1)} %get-tuple-element.23), channel_id=1, source_target_pairs={{0,2},{1,5},{2,0},{3,7},{4,6},{5,1},{6,4},{7,3},{8,10},{9,13},{10,... | collective-permute-start | bytes 786440 | tf_op jit(solution)/shard_map/ppermute | solution.py:342
  9.7 8.4 %collective-permute-start.1 = (f32[4,136,128]{2,1,0:T(8,128)S(1)}, f32[4,136,128]{2,1,0:T(8,128)S(1)}, u32[]{:S(2)}, u32[]{:S(2)}) collective-permute-start(f32[4,136,128]{2,1,0:T(8,128)S(1)} %get-tuple-element.19), channel_id=1, source_target_pairs={{0,2},{1,5},{2,0},{3,7},{4,6},{5,1},{6,4},{7,3},{8,10},{9,13},{10,... | collective-permute-start | bytes 835592 | tf_op jit(solution)/shard_map/ppermute | solution.py:342
  10.3 9.4 %collective-permute-start.3 = (f32[4,136,128]{2,1,0:T(8,128)S(1)}, f32[4,136,128]{2,1,0:T(8,128)S(1)}, u32[]{:S(2)}, u32[]{:S(2)}) collective-permute-start(f32[4,136,128]{2,1,0:T(8,128)S(1)} %get-tuple-element.21), channel_id=1, source_target_pairs={{0,4},{1,3},{2,6},{3,1},{4,0},{5,7},{6,2},{7,5},{8,12},{9,11},{10,... | collective-permute-start | bytes 835592 | tf_op jit(solution)/shard_map/ppermute | solution.py:342
  13.8 4.3 %collective-permute-start = (f32[2,128]{1,0:T(2,128)S(1)}, f32[2,128]{1,0:T(2,128)S(1)}, u32[]{:S(2)}, u32[]{:S(2)}) collective-permute-start(f32[2,128]{1,0:T(2,128)S(1)} %slice_bitcast_fusion.2), channel_id=1, source_target_pairs={{0,1},{1,0},{2,3},{3,2},{4,5},{5,4},{6,7},{7,6},{8,9},{9,8},{10,11... | collective-permute-start | bytes 3080 | tf_op jit(solution)/shard_map/ppermute | solution.py:342
  14.0 17.2 %collective-permute-start.8 = (f32[2,112,128]{2,1,0:T(8,128)S(1)}, f32[2,112,128]{2,1,0:T(8,128)S(1)}, u32[]{:S(2)}, u32[]{:S(2)}) collective-permute-start(f32[2,112,128]{2,1,0:T(8,128)S(1)} %get-tuple-element.37), channel_id=1, source_target_pairs={{0,2},{1,5},{2,0},{3,7},{4,6},{5,1},{6,4},{7,3},{8,10},{9,13},{10,... | collective-permute-start | bytes 344072 | tf_op jit(solution)/shard_map/ppermute | solution.py:342
  15.9 5.3 %collective-permute-start.6 = (f32[2,128,128]{2,1,0:T(8,128)S(1)}, f32[2,128,128]{2,1,0:T(8,128)S(1)}, u32[]{:S(2)}, u32[]{:S(2)}) collective-permute-start(f32[2,128,128]{2,1,0:T(8,128)S(1)} %get-tuple-element.35), channel_id=1, source_target_pairs={{0,4},{1,3},{2,6},{3,1},{4,0},{5,7},{6,2},{7,5},{8,12},{9,11},{10,... | collective-permute-start | bytes 393224 | tf_op jit(solution)/shard_map/ppermute | solution.py:342
  18.2 6.1 %collective-permute-start.2 = (f32[2,136,128]{2,1,0:T(8,128)S(1)}, f32[2,136,128]{2,1,0:T(8,128)S(1)}, u32[]{:S(2)}, u32[]{:S(2)}) collective-permute-start(f32[2,136,128]{2,1,0:T(8,128)S(1)} %bitcast_dynamic-update-slice_fusion.2), channel_id=1, source_target_pairs={{0,4},{1,3},{2,6},{3,1},{4,0},{5,7},{6,2},{7,5},{8,12},{9,11},{10,... | collective-permute-start | bytes 417800 | tf_op jit(solution)/shard_map/ppermute | solution.py:342
  21.2 16.6 %collective-permute-start.9 = (f32[1,128,128]{2,1,0:T(8,128)S(1)}, f32[1,128,128]{2,1,0:T(8,128)S(1)}, u32[]{:S(2)}, u32[]{:S(2)}) collective-permute-start(f32[1,128,128]{2,1,0:T(8,128)S(1)} %get-tuple-element.42), channel_id=1, source_target_pairs={{0,8},{1,9},{2,10},{3,11},{4,12},{5,13},{6,14},{7,15},{8,0},{9,1},... | collective-permute-start | bytes 196616 | tf_op jit(solution)/shard_map/ppermute | solution.py:342
  24.3 5.1 %collective-permute-start.4 = (f32[2,136,128]{2,1,0:T(8,128)S(1)}, f32[2,136,128]{2,1,0:T(8,128)S(1)}, u32[]{:S(2)}, u32[]{:S(2)}) collective-permute-start(f32[2,136,128]{2,1,0:T(8,128)S(1)} %bitcast_dynamic-update-slice_fusion.1), channel_id=1, source_target_pairs={{0,2},{1,5},{2,0},{3,7},{4,6},{5,1},{6,4},{7,3},{8,10},{9,13},{10,... | collective-permute-start | bytes 417800 | tf_op jit(solution)/shard_map/ppermute | solution.py:342
  25.0 12.8 %collective-permute-start.10 = (f32[1,136,128]{2,1,0:T(8,128)S(1)}, f32[1,136,128]{2,1,0:T(8,128)S(1)}, u32[]{:S(2)}, u32[]{:S(2)}) collective-permute-start(f32[1,136,128]{2,1,0:T(8,128)S(1)} %get-tuple-element.38), channel_id=1, source_target_pairs={{0,8},{1,9},{2,10},{3,11},{4,12},{5,13},{6,14},{7,15},{8,0},{9,1},... | collective-permute-start | bytes 208904 | tf_op jit(solution)/shard_map/ppermute | solution.py:342
  29.5 8.4 %collective-permute-start.12 = (f32[1,136,128]{2,1,0:T(8,128)S(1)}, f32[1,136,128]{2,1,0:T(8,128)S(1)}, u32[]{:S(2)}, u32[]{:S(2)}) collective-permute-start(f32[1,136,128]{2,1,0:T(8,128)S(1)} %get-tuple-element.28), channel_id=1, source_target_pairs={{0,8},{1,9},{2,10},{3,11},{4,12},{5,13},{6,14},{7,15},{8,0},{9,1},... | collective-permute-start | bytes 208904 | tf_op jit(solution)/shard_map/ppermute | solution.py:342
  31.2 6.7 %collective-permute-start.11 = (f32[1,112,128]{2,1,0:T(8,128)S(1)}, f32[1,112,128]{2,1,0:T(8,128)S(1)}, u32[]{:S(2)}, u32[]{:S(2)}) collective-permute-start(f32[1,112,128]{2,1,0:T(8,128)S(1)} %get-tuple-element.44), channel_id=1, source_target_pairs={{0,8},{1,9},{2,10},{3,11},{4,12},{5,13},{6,14},{7,15},{8,0},{9,1},... | collective-permute-start | bytes 172040 | tf_op jit(solution)/shard_map/ppermute | solution.py:342

commit v6 on v5

--- a/solution.py
+++ b/solution.py
@@ -245,83 +245,165 @@
     return chunks, notes
 
 
-def finish_body(pieces, count_a, total, *refs):
-    n = len(pieces)
-    trace_ref, owns, gots = refs[0], refs[1 : n + 1], refs[n + 1 : 2 * n + 1]
-    a_ref, g_ref = refs[2 * n + 1 :]
+def halve_body(traced, n, *refs):
+    keeps, gots, refs = refs[:n], refs[n : 2 * n], refs[2 * n :]
+    traces, outs = refs[:-2 * n], refs[-2 * n :]
+    for k in range(n):
+        half = keeps[k].shape[0] // 2
+        for part in range(2):
+            here = slice(part * half, (part + 1) * half)
+            outs[2 * k + part][...] = keeps[k][here] + gots[k][here]
+    if traced:
+        value = sum((trace[...] for trace in traces[1:]), traces[0][...])
+        if len(traces) > 1:
+            value = value + sum(got[0, -2:, :] for got in gots)
+        for out in outs:
+            out[0, -2:, :] = value
+
+
+def halve(keeps, gots, traces=()):
+    n = len(keeps)
+    args = (*keeps, *gots, *traces)
+    shapes = [(keep.shape[0] // 2, *keep.shape[1:]) for keep in keeps for _ in range(2)]
+    outs = pl.pallas_call(
+        functools.partial(halve_body, bool(traces), n),
+        in_specs=[pl.BlockSpec(memory_space=pltpu.VMEM)] * len(args),
+        out_specs=[pl.BlockSpec(memory_space=pltpu.VMEM)] * (2 * n),
+        out_shape=[jax.ShapeDtypeStruct(shape, jnp.float32) for shape in shapes],
+        compiler_params=pltpu.CompilerParams(vmem_limit_bytes=32 * 2**20),
+        cost_estimate=pl.CostEstimate(flops=1, bytes_accessed=1, transcendentals=0),
+    )(*args)
+    return outs[0::2], outs[1::2]
+
+
+def mean_of(value, total):
+    return value * (1.0 / total) if math.frexp(total)[0] == 0.5 else value / total
+
+
+def turn(folded):
+    return jnp.concatenate([folded] * (B // folded.shape[0]), axis=0).T
+
+
+def unfold(folded, put):
+    row, col = iotas(H)
+    turned = turn(folded)
+    last = pltpu.roll(jnp.where(col < row, folded, turned[:H]), H, 1)
+    put(0, jnp.where(col < row, turned[:H], folded))
+    put(H, jnp.where(col < H, turned[H:], last))
+
+
+def unfold_half(square, rest, odd, put):
+    quarter = H // 2
+    row, col = iotas(quarter)
+    turned = turn(square)
+    upper = jnp.where(col < row, turned[:quarter], square)
+    last = pltpu.roll(jnp.where(col < row, square, turned[:quarter]), quarter, 1)
+    lower = jnp.where(col < quarter, turned[quarter:H], last)
+    rest = jnp.concatenate([rest, pltpu.roll(rest, H, 1)], axis=0)
+    part = jnp.concatenate([upper, jnp.where(col < H, lower, rest)], axis=0)
+    put(0, jnp.where(odd == 1, pltpu.roll(part, H, 1), part))
+
+
+def places(pieces, ks, count_a):
+    full, half = split_rows(count_a)
+    odd = lax.axis_index("dp") & half
+    for k in ks:
+        a_blocks, a_half, g_blocks, kind = pieces[k]
+        index = corner_indices(pieces, k)
+        for b in a_blocks:
+            start = pl.multiple_of(b * B + odd * H, H) if half else b * B
+            yield k, 0, start, H, next(index)
+        if a_half:
+            yield k, 0, pl.multiple_of((1 - odd) * full * B, H), H * 3 // 4, next(index)
+        for b in g_blocks:
+            yield k, 1, b * B, H, next(index)
+
+
+def unfold_body(pieces, ks, count_a, total, owns, gots, outs):
+    odd = lax.axis_index("dp") & 1
+    at = dict.fromkeys(ks, 0)
+
+    def take(k, rows):
+        i = ks.index(k)
+        at[k] = at[k] + rows
+        part = slice(at[k] - rows, at[k])
+        return mean_of(owns[i][0, part, :] + gots[i][0, part, :], total)
+
+    for k, which, start, rows, _ in places(pieces, ks, count_a):
+        def put(offset, value):
+            outs[which][pl.ds(start + offset, value.shape[0]), :] = value
+
+        if rows == H:
+            unfold(take(k, H), put)
+        else:
+            unfold_half(take(k, H // 2), take(k, H // 4), odd, put)
+
+
+def early_body(pieces, ks, count_a, total, *refs):
+    n = len(ks)
+    unfold_body(pieces, ks, count_a, total, refs[:n], refs[n : 2 * n], refs[2 * n :])
+
+
+def finish_body(pieces, early, late, count_a, total, *refs):
+    n = len(late)
+    owns, gots, (early_a, early_g, a_ref, g_ref) = refs[:n], refs[n : 2 * n], refs[2 * n :]
+    outs = (a_ref, g_ref)
     full, half = split_rows(count_a)
     odd = lax.axis_index("dp") & half
     row, col = iotas(H)
-    quarter = H // 2
-    row_q, col_q = row[:quarter], col[:quarter]
-
-    def mean(value):
-        return value * (1.0 / total) if math.frexp(total)[0] == 0.5 else value / total
-
-    sums = mean(jnp.sum(trace_ref[...] + gots[-1][0, -2:, :], axis=1, keepdims=True))
+
+    unfold_body(pieces, late, count_a, total, owns, gots, outs)
+
+    edges = {}
+    for i, k in enumerate(late):
+        edge = mean_of(owns[i][0, -EDGE:, :] + gots[i][0, -EDGE:, :], total)
+        edges[pieces[k][3]] = (edge, pltpu.roll(edge, H, 1))
+    sums = jnp.sum(edge[-2:], axis=1, keepdims=True)
     ratio = jnp.sqrt(sums[0:1] / D / (sums[1:2] / FFW))
     damp = jnp.sqrt(jnp.full((1, 1), 0.1, jnp.float32))
-    shift_a, shift_g = ratio * damp, damp / ratio
-
-    edges = {}
-    for k in range(n):
-        if has_edge(pieces, k):
-            edge = mean(owns[k][0, -EDGE:, :] + gots[k][0, -EDGE:, :])
-            edges[pieces[k][3]] = (edge, pltpu.roll(edge, H, 1))
+    shifts = (ratio * damp, damp / ratio)
 
     def corner(kind, index, natural):
         line = index // 2
         return edges[kind][0 if index % 2 == natural else 1][line : line + 1]
 
-    def turn(folded):
-        return jnp.concatenate([folded] * (B // folded.shape[0]), axis=0).T
-
-    def unfold(folded, kind, index, shift, out, start):
-        turned = turn(folded)
-        top = jnp.where(col < row, turned[:H], folded)
-        last = pltpu.roll(jnp.where(col < row, folded, turned[:H]), H, 1)
-        bottom = jnp.where(
-            col < H, turned[H:], jnp.where(col == row + H, corner(kind, index, 0), last)
-        )
-        out[pl.ds(start, H), :] = top + jnp.where(col == row, shift, 0.0)
-        out[pl.ds(start + H, H), :] = bottom + jnp.where(col == row + H, shift, 0.0)
-
-    def unfold_half(square, rest, kind, index, shift, out, start):
-        turned = turn(square)
-        upper = jnp.where(col_q < row_q, turned[:quarter], square)
-        last = pltpu.roll(jnp.where(col_q < row_q, square, turned[:quarter]), quarter, 1)
-        last = jnp.where(col_q == row_q + quarter, corner(kind, index, 1), last)
-        lower = jnp.where(col_q < quarter, turned[quarter:H], last)
-        rest = jnp.concatenate([rest, pltpu.roll(rest, H, 1)], axis=0)
-        lower = jnp.where(col_q < H, lower, rest)
-        part = jnp.concatenate([upper, lower], axis=0) + jnp.where(col == row, shift, 0.0)
-        out[pl.ds(start, H), :] = jnp.where(odd == 1, pltpu.roll(part, H, 1), part)
-
-    for k, (own, got) in enumerate(zip(owns, gots)):
-        a_blocks, a_half, g_blocks, kind = pieces[k]
-        index = corner_indices(pieces, k)
-        at = 0
-
-        def take(rows):
-            nonlocal at
-            at = at + rows
-            return mean(own[0, at - rows : at, :] + got[0, at - rows : at, :])
-
-        for b in a_blocks:
-            start = pl.multiple_of(b * B + odd * H, H) if half else b * B
-            unfold(take(H), kind, next(index), shift_a, a_ref, start)
-        if a_half:
-            square, rest = take(quarter), take(quarter // 2)
-            start = pl.multiple_of((1 - odd) * full * B, H)
-            unfold_half(square, rest, kind, next(index), shift_a, a_ref, start)
-        for b in g_blocks:
-            unfold(take(H), kind, next(index), shift_g, g_ref, b * B)
-
-
-def finish(pieces, trace, owns, gots, count_a, count_g, total):
-    args = (trace, *owns, *gots)
+    for ks in (early, late):
+        ins = (early_a, early_g) if ks is early else outs
+        for k, which, start, rows, index in places(pieces, ks, count_a):
+            src, out, shift, kind = ins[which], outs[which], shifts[which], pieces[k][3]
+            here = pl.ds(start, H)
+            if rows == H:
+                low = pl.ds(start + H, H)
+                out[here, :] = src[here, :] + jnp.where(col == row, shift, 0.0)
+                value = corner(kind, index, 0) + shift
+                out[low, :] = jnp.where(col == row + H, value, src[low, :])
+            else:
+                value = src[here, :] + jnp.where(col == row + odd * H, shift, 0.0)
+                line = corner(kind, index, 1)
+                line = jnp.where(odd == 1, pltpu.roll(line, H, 1), line) + shift
+                last = jnp.logical_and(col == row + odd * H, row >= H // 2)
+                out[here, :] = jnp.where(last, line, value)
+
+
+def unfold_early(pieces, ks, owns, gots, count_a, count_g, total):
+    args = (*owns, *gots)
     return pl.pallas_call(
-        functools.partial(finish_body, pieces, count_a, total),
+        functools.partial(early_body, pieces, ks, count_a, total),
+        in_specs=[pl.BlockSpec(memory_space=pltpu.VMEM)] * len(args),
+        out_specs=[pl.BlockSpec(memory_space=pltpu.VMEM)] * 2,
+        out_shape=[
+            jax.ShapeDtypeStruct((count_a, B), jnp.float32),
+            jax.ShapeDtypeStruct((count_g, B), jnp.float32),
+        ],
+        compiler_params=pltpu.CompilerParams(vmem_limit_bytes=32 * 2**20),
+        cost_estimate=pl.CostEstimate(flops=4 * 10**9, bytes_accessed=1, transcendentals=0),
+    )(*args)
+
+
+def finish(pieces, early, late, owns, gots, first, count_a, count_g, total):
+    args = (*owns, *gots, *first)
+    return pl.pallas_call(
+        functools.partial(finish_body, pieces, early, late, count_a, total),
         in_specs=[pl.BlockSpec(memory_space=pltpu.VMEM)] * len(args),
         out_specs=[pl.BlockSpec(memory_space=pltpu.VMEM)] * 2,
         out_shape=[
@@ -344,15 +426,6 @@
 
 def along(stage, kind):
     return lambda i, j: (i ^ (1 << KINDS[kind][j][stage]), j)
-
-
-def halve(keep, got):
-    half = keep.shape[0] // 2
-    return keep[:half] + got[:half], keep[half:] + got[half:]
-
-
-def with_trace(send, trace):
-    return lax.dynamic_update_slice(send, trace[None], (0, send.shape[1] - 2, 0))
 
 
 def packed(saved_input, saved_pre, grad_act):
@@ -373,19 +446,13 @@
         pltpu.with_memory_space_constraint(array, pltpu.HBM)
         for array in (saved_input, saved_pre, grad_act)
     )
-    chunks = range(len(pieces))
-    last = len(pieces) - 1
     keep, send = 0, SLOTS // 2
-
+    early, late = (0, 2), (1, 3)
     keeps, gots, notes = {}, {}, None
-    calls = (
-        ((0, send), (2, send)),
-        ((1, send), (3, send)),
-        ((0, keep), (2, keep), (1, keep), (3, keep)),
-    )
-    for items in calls:
+    for first, ks in ((send, early), (send, late), (keep, early + late)):
+        items = tuple((k, first) for k in ks)
         parts, notes = pack(arrays, pieces, items, count_a, count_g, notes)
-        for (k, first), part in zip(items, parts):
+        for k, part in zip(ks, parts):
             if first == send:
                 gots[k] = swap(part, along(0, pieces[k][3]))
             else:
@@ -393,20 +460,22 @@
 
     trace = notes[NOTES, :2, :]
     trace = trace + swap(trace, lambda i, j: (i, j ^ 1))
-    carriers = ((1, 1), (last, 1), (last, 2))
+    across = swap(trace, lambda i, j: (i ^ (1 << X) ^ (1 << NEAR), j))
+    traces = {early: ((), ()), late: ((trace,), (trace, across))}
     for stage in (1, 2):
-        for k in chunks:
-            keeps[k], part = halve(keeps[k], gots[k])
-            if (k, stage) in carriers:
-                if (k, stage) != carriers[0]:
-                    trace = trace + news[0, -2:, :]
-                part = with_trace(part, trace)
-            gots[k] = swap(part, along(stage, pieces[k][3]))
-            if (k, stage) in carriers:
-                news = gots[k]
-
+        for ks in (early, late):
+            own, parts = halve(
+                [keeps[k] for k in ks], [gots[k] for k in ks], traces[ks][stage - 1]
+            )
+            for k, mine, part in zip(ks, own, parts):
+                keeps[k], gots[k] = mine, swap(part, along(stage, pieces[k][3]))
+
+    def both(ks):
+        return [keeps[k] for k in ks], [gots[k] for k in ks]
+
+    first = unfold_early(pieces, early, *both(early), count_a, count_g, total)
     a_factor, g_factor = finish(
-        pieces, trace, [keeps[k] for k in chunks], [gots[k] for k in chunks], count_a, count_g, total
+        pieces, early, late, *both(late), first, count_a, count_g, total
     )
     return a_factor[None], g_factor[None]
 

time: 39.3 us -> 39.3 us (level)
  starting transfers between devices: 19.8 us -> 18.8 us
  waiting for transfers between devices: 9.1 us -> 10 us
  Pallas kernels: 9.07 us -> 9.48 us
    ppermute x13 -> x14, starting transfers between devices: 19.8 us -> 18.8 us  [swap(): return lax.ppermute(value, ('dp', 'tensor'), pairs)]
    ppermute x13 -> x14, waiting for transfers between devices: 9.1 us -> 10 us  [swap(): return lax.ppermute(value, ('dp', 'tensor'), pairs)]
    pallas_call x1 -> x6, Pallas kernels: 1.15 us -> 1.56 us  [the longest x1 1.1 us: finish(): pl.pallas_call(functools.partial(finish_body, pieces, early, late, count_...]
  transfers between devices with their start and end apart: 13 -> 14, of which waited for: 4 -> 4; matrix products, arithmetic and copies ran while one was open for 1% -> 0% of each run, Pallas kernels for 15% -> 16%
where the time goes in v6:
time: 39.3 us; the launch traced here: 39 us
  starting transfers between devices  18.8 us (48%)
  waiting for transfers between devices  10 us (25%)
  Pallas kernels  9.48 us (24%)
  between operations  0.73 us (2%)
    ppermute x14, starting transfers between devices, swap(): return lax.ppermute(value, ('dp', 'tensor'), pairs)  18.8 us
    ppermute x14, waiting for transfers between devices, swap(): return lax.ppermute(value, ('dp', 'tensor'), pairs)  10 us
    pallas_call x3, Pallas kernels, pack(): pl.pallas_call(functools.partial(pack_body, pieces, items, count_a, count...  7.92 us
    pallas_call x1, Pallas kernels, finish(): pl.pallas_call(functools.partial(finish_body, pieces, early, late, count_...  1.1 us
  transfers between devices with their start and end apart: 14, of which 4 were waited for; matrix products, arithmetic and copies ran while one was open for 0% of the time, Pallas kernels for 16%

profile of v6, /device:TPU:0, one launch (start us, length us, event | category | flops | bytes accessed | tf_op | source)
XLA Modules:
  0.0 39.0 jit_solution(3966832387194276338)
XLA Ops:
  0.6 2.0 %shard_map.50 = (f32[4,128,128]{2,1,0:T(8,128)S(1)}, f32[4,112,128]{2,1,0:T(8,128)S(1)}, f32[17,8,128]{2,1,0:T(8,128)S(1)}) custom-call(bf16[128,2560]{1,0:T(8,128)(2,1)} %refs_0_.5, bf16[128,5120]{1,0:T(8,128)(2,1)} %refs_1_.5, bf16[128,5120]{1,0:T(8,128)(2,1)} %refs_2_.5), custom_call_target="tpu_custom_call" | custom-call | flops 1 | bytes 1 | tf_op jit(solution)/shard_map/pallas_call | solution.py:231
  2.7 3.0 %collective-permute-start.8 = (f32[4,128,128]{2,1,0:T(8,128)S(1)}, f32[4,128,128]{2,1,0:T(8,128)S(1)}, u32[]{:S(2)}, u32[]{:S(2)}) collective-permute-start(f32[4,128,128]{2,1,0:T(8,128)S(1)} %get-tuple-element.50), channel_id=1, source_target_pairs={{0,2},{1,5},{2,0},{3,7},{4,6},{5,1},{6,4},{7,3},{8,10},{9,13},{10,... | collective-permute-start | bytes 786440 | tf_op jit(solution)/shard_map/ppermute | solution.py:424
  5.7 1.6 %collective-permute-start.9 = (f32[4,112,128]{2,1,0:T(8,128)S(1)}, f32[4,112,128]{2,1,0:T(8,128)S(1)}, u32[]{:S(2)}, u32[]{:S(2)}) collective-permute-start(f32[4,112,128]{2,1,0:T(8,128)S(1)} %get-tuple-element.51), channel_id=1, source_target_pairs={{0,4},{1,3},{2,6},{3,1},{4,0},{5,7},{6,2},{7,5},{8,12},{9,11},{10,... | collective-permute-start | bytes 688136 | tf_op jit(solution)/shard_map/ppermute | solution.py:424
  7.3 2.4 %shard_map.51 = (f32[4,136,128]{2,1,0:T(8,128)S(1)}, f32[4,136,128]{2,1,0:T(8,128)S(1)}, f32[17,8,128]{2,1,0:T(8,128)S(1)}) custom-call(bf16[128,2560]{1,0:T(8,128)(2,1)} %refs_0_.5, bf16[128,5120]{1,0:T(8,128)(2,1)} %refs_1_.5, bf16[128,5120]{1,0:T(8,128)(2,1)} %refs_2_.5, f32[17,8,128]{2,1,0:T(8,128)S(1)} %get-tuple-element.33.refs_3_), custom_call_target="tpu_custom_call" | custom-call | flops 1 | bytes 1 | tf_op jit(solution)/shard_map/pallas_call | solution.py:231
  9.7 0.6 %collective-permute-start = (f32[4,136,128]{2,1,0:T(8,128)S(1)}, f32[4,136,128]{2,1,0:T(8,128)S(1)}, u32[]{:S(2)}, u32[]{:S(2)}) collective-permute-start(f32[4,136,128]{2,1,0:T(8,128)S(1)} %get-tuple-element.37), channel_id=1, source_target_pairs={{0,2},{1,5},{2,0},{3,7},{4,6},{5,1},{6,4},{7,3},{8,10},{9,13},{10,... | collective-permute-start | bytes 835592 | tf_op jit(solution)/shard_map/ppermute | solution.py:424
  10.3 3.4 %shard_map.52 = (f32[4,128,128]{2,1,0:T(8,128)S(1)}, f32[4,112,128]{2,1,0:T(8,128)S(1)}, f32[4,136,128]{2,1,0:T(8,128)S(1)}, f32[4,136,128]{2,1,0:T(8,128)S(1)}, f32[17,8,128]{2,1,0:T(8,128)S(1)}) custom-call(bf16[128,2560]{1,0:T(8,128)(2,1)} %refs_0_.5, bf16[128,5120]{1,0:T(8,128)(2,1)} %refs_1_.5, bf16[128,5120]{1,0:T(8,128)(2,1)} %refs_2_.5, ...), custom_call_target="tpu_custom_call" | custom-call | flops 1 | bytes 1 | tf_op jit(solution)/shard_map/pallas_call | solution.py:231
  13.8 0.1 collective-permute-start.2
  13.9 0.1 shard_map.55
  13.9 2.1 %collective-permute-start.10 = (f32[2,128,128]{2,1,0:T(8,128)S(1)}, f32[2,128,128]{2,1,0:T(8,128)S(1)}, u32[]{:S(2)}, u32[]{:S(2)}) collective-permute-start(f32[2,128,128]{2,1,0:T(8,128)S(1)} %get-tuple-element.54), channel_id=1, source_target_pairs={{0,4},{1,3},{2,6},{3,1},{4,0},{5,7},{6,2},{7,5},{8,12},{9,11},{10,... | collective-permute-start | bytes 393224 | tf_op jit(solution)/shard_map/ppermute | solution.py:424
  16.0 1.5 %collective-permute-start.11 = (f32[2,112,128]{2,1,0:T(8,128)S(1)}, f32[2,112,128]{2,1,0:T(8,128)S(1)}, u32[]{:S(2)}, u32[]{:S(2)}) collective-permute-start(f32[2,112,128]{2,1,0:T(8,128)S(1)} %get-tuple-element.55), channel_id=1, source_target_pairs={{0,2},{1,5},{2,0},{3,7},{4,6},{5,1},{6,4},{7,3},{8,10},{9,13},{10,... | collective-permute-start | bytes 344072 | tf_op jit(solution)/shard_map/ppermute | solution.py:424
  17.5 1.9 %collective-permute-done.refs_2_ = f32[4,136,128]{2,1,0:T(8,128)S(1)} collective-permute-done((f32[4,136,128]{2,1,0:T(8,128)S(1)}, f32[4,136,128]{2,1,0:T(8,128)S(1)}, u32[]{:S(2)}, u32[]{:S(2)}) %collective-permute-start) | collective-permute-done | bytes 278560 | tf_op jit(solution)/shard_map/ppermute | solution.py:424
  19.4 0.1 shard_map.53
  19.4 0.4 %collective-permute-start.3 = (f32[2,136,128]{2,1,0:T(8,128)S(1)}, f32[2,136,128]{2,1,0:T(8,128)S(1)}, u32[]{:S(2)}, u32[]{:S(2)}) collective-permute-start(f32[2,136,128]{2,1,0:T(8,128)S(1)} %get-tuple-element.42), channel_id=1, source_target_pairs={{0,4},{1,3},{2,6},{3,1},{4,0},{5,7},{6,2},{7,5},{8,12},{9,11},{10,... | collective-permute-start | bytes 417800 | tf_op jit(solution)/shard_map/ppermute | solution.py:424
  19.9 1.8 %collective-permute-start.4 = (f32[2,136,128]{2,1,0:T(8,128)S(1)}, f32[2,136,128]{2,1,0:T(8,128)S(1)}, u32[]{:S(2)}, u32[]{:S(2)}) collective-permute-start(f32[2,136,128]{2,1,0:T(8,128)S(1)} %get-tuple-element.43), channel_id=1, source_target_pairs={{0,2},{1,5},{2,0},{3,7},{4,6},{5,1},{6,4},{7,3},{8,10},{9,13},{10,... | collective-permute-start | bytes 417800 | tf_op jit(solution)/shard_map/ppermute | solution.py:424
  21.7 2.7 %collective-permute-start.12 = (f32[1,128,128]{2,1,0:T(8,128)S(1)}, f32[1,128,128]{2,1,0:T(8,128)S(1)}, u32[]{:S(2)}, u32[]{:S(2)}) collective-permute-start(f32[1,128,128]{2,1,0:T(8,128)S(1)} %get-tuple-element.58), channel_id=1, source_target_pairs={{0,8},{1,9},{2,10},{3,11},{4,12},{5,13},{6,14},{7,15},{8,0},{9,1},... | collective-permute-start | bytes 196616 | tf_op jit(solution)/shard_map/ppermute | solution.py:424
  24.4 0.3 collective-permute-start.13
  24.7 1.8 %collective-permute-start.5 = (f32[2,128]{1,0:T(2,128)S(1)}, f32[2,128]{1,0:T(2,128)S(1)}, u32[]{:S(2)}, u32[]{:S(2)}) collective-permute-start(f32[2,128]{1,0:T(2,128)S(1)} %fusion.refs_4_), channel_id=1, source_target_pairs={{0,6},{1,7},{2,4},{3,5},{4,2},{5,3},{6,0},{7,1},{8,14},{9,15},{10,... | collective-permute-start | bytes 3080 | tf_op jit(solution)/shard_map/ppermute | solution.py:424
  26.5 2.7 %collective-permute-done.5.refs_5_ = f32[2,128]{1,0:T(2,128)S(1)} collective-permute-done((f32[2,128]{1,0:T(2,128)S(1)}, f32[2,128]{1,0:T(2,128)S(1)}, u32[]{:S(2)}, u32[]{:S(2)}) %collective-permute-start.5) | collective-permute-done | bytes 1056 | tf_op jit(solution)/shard_map/ppermute | solution.py:424
  29.2 2.7 %collective-permute-start.6 = (f32[1,136,128]{2,1,0:T(8,128)S(1)}, f32[1,136,128]{2,1,0:T(8,128)S(1)}, u32[]{:S(2)}, u32[]{:S(2)}) collective-permute-start(f32[1,136,128]{2,1,0:T(8,128)S(1)} %get-tuple-element.46), channel_id=1, source_target_pairs={{0,8},{1,9},{2,10},{3,11},{4,12},{5,13},{6,14},{7,15},{8,0},{9,1},... | collective-permute-start | bytes 208904 | tf_op jit(solution)/shard_map/ppermute | solution.py:424
  31.9 0.3 collective-permute-start.7
  32.2 0.3 shard_map.57
  32.5 3.9 %collective-permute-done.6.refs_2_ = f32[1,136,128]{2,1,0:T(8,128)S(1)} collective-permute-done((f32[1,136,128]{2,1,0:T(8,128)S(1)}, f32[1,136,128]{2,1,0:T(8,128)S(1)}, u32[]{:S(2)}, u32[]{:S(2)}) %collective-permute-start.6) | collective-permute-done | bytes 69664 | tf_op jit(solution)/shard_map/ppermute | solution.py:424
  36.4 1.5 %collective-permute-done.7.refs_3_ = f32[1,136,128]{2,1,0:T(8,128)S(1)} collective-permute-done((f32[1,136,128]{2,1,0:T(8,128)S(1)}, f32[1,136,128]{2,1,0:T(8,128)S(1)}, u32[]{:S(2)}, u32[]{:S(2)}) %collective-permute-start.7) | collective-permute-done | bytes 69664 | tf_op jit(solution)/shard_map/ppermute | solution.py:424
  37.9 1.1 %shard_map.58 = (f32[320,128]{1,0:T(8,128)}, f32[640,128]{1,0:T(8,128)}) custom-call(f32[1,136,128]{2,1,0:T(8,128)S(1)} %get-tuple-element.44.refs_0_, f32[1,136,128]{2,1,0:T(8,128)S(1)} %get-tuple-element.45.refs_1_, f32[1,136,128]{2,1,0:T(8,128)S(1)} %collective-permute-done.6.refs_2_, f32[1,136,128]{2,1,0:T(8,128)S(1)} %collective-permute-done.7.refs_3_, ...), custom_call_target="tpu_custom_call" | custom-call | tf_op jit(solution)/shard_map/pallas_call | solution.py:405
  (15 shorter events, 0.1 us)
Async XLA Ops:
  2.7 11.2 %collective-permute-start.8 = (f32[4,128,128]{2,1,0:T(8,128)S(1)}, f32[4,128,128]{2,1,0:T(8,128)S(1)}, u32[]{:S(2)}, u32[]{:S(2)}) collective-permute-start(f32[4,128,128]{2,1,0:T(8,128)S(1)} %get-tuple-element.50), channel_id=1, source_target_pairs={{0,2},{1,5},{2,0},{3,7},{4,6},{5,1},{6,4},{7,3},{8,10},{9,13},{10,... | collective-permute-start | bytes 786440 | tf_op jit(solution)/shard_map/ppermute | solution.py:424
  5.7 8.2 %collective-permute-start.9 = (f32[4,112,128]{2,1,0:T(8,128)S(1)}, f32[4,112,128]{2,1,0:T(8,128)S(1)}, u32[]{:S(2)}, u32[]{:S(2)}) collective-permute-start(f32[4,112,128]{2,1,0:T(8,128)S(1)} %get-tuple-element.51), channel_id=1, source_target_pairs={{0,4},{1,3},{2,6},{3,1},{4,0},{5,7},{6,2},{7,5},{8,12},{9,11},{10,... | collective-permute-start | bytes 688136 | tf_op jit(solution)/shard_map/ppermute | solution.py:424
  9.7 9.7 %collective-permute-start = (f32[4,136,128]{2,1,0:T(8,128)S(1)}, f32[4,136,128]{2,1,0:T(8,128)S(1)}, u32[]{:S(2)}, u32[]{:S(2)}) collective-permute-start(f32[4,136,128]{2,1,0:T(8,128)S(1)} %get-tuple-element.37), channel_id=1, source_target_pairs={{0,2},{1,5},{2,0},{3,7},{4,6},{5,1},{6,4},{7,3},{8,10},{9,13},{10,... | collective-permute-start | bytes 835592 | tf_op jit(solution)/shard_map/ppermute | solution.py:424
  10.3 9.1 %collective-permute-start.1 = (f32[4,136,128]{2,1,0:T(8,128)S(1)}, f32[4,136,128]{2,1,0:T(8,128)S(1)}, u32[]{:S(2)}, u32[]{:S(2)}) collective-permute-start(f32[4,136,128]{2,1,0:T(8,128)S(1)} %get-tuple-element.38), channel_id=1, source_target_pairs={{0,4},{1,3},{2,6},{3,1},{4,0},{5,7},{6,2},{7,5},{8,12},{9,11},{10,... | collective-permute-start | bytes 835592 | tf_op jit(solution)/shard_map/ppermute | solution.py:424
  13.8 3.7 %collective-permute-start.2 = (f32[2,128]{1,0:T(2,128)S(1)}, f32[2,128]{1,0:T(2,128)S(1)}, u32[]{:S(2)}, u32[]{:S(2)}) collective-permute-start(f32[2,128]{1,0:T(2,128)S(1)} %slice_bitcast_fusion), channel_id=1, source_target_pairs={{0,1},{1,0},{2,3},{3,2},{4,5},{5,4},{6,7},{7,6},{8,9},{9,8},{10,11... | collective-permute-start | bytes 3080 | tf_op jit(solution)/shard_map/ppermute | solution.py:424
  13.9 7.8 %collective-permute-start.10 = (f32[2,128,128]{2,1,0:T(8,128)S(1)}, f32[2,128,128]{2,1,0:T(8,128)S(1)}, u32[]{:S(2)}, u32[]{:S(2)}) collective-permute-start(f32[2,128,128]{2,1,0:T(8,128)S(1)} %get-tuple-element.54), channel_id=1, source_target_pairs={{0,4},{1,3},{2,6},{3,1},{4,0},{5,7},{6,2},{7,5},{8,12},{9,11},{10,... | collective-permute-start | bytes 393224 | tf_op jit(solution)/shard_map/ppermute | solution.py:424
  16.0 5.7 %collective-permute-start.11 = (f32[2,112,128]{2,1,0:T(8,128)S(1)}, f32[2,112,128]{2,1,0:T(8,128)S(1)}, u32[]{:S(2)}, u32[]{:S(2)}) collective-permute-start(f32[2,112,128]{2,1,0:T(8,128)S(1)} %get-tuple-element.55), channel_id=1, source_target_pairs={{0,2},{1,5},{2,0},{3,7},{4,6},{5,1},{6,4},{7,3},{8,10},{9,13},{10,... | collective-permute-start | bytes 344072 | tf_op jit(solution)/shard_map/ppermute | solution.py:424
  19.4 9.7 %collective-permute-start.3 = (f32[2,136,128]{2,1,0:T(8,128)S(1)}, f32[2,136,128]{2,1,0:T(8,128)S(1)}, u32[]{:S(2)}, u32[]{:S(2)}) collective-permute-start(f32[2,136,128]{2,1,0:T(8,128)S(1)} %get-tuple-element.42), channel_id=1, source_target_pairs={{0,4},{1,3},{2,6},{3,1},{4,0},{5,7},{6,2},{7,5},{8,12},{9,11},{10,... | collective-permute-start | bytes 417800 | tf_op jit(solution)/shard_map/ppermute | solution.py:424
  19.9 9.3 %collective-permute-start.4 = (f32[2,136,128]{2,1,0:T(8,128)S(1)}, f32[2,136,128]{2,1,0:T(8,128)S(1)}, u32[]{:S(2)}, u32[]{:S(2)}) collective-permute-start(f32[2,136,128]{2,1,0:T(8,128)S(1)} %get-tuple-element.43), channel_id=1, source_target_pairs={{0,2},{1,5},{2,0},{3,7},{4,6},{5,1},{6,4},{7,3},{8,10},{9,13},{10,... | collective-permute-start | bytes 417800 | tf_op jit(solution)/shard_map/ppermute | solution.py:424
  21.7 10.5 %collective-permute-start.12 = (f32[1,128,128]{2,1,0:T(8,128)S(1)}, f32[1,128,128]{2,1,0:T(8,128)S(1)}, u32[]{:S(2)}, u32[]{:S(2)}) collective-permute-start(f32[1,128,128]{2,1,0:T(8,128)S(1)} %get-tuple-element.58), channel_id=1, source_target_pairs={{0,8},{1,9},{2,10},{3,11},{4,12},{5,13},{6,14},{7,15},{8,0},{9,1},... | collective-permute-start | bytes 196616 | tf_op jit(solution)/shard_map/ppermute | solution.py:424
  24.4 7.8 %collective-permute-start.13 = (f32[1,112,128]{2,1,0:T(8,128)S(1)}, f32[1,112,128]{2,1,0:T(8,128)S(1)}, u32[]{:S(2)}, u32[]{:S(2)}) collective-permute-start(f32[1,112,128]{2,1,0:T(8,128)S(1)} %get-tuple-element.59), channel_id=1, source_target_pairs={{0,8},{1,9},{2,10},{3,11},{4,12},{5,13},{6,14},{7,15},{8,0},{9,1},... | collective-permute-start | bytes 172040 | tf_op jit(solution)/shard_map/ppermute | solution.py:424
  24.7 4.5 %collective-permute-start.5 = (f32[2,128]{1,0:T(2,128)S(1)}, f32[2,128]{1,0:T(2,128)S(1)}, u32[]{:S(2)}, u32[]{:S(2)}) collective-permute-start(f32[2,128]{1,0:T(2,128)S(1)} %fusion.refs_4_), channel_id=1, source_target_pairs={{0,6},{1,7},{2,4},{3,5},{4,2},{5,3},{6,0},{7,1},{8,14},{9,15},{10,... | collective-permute-start | bytes 3080 | tf_op jit(solution)/shard_map/ppermute | solution.py:424
  29.2 7.2 %collective-permute-start.6 = (f32[1,136,128]{2,1,0:T(8,128)S(1)}, f32[1,136,128]{2,1,0:T(8,128)S(1)}, u32[]{:S(2)}, u32[]{:S(2)}) collective-permute-start(f32[1,136,128]{2,1,0:T(8,128)S(1)} %get-tuple-element.46), channel_id=1, source_target_pairs={{0,8},{1,9},{2,10},{3,11},{4,12},{5,13},{6,14},{7,15},{8,0},{9,1},... | collective-permute-start | bytes 208904 | tf_op jit(solution)/shard_map/ppermute | solution.py:424
  31.9 6.0 %collective-permute-start.7 = (f32[1,136,128]{2,1,0:T(8,128)S(1)}, f32[1,136,128]{2,1,0:T(8,128)S(1)}, u32[]{:S(2)}, u32[]{:S(2)}) collective-permute-start(f32[1,136,128]{2,1,0:T(8,128)S(1)} %get-tuple-element.47), channel_id=1, source_target_pairs={{0,8},{1,9},{2,10},{3,11},{4,12},{5,13},{6,14},{7,15},{8,0},{9,1},... | collective-permute-start | bytes 208904 | tf_op jit(solution)/shard_map/ppermute | solution.py:424

commit v7 on v6

--- a/solution.py
+++ b/solution.py
@@ -62,6 +62,8 @@
 KINDS = (((X, NEAR, FAR), (NEAR, X, FAR)), ((NEAR, X, FAR), (X, NEAR, FAR)))
 NOTES = len(KINDS) * SLOTS
 
+WEIGHTS = {((0, 2), 2): 2 * 10**9}
+
 
 def split_rows(count):
     return count // B, (count % B) // H
@@ -99,44 +101,73 @@
     return pl.ds(start if isinstance(start, int) else pl.multiple_of(start, B), size)
 
 
-def pack_body(pieces, items, count_a, count_g, fresh, *refs):
-    a_hbm, pre_hbm, grad_hbm = refs[:3]
-    notes_in = None if fresh else refs[3]
-    refs = refs[3 if fresh else 4 :]
-    n = len(items)
-    outs, notes = refs[:n], refs[n]
-    buffers, sems = refs[n + 1 : 5 * n + 1], refs[5 * n + 1]
+def columns(pieces, item, count_a, count_g):
+    k, first = item
+    a_blocks, a_half, g_blocks, kind = pieces[k]
     full, half = split_rows(count_a)
+
+    def base(slot):
+        owner = slot_owner(first + slot, KINDS[kind])
+        return (owner >> half) * (full * (1 + half) + half) * B, owner & half, owner
+
+    found = []
+    if a_blocks:
+
+        def whole(slot):
+            start, odd, _ = base(slot)
+            return start + odd * (full + 1) * B + a_blocks[0] * B
+
+        found.append((0, whole, len(a_blocks) * B))
+    if a_half:
+        found.append((0, lambda slot: base(slot)[0] + full * B, B))
+    if g_blocks:
+
+        def part(slot):
+            return base(slot)[2] * count_g + g_blocks[0] * B
+
+        found += [(1, part, len(g_blocks) * B), (2, part, len(g_blocks) * B)]
+    return found
+
+
+def pack_body(pieces, items, ahead, count_a, count_g, fresh, *refs):
+    def reads(of):
+        return [
+            (array, start, size)
+            for item in of
+            for array, start, size in columns(pieces, item, count_a, count_g)
+        ]
+
+    refs = list(refs)
+
+    def pop(count):
+        taken = refs[:count]
+        del refs[:count]
+        return taken
+
+    n, own, after = len(items), reads(items), reads(ahead)
     slots = SLOTS // 2
-
-    def copies(i, slot):
-        k, first = items[i]
-        a_blocks, a_half, g_blocks, kind = pieces[k]
-        a_buf, half_buf, pre_buf, grad_buf = buffers[4 * i : 4 * i + 4]
-        owner = slot_owner(first + slot, KINDS[kind])
-        odd = owner & half
-        base = (owner >> half) * (full * (1 + half) + half) * B
-        moves = []
-        if a_blocks:
-            start = base + odd * (full + 1) * B + a_blocks[0] * B
-            moves.append((a_hbm, start, a_buf))
-        if a_half:
-            moves.append((a_hbm, base + full * B, half_buf))
-        if g_blocks:
-            start = owner * count_g + g_blocks[0] * B
-            moves += [(pre_hbm, start, pre_buf), (grad_hbm, start, grad_buf)]
+    hbm = pop(3)
+    notes_in, buffers = (None, None) if fresh else (pop(1)[0], pop(len(own)))
+    outs, (notes,), nexts = pop(n), pop(1), pop(len(after))
+    if fresh:
+        buffers = pop(len(own))
+    sems = refs
+
+    def copies(moves, into, sem):
         return [
             pltpu.make_async_copy(
-                src.at[:, lanes(start, dst.shape[2])], dst.at[slot], sems.at[i, slot, m]
+                hbm[array].at[:, lanes(start(slot), size)], into[m].at[slot], sem.at[m, slot]
             )
-            for m, (src, start, dst) in enumerate(moves)
+            for m, (array, start, size) in enumerate(moves)
+            for slot in range(slots)
         ]
 
-    for i in range(n):
-        for slot in range(slots):
-            for copy in copies(i, slot):
-                copy.start()
-
+    mine = copies(own, buffers, sems.pop(0)) if fresh else []
+    later = copies(after, nexts, sems.pop(0)) if after else []
+    for copy in mine + later:
+        copy.start()
+
+    full, half = split_rows(count_a)
     row, col = iotas(H)
     low = col < row
     diag_low, diag_high = col == row, col == row + H
@@ -178,11 +209,13 @@
 
     for i, (k, first) in enumerate(items):
         a_blocks, a_half, g_blocks, kind = pieces[k]
-        a_buf, half_buf, pre_buf, grad_buf = buffers[4 * i : 4 * i + 4]
         out = outs[i]
-        for slot in range(slots):
-            for copy in copies(i, slot):
-                copy.wait()
+        count = len(columns(pieces, (k, first), count_a, count_g))
+        (*a_bufs, pre_buf, grad_buf) = buffers[:count] if g_blocks else [*buffers[:count], None, None]
+        del buffers[:count]
+        for copy in mine[: count * slots]:
+            copy.wait()
+        del mine[: count * slots]
         for slot in range(slots):
             here = kind * SLOTS + first + slot
             if here not in tiles:
@@ -190,12 +223,12 @@
             index = corner_indices(pieces, k)
             at = 0
             for b in range(len(a_blocks)):
-                block = cov(a_buf[slot, :, b * B : (b + 1) * B])
+                block = cov(a_bufs[0][slot, :, b * B : (b + 1) * B])
                 out[slot, at : at + H, :] = fold(block, here, next(index), 0)
                 at = at + H
             if a_half:
                 odd = slot_owner(first + slot, KINDS[kind]) & 1
-                square, rest = fold_half(cov(half_buf[slot]), odd, here, next(index))
+                square, rest = fold_half(cov(a_bufs[-1][slot]), odd, here, next(index))
                 out[slot, at : at + quarter, :] = square
                 out[slot, at + quarter : at + quarter * 3 // 2, :] = rest
                 at = at + quarter * 3 // 2
@@ -217,63 +250,81 @@
     lines = [jnp.sum(trace, axis=0, keepdims=True) for trace in traces]
     tile = jnp.where(note_row == 0, lines[0], jnp.where(note_row == 1, lines[1], 0.0))
     notes[NOTES] = tile if fresh else notes_in[NOTES] + tile
-
-
-def pack(arrays, pieces, items, count_a, count_g, notes):
+    for copy in later:
+        copy.wait()
+
+
+def pack(arrays, pieces, items, ahead, count_a, count_g, notes, buffers):
     tokens, dtype = arrays[0].shape[0], arrays[0].dtype
     slots = SLOTS // 2
-    scratch = []
-    for k, _ in items:
-        a_blocks, _, g_blocks, _ = pieces[k]
-        for size in (len(a_blocks), 1, len(g_blocks), len(g_blocks)):
-            scratch.append(pltpu.VMEM((slots, tokens, max(size, 1) * B), dtype))
+
+    def shapes(of):
+        return [
+            (slots, tokens, size)
+            for item in of
+            for _, _, size in columns(pieces, item, count_a, count_g)
+        ]
+
     fresh = notes is None
-    *chunks, notes = pl.pallas_call(
-        functools.partial(pack_body, pieces, items, count_a, count_g, fresh),
+    own, after = shapes(items), shapes(ahead)
+    scratch = [pltpu.VMEM(shape, dtype) for shape in own] if fresh else []
+    for moves in ((own if fresh else []), after):
+        if moves:
+            scratch.append(pltpu.SemaphoreType.DMA((len(moves), slots)))
+    extra = [] if fresh else [notes, *buffers]
+    out_shape = [
+        jax.ShapeDtypeStruct((slots, piece_rows(pieces, k), B), jnp.float32) for k, _ in items
+    ]
+    out_shape.append(jax.ShapeDtypeStruct((NOTES + 1, EDGE, B), jnp.float32))
+    out_shape += [jax.ShapeDtypeStruct(shape, dtype) for shape in after]
+    outs = pl.pallas_call(
+        functools.partial(pack_body, pieces, items, ahead, count_a, count_g, fresh),
         in_specs=[pl.BlockSpec(memory_space=pltpu.HBM)] * 3
-        + [pl.BlockSpec(memory_space=pltpu.VMEM)] * (not fresh),
-        out_specs=[pl.BlockSpec(memory_space=pltpu.VMEM)] * (len(items) + 1),
-        out_shape=[
-            jax.ShapeDtypeStruct((slots, piece_rows(pieces, k), B), jnp.float32)
-            for k, _ in items
-        ]
-        + [jax.ShapeDtypeStruct((NOTES + 1, EDGE, B), jnp.float32)],
-        scratch_shapes=scratch + [pltpu.SemaphoreType.DMA((len(items), slots, 4))],
+        + [pl.BlockSpec(memory_space=pltpu.VMEM)] * len(extra),
+        out_specs=[pl.BlockSpec(memory_space=pltpu.VMEM)] * len(out_shape),
+        out_shape=out_shape,
+        scratch_shapes=scratch,
         compiler_params=pltpu.CompilerParams(vmem_limit_bytes=32 * 2**20),
         cost_estimate=pl.CostEstimate(flops=1, bytes_accessed=1, transcendentals=0),
-    )(*arrays, *([] if fresh else [notes]))
-    return chunks, notes
-
-
-def halve_body(traced, n, *refs):
+    )(*arrays, *extra)
+    n = len(items)
+    return outs[:n], outs[n], outs[n + 1 :]
+
+
+def halve_body(n, summed, gathered, *refs):
     keeps, gots, refs = refs[:n], refs[n : 2 * n], refs[2 * n :]
-    traces, outs = refs[:-2 * n], refs[-2 * n :]
+    split = len(refs) - 2 * n - summed
+    traces, outs = refs[:split], refs[split:]
     for k in range(n):
         half = keeps[k].shape[0] // 2
         for part in range(2):
             here = slice(part * half, (part + 1) * half)
             outs[2 * k + part][...] = keeps[k][here] + gots[k][here]
-    if traced:
-        value = sum((trace[...] for trace in traces[1:]), traces[0][...])
-        if len(traces) > 1:
+    if summed:
+        outs[-1][...] = traces[0][...] + traces[1][...]
+    elif traces:
+        value = traces[0][...]
+        if gathered:
             value = value + sum(got[0, -2:, :] for got in gots)
         for out in outs:
             out[0, -2:, :] = value
 
 
-def halve(keeps, gots, traces=()):
+def halve(keeps, gots, traces=(), gathered=False, weight=1):
+    summed = len(traces) == 2
     n = len(keeps)
     args = (*keeps, *gots, *traces)
     shapes = [(keep.shape[0] // 2, *keep.shape[1:]) for keep in keeps for _ in range(2)]
+    shapes += [trace.shape for trace in traces[:summed]]
     outs = pl.pallas_call(
-        functools.partial(halve_body, bool(traces), n),
+        functools.partial(halve_body, n, summed, gathered),
         in_specs=[pl.BlockSpec(memory_space=pltpu.VMEM)] * len(args),
-        out_specs=[pl.BlockSpec(memory_space=pltpu.VMEM)] * (2 * n),
+        out_specs=[pl.BlockSpec(memory_space=pltpu.VMEM)] * len(shapes),
         out_shape=[jax.ShapeDtypeStruct(shape, jnp.float32) for shape in shapes],
         compiler_params=pltpu.CompilerParams(vmem_limit_bytes=32 * 2**20),
-        cost_estimate=pl.CostEstimate(flops=1, bytes_accessed=1, transcendentals=0),
+        cost_estimate=pl.CostEstimate(flops=weight, bytes_accessed=1, transcendentals=0),
     )(*args)
-    return outs[0::2], outs[1::2]
+    return outs[0 : 2 * n : 2], outs[1 : 2 * n : 2], outs[2 * n :]
 
 
 def mean_of(value, total):
@@ -448,11 +499,16 @@
     )
     keep, send = 0, SLOTS // 2
     early, late = (0, 2), (1, 3)
-    keeps, gots, notes = {}, {}, None
-    for first, ks in ((send, early), (send, late), (keep, early + late)):
-        items = tuple((k, first) for k in ks)
-        parts, notes = pack(arrays, pieces, items, count_a, count_g, notes)
-        for k, part in zip(ks, parts):
+    keeps, gots, notes, buffers = {}, {}, None, None
+    calls = [
+        tuple((k, first) for k in ks)
+        for first, ks in ((send, early), (send, late), (keep, early), (keep, late))
+    ]
+    for items, ahead in zip(calls, calls[1:] + [()]):
+        parts, notes, buffers = pack(
+            arrays, pieces, items, ahead, count_a, count_g, notes, buffers
+        )
+        for (k, first), part in zip(items, parts):
             if first == send:
                 gots[k] = swap(part, along(0, pieces[k][3]))
             else:
@@ -461,12 +517,17 @@
     trace = notes[NOTES, :2, :]
     trace = trace + swap(trace, lambda i, j: (i, j ^ 1))
     across = swap(trace, lambda i, j: (i ^ (1 << X) ^ (1 << NEAR), j))
-    traces = {early: ((), ()), late: ((trace,), (trace, across))}
     for stage in (1, 2):
         for ks in (early, late):
-            own, parts = halve(
-                [keeps[k] for k in ks], [gots[k] for k in ks], traces[ks][stage - 1]
+            if ks == late:
+                traces = (trace,)
+            else:
+                traces = (trace, across) if stage == 2 else ()
+            own, parts, news = halve(
+                [keeps[k] for k in ks], [gots[k] for k in ks], traces,
+                gathered=stage == 2, weight=WEIGHTS.get((ks, stage), 1)
             )
+            trace = news[0] if news else trace
             for k, mine, part in zip(ks, own, parts):
                 keeps[k], gots[k] = mine, swap(part, along(stage, pieces[k][3]))
 

time: 39.3 us -> 39.2 us (level)
  Pallas kernels: 9.48 us -> 8.33 us
  waiting for transfers between devices: 10 us -> 11 us
    pallas_call x7 -> x8, Pallas kernels: 8.1 us -> 6.95 us  [the longest x4 6.75 us: pack(): pl.pallas_call(functools.partial(pack_body, pieces, items, ahead, count_a...]
    ppermute x14, waiting for transfers between devices: 10 us -> 11 us  [swap(): return lax.ppermute(value, ('dp', 'tensor'), pairs)]
  transfers between devices with their start and end apart: 14 -> 14, of which waited for: 4 -> 6; matrix products, arithmetic and copies ran while one was open for 0% -> 0% of each run, Pallas kernels for 16% -> 13%
where the time goes in v7:
time: 39.2 us; the launch traced here: 38.9 us
  starting transfers between devices  18.8 us (48%)
  waiting for transfers between devices  11 us (28%)
  Pallas kernels  8.33 us (21%)
  between operations  0.71 us (2%)
    ppermute x14, starting transfers between devices, swap(): return lax.ppermute(value, ('dp', 'tensor'), pairs)  18.8 us
    ppermute x14, waiting for transfers between devices, swap(): return lax.ppermute(value, ('dp', 'tensor'), pairs)  11 us
    pallas_call x4, Pallas kernels, pack(): pl.pallas_call(functools.partial(pack_body, pieces, items, ahead, count_a...  6.75 us
    pallas_call x1, Pallas kernels, finish(): pl.pallas_call(functools.partial(finish_body, pieces, early, late, count_...  1.1 us
  transfers between devices with their start and end apart: 14, of which 6 were waited for; matrix products, arithmetic and copies ran while one was open for 0% of the time, Pallas kernels for 13%

profile of v7, /device:TPU:0, one launch (start us, length us, event | category | flops | bytes accessed | tf_op | source)
XLA Modules:
  0.0 38.9 jit_solution(12269561002169689804)
XLA Ops:
  0.6 2.2 %shard_map.50 = (f32[4,128,128]{2,1,0:T(8,128)S(1)}, f32[4,112,128]{2,1,0:T(8,128)S(1)}, f32[17,8,128]{2,1,0:T(8,128)S(1)}, bf16[4,128,256]{2,1,0:T(8,128)(2,1)S...) custom-call(bf16[128,2560]{1,0:T(8,128)(2,1)} %refs_0_.7, ...), custom_call_target="tpu_custom_call" | custom-call | flops 1 | bytes 1 | tf_op jit(solution)/shard_map/pallas_call | solution.py:280
  2.8 3.0 %collective-permute-start.5 = (f32[4,128,128]{2,1,0:T(8,128)S(1)}, f32[4,128,128]{2,1,0:T(8,128)S(1)}, u32[]{:S(2)}, u32[]{:S(2)}) collective-permute-start(f32[4,128,128]{2,1,0:T(8,128)S(1)} %get-tuple-element.73), channel_id=1, source_target_pairs={{0,2},{1,5},{2,0},{3,7},{4,6},{5,1},{6,4},{7,3},{8,10},{9,13},{10,... | collective-permute-start | bytes 786440 | tf_op jit(solution)/shard_map/ppermute | solution.py:475
  5.8 1.6 %collective-permute-start.6 = (f32[4,112,128]{2,1,0:T(8,128)S(1)}, f32[4,112,128]{2,1,0:T(8,128)S(1)}, u32[]{:S(2)}, u32[]{:S(2)}) collective-permute-start(f32[4,112,128]{2,1,0:T(8,128)S(1)} %get-tuple-element.74), channel_id=1, source_target_pairs={{0,4},{1,3},{2,6},{3,1},{4,0},{5,7},{6,2},{7,5},{8,12},{9,11},{10,... | collective-permute-start | bytes 688136 | tf_op jit(solution)/shard_map/ppermute | solution.py:475
  7.4 2.0 %shard_map.51 = (f32[4,136,128]{2,1,0:T(8,128)S(1)}, f32[4,136,128]{2,1,0:T(8,128)S(1)}, f32[17,8,128]{2,1,0:T(8,128)S(1)}, bf16[4,128,256]{2,1,0:T(8,128)(2,1)S...) custom-call(bf16[128,2560]{1,0:T(8,128)(2,1)} %refs_0_.7, ...), custom_call_target="tpu_custom_call" | custom-call | flops 1 | bytes 1 | tf_op jit(solution)/shard_map/pallas_call | solution.py:280
  9.4 0.5 %collective-permute-start = (f32[4,136,128]{2,1,0:T(8,128)S(1)}, f32[4,136,128]{2,1,0:T(8,128)S(1)}, u32[]{:S(2)}, u32[]{:S(2)}) collective-permute-start(f32[4,136,128]{2,1,0:T(8,128)S(1)} %get-tuple-element.64), channel_id=1, source_target_pairs={{0,2},{1,5},{2,0},{3,7},{4,6},{5,1},{6,4},{7,3},{8,10},{9,13},{10,... | collective-permute-start | bytes 835592 | tf_op jit(solution)/shard_map/ppermute | solution.py:475
  9.9 1.8 %shard_map.52 = (f32[4,128,128]{2,1,0:T(8,128)S(1)}, f32[4,112,128]{2,1,0:T(8,128)S(1)}, f32[17,8,128]{2,1,0:T(8,128)S(1)}, bf16[4,128,256]{2,1,0:T(8,128)(2,1)S...) custom-call(bf16[128,2560]{1,0:T(8,128)(2,1)} %refs_0_.7, ...), custom_call_target="tpu_custom_call" | custom-call | flops 1 | bytes 1 | tf_op jit(solution)/shard_map/pallas_call | solution.py:280
  11.7 0.8 %shard_map.53 = (f32[4,136,128]{2,1,0:T(8,128)S(1)}, f32[4,136,128]{2,1,0:T(8,128)S(1)}, f32[17,8,128]{2,1,0:T(8,128)S(1)}) custom-call(bf16[128,2560]{1,0:T(8,128)(2,1)} %refs_0_.7, bf16[128,5120]{1,0:T(8,128)(2,1)} %refs_1_.7, bf16[128,5120]{1,0:T(8,128)(2,1)} %refs_2_.7, f32[17,8,128]{2,1,0:T(8,128)S(1)} %get-tuple-element.57.refs_3_, ...), custom_call_target="tpu_custom_call" | custom-call | flops 1 | bytes 1 | tf_op jit(solution)/shard_map/pallas_call | solution.py:280
  12.6 0.5 %collective-permute-done.6.refs_3_ = f32[4,112,128]{2,1,0:T(8,128)S(1)} collective-permute-done((f32[4,112,128]{2,1,0:T(8,128)S(1)}, f32[4,112,128]{2,1,0:T(8,128)S(1)}, u32[]{:S(2)}, u32[]{:S(2)}) %collective-permute-start.6) | collective-permute-done | bytes 229408 | tf_op jit(solution)/shard_map/ppermute | solution.py:475
  13.1 1.8 %collective-permute-start.8 = (f32[2,112,128]{2,1,0:T(8,128)S(1)}, f32[2,112,128]{2,1,0:T(8,128)S(1)}, u32[]{:S(2)}, u32[]{:S(2)}) collective-permute-start(f32[2,112,128]{2,1,0:T(8,128)S(1)} %get-tuple-element.78), channel_id=1, source_target_pairs={{0,2},{1,5},{2,0},{3,7},{4,6},{5,1},{6,4},{7,3},{8,10},{9,13},{10,... | collective-permute-start | bytes 344072 | tf_op jit(solution)/shard_map/ppermute | solution.py:475
  15.0 1.7 %collective-permute-start.7 = (f32[2,128,128]{2,1,0:T(8,128)S(1)}, f32[2,128,128]{2,1,0:T(8,128)S(1)}, u32[]{:S(2)}, u32[]{:S(2)}) collective-permute-start(f32[2,128,128]{2,1,0:T(8,128)S(1)} %get-tuple-element.77), channel_id=1, source_target_pairs={{0,4},{1,3},{2,6},{3,1},{4,0},{5,7},{6,2},{7,5},{8,12},{9,11},{10,... | collective-permute-start | bytes 393224 | tf_op jit(solution)/shard_map/ppermute | solution.py:475
  16.7 0.5 %collective-permute-start.9 = (f32[2,128]{1,0:T(2,128)S(1)}, f32[2,128]{1,0:T(2,128)S(1)}, u32[]{:S(2)}, u32[]{:S(2)}) collective-permute-start(f32[2,128]{1,0:T(2,128)S(1)} %fusion.refs_4_), channel_id=1, source_target_pairs={{0,6},{1,7},{2,4},{3,5},{4,2},{5,3},{6,0},{7,1},{8,14},{9,15},{10,... | collective-permute-start | bytes 3080 | tf_op jit(solution)/shard_map/ppermute | solution.py:475
  17.2 1.8 %collective-permute-done.refs_2_ = f32[4,136,128]{2,1,0:T(8,128)S(1)} collective-permute-done((f32[4,136,128]{2,1,0:T(8,128)S(1)}, f32[4,136,128]{2,1,0:T(8,128)S(1)}, u32[]{:S(2)}, u32[]{:S(2)}) %collective-permute-start) | collective-permute-done | bytes 278560 | tf_op jit(solution)/shard_map/ppermute | solution.py:475
  19.1 1.8 %collective-permute-start.3 = (f32[2,136,128]{2,1,0:T(8,128)S(1)}, f32[2,136,128]{2,1,0:T(8,128)S(1)}, u32[]{:S(2)}, u32[]{:S(2)}) collective-permute-start(f32[2,136,128]{2,1,0:T(8,128)S(1)} %get-tuple-element.69), channel_id=1, source_target_pairs={{0,4},{1,3},{2,6},{3,1},{4,0},{5,7},{6,2},{7,5},{8,12},{9,11},{10,... | collective-permute-start | bytes 417800 | tf_op jit(solution)/shard_map/ppermute | solution.py:475
  20.9 1.7 %collective-permute-start.4 = (f32[2,136,128]{2,1,0:T(8,128)S(1)}, f32[2,136,128]{2,1,0:T(8,128)S(1)}, u32[]{:S(2)}, u32[]{:S(2)}) collective-permute-start(f32[2,136,128]{2,1,0:T(8,128)S(1)} %get-tuple-element.70), channel_id=1, source_target_pairs={{0,2},{1,5},{2,0},{3,7},{4,6},{5,1},{6,4},{7,3},{8,10},{9,13},{10,... | collective-permute-start | bytes 417800 | tf_op jit(solution)/shard_map/ppermute | solution.py:475
  22.7 2.7 %collective-permute-start.12 = (f32[1,128,128]{2,1,0:T(8,128)S(1)}, f32[1,128,128]{2,1,0:T(8,128)S(1)}, u32[]{:S(2)}, u32[]{:S(2)}) collective-permute-start(f32[1,128,128]{2,1,0:T(8,128)S(1)} %get-tuple-element.86), channel_id=1, source_target_pairs={{0,8},{1,9},{2,10},{3,11},{4,12},{5,13},{6,14},{7,15},{8,0},{9,1},... | collective-permute-start | bytes 196616 | tf_op jit(solution)/shard_map/ppermute | solution.py:475
  25.4 0.3 collective-permute-start.13
  25.7 0.3 collective-permute-done.4.refs_3_
  26.0 2.7 %collective-permute-start.10 = (f32[1,136,128]{2,1,0:T(8,128)S(1)}, f32[1,136,128]{2,1,0:T(8,128)S(1)}, u32[]{:S(2)}, u32[]{:S(2)}) collective-permute-start(f32[1,136,128]{2,1,0:T(8,128)S(1)} %get-tuple-element.82), channel_id=1, source_target_pairs={{0,8},{1,9},{2,10},{3,11},{4,12},{5,13},{6,14},{7,15},{8,0},{9,1},... | collective-permute-start | bytes 208904 | tf_op jit(solution)/shard_map/ppermute | solution.py:475
  28.7 0.3 collective-permute-start.11
  29.0 6.0 %collective-permute-done.13.refs_3_ = f32[1,112,128]{2,1,0:T(8,128)S(1)} collective-permute-done((f32[1,112,128]{2,1,0:T(8,128)S(1)}, f32[1,112,128]{2,1,0:T(8,128)S(1)}, u32[]{:S(2)}, u32[]{:S(2)}) %collective-permute-start.13) | collective-permute-done | bytes 57376 | tf_op jit(solution)/shard_map/ppermute | solution.py:475
  35.1 0.3 shard_map.58
  35.4 1.2 %collective-permute-done.10.refs_2_ = f32[1,136,128]{2,1,0:T(8,128)S(1)} collective-permute-done((f32[1,136,128]{2,1,0:T(8,128)S(1)}, f32[1,136,128]{2,1,0:T(8,128)S(1)}, u32[]{:S(2)}, u32[]{:S(2)}) %collective-permute-start.10) | collective-permute-done | bytes 69664 | tf_op jit(solution)/shard_map/ppermute | solution.py:475
  36.6 1.2 %collective-permute-done.11.refs_3_ = f32[1,136,128]{2,1,0:T(8,128)S(1)} collective-permute-done((f32[1,136,128]{2,1,0:T(8,128)S(1)}, f32[1,136,128]{2,1,0:T(8,128)S(1)}, u32[]{:S(2)}, u32[]{:S(2)}) %collective-permute-start.11) | collective-permute-done | bytes 69664 | tf_op jit(solution)/shard_map/ppermute | solution.py:475
  37.8 1.1 %shard_map.59 = (f32[320,128]{1,0:T(8,128)}, f32[640,128]{1,0:T(8,128)}) custom-call(f32[1,136,128]{2,1,0:T(8,128)S(1)} %get-tuple-element.80.refs_0_, f32[1,136,128]{2,1,0:T(8,128)S(1)} %get-tuple-element.81.refs_1_, f32[1,136,128]{2,1,0:T(8,128)S(1)} %collective-permute-done.10.refs_2_, f32[1,136,128]{2,1,0:T(8,128)S(1)} %collective-permute-done.11.refs_3_, ...), custom_call_target="tpu_custom_call" | custom-call | tf_op jit(solution)/shard_map/pallas_call | solution.py:456
  (16 shorter events, 0.3 us)
Async XLA Ops:
  2.8 10.3 %collective-permute-start.5 = (f32[4,128,128]{2,1,0:T(8,128)S(1)}, f32[4,128,128]{2,1,0:T(8,128)S(1)}, u32[]{:S(2)}, u32[]{:S(2)}) collective-permute-start(f32[4,128,128]{2,1,0:T(8,128)S(1)} %get-tuple-element.73), channel_id=1, source_target_pairs={{0,2},{1,5},{2,0},{3,7},{4,6},{5,1},{6,4},{7,3},{8,10},{9,13},{10,... | collective-permute-start | bytes 786440 | tf_op jit(solution)/shard_map/ppermute | solution.py:475
  5.8 7.3 %collective-permute-start.6 = (f32[4,112,128]{2,1,0:T(8,128)S(1)}, f32[4,112,128]{2,1,0:T(8,128)S(1)}, u32[]{:S(2)}, u32[]{:S(2)}) collective-permute-start(f32[4,112,128]{2,1,0:T(8,128)S(1)} %get-tuple-element.74), channel_id=1, source_target_pairs={{0,4},{1,3},{2,6},{3,1},{4,0},{5,7},{6,2},{7,5},{8,12},{9,11},{10,... | collective-permute-start | bytes 688136 | tf_op jit(solution)/shard_map/ppermute | solution.py:475
  9.4 9.7 %collective-permute-start = (f32[4,136,128]{2,1,0:T(8,128)S(1)}, f32[4,136,128]{2,1,0:T(8,128)S(1)}, u32[]{:S(2)}, u32[]{:S(2)}) collective-permute-start(f32[4,136,128]{2,1,0:T(8,128)S(1)} %get-tuple-element.64), channel_id=1, source_target_pairs={{0,2},{1,5},{2,0},{3,7},{4,6},{5,1},{6,4},{7,3},{8,10},{9,13},{10,... | collective-permute-start | bytes 835592 | tf_op jit(solution)/shard_map/ppermute | solution.py:475
  9.9 9.2 %collective-permute-start.1 = (f32[4,136,128]{2,1,0:T(8,128)S(1)}, f32[4,136,128]{2,1,0:T(8,128)S(1)}, u32[]{:S(2)}, u32[]{:S(2)}) collective-permute-start(f32[4,136,128]{2,1,0:T(8,128)S(1)} %get-tuple-element.65), channel_id=1, source_target_pairs={{0,4},{1,3},{2,6},{3,1},{4,0},{5,7},{6,2},{7,5},{8,12},{9,11},{10,... | collective-permute-start | bytes 835592 | tf_op jit(solution)/shard_map/ppermute | solution.py:475
  12.5 4.2 %collective-permute-start.2 = (f32[2,128]{1,0:T(2,128)S(1)}, f32[2,128]{1,0:T(2,128)S(1)}, u32[]{:S(2)}, u32[]{:S(2)}) collective-permute-start(f32[2,128]{1,0:T(2,128)S(1)} %slice_bitcast_fusion), channel_id=1, source_target_pairs={{0,1},{1,0},{2,3},{3,2},{4,5},{5,4},{6,7},{7,6},{8,9},{9,8},{10,11... | collective-permute-start | bytes 3080 | tf_op jit(solution)/shard_map/ppermute | solution.py:475
  13.1 9.5 %collective-permute-start.8 = (f32[2,112,128]{2,1,0:T(8,128)S(1)}, f32[2,112,128]{2,1,0:T(8,128)S(1)}, u32[]{:S(2)}, u32[]{:S(2)}) collective-permute-start(f32[2,112,128]{2,1,0:T(8,128)S(1)} %get-tuple-element.78), channel_id=1, source_target_pairs={{0,2},{1,5},{2,0},{3,7},{4,6},{5,1},{6,4},{7,3},{8,10},{9,13},{10,... | collective-permute-start | bytes 344072 | tf_op jit(solution)/shard_map/ppermute | solution.py:475
  15.0 7.7 %collective-permute-start.7 = (f32[2,128,128]{2,1,0:T(8,128)S(1)}, f32[2,128,128]{2,1,0:T(8,128)S(1)}, u32[]{:S(2)}, u32[]{:S(2)}) collective-permute-start(f32[2,128,128]{2,1,0:T(8,128)S(1)} %get-tuple-element.77), channel_id=1, source_target_pairs={{0,4},{1,3},{2,6},{3,1},{4,0},{5,7},{6,2},{7,5},{8,12},{9,11},{10,... | collective-permute-start | bytes 393224 | tf_op jit(solution)/shard_map/ppermute | solution.py:475
  16.7 6.0 %collective-permute-start.9 = (f32[2,128]{1,0:T(2,128)S(1)}, f32[2,128]{1,0:T(2,128)S(1)}, u32[]{:S(2)}, u32[]{:S(2)}) collective-permute-start(f32[2,128]{1,0:T(2,128)S(1)} %fusion.refs_4_), channel_id=1, source_target_pairs={{0,6},{1,7},{2,4},{3,5},{4,2},{5,3},{6,0},{7,1},{8,14},{9,15},{10,... | collective-permute-start | bytes 3080 | tf_op jit(solution)/shard_map/ppermute | solution.py:475
  19.1 6.6 %collective-permute-start.3 = (f32[2,136,128]{2,1,0:T(8,128)S(1)}, f32[2,136,128]{2,1,0:T(8,128)S(1)}, u32[]{:S(2)}, u32[]{:S(2)}) collective-permute-start(f32[2,136,128]{2,1,0:T(8,128)S(1)} %get-tuple-element.69), channel_id=1, source_target_pairs={{0,4},{1,3},{2,6},{3,1},{4,0},{5,7},{6,2},{7,5},{8,12},{9,11},{10,... | collective-permute-start | bytes 417800 | tf_op jit(solution)/shard_map/ppermute | solution.py:475
  20.9 5.1 %collective-permute-start.4 = (f32[2,136,128]{2,1,0:T(8,128)S(1)}, f32[2,136,128]{2,1,0:T(8,128)S(1)}, u32[]{:S(2)}, u32[]{:S(2)}) collective-permute-start(f32[2,136,128]{2,1,0:T(8,128)S(1)} %get-tuple-element.70), channel_id=1, source_target_pairs={{0,2},{1,5},{2,0},{3,7},{4,6},{5,1},{6,4},{7,3},{8,10},{9,13},{10,... | collective-permute-start | bytes 417800 | tf_op jit(solution)/shard_map/ppermute | solution.py:475
  22.7 12.3 %collective-permute-start.12 = (f32[1,128,128]{2,1,0:T(8,128)S(1)}, f32[1,128,128]{2,1,0:T(8,128)S(1)}, u32[]{:S(2)}, u32[]{:S(2)}) collective-permute-start(f32[1,128,128]{2,1,0:T(8,128)S(1)} %get-tuple-element.86), channel_id=1, source_target_pairs={{0,8},{1,9},{2,10},{3,11},{4,12},{5,13},{6,14},{7,15},{8,0},{9,1},... | collective-permute-start | bytes 196616 | tf_op jit(solution)/shard_map/ppermute | solution.py:475
  25.4 9.7 %collective-permute-start.13 = (f32[1,112,128]{2,1,0:T(8,128)S(1)}, f32[1,112,128]{2,1,0:T(8,128)S(1)}, u32[]{:S(2)}, u32[]{:S(2)}) collective-permute-start(f32[1,112,128]{2,1,0:T(8,128)S(1)} %get-tuple-element.87), channel_id=1, source_target_pairs={{0,8},{1,9},{2,10},{3,11},{4,12},{5,13},{6,14},{7,15},{8,0},{9,1},... | collective-permute-start | bytes 172040 | tf_op jit(solution)/shard_map/ppermute | solution.py:475
  26.0 10.5 %collective-permute-start.10 = (f32[1,136,128]{2,1,0:T(8,128)S(1)}, f32[1,136,128]{2,1,0:T(8,128)S(1)}, u32[]{:S(2)}, u32[]{:S(2)}) collective-permute-start(f32[1,136,128]{2,1,0:T(8,128)S(1)} %get-tuple-element.82), channel_id=1, source_target_pairs={{0,8},{1,9},{2,10},{3,11},{4,12},{5,13},{6,14},{7,15},{8,0},{9,1},... | collective-permute-start | bytes 208904 | tf_op jit(solution)/shard_map/ppermute | solution.py:475
  28.7 9.1 %collective-permute-start.11 = (f32[1,136,128]{2,1,0:T(8,128)S(1)}, f32[1,136,128]{2,1,0:T(8,128)S(1)}, u32[]{:S(2)}, u32[]{:S(2)}) collective-permute-start(f32[1,136,128]{2,1,0:T(8,128)S(1)} %get-tuple-element.83), channel_id=1, source_target_pairs={{0,8},{1,9},{2,10},{3,11},{4,12},{5,13},{6,14},{7,15},{8,0},{9,1},... | collective-permute-start | bytes 208904 | tf_op jit(solution)/shard_map/ppermute | solution.py:475

commit v8 on v7

--- a/solution.py
+++ b/solution.py
@@ -502,7 +502,7 @@
     keeps, gots, notes, buffers = {}, {}, None, None
     calls = [
         tuple((k, first) for k in ks)
-        for first, ks in ((send, early), (send, late), (keep, early), (keep, late))
+        for first, ks in ((send, early), (keep, early), (keep, late), (send, late))
     ]
     for items, ahead in zip(calls, calls[1:] + [()]):
         parts, notes, buffers = pack(

time: 39.2 us -> 39.5 us (level)
  waiting for transfers between devices: 11 us -> 14 us
  starting transfers between devices: 18.8 us -> 16 us
    ppermute x14, waiting for transfers between devices: 11 us -> 14 us  [swap(): return lax.ppermute(value, ('dp', 'tensor'), pairs)]
    ppermute x14, starting transfers between devices: 18.8 us -> 16 us  [swap(): return lax.ppermute(value, ('dp', 'tensor'), pairs)]
  transfers between devices with their start and end apart: 14 -> 14, of which waited for: 6 -> 7; matrix products, arithmetic and copies ran while one was open for 0% -> 0% of each run, Pallas kernels for 13% -> 13%
where the time goes in v8:
time: 39.5 us; the launch traced here: 39.2 us
  starting transfers between devices  16 us (41%)
  waiting for transfers between devices  14 us (35%)
  Pallas kernels  8.47 us (21%)
  between operations  0.72 us (2%)
    ppermute x14, starting transfers between devices, swap(): return lax.ppermute(value, ('dp', 'tensor'), pairs)  16 us
    ppermute x14, waiting for transfers between devices, swap(): return lax.ppermute(value, ('dp', 'tensor'), pairs)  14 us
    pallas_call x4, Pallas kernels, pack(): pl.pallas_call(functools.partial(pack_body, pieces, items, ahead, count_a...  6.91 us
    pallas_call x1, Pallas kernels, finish(): pl.pallas_call(functools.partial(finish_body, pieces, early, late, count_...  1.1 us
  transfers between devices with their start and end apart: 14, of which 7 were waited for; matrix products, arithmetic and copies ran while one was open for 0% of the time, Pallas kernels for 13%

profile of v8, /device:TPU:0, one launch (start us, length us, event | category | flops | bytes accessed | tf_op | source)
XLA Modules:
  0.0 39.2 jit_solution(15883680639739393044)
XLA Ops:
  0.6 2.2 %shard_map.50 = (f32[4,128,128]{2,1,0:T(8,128)S(1)}, f32[4,112,128]{2,1,0:T(8,128)S(1)}, f32[17,8,128]{2,1,0:T(8,128)S(1)}, bf16[4,128,256]{2,1,0:T(8,128)(2,1)S...) custom-call(bf16[128,2560]{1,0:T(8,128)(2,1)} %refs_0_.7, ...), custom_call_target="tpu_custom_call" | custom-call | flops 1 | bytes 1 | tf_op jit(solution)/shard_map/pallas_call | solution.py:280
  2.8 3.0 %collective-permute-start.5 = (f32[4,128,128]{2,1,0:T(8,128)S(1)}, f32[4,128,128]{2,1,0:T(8,128)S(1)}, u32[]{:S(2)}, u32[]{:S(2)}) collective-permute-start(f32[4,128,128]{2,1,0:T(8,128)S(1)} %get-tuple-element.73), channel_id=1, source_target_pairs={{0,2},{1,5},{2,0},{3,7},{4,6},{5,1},{6,4},{7,3},{8,10},{9,13},{10,... | collective-permute-start | bytes 786440 | tf_op jit(solution)/shard_map/ppermute | solution.py:475
  5.8 1.6 %collective-permute-start.6 = (f32[4,112,128]{2,1,0:T(8,128)S(1)}, f32[4,112,128]{2,1,0:T(8,128)S(1)}, u32[]{:S(2)}, u32[]{:S(2)}) collective-permute-start(f32[4,112,128]{2,1,0:T(8,128)S(1)} %get-tuple-element.74), channel_id=1, source_target_pairs={{0,4},{1,3},{2,6},{3,1},{4,0},{5,7},{6,2},{7,5},{8,12},{9,11},{10,... | collective-permute-start | bytes 688136 | tf_op jit(solution)/shard_map/ppermute | solution.py:475
  7.4 1.8 %shard_map.51 = (f32[4,128,128]{2,1,0:T(8,128)S(1)}, f32[4,112,128]{2,1,0:T(8,128)S(1)}, f32[17,8,128]{2,1,0:T(8,128)S(1)}, bf16[4,128,256]{2,1,0:T(8,128)(2,1)S...) custom-call(bf16[128,2560]{1,0:T(8,128)(2,1)} %refs_0_.7, ...), custom_call_target="tpu_custom_call" | custom-call | flops 1 | bytes 1 | tf_op jit(solution)/shard_map/pallas_call | solution.py:280
  9.2 2.1 %shard_map.52 = (f32[4,136,128]{2,1,0:T(8,128)S(1)}, f32[4,136,128]{2,1,0:T(8,128)S(1)}, f32[17,8,128]{2,1,0:T(8,128)S(1)}, bf16[4,128,256]{2,1,0:T(8,128)(2,1)S...) custom-call(bf16[128,2560]{1,0:T(8,128)(2,1)} %refs_0_.7, ...), custom_call_target="tpu_custom_call" | custom-call | flops 1 | bytes 1 | tf_op jit(solution)/shard_map/pallas_call | solution.py:280
  11.4 0.8 %shard_map.53 = (f32[4,136,128]{2,1,0:T(8,128)S(1)}, f32[4,136,128]{2,1,0:T(8,128)S(1)}, f32[17,8,128]{2,1,0:T(8,128)S(1)}) custom-call(bf16[128,2560]{1,0:T(8,128)(2,1)} %refs_0_.7, bf16[128,5120]{1,0:T(8,128)(2,1)} %refs_1_.7, bf16[128,5120]{1,0:T(8,128)(2,1)} %refs_2_.7, f32[17,8,128]{2,1,0:T(8,128)S(1)} %get-tuple-element.59.refs_3_, ...), custom_call_target="tpu_custom_call" | custom-call | flops 1 | bytes 1 | tf_op jit(solution)/shard_map/pallas_call | solution.py:280
  12.2 0.6 %collective-permute-start = (f32[4,136,128]{2,1,0:T(8,128)S(1)}, f32[4,136,128]{2,1,0:T(8,128)S(1)}, u32[]{:S(2)}, u32[]{:S(2)}) collective-permute-start(f32[4,136,128]{2,1,0:T(8,128)S(1)} %get-tuple-element.64), channel_id=1, source_target_pairs={{0,2},{1,5},{2,0},{3,7},{4,6},{5,1},{6,4},{7,3},{8,10},{9,13},{10,... | collective-permute-start | bytes 835592 | tf_op jit(solution)/shard_map/ppermute | solution.py:475
  12.8 2.0 %collective-permute-start.8 = (f32[2,112,128]{2,1,0:T(8,128)S(1)}, f32[2,112,128]{2,1,0:T(8,128)S(1)}, u32[]{:S(2)}, u32[]{:S(2)}) collective-permute-start(f32[2,112,128]{2,1,0:T(8,128)S(1)} %get-tuple-element.78), channel_id=1, source_target_pairs={{0,2},{1,5},{2,0},{3,7},{4,6},{5,1},{6,4},{7,3},{8,10},{9,13},{10,... | collective-permute-start | bytes 344072 | tf_op jit(solution)/shard_map/ppermute | solution.py:475
  14.8 1.6 %collective-permute-start.7 = (f32[2,128,128]{2,1,0:T(8,128)S(1)}, f32[2,128,128]{2,1,0:T(8,128)S(1)}, u32[]{:S(2)}, u32[]{:S(2)}) collective-permute-start(f32[2,128,128]{2,1,0:T(8,128)S(1)} %get-tuple-element.77), channel_id=1, source_target_pairs={{0,4},{1,3},{2,6},{3,1},{4,0},{5,7},{6,2},{7,5},{8,12},{9,11},{10,... | collective-permute-start | bytes 393224 | tf_op jit(solution)/shard_map/ppermute | solution.py:475
  16.4 0.4 %collective-permute-start.9 = (f32[2,128]{1,0:T(2,128)S(1)}, f32[2,128]{1,0:T(2,128)S(1)}, u32[]{:S(2)}, u32[]{:S(2)}) collective-permute-start(f32[2,128]{1,0:T(2,128)S(1)} %fusion.refs_4_), channel_id=1, source_target_pairs={{0,6},{1,7},{2,4},{3,5},{4,2},{5,3},{6,0},{7,1},{8,14},{9,15},{10,... | collective-permute-start | bytes 3080 | tf_op jit(solution)/shard_map/ppermute | solution.py:475
  16.9 4.9 %collective-permute-done.refs_2_ = f32[4,136,128]{2,1,0:T(8,128)S(1)} collective-permute-done((f32[4,136,128]{2,1,0:T(8,128)S(1)}, f32[4,136,128]{2,1,0:T(8,128)S(1)}, u32[]{:S(2)}, u32[]{:S(2)}) %collective-permute-start) | collective-permute-done | bytes 278560 | tf_op jit(solution)/shard_map/ppermute | solution.py:475
  21.8 0.4 %collective-permute-start.3 = (f32[2,136,128]{2,1,0:T(8,128)S(1)}, f32[2,136,128]{2,1,0:T(8,128)S(1)}, u32[]{:S(2)}, u32[]{:S(2)}) collective-permute-start(f32[2,136,128]{2,1,0:T(8,128)S(1)} %get-tuple-element.69), channel_id=1, source_target_pairs={{0,4},{1,3},{2,6},{3,1},{4,0},{5,7},{6,2},{7,5},{8,12},{9,11},{10,... | collective-permute-start | bytes 417800 | tf_op jit(solution)/shard_map/ppermute | solution.py:475
  22.3 0.4 collective-permute-start.4
  22.9 1.3 %collective-permute-done.8.refs_3_ = f32[2,112,128]{2,1,0:T(8,128)S(1)} collective-permute-done((f32[2,112,128]{2,1,0:T(8,128)S(1)}, f32[2,112,128]{2,1,0:T(8,128)S(1)}, u32[]{:S(2)}, u32[]{:S(2)}) %collective-permute-start.8) | collective-permute-done | bytes 114720 | tf_op jit(solution)/shard_map/ppermute | solution.py:475
  24.2 2.7 %collective-permute-start.12 = (f32[1,128,128]{2,1,0:T(8,128)S(1)}, f32[1,128,128]{2,1,0:T(8,128)S(1)}, u32[]{:S(2)}, u32[]{:S(2)}) collective-permute-start(f32[1,128,128]{2,1,0:T(8,128)S(1)} %get-tuple-element.86), channel_id=1, source_target_pairs={{0,8},{1,9},{2,10},{3,11},{4,12},{5,13},{6,14},{7,15},{8,0},{9,1},... | collective-permute-start | bytes 196616 | tf_op jit(solution)/shard_map/ppermute | solution.py:475
  26.9 0.4 collective-permute-start.13
  27.3 0.4 collective-permute-done.3.refs_2_
  27.7 2.6 %collective-permute-start.10 = (f32[1,136,128]{2,1,0:T(8,128)S(1)}, f32[1,136,128]{2,1,0:T(8,128)S(1)}, u32[]{:S(2)}, u32[]{:S(2)}) collective-permute-start(f32[1,136,128]{2,1,0:T(8,128)S(1)} %get-tuple-element.82), channel_id=1, source_target_pairs={{0,8},{1,9},{2,10},{3,11},{4,12},{5,13},{6,14},{7,15},{8,0},{9,1},... | collective-permute-start | bytes 208904 | tf_op jit(solution)/shard_map/ppermute | solution.py:475
  30.3 0.3 collective-permute-start.11
  30.7 5.0 %collective-permute-done.13.refs_3_ = f32[1,112,128]{2,1,0:T(8,128)S(1)} collective-permute-done((f32[1,112,128]{2,1,0:T(8,128)S(1)}, f32[1,112,128]{2,1,0:T(8,128)S(1)}, u32[]{:S(2)}, u32[]{:S(2)}) %collective-permute-start.13) | collective-permute-done | bytes 57376 | tf_op jit(solution)/shard_map/ppermute | solution.py:475
  35.7 0.3 shard_map.58
  36.0 1.4 %collective-permute-done.10.refs_2_ = f32[1,136,128]{2,1,0:T(8,128)S(1)} collective-permute-done((f32[1,136,128]{2,1,0:T(8,128)S(1)}, f32[1,136,128]{2,1,0:T(8,128)S(1)}, u32[]{:S(2)}, u32[]{:S(2)}) %collective-permute-start.10) | collective-permute-done | bytes 69664 | tf_op jit(solution)/shard_map/ppermute | solution.py:475
  37.3 0.7 %collective-permute-done.11.refs_3_ = f32[1,136,128]{2,1,0:T(8,128)S(1)} collective-permute-done((f32[1,136,128]{2,1,0:T(8,128)S(1)}, f32[1,136,128]{2,1,0:T(8,128)S(1)}, u32[]{:S(2)}, u32[]{:S(2)}) %collective-permute-start.11) | collective-permute-done | bytes 69664 | tf_op jit(solution)/shard_map/ppermute | solution.py:475
  38.1 1.1 %shard_map.59 = (f32[320,128]{1,0:T(8,128)}, f32[640,128]{1,0:T(8,128)}) custom-call(f32[1,136,128]{2,1,0:T(8,128)S(1)} %get-tuple-element.80.refs_0_, f32[1,136,128]{2,1,0:T(8,128)S(1)} %get-tuple-element.81.refs_1_, f32[1,136,128]{2,1,0:T(8,128)S(1)} %collective-permute-done.10.refs_2_, f32[1,136,128]{2,1,0:T(8,128)S(1)} %collective-permute-done.11.refs_3_, ...), custom_call_target="tpu_custom_call" | custom-call | tf_op jit(solution)/shard_map/pallas_call | solution.py:456
  (16 shorter events, 0.5 us)
Async XLA Ops:
  2.8 10.0 %collective-permute-start.5 = (f32[4,128,128]{2,1,0:T(8,128)S(1)}, f32[4,128,128]{2,1,0:T(8,128)S(1)}, u32[]{:S(2)}, u32[]{:S(2)}) collective-permute-start(f32[4,128,128]{2,1,0:T(8,128)S(1)} %get-tuple-element.73), channel_id=1, source_target_pairs={{0,2},{1,5},{2,0},{3,7},{4,6},{5,1},{6,4},{7,3},{8,10},{9,13},{10,... | collective-permute-start | bytes 786440 | tf_op jit(solution)/shard_map/ppermute | solution.py:475
  5.8 6.9 %collective-permute-start.6 = (f32[4,112,128]{2,1,0:T(8,128)S(1)}, f32[4,112,128]{2,1,0:T(8,128)S(1)}, u32[]{:S(2)}, u32[]{:S(2)}) collective-permute-start(f32[4,112,128]{2,1,0:T(8,128)S(1)} %get-tuple-element.74), channel_id=1, source_target_pairs={{0,4},{1,3},{2,6},{3,1},{4,0},{5,7},{6,2},{7,5},{8,12},{9,11},{10,... | collective-permute-start | bytes 688136 | tf_op jit(solution)/shard_map/ppermute | solution.py:475
  12.2 9.6 %collective-permute-start = (f32[4,136,128]{2,1,0:T(8,128)S(1)}, f32[4,136,128]{2,1,0:T(8,128)S(1)}, u32[]{:S(2)}, u32[]{:S(2)}) collective-permute-start(f32[4,136,128]{2,1,0:T(8,128)S(1)} %get-tuple-element.64), channel_id=1, source_target_pairs={{0,2},{1,5},{2,0},{3,7},{4,6},{5,1},{6,4},{7,3},{8,10},{9,13},{10,... | collective-permute-start | bytes 835592 | tf_op jit(solution)/shard_map/ppermute | solution.py:475
  12.8 9.0 %collective-permute-start.1 = (f32[4,136,128]{2,1,0:T(8,128)S(1)}, f32[4,136,128]{2,1,0:T(8,128)S(1)}, u32[]{:S(2)}, u32[]{:S(2)}) collective-permute-start(f32[4,136,128]{2,1,0:T(8,128)S(1)} %get-tuple-element.65), channel_id=1, source_target_pairs={{0,4},{1,3},{2,6},{3,1},{4,0},{5,7},{6,2},{7,5},{8,12},{9,11},{10,... | collective-permute-start | bytes 835592 | tf_op jit(solution)/shard_map/ppermute | solution.py:475
  12.8 3.7 %collective-permute-start.2 = (f32[2,128]{1,0:T(2,128)S(1)}, f32[2,128]{1,0:T(2,128)S(1)}, u32[]{:S(2)}, u32[]{:S(2)}) collective-permute-start(f32[2,128]{1,0:T(2,128)S(1)} %slice_bitcast_fusion), channel_id=1, source_target_pairs={{0,1},{1,0},{2,3},{3,2},{4,5},{5,4},{6,7},{7,6},{8,9},{9,8},{10,11... | collective-permute-start | bytes 3080 | tf_op jit(solution)/shard_map/ppermute | solution.py:475
  12.8 11.4 %collective-permute-start.8 = (f32[2,112,128]{2,1,0:T(8,128)S(1)}, f32[2,112,128]{2,1,0:T(8,128)S(1)}, u32[]{:S(2)}, u32[]{:S(2)}) collective-permute-start(f32[2,112,128]{2,1,0:T(8,128)S(1)} %get-tuple-element.78), channel_id=1, source_target_pairs={{0,2},{1,5},{2,0},{3,7},{4,6},{5,1},{6,4},{7,3},{8,10},{9,13},{10,... | collective-permute-start | bytes 344072 | tf_op jit(solution)/shard_map/ppermute | solution.py:475
  14.8 9.4 %collective-permute-start.7 = (f32[2,128,128]{2,1,0:T(8,128)S(1)}, f32[2,128,128]{2,1,0:T(8,128)S(1)}, u32[]{:S(2)}, u32[]{:S(2)}) collective-permute-start(f32[2,128,128]{2,1,0:T(8,128)S(1)} %get-tuple-element.77), channel_id=1, source_target_pairs={{0,4},{1,3},{2,6},{3,1},{4,0},{5,7},{6,2},{7,5},{8,12},{9,11},{10,... | collective-permute-start | bytes 393224 | tf_op jit(solution)/shard_map/ppermute | solution.py:475
  16.4 6.5 %collective-permute-start.9 = (f32[2,128]{1,0:T(2,128)S(1)}, f32[2,128]{1,0:T(2,128)S(1)}, u32[]{:S(2)}, u32[]{:S(2)}) collective-permute-start(f32[2,128]{1,0:T(2,128)S(1)} %fusion.refs_4_), channel_id=1, source_target_pairs={{0,6},{1,7},{2,4},{3,5},{4,2},{5,3},{6,0},{7,1},{8,14},{9,15},{10,... | collective-permute-start | bytes 3080 | tf_op jit(solution)/shard_map/ppermute | solution.py:475
  21.8 5.8 %collective-permute-start.3 = (f32[2,136,128]{2,1,0:T(8,128)S(1)}, f32[2,136,128]{2,1,0:T(8,128)S(1)}, u32[]{:S(2)}, u32[]{:S(2)}) collective-permute-start(f32[2,136,128]{2,1,0:T(8,128)S(1)} %get-tuple-element.69), channel_id=1, source_target_pairs={{0,4},{1,3},{2,6},{3,1},{4,0},{5,7},{6,2},{7,5},{8,12},{9,11},{10,... | collective-permute-start | bytes 417800 | tf_op jit(solution)/shard_map/ppermute | solution.py:475
  22.3 5.4 %collective-permute-start.4 = (f32[2,136,128]{2,1,0:T(8,128)S(1)}, f32[2,136,128]{2,1,0:T(8,128)S(1)}, u32[]{:S(2)}, u32[]{:S(2)}) collective-permute-start(f32[2,136,128]{2,1,0:T(8,128)S(1)} %get-tuple-element.70), channel_id=1, source_target_pairs={{0,2},{1,5},{2,0},{3,7},{4,6},{5,1},{6,4},{7,3},{8,10},{9,13},{10,... | collective-permute-start | bytes 417800 | tf_op jit(solution)/shard_map/ppermute | solution.py:475
  24.2 11.4 %collective-permute-start.12 = (f32[1,128,128]{2,1,0:T(8,128)S(1)}, f32[1,128,128]{2,1,0:T(8,128)S(1)}, u32[]{:S(2)}, u32[]{:S(2)}) collective-permute-start(f32[1,128,128]{2,1,0:T(8,128)S(1)} %get-tuple-element.86), channel_id=1, source_target_pairs={{0,8},{1,9},{2,10},{3,11},{4,12},{5,13},{6,14},{7,15},{8,0},{9,1},... | collective-permute-start | bytes 196616 | tf_op jit(solution)/shard_map/ppermute | solution.py:475
  26.9 8.8 %collective-permute-start.13 = (f32[1,112,128]{2,1,0:T(8,128)S(1)}, f32[1,112,128]{2,1,0:T(8,128)S(1)}, u32[]{:S(2)}, u32[]{:S(2)}) collective-permute-start(f32[1,112,128]{2,1,0:T(8,128)S(1)} %get-tuple-element.87), channel_id=1, source_target_pairs={{0,8},{1,9},{2,10},{3,11},{4,12},{5,13},{6,14},{7,15},{8,0},{9,1},... | collective-permute-start | bytes 172040 | tf_op jit(solution)/shard_map/ppermute | solution.py:475
  27.7 9.6 %collective-permute-start.10 = (f32[1,136,128]{2,1,0:T(8,128)S(1)}, f32[1,136,128]{2,1,0:T(8,128)S(1)}, u32[]{:S(2)}, u32[]{:S(2)}) collective-permute-start(f32[1,136,128]{2,1,0:T(8,128)S(1)} %get-tuple-element.82), channel_id=1, source_target_pairs={{0,8},{1,9},{2,10},{3,11},{4,12},{5,13},{6,14},{7,15},{8,0},{9,1},... | collective-permute-start | bytes 208904 | tf_op jit(solution)/shard_map/ppermute | solution.py:475
  30.3 7.7 %collective-permute-start.11 = (f32[1,136,128]{2,1,0:T(8,128)S(1)}, f32[1,136,128]{2,1,0:T(8,128)S(1)}, u32[]{:S(2)}, u32[]{:S(2)}) collective-permute-start(f32[1,136,128]{2,1,0:T(8,128)S(1)} %get-tuple-element.83), channel_id=1, source_target_pairs={{0,8},{1,9},{2,10},{3,11},{4,12},{5,13},{6,14},{7,15},{8,0},{9,1},... | collective-permute-start | bytes 208904 | tf_op jit(solution)/shard_map/ppermute | solution.py:475

commit v9 on v8

--- a/solution.py
+++ b/solution.py
@@ -61,8 +61,6 @@
 X, NEAR, FAR = 0, 1, 2
 KINDS = (((X, NEAR, FAR), (NEAR, X, FAR)), ((NEAR, X, FAR), (X, NEAR, FAR)))
 NOTES = len(KINDS) * SLOTS
-
-WEIGHTS = {((0, 2), 2): 2 * 10**9}
 
 
 def split_rows(count):
@@ -291,40 +289,44 @@
     return outs[:n], outs[n], outs[n + 1 :]
 
 
-def halve_body(n, summed, gathered, *refs):
-    keeps, gots, refs = refs[:n], refs[n : 2 * n], refs[2 * n :]
-    split = len(refs) - 2 * n - summed
-    traces, outs = refs[:split], refs[split:]
-    for k in range(n):
-        half = keeps[k].shape[0] // 2
-        for part in range(2):
-            here = slice(part * half, (part + 1) * half)
-            outs[2 * k + part][...] = keeps[k][here] + gots[k][here]
-    if summed:
-        outs[-1][...] = traces[0][...] + traces[1][...]
-    elif traces:
-        value = traces[0][...]
-        if gathered:
-            value = value + sum(got[0, -2:, :] for got in gots)
-        for out in outs:
-            out[0, -2:, :] = value
-
-
-def halve(keeps, gots, traces=(), gathered=False, weight=1):
-    summed = len(traces) == 2
-    n = len(keeps)
-    args = (*keeps, *gots, *traces)
-    shapes = [(keep.shape[0] // 2, *keep.shape[1:]) for keep in keeps for _ in range(2)]
-    shapes += [trace.shape for trace in traces[:summed]]
-    outs = pl.pallas_call(
-        functools.partial(halve_body, n, summed, gathered),
+def halve_body(trace, came, put, passed, *refs):
+    refs = list(refs)
+    keep, got = refs[:2]
+    kept, sent, *sums = refs[2 + trace + passed :]
+    sums = sums[passed:]
+    half, rows, _ = kept.shape
+    kept[...] = keep[:half] + got[:half, :rows, :]
+    sent[:, :rows, :] = keep[half:] + got[half:, :rows, :]
+    if trace:
+        value = refs[2][...]
+        if came:
+            value = value + got[0, -2:, :]
+        for out in sums:
+            out[...] = value
+        if put:
+            tail = sent.shape[1] - rows
+            if tail:
+                sent[:, rows:, :] = jnp.zeros((half, tail, B), jnp.float32)
+            for out in (sent,) if tail else (kept, sent):
+                out[0, -2:, :] = value
+
+
+def halve(keep, got, trace=None, came=False, put=False, tail=False, emit=False, passes=()):
+    args = [keep, got, *([] if trace is None else [trace]), *passes]
+    slots, rows, _ = keep.shape
+    shapes = [(slots // 2, rows, B), (slots // 2, rows + EDGE * tail, B)]
+    shapes += [*(array.shape for array in passes), *([(2, B)] * emit)]
+    first = len(args) - len(passes)
+    kept, sent, *others = pl.pallas_call(
+        functools.partial(halve_body, trace is not None, came, put, len(passes)),
         in_specs=[pl.BlockSpec(memory_space=pltpu.VMEM)] * len(args),
         out_specs=[pl.BlockSpec(memory_space=pltpu.VMEM)] * len(shapes),
         out_shape=[jax.ShapeDtypeStruct(shape, jnp.float32) for shape in shapes],
+        input_output_aliases={first + i: 2 + i for i in range(len(passes))},
         compiler_params=pltpu.CompilerParams(vmem_limit_bytes=32 * 2**20),
-        cost_estimate=pl.CostEstimate(flops=weight, bytes_accessed=1, transcendentals=0),
+        cost_estimate=pl.CostEstimate(flops=1, bytes_accessed=1, transcendentals=0),
     )(*args)
-    return outs[0 : 2 * n : 2], outs[1 : 2 * n : 2], outs[2 * n :]
+    return kept, sent, others
 
 
 def mean_of(value, total):
@@ -406,8 +408,8 @@
     unfold_body(pieces, late, count_a, total, owns, gots, outs)
 
     edges = {}
-    for i, k in enumerate(late):
-        edge = mean_of(owns[i][0, -EDGE:, :] + gots[i][0, -EDGE:, :], total)
+    for k, own, got in zip(late, owns, gots):
+        edge = mean_of(own[0, -EDGE:, :] + got[0, -EDGE:, :], total)
         edges[pieces[k][3]] = (edge, pltpu.roll(edge, H, 1))
     sums = jnp.sum(edge[-2:], axis=1, keepdims=True)
     ratio = jnp.sqrt(sums[0:1] / D / (sums[1:2] / FFW))
@@ -489,8 +491,8 @@
     some = 1 + (full_g - 1) // 2
     pieces = (
         (tuple(range(full_a)), 0, (), 0),
+        ((), half_a, (0,), 1),
         ((), 0, tuple(range(1, some)), 0),
-        ((), half_a, (0,), 1),
         ((), 0, tuple(range(some, full_g)), 1),
     )
     arrays = tuple(
@@ -498,38 +500,47 @@
         for array in (saved_input, saved_pre, grad_act)
     )
     keep, send = 0, SLOTS // 2
-    early, late = (0, 2), (1, 3)
+    early, late = (0, 1), (2, 3)
     keeps, gots, notes, buffers = {}, {}, None, None
     calls = [
         tuple((k, first) for k in ks)
         for first, ks in ((send, early), (keep, early), (keep, late), (send, late))
     ]
-    for items, ahead in zip(calls, calls[1:] + [()]):
+
+    def pack_next():
+        nonlocal notes, buffers
+        items, ahead = calls.pop(0), calls[0] if calls else ()
         parts, notes, buffers = pack(
             arrays, pieces, items, ahead, count_a, count_g, notes, buffers
         )
-        for (k, first), part in zip(items, parts):
-            if first == send:
-                gots[k] = swap(part, along(0, pieces[k][3]))
-            else:
-                keeps[k] = part
+        return dict(zip((k for k, _ in items), parts))
+
+    def exchange(k, part, stage):
+        gots[k] = swap(part, along(stage, pieces[k][3]))
+
+    def halve_piece(k, stage, **kinds):
+        keeps[k], part, others = halve(keeps[k], gots[k], **kinds)
+        exchange(k, part, stage)
+        return others
+
+    for k, part in pack_next().items():
+        exchange(k, part, 0)
+    keeps.update(pack_next())
+    keeps.update(pack_next())
+    waiting = pack_next()
 
     trace = notes[NOTES, :2, :]
     trace = trace + swap(trace, lambda i, j: (i, j ^ 1))
-    across = swap(trace, lambda i, j: (i ^ (1 << X) ^ (1 << NEAR), j))
-    for stage in (1, 2):
-        for ks in (early, late):
-            if ks == late:
-                traces = (trace,)
-            else:
-                traces = (trace, across) if stage == 2 else ()
-            own, parts, news = halve(
-                [keeps[k] for k in ks], [gots[k] for k in ks], traces,
-                gathered=stage == 2, weight=WEIGHTS.get((ks, stage), 1)
-            )
-            trace = news[0] if news else trace
-            for k, mine, part in zip(ks, own, parts):
-                keeps[k], gots[k] = mine, swap(part, along(stage, pieces[k][3]))
+    (part,) = halve_piece(0, 1, trace=trace, put=True, tail=True, passes=(waiting[2],))
+    exchange(2, part, 0)
+    (part,) = halve_piece(1, 1, passes=(waiting[3],))
+    exchange(3, part, 0)
+    (trace,) = halve_piece(0, 2, trace=trace, came=True, emit=True)
+    halve_piece(1, 2)
+    (gots[0],) = halve_piece(2, 1, passes=(gots[0],))
+    (gots[1],) = halve_piece(3, 1, trace=trace, put=True, passes=(gots[1],))
+    halve_piece(2, 2)
+    halve_piece(3, 2, trace=trace, came=True, put=True)
 
     def both(ks):
         return [keeps[k] for k in ks], [gots[k] for k in ks]

time: 39.5 us -> 48.6 us (1.23)
  waiting for transfers between devices: 14 us -> 22.9 us
    ppermute x14 -> x13, waiting for transfers between devices: 14 us -> 22.9 us  [swap(): return lax.ppermute(value, ('dp', 'tensor'), pairs)]
    ppermute x14 -> x13, starting transfers between devices: 16 us -> 16.1 us  [swap(): return lax.ppermute(value, ('dp', 'tensor'), pairs)]
  transfers between devices with their start and end apart: 14 -> 13, of which waited for: 7 -> 6; matrix products, arithmetic and copies ran while one was open for 0% -> 0% of each run, Pallas kernels for 13% -> 11%
where the time goes in v9:
time: 48.6 us; the launch traced here: 48.2 us
  waiting for transfers between devices  22.9 us (47%)
  starting transfers between devices  16.1 us (33%)
  Pallas kernels  8.48 us (17%)
  between operations  0.74 us (2%)
    ppermute x13, waiting for transfers between devices, swap(): return lax.ppermute(value, ('dp', 'tensor'), pairs)  22.9 us
    ppermute x13, starting transfers between devices, swap(): return lax.ppermute(value, ('dp', 'tensor'), pairs)  16.1 us
    pallas_call x4, Pallas kernels, pack(): pl.pallas_call(functools.partial(pack_body, pieces, items, ahead, count_a...  6.91 us
    pallas_call x1, Pallas kernels, finish(): pl.pallas_call(functools.partial(finish_body, pieces, early, late, count_...  1.1 us
  transfers between devices with their start and end apart: 13, of which 6 were waited for; matrix products, arithmetic and copies ran while one was open for 0% of the time, Pallas kernels for 11%

profile of v9, /device:TPU:0, one launch (start us, length us, event | category | flops | bytes accessed | tf_op | source)
XLA Modules:
  0.0 48.2 jit_solution(16328190509401801093)
XLA Ops:
  0.6 2.2 %shard_map.50 = (f32[4,128,128]{2,1,0:T(8,128)S(1)}, f32[4,112,128]{2,1,0:T(8,128)S(1)}, f32[17,8,128]{2,1,0:T(8,128)S(1)}, bf16[4,128,256]{2,1,0:T(8,128)(2,1)S...) custom-call(bf16[128,2560]{1,0:T(8,128)(2,1)} %refs_0_.7, ...), custom_call_target="tpu_custom_call" | custom-call | flops 1 | bytes 1 | tf_op jit(solution)/shard_map/pallas_call | solution.py:278
  2.8 3.1 %collective-permute-start.6 = (f32[4,112,128]{2,1,0:T(8,128)S(1)}, f32[4,112,128]{2,1,0:T(8,128)S(1)}, u32[]{:S(2)}, u32[]{:S(2)}) collective-permute-start(f32[4,112,128]{2,1,0:T(8,128)S(1)} %get-tuple-element.80), channel_id=1, source_target_pairs={{0,4},{1,3},{2,6},{3,1},{4,0},{5,7},{6,2},{7,5},{8,12},{9,11},{10,... | collective-permute-start | bytes 688136 | tf_op jit(solution)/shard_map/ppermute | solution.py:477
  5.9 1.5 %collective-permute-start = (f32[4,128,128]{2,1,0:T(8,128)S(1)}, f32[4,128,128]{2,1,0:T(8,128)S(1)}, u32[]{:S(2)}, u32[]{:S(2)}) collective-permute-start(f32[4,128,128]{2,1,0:T(8,128)S(1)} %get-tuple-element.63), channel_id=1, source_target_pairs={{0,2},{1,5},{2,0},{3,7},{4,6},{5,1},{6,4},{7,3},{8,10},{9,13},{10,... | collective-permute-start | bytes 786440 | tf_op jit(solution)/shard_map/ppermute | solution.py:477
  7.4 1.8 %shard_map.51 = (f32[4,128,128]{2,1,0:T(8,128)S(1)}, f32[4,112,128]{2,1,0:T(8,128)S(1)}, f32[17,8,128]{2,1,0:T(8,128)S(1)}, bf16[4,128,256]{2,1,0:T(8,128)(2,1)S...) custom-call(bf16[128,2560]{1,0:T(8,128)(2,1)} %refs_0_.7, ...), custom_call_target="tpu_custom_call" | custom-call | flops 1 | bytes 1 | tf_op jit(solution)/shard_map/pallas_call | solution.py:278
  9.2 2.1 %shard_map.52 = (f32[4,136,128]{2,1,0:T(8,128)S(1)}, f32[4,136,128]{2,1,0:T(8,128)S(1)}, f32[17,8,128]{2,1,0:T(8,128)S(1)}, bf16[4,128,256]{2,1,0:T(8,128)(2,1)S...) custom-call(bf16[128,2560]{1,0:T(8,128)(2,1)} %refs_0_.7, ...), custom_call_target="tpu_custom_call" | custom-call | flops 1 | bytes 1 | tf_op jit(solution)/shard_map/pallas_call | solution.py:278
  11.4 0.8 %shard_map.53 = (f32[4,136,128]{2,1,0:T(8,128)S(1)}, f32[4,136,128]{2,1,0:T(8,128)S(1)}, f32[17,8,128]{2,1,0:T(8,128)S(1)}) custom-call(bf16[128,2560]{1,0:T(8,128)(2,1)} %refs_0_.7, bf16[128,5120]{1,0:T(8,128)(2,1)} %refs_1_.7, bf16[128,5120]{1,0:T(8,128)(2,1)} %refs_2_.7, f32[17,8,128]{2,1,0:T(8,128)S(1)} %get-tuple-element.64.refs_3_, ...), custom_call_target="tpu_custom_call" | custom-call | flops 1 | bytes 1 | tf_op jit(solution)/shard_map/pallas_call | solution.py:278
  12.3 2.1 %collective-permute-start.7 = (f32[4,136,128]{2,1,0:T(8,128)S(1)}, f32[4,136,128]{2,1,0:T(8,128)S(1)}, u32[]{:S(2)}, u32[]{:S(2)}) collective-permute-start(f32[4,136,128]{2,1,0:T(8,128)S(1)} %get-tuple-element.82), channel_id=1, source_target_pairs={{0,4},{1,3},{2,6},{3,1},{4,0},{5,7},{6,2},{7,5},{8,12},{9,11},{10,... | collective-permute-start | bytes 835592 | tf_op jit(solution)/shard_map/ppermute | solution.py:477
  14.5 1.1 %collective-permute-start.2 = (f32[4,136,128]{2,1,0:T(8,128)S(1)}, f32[4,136,128]{2,1,0:T(8,128)S(1)}, u32[]{:S(2)}, u32[]{:S(2)}) collective-permute-start(f32[4,136,128]{2,1,0:T(8,128)S(1)} %get-tuple-element.71), channel_id=1, source_target_pairs={{0,2},{1,5},{2,0},{3,7},{4,6},{5,1},{6,4},{7,3},{8,10},{9,13},{10,... | collective-permute-start | bytes 835592 | tf_op jit(solution)/shard_map/ppermute | solution.py:477
  15.6 0.3 collective-permute-start.3
  15.8 0.7 %collective-permute-start.8 = (f32[2,112,128]{2,1,0:T(8,128)S(1)}, f32[2,112,128]{2,1,0:T(8,128)S(1)}, u32[]{:S(2)}, u32[]{:S(2)}) collective-permute-start(f32[2,112,128]{2,1,0:T(8,128)S(1)} %get-tuple-element.85), channel_id=1, source_target_pairs={{0,2},{1,5},{2,0},{3,7},{4,6},{5,1},{6,4},{7,3},{8,10},{9,13},{10,... | collective-permute-start | bytes 344072 | tf_op jit(solution)/shard_map/ppermute | solution.py:477
  16.6 8.0 %collective-permute-done.3.refs_1_ = f32[2,136,128]{2,1,0:T(8,128)S(1)} collective-permute-done((f32[2,136,128]{2,1,0:T(8,128)S(1)}, f32[2,136,128]{2,1,0:T(8,128)S(1)}, u32[]{:S(2)}, u32[]{:S(2)}) %collective-permute-start.3) | collective-permute-done | bytes 139296 | tf_op jit(solution)/shard_map/ppermute | solution.py:477
  24.6 3.4 %collective-permute-start.4 = (f32[1,128,128]{2,1,0:T(8,128)S(1)}, f32[1,128,128]{2,1,0:T(8,128)S(1)}, u32[]{:S(2)}, u32[]{:S(2)}) collective-permute-start(f32[1,128,128]{2,1,0:T(8,128)S(1)} %get-tuple-element.74), channel_id=1, source_target_pairs={{0,8},{1,9},{2,10},{3,11},{4,12},{5,13},{6,14},{7,15},{8,0},{9,1},... | collective-permute-start | bytes 196616 | tf_op jit(solution)/shard_map/ppermute | solution.py:477
  28.0 0.1 collective-permute-start.9
  28.1 5.2 %collective-permute-done.9.refs_3_ = f32[1,112,128]{2,1,0:T(8,128)S(1)} collective-permute-done((f32[1,112,128]{2,1,0:T(8,128)S(1)}, f32[1,112,128]{2,1,0:T(8,128)S(1)}, u32[]{:S(2)}, u32[]{:S(2)}) %collective-permute-start.9) | collective-permute-done | bytes 57376 | tf_op jit(solution)/shard_map/ppermute | solution.py:477
  33.3 1.7 %collective-permute-start.10 = (f32[2,136,128]{2,1,0:T(8,128)S(1)}, f32[2,136,128]{2,1,0:T(8,128)S(1)}, u32[]{:S(2)}, u32[]{:S(2)}) collective-permute-start(f32[2,136,128]{2,1,0:T(8,128)S(1)} %get-tuple-element.88), channel_id=1, source_target_pairs={{0,2},{1,5},{2,0},{3,7},{4,6},{5,1},{6,4},{7,3},{8,10},{9,13},{10,... | collective-permute-start | bytes 417800 | tf_op jit(solution)/shard_map/ppermute | solution.py:477
  35.1 0.2 collective-permute-start.5
  35.3 3.2 %collective-permute-done.10.refs_1_ = f32[2,136,128]{2,1,0:T(8,128)S(1)} collective-permute-done((f32[2,136,128]{2,1,0:T(8,128)S(1)}, f32[2,136,128]{2,1,0:T(8,128)S(1)}, u32[]{:S(2)}, u32[]{:S(2)}) %collective-permute-start.10) | collective-permute-done | bytes 139296 | tf_op jit(solution)/shard_map/ppermute | solution.py:477
  38.5 1.4 %collective-permute-start.12 = (f32[1,136,128]{2,1,0:T(8,128)S(1)}, f32[1,136,128]{2,1,0:T(8,128)S(1)}, u32[]{:S(2)}, u32[]{:S(2)}) collective-permute-start(f32[1,136,128]{2,1,0:T(8,128)S(1)} %get-tuple-element.91), channel_id=1, source_target_pairs={{0,8},{1,9},{2,10},{3,11},{4,12},{5,13},{6,14},{7,15},{8,0},{9,1},... | collective-permute-start | bytes 208904 | tf_op jit(solution)/shard_map/ppermute | solution.py:477
  39.8 1.3 %collective-permute-done.5.refs_1_ = f32[2,136,128]{2,1,0:T(8,128)S(1)} collective-permute-done((f32[2,136,128]{2,1,0:T(8,128)S(1)}, f32[2,136,128]{2,1,0:T(8,128)S(1)}, u32[]{:S(2)}, u32[]{:S(2)}) %collective-permute-start.5) | collective-permute-done | bytes 139296 | tf_op jit(solution)/shard_map/ppermute | solution.py:477
  41.1 0.4 collective-permute-start.11
  41.5 0.3 shard_map.62
  41.8 1.9 %collective-permute-done.12.refs_3_ = f32[1,136,128]{2,1,0:T(8,128)S(1)} collective-permute-done((f32[1,136,128]{2,1,0:T(8,128)S(1)}, f32[1,136,128]{2,1,0:T(8,128)S(1)}, u32[]{:S(2)}, u32[]{:S(2)}) %collective-permute-start.12) | collective-permute-done | bytes 69664 | tf_op jit(solution)/shard_map/ppermute | solution.py:477
  43.7 3.4 %collective-permute-done.11.refs_2_ = f32[1,136,128]{2,1,0:T(8,128)S(1)} collective-permute-done((f32[1,136,128]{2,1,0:T(8,128)S(1)}, f32[1,136,128]{2,1,0:T(8,128)S(1)}, u32[]{:S(2)}, u32[]{:S(2)}) %collective-permute-start.11) | collective-permute-done | bytes 69664 | tf_op jit(solution)/shard_map/ppermute | solution.py:477
  47.1 1.1 %shard_map.63 = (f32[320,128]{1,0:T(8,128)}, f32[640,128]{1,0:T(8,128)}) custom-call(f32[1,136,128]{2,1,0:T(8,128)S(1)} %get-tuple-element.77.refs_0_, f32[1,136,128]{2,1,0:T(8,128)S(1)} %get-tuple-element.89.refs_1_, f32[1,136,128]{2,1,0:T(8,128)S(1)} %collective-permute-done.11.refs_2_, f32[1,136,128]{2,1,0:T(8,128)S(1)} %collective-permute-done.12.refs_3_, ...), custom_call_target="tpu_custom_call" | custom-call | tf_op jit(solution)/shard_map/pallas_call | solution.py:458
  (18 shorter events, 0.3 us)
Async XLA Ops:
  2.8 9.4 %collective-permute-start.6 = (f32[4,112,128]{2,1,0:T(8,128)S(1)}, f32[4,112,128]{2,1,0:T(8,128)S(1)}, u32[]{:S(2)}, u32[]{:S(2)}) collective-permute-start(f32[4,112,128]{2,1,0:T(8,128)S(1)} %get-tuple-element.80), channel_id=1, source_target_pairs={{0,4},{1,3},{2,6},{3,1},{4,0},{5,7},{6,2},{7,5},{8,12},{9,11},{10,... | collective-permute-start | bytes 688136 | tf_op jit(solution)/shard_map/ppermute | solution.py:477
  5.9 8.5 %collective-permute-start = (f32[4,128,128]{2,1,0:T(8,128)S(1)}, f32[4,128,128]{2,1,0:T(8,128)S(1)}, u32[]{:S(2)}, u32[]{:S(2)}) collective-permute-start(f32[4,128,128]{2,1,0:T(8,128)S(1)} %get-tuple-element.63), channel_id=1, source_target_pairs={{0,2},{1,5},{2,0},{3,7},{4,6},{5,1},{6,4},{7,3},{8,10},{9,13},{10,... | collective-permute-start | bytes 786440 | tf_op jit(solution)/shard_map/ppermute | solution.py:477
  12.2 2.2 %collective-permute-start.1 = (f32[2,128]{1,0:T(2,128)S(1)}, f32[2,128]{1,0:T(2,128)S(1)}, u32[]{:S(2)}, u32[]{:S(2)}) collective-permute-start(f32[2,128]{1,0:T(2,128)S(1)} %slice_bitcast_fusion), channel_id=1, source_target_pairs={{0,1},{1,0},{2,3},{3,2},{4,5},{5,4},{6,7},{7,6},{8,9},{9,8},{10,11... | collective-permute-start | bytes 3080 | tf_op jit(solution)/shard_map/ppermute | solution.py:477
  12.3 21.0 %collective-permute-start.7 = (f32[4,136,128]{2,1,0:T(8,128)S(1)}, f32[4,136,128]{2,1,0:T(8,128)S(1)}, u32[]{:S(2)}, u32[]{:S(2)}) collective-permute-start(f32[4,136,128]{2,1,0:T(8,128)S(1)} %get-tuple-element.82), channel_id=1, source_target_pairs={{0,4},{1,3},{2,6},{3,1},{4,0},{5,7},{6,2},{7,5},{8,12},{9,11},{10,... | collective-permute-start | bytes 835592 | tf_op jit(solution)/shard_map/ppermute | solution.py:477
  14.5 20.6 %collective-permute-start.2 = (f32[4,136,128]{2,1,0:T(8,128)S(1)}, f32[4,136,128]{2,1,0:T(8,128)S(1)}, u32[]{:S(2)}, u32[]{:S(2)}) collective-permute-start(f32[4,136,128]{2,1,0:T(8,128)S(1)} %get-tuple-element.71), channel_id=1, source_target_pairs={{0,2},{1,5},{2,0},{3,7},{4,6},{5,1},{6,4},{7,3},{8,10},{9,13},{10,... | collective-permute-start | bytes 835592 | tf_op jit(solution)/shard_map/ppermute | solution.py:477
  15.6 9.0 %collective-permute-start.3 = (f32[2,136,128]{2,1,0:T(8,128)S(1)}, f32[2,136,128]{2,1,0:T(8,128)S(1)}, u32[]{:S(2)}, u32[]{:S(2)}) collective-permute-start(f32[2,136,128]{2,1,0:T(8,128)S(1)} %get-tuple-element.73), channel_id=1, source_target_pairs={{0,4},{1,3},{2,6},{3,1},{4,0},{5,7},{6,2},{7,5},{8,12},{9,11},{10,... | collective-permute-start | bytes 417800 | tf_op jit(solution)/shard_map/ppermute | solution.py:477
  15.8 12.2 %collective-permute-start.8 = (f32[2,112,128]{2,1,0:T(8,128)S(1)}, f32[2,112,128]{2,1,0:T(8,128)S(1)}, u32[]{:S(2)}, u32[]{:S(2)}) collective-permute-start(f32[2,112,128]{2,1,0:T(8,128)S(1)} %get-tuple-element.85), channel_id=1, source_target_pairs={{0,2},{1,5},{2,0},{3,7},{4,6},{5,1},{6,4},{7,3},{8,10},{9,13},{10,... | collective-permute-start | bytes 344072 | tf_op jit(solution)/shard_map/ppermute | solution.py:477
  24.6 10.4 %collective-permute-start.4 = (f32[1,128,128]{2,1,0:T(8,128)S(1)}, f32[1,128,128]{2,1,0:T(8,128)S(1)}, u32[]{:S(2)}, u32[]{:S(2)}) collective-permute-start(f32[1,128,128]{2,1,0:T(8,128)S(1)} %get-tuple-element.74), channel_id=1, source_target_pairs={{0,8},{1,9},{2,10},{3,11},{4,12},{5,13},{6,14},{7,15},{8,0},{9,1},... | collective-permute-start | bytes 196616 | tf_op jit(solution)/shard_map/ppermute | solution.py:477
  28.0 5.2 %collective-permute-start.9 = (f32[1,112,128]{2,1,0:T(8,128)S(1)}, f32[1,112,128]{2,1,0:T(8,128)S(1)}, u32[]{:S(2)}, u32[]{:S(2)}) collective-permute-start(f32[1,112,128]{2,1,0:T(8,128)S(1)} %get-tuple-element.86), channel_id=1, source_target_pairs={{0,8},{1,9},{2,10},{3,11},{4,12},{5,13},{6,14},{7,15},{8,0},{9,1},... | collective-permute-start | bytes 172040 | tf_op jit(solution)/shard_map/ppermute | solution.py:477
  33.3 5.1 %collective-permute-start.10 = (f32[2,136,128]{2,1,0:T(8,128)S(1)}, f32[2,136,128]{2,1,0:T(8,128)S(1)}, u32[]{:S(2)}, u32[]{:S(2)}) collective-permute-start(f32[2,136,128]{2,1,0:T(8,128)S(1)} %get-tuple-element.88), channel_id=1, source_target_pairs={{0,2},{1,5},{2,0},{3,7},{4,6},{5,1},{6,4},{7,3},{8,10},{9,13},{10,... | collective-permute-start | bytes 417800 | tf_op jit(solution)/shard_map/ppermute | solution.py:477
  35.1 6.0 %collective-permute-start.5 = (f32[2,136,128]{2,1,0:T(8,128)S(1)}, f32[2,136,128]{2,1,0:T(8,128)S(1)}, u32[]{:S(2)}, u32[]{:S(2)}) collective-permute-start(f32[2,136,128]{2,1,0:T(8,128)S(1)} %get-tuple-element.76), channel_id=1, source_target_pairs={{0,4},{1,3},{2,6},{3,1},{4,0},{5,7},{6,2},{7,5},{8,12},{9,11},{10,... | collective-permute-start | bytes 417800 | tf_op jit(solution)/shard_map/ppermute | solution.py:477
  38.5 5.3 %collective-permute-start.12 = (f32[1,136,128]{2,1,0:T(8,128)S(1)}, f32[1,136,128]{2,1,0:T(8,128)S(1)}, u32[]{:S(2)}, u32[]{:S(2)}) collective-permute-start(f32[1,136,128]{2,1,0:T(8,128)S(1)} %get-tuple-element.91), channel_id=1, source_target_pairs={{0,8},{1,9},{2,10},{3,11},{4,12},{5,13},{6,14},{7,15},{8,0},{9,1},... | collective-permute-start | bytes 208904 | tf_op jit(solution)/shard_map/ppermute | solution.py:477
  41.1 6.0 %collective-permute-start.11 = (f32[1,136,128]{2,1,0:T(8,128)S(1)}, f32[1,136,128]{2,1,0:T(8,128)S(1)}, u32[]{:S(2)}, u32[]{:S(2)}) collective-permute-start(f32[1,136,128]{2,1,0:T(8,128)S(1)} %get-tuple-element.90), channel_id=1, source_target_pairs={{0,8},{1,9},{2,10},{3,11},{4,12},{5,13},{6,14},{7,15},{8,0},{9,1},... | collective-permute-start | bytes 208904 | tf_op jit(solution)/shard_map/ppermute | solution.py:477

commit v10 on v6

--- a/solution.py
+++ b/solution.py
@@ -62,6 +62,8 @@
 KINDS = (((X, NEAR, FAR), (NEAR, X, FAR)), ((NEAR, X, FAR), (X, NEAR, FAR)))
 NOTES = len(KINDS) * SLOTS
 
+WEIGHTS = {((0, 2), 2): 2 * 10**9}
+
 
 def split_rows(count):
     return count // B, (count % B) // H
@@ -99,43 +101,38 @@
     return pl.ds(start if isinstance(start, int) else pl.multiple_of(start, B), size)
 
 
+LOADS = 4
+
+
 def pack_body(pieces, items, count_a, count_g, fresh, *refs):
-    a_hbm, pre_hbm, grad_hbm = refs[:3]
-    notes_in = None if fresh else refs[3]
-    refs = refs[3 if fresh else 4 :]
     n = len(items)
-    outs, notes = refs[:n], refs[n]
-    buffers, sems = refs[n + 1 : 5 * n + 1], refs[5 * n + 1]
+    if fresh:
+        arrays, outs, (notes, *held), sems = refs[:3], refs[3 : 3 + n], refs[3 + n : -1], refs[-1]
+    else:
+        notes_in, held, outs, notes = refs[0], refs[1:4], refs[4 : 4 + n], refs[-1]
     full, half = split_rows(count_a)
     slots = SLOTS // 2
 
-    def copies(i, slot):
-        k, first = items[i]
-        a_blocks, a_half, g_blocks, kind = pieces[k]
-        a_buf, half_buf, pre_buf, grad_buf = buffers[4 * i : 4 * i + 4]
-        owner = slot_owner(first + slot, KINDS[kind])
-        odd = owner & half
-        base = (owner >> half) * (full * (1 + half) + half) * B
-        moves = []
-        if a_blocks:
-            start = base + odd * (full + 1) * B + a_blocks[0] * B
-            moves.append((a_hbm, start, a_buf))
-        if a_half:
-            moves.append((a_hbm, base + full * B, half_buf))
-        if g_blocks:
-            start = owner * count_g + g_blocks[0] * B
-            moves += [(pre_hbm, start, pre_buf), (grad_hbm, start, grad_buf)]
+    def copies(i):
+        rows = arrays[i].shape[0] // LOADS
+        parts = [slice(part * rows, (part + 1) * rows) for part in range(LOADS)]
         return [
-            pltpu.make_async_copy(
-                src.at[:, lanes(start, dst.shape[2])], dst.at[slot], sems.at[i, slot, m]
-            )
-            for m, (src, start, dst) in enumerate(moves)
+            pltpu.make_async_copy(arrays[i].at[part], held[i].at[part], sems.at[i, part_no])
+            for part_no, part in enumerate(parts)
         ]
 
-    for i in range(n):
-        for slot in range(slots):
-            for copy in copies(i, slot):
-                copy.start()
+    waiting = [0, 1, 2] if fresh else []
+    for i in waiting:
+        for copy in copies(i):
+            copy.start()
+
+    def arrive(upto):
+        while waiting and waiting[0] <= upto:
+            for copy in copies(waiting.pop(0)):
+                copy.wait()
+
+    def read(i, start):
+        return held[i][:, pl.ds(pl.multiple_of(start, B), B)]
 
     row, col = iotas(H)
     low = col < row
@@ -176,38 +173,51 @@
         rest = jnp.where(col[: quarter // 2] < H, pltpu.roll(rest[1], H, 1), rest[0])
         return square, rest
 
-    for i, (k, first) in enumerate(items):
-        a_blocks, a_half, g_blocks, kind = pieces[k]
-        a_buf, half_buf, pre_buf, grad_buf = buffers[4 * i : 4 * i + 4]
-        out = outs[i]
+    def a_parts(out, k, first, slot, index):
+        a_blocks, a_half, _, kind = pieces[k]
+        owner = slot_owner(first + slot, KINDS[kind])
+        here, odd = kind * SLOTS + first + slot, owner & half
+        base = (owner >> half) * (full * (1 + half) + half) * B
+        at = 0
+        for b in a_blocks:
+            block = cov(read(0, base + (odd * (full + 1) + b) * B))
+            out[slot, at : at + H, :] = fold(block, here, next(index), 0)
+            at = at + H
+        if a_half:
+            block = cov(read(0, base + full * B))
+            square, rest = fold_half(block, odd, here, next(index))
+            out[slot, at : at + quarter, :] = square
+            out[slot, at + quarter : at + quarter * 3 // 2, :] = rest
+            at = at + quarter * 3 // 2
+        return at
+
+    def g_parts(out, k, first, slot, index, at):
+        _, _, g_blocks, kind = pieces[k]
+        owner = slot_owner(first + slot, KINDS[kind])
+        here = kind * SLOTS + first + slot
+        for b in g_blocks:
+            start = owner * count_g + b * B
+            value = read(1, start).astype(jnp.float32)
+            grad = read(2, start).astype(jnp.float32)
+            block = cov((grad * gelu_slope(value)).astype(jnp.bfloat16))
+            out[slot, at : at + H, :] = fold(block, here, next(index), 1)
+            at = at + H
+        return at
+
+    arrive(0)
+    begun = []
+    for out, (k, first) in zip(outs, items):
         for slot in range(slots):
-            for copy in copies(i, slot):
-                copy.wait()
-        for slot in range(slots):
-            here = kind * SLOTS + first + slot
+            here = pieces[k][3] * SLOTS + first + slot
             if here not in tiles:
                 tiles[here] = jnp.zeros((EDGE, B), jnp.float32) if fresh else notes_in[here]
             index = corner_indices(pieces, k)
-            at = 0
-            for b in range(len(a_blocks)):
-                block = cov(a_buf[slot, :, b * B : (b + 1) * B])
-                out[slot, at : at + H, :] = fold(block, here, next(index), 0)
-                at = at + H
-            if a_half:
-                odd = slot_owner(first + slot, KINDS[kind]) & 1
-                square, rest = fold_half(cov(half_buf[slot]), odd, here, next(index))
-                out[slot, at : at + quarter, :] = square
-                out[slot, at + quarter : at + quarter * 3 // 2, :] = rest
-                at = at + quarter * 3 // 2
-            for b in range(len(g_blocks)):
-                part = slice(b * B, (b + 1) * B)
-                value = pre_buf[slot, :, part].astype(jnp.float32)
-                grad = grad_buf[slot, :, part].astype(jnp.float32)
-                block = cov((grad * gelu_slope(value)).astype(jnp.bfloat16))
-                out[slot, at : at + H, :] = fold(block, here, next(index), 1)
-                at = at + H
-            if has_edge(pieces, k):
-                out[slot, at:, :] = tiles[here]
+            begun.append((out, k, first, slot, index, a_parts(out, k, first, slot, index)))
+    arrive(2)
+    for out, k, first, slot, index, at in begun:
+        at = g_parts(out, k, first, slot, index, at)
+        if has_edge(pieces, k):
+            out[slot, at:, :] = tiles[pieces[k][3] * SLOTS + first + slot]
 
     for slot in range(NOTES):
         if slot in tiles:
@@ -220,60 +230,70 @@
 
 
 def pack(arrays, pieces, items, count_a, count_g, notes):
-    tokens, dtype = arrays[0].shape[0], arrays[0].dtype
-    slots = SLOTS // 2
-    scratch = []
-    for k, _ in items:
-        a_blocks, _, g_blocks, _ = pieces[k]
-        for size in (len(a_blocks), 1, len(g_blocks), len(g_blocks)):
-            scratch.append(pltpu.VMEM((slots, tokens, max(size, 1) * B), dtype))
     fresh = notes is None
-    *chunks, notes = pl.pallas_call(
+    out_shape = [
+        jax.ShapeDtypeStruct((SLOTS // 2, piece_rows(pieces, k), B), jnp.float32)
+        for k, _ in items
+    ]
+    out_shape.append(jax.ShapeDtypeStruct((NOTES + 1, EDGE, B), jnp.float32))
+    if fresh:
+        out_shape += [jax.ShapeDtypeStruct(array.shape, array.dtype) for array in arrays]
+    args = arrays if fresh else (notes, *arrays)
+    space = pltpu.HBM if fresh else pltpu.VMEM
+    outs = pl.pallas_call(
         functools.partial(pack_body, pieces, items, count_a, count_g, fresh),
-        in_specs=[pl.BlockSpec(memory_space=pltpu.HBM)] * 3
-        + [pl.BlockSpec(memory_space=pltpu.VMEM)] * (not fresh),
-        out_specs=[pl.BlockSpec(memory_space=pltpu.VMEM)] * (len(items) + 1),
-        out_shape=[
-            jax.ShapeDtypeStruct((slots, piece_rows(pieces, k), B), jnp.float32)
-            for k, _ in items
-        ]
-        + [jax.ShapeDtypeStruct((NOTES + 1, EDGE, B), jnp.float32)],
-        scratch_shapes=scratch + [pltpu.SemaphoreType.DMA((len(items), slots, 4))],
-        compiler_params=pltpu.CompilerParams(vmem_limit_bytes=32 * 2**20),
-        cost_estimate=pl.CostEstimate(flops=1, bytes_accessed=1, transcendentals=0),
-    )(*arrays, *([] if fresh else [notes]))
-    return chunks, notes
-
-
-def halve_body(traced, n, *refs):
-    keeps, gots, refs = refs[:n], refs[n : 2 * n], refs[2 * n :]
-    traces, outs = refs[:-2 * n], refs[-2 * n :]
-    for k in range(n):
-        half = keeps[k].shape[0] // 2
-        for part in range(2):
-            here = slice(part * half, (part + 1) * half)
-            outs[2 * k + part][...] = keeps[k][here] + gots[k][here]
-    if traced:
-        value = sum((trace[...] for trace in traces[1:]), traces[0][...])
-        if len(traces) > 1:
-            value = value + sum(got[0, -2:, :] for got in gots)
-        for out in outs:
-            out[0, -2:, :] = value
-
-
-def halve(keeps, gots, traces=()):
-    n = len(keeps)
-    args = (*keeps, *gots, *traces)
-    shapes = [(keep.shape[0] // 2, *keep.shape[1:]) for keep in keeps for _ in range(2)]
-    outs = pl.pallas_call(
-        functools.partial(halve_body, bool(traces), n),
-        in_specs=[pl.BlockSpec(memory_space=pltpu.VMEM)] * len(args),
-        out_specs=[pl.BlockSpec(memory_space=pltpu.VMEM)] * (2 * n),
-        out_shape=[jax.ShapeDtypeStruct(shape, jnp.float32) for shape in shapes],
+        in_specs=[pl.BlockSpec(memory_space=space)] * len(args),
+        out_specs=[pl.BlockSpec(memory_space=pltpu.VMEM)] * len(out_shape),
+        out_shape=out_shape,
+        scratch_shapes=[pltpu.SemaphoreType.DMA((len(arrays), LOADS))] * fresh,
         compiler_params=pltpu.CompilerParams(vmem_limit_bytes=32 * 2**20),
         cost_estimate=pl.CostEstimate(flops=1, bytes_accessed=1, transcendentals=0),
     )(*args)
-    return outs[0::2], outs[1::2]
+    n = len(items)
+    return outs[:n], outs[n], outs[n + 1 :]
+
+
+def halve_body(n, terms, came, put, merged, *refs):
+    keeps, gots, refs = refs[:n], refs[n : 2 * n], refs[2 * n :]
+    terms, kept, refs = refs[:terms], refs[terms : terms + n], refs[terms + n :]
+    sent, sums = (refs[:1], refs[1:]) if merged else (refs[:n], refs[n:])
+    if merged:
+        ends = [sum(ref.shape[1] for ref in kept[: k + 1]) for k in range(n)]
+        sent = [
+            sent[0].at[:, end - ref.shape[1] : end, :] for end, ref in zip(ends, kept)
+        ]
+    for k in range(n):
+        half = kept[k].shape[0]
+        kept[k][...] = keeps[k][:half] + gots[k][:half]
+        sent[k][...] = keeps[k][half:] + gots[k][half:]
+    if terms:
+        value = sum((term[...] for term in terms[1:]), terms[0][...])
+        for k in came:
+            value = value + gots[k][0, -2:, :]
+        for out in sums:
+            out[...] = value
+        for k in put:
+            rows = kept[k].shape[1]
+            kept[k][0, rows - 2 :, :] = value
+            sent[k][0, rows - 2 :, :] = value
+
+
+def halve(keeps, gots, terms=(), came=(), put=(), merged=False, weight=1):
+    n = len(keeps)
+    emit = bool(terms) and not put
+    args = [*keeps, *gots, *terms]
+    kept = [(keep.shape[0] // 2, *keep.shape[1:]) for keep in keeps]
+    sent = [(kept[0][0], sum(shape[1] for shape in kept), B)] if merged else kept
+    shapes = [*kept, *sent, *([(2, B)] * emit)]
+    outs = pl.pallas_call(
+        functools.partial(halve_body, n, len(terms), came, put, merged),
+        in_specs=[pl.BlockSpec(memory_space=pltpu.VMEM)] * len(args),
+        out_specs=[pl.BlockSpec(memory_space=pltpu.VMEM)] * len(shapes),
+        out_shape=[jax.ShapeDtypeStruct(shape, jnp.float32) for shape in shapes],
+        compiler_params=pltpu.CompilerParams(vmem_limit_bytes=32 * 2**20),
+        cost_estimate=pl.CostEstimate(flops=weight, bytes_accessed=1, transcendentals=0),
+    )(*args)
+    return outs[:n], outs[n : n + len(sent)], outs[n + len(sent) :]
 
 
 def mean_of(value, total):
@@ -319,15 +339,22 @@
             yield k, 1, b * B, H, next(index)
 
 
-def unfold_body(pieces, ks, count_a, total, owns, gots, outs):
+def row_begins(pieces, ks):
+    rows = [piece_rows(pieces, k) for k in ks]
+    return {k: sum(rows[:i]) for i, k in enumerate(ks)}
+
+
+def unfold_body(pieces, ks, count_a, total, owns, got, outs):
     odd = lax.axis_index("dp") & 1
     at = dict.fromkeys(ks, 0)
+    begins = row_begins(pieces, ks)
 
     def take(k, rows):
-        i = ks.index(k)
-        at[k] = at[k] + rows
-        part = slice(at[k] - rows, at[k])
-        return mean_of(owns[i][0, part, :] + gots[i][0, part, :], total)
+        begin = at[k]
+        at[k] = begin + rows
+        mine = owns[ks.index(k)][0, begin : begin + rows, :]
+        begin = begin + begins[k]
+        return mean_of(mine + got[0, begin : begin + rows, :], total)
 
     for k, which, start, rows, _ in places(pieces, ks, count_a):
         def put(offset, value):
@@ -341,22 +368,23 @@
 
 def early_body(pieces, ks, count_a, total, *refs):
     n = len(ks)
-    unfold_body(pieces, ks, count_a, total, refs[:n], refs[n : 2 * n], refs[2 * n :])
+    unfold_body(pieces, ks, count_a, total, refs[:n], refs[n], refs[n + 1 :])
 
 
 def finish_body(pieces, early, late, count_a, total, *refs):
     n = len(late)
-    owns, gots, (early_a, early_g, a_ref, g_ref) = refs[:n], refs[n : 2 * n], refs[2 * n :]
+    owns, got, (early_a, early_g, a_ref, g_ref) = refs[:n], refs[n], refs[n + 1 :]
     outs = (a_ref, g_ref)
     full, half = split_rows(count_a)
     odd = lax.axis_index("dp") & half
     row, col = iotas(H)
 
-    unfold_body(pieces, late, count_a, total, owns, gots, outs)
+    unfold_body(pieces, late, count_a, total, owns, got, outs)
 
     edges = {}
-    for i, k in enumerate(late):
-        edge = mean_of(owns[i][0, -EDGE:, :] + gots[i][0, -EDGE:, :], total)
+    for k, own in zip(late, owns):
+        end = row_begins(pieces, late)[k] + piece_rows(pieces, k)
+        edge = mean_of(own[0, -EDGE:, :] + got[0, end - EDGE : end, :], total)
         edges[pieces[k][3]] = (edge, pltpu.roll(edge, H, 1))
     sums = jnp.sum(edge[-2:], axis=1, keepdims=True)
     ratio = jnp.sqrt(sums[0:1] / D / (sums[1:2] / FFW))
@@ -385,8 +413,8 @@
                 out[here, :] = jnp.where(last, line, value)
 
 
-def unfold_early(pieces, ks, owns, gots, count_a, count_g, total):
-    args = (*owns, *gots)
+def unfold_early(pieces, ks, owns, got, count_a, count_g, total):
+    args = (*owns, got)
     return pl.pallas_call(
         functools.partial(early_body, pieces, ks, count_a, total),
         in_specs=[pl.BlockSpec(memory_space=pltpu.VMEM)] * len(args),
@@ -400,8 +428,8 @@
     )(*args)
 
 
-def finish(pieces, early, late, owns, gots, first, count_a, count_g, total):
-    args = (*owns, *gots, *first)
+def finish(pieces, early, late, owns, got, first, count_a, count_g, total):
+    args = (*owns, got, *first)
     return pl.pallas_call(
         functools.partial(finish_body, pieces, early, late, count_a, total),
         in_specs=[pl.BlockSpec(memory_space=pltpu.VMEM)] * len(args),
@@ -449,29 +477,45 @@
     keep, send = 0, SLOTS // 2
     early, late = (0, 2), (1, 3)
     keeps, gots, notes = {}, {}, None
-    for first, ks in ((send, early), (send, late), (keep, early + late)):
+
+    def pack_next(first, ks):
+        nonlocal notes, arrays
         items = tuple((k, first) for k in ks)
-        parts, notes = pack(arrays, pieces, items, count_a, count_g, notes)
-        for k, part in zip(ks, parts):
-            if first == send:
-                gots[k] = swap(part, along(0, pieces[k][3]))
-            else:
-                keeps[k] = part
+        parts, notes, held = pack(arrays, pieces, items, count_a, count_g, notes)
+        arrays = held or arrays
+        return dict(zip(ks, parts))
+
+    def exchange(parts, stage):
+        for k, part in parts.items():
+            gots[k] = swap(part, along(stage, pieces[k][3]))
+
+    def halve_pair(ks, stage, **kinds):
+        own, parts, others = halve(
+            [keeps[k] for k in ks], [gots[k] for k in ks], merged=stage == 2,
+            weight=WEIGHTS.get((ks, stage), 1), **kinds
+        )
+        keeps.update(zip(ks, own))
+        if stage == 2:
+            gots[ks] = swap(parts[0], lambda i, j: (i ^ (1 << FAR), j))
+        else:
+            exchange(dict(zip(ks, parts)), stage)
+        return others
+
+    exchange(pack_next(send, early), 0)
+    exchange(pack_next(send, late), 0)
+    keeps.update(pack_next(keep, early))
+    keeps.update(pack_next(keep, late))
 
     trace = notes[NOTES, :2, :]
     trace = trace + swap(trace, lambda i, j: (i, j ^ 1))
     across = swap(trace, lambda i, j: (i ^ (1 << X) ^ (1 << NEAR), j))
-    traces = {early: ((), ()), late: ((trace,), (trace, across))}
-    for stage in (1, 2):
-        for ks in (early, late):
-            own, parts = halve(
-                [keeps[k] for k in ks], [gots[k] for k in ks], traces[ks][stage - 1]
-            )
-            for k, mine, part in zip(ks, own, parts):
-                keeps[k], gots[k] = mine, swap(part, along(stage, pieces[k][3]))
+    halve_pair(early, 1)
+    halve_pair(late, 1, terms=(trace,), put=(0, 1))
+    (trace,) = halve_pair(early, 2, terms=(trace, across))
+    halve_pair(late, 2, terms=(trace,), came=(0, 1), put=(0, 1))
 
     def both(ks):
-        return [keeps[k] for k in ks], [gots[k] for k in ks]
+        return [keeps[k] for k in ks], gots[ks]
 
     first = unfold_early(pieces, early, *both(early), count_a, count_g, total)
     a_factor, g_factor = finish(

time: 39.3 us -> 38.7 us (0.985)
  waiting for transfers between devices: 10 us -> 13.7 us
  Pallas kernels: 9.48 us -> 6.19 us
  starting transfers between devices: 18.8 us -> 18 us
    ppermute x14 -> x12, waiting for transfers between devices: 10 us -> 13.7 us  [swap(): return lax.ppermute(value, ('dp', 'tensor'), pairs)]
    pallas_call x3 -> x4, Pallas kernels: 7.92 us -> 4.61 us  [pack(): pl.pallas_call(functools.partial(pack_body, pieces, items, count_a, count...]
    ppermute x14 -> x12, starting transfers between devices: 18.8 us -> 18 us  [swap(): return lax.ppermute(value, ('dp', 'tensor'), pairs)]
  transfers between devices with their start and end apart: 14 -> 12, of which waited for: 4 -> 6; matrix products, arithmetic and copies ran while one was open for 0% -> 0% of each run, Pallas kernels for 16% -> 7%
where the time goes in v10:
time: 38.7 us; the launch traced here: 38.6 us
  starting transfers between devices  18 us (47%)
  waiting for transfers between devices  13.7 us (35%)
  Pallas kernels  6.19 us (16%)
  between operations  0.71 us (2%)
    ppermute x12, starting transfers between devices, swap(): return lax.ppermute(value, ('dp', 'tensor'), pairs)  18 us
    ppermute x12, waiting for transfers between devices, swap(): return lax.ppermute(value, ('dp', 'tensor'), pairs)  13.7 us
    pallas_call x4, Pallas kernels, pack(): pl.pallas_call(functools.partial(pack_body, pieces, items, count_a, count...  4.61 us
    pallas_call x1, Pallas kernels, finish(): pl.pallas_call(functools.partial(finish_body, pieces, early, late, count_...  1.1 us
  transfers between devices with their start and end apart: 12, of which 6 were waited for; matrix products, arithmetic and copies ran while one was open for 0% of the time, Pallas kernels for 7%

profile of v10, /device:TPU:0, one launch (start us, length us, event | category | flops | bytes accessed | tf_op | source)
XLA Modules:
  0.0 38.6 jit_solution(11047436564210918862)
XLA Ops:
  0.6 2.5 %shard_map.50 = (f32[4,128,128]{2,1,0:T(8,128)S(1)}, f32[4,112,128]{2,1,0:T(8,128)S(1)}, f32[17,8,128]{2,1,0:T(8,128)S(1)}, bf16[128,2560]{1,0:T(8,128)(2,1)S(1)...) custom-call(bf16[128,2560]{1,0:T(8,128)(2,1)} %refs_0_.1, bf16[128,5120]{1,0:T(8,128)(2,1)} %refs_1_.1, ...), custom_call_target="tpu_custom_call" | custom-call | flops 1 | bytes 1 | tf_op jit(solution)/shard_map/pallas_call | solution.py:243
  3.1 3.0 %collective-permute-start.5 = (f32[4,128,128]{2,1,0:T(8,128)S(1)}, f32[4,128,128]{2,1,0:T(8,128)S(1)}, u32[]{:S(2)}, u32[]{:S(2)}) collective-permute-start(f32[4,128,128]{2,1,0:T(8,128)S(1)} %get-tuple-element.53), channel_id=1, source_target_pairs={{0,2},{1,5},{2,0},{3,7},{4,6},{5,1},{6,4},{7,3},{8,10},{9,13},{10,... | collective-permute-start | bytes 786440 | tf_op jit(solution)/shard_map/ppermute | solution.py:452
  6.1 1.6 %collective-permute-start.6 = (f32[4,112,128]{2,1,0:T(8,128)S(1)}, f32[4,112,128]{2,1,0:T(8,128)S(1)}, u32[]{:S(2)}, u32[]{:S(2)}) collective-permute-start(f32[4,112,128]{2,1,0:T(8,128)S(1)} %get-tuple-element.54), channel_id=1, source_target_pairs={{0,4},{1,3},{2,6},{3,1},{4,0},{5,7},{6,2},{7,5},{8,12},{9,11},{10,... | collective-permute-start | bytes 688136 | tf_op jit(solution)/shard_map/ppermute | solution.py:452
  7.7 0.8 %shard_map.51 = (f32[4,136,128]{2,1,0:T(8,128)S(1)}, f32[4,136,128]{2,1,0:T(8,128)S(1)}, f32[17,8,128]{2,1,0:T(8,128)S(1)}) custom-call(f32[17,8,128]{2,1,0:T(8,128)S(1)} %get-tuple-element.36.refs_0_, bf16[128,2560]{1,0:T(8,128)(2,1)S(1)} %get-tuple-element.37.refs_1_, bf16[128,5120]{1,0:T(8,128)(2,1)S(1)} %get-tuple-element.38.refs_2_, ...), custom_call_target="tpu_custom_call" | custom-call | flops 1 | bytes 1 | tf_op jit(solution)/shard_map/pallas_call | solution.py:243
  8.5 0.6 %collective-permute-start = (f32[4,136,128]{2,1,0:T(8,128)S(1)}, f32[4,136,128]{2,1,0:T(8,128)S(1)}, u32[]{:S(2)}, u32[]{:S(2)}) collective-permute-start(f32[4,136,128]{2,1,0:T(8,128)S(1)} %get-tuple-element.44), channel_id=1, source_target_pairs={{0,2},{1,5},{2,0},{3,7},{4,6},{5,1},{6,4},{7,3},{8,10},{9,13},{10,... | collective-permute-start | bytes 835592 | tf_op jit(solution)/shard_map/ppermute | solution.py:452
  9.1 0.5 %shard_map.52 = (f32[4,128,128]{2,1,0:T(8,128)S(1)}, f32[4,112,128]{2,1,0:T(8,128)S(1)}, f32[17,8,128]{2,1,0:T(8,128)S(1)}) custom-call(f32[17,8,128]{2,1,0:T(8,128)S(1)} %get-tuple-element.40.refs_0_, bf16[128,2560]{1,0:T(8,128)(2,1)S(1)} %get-tuple-element.37.refs_1_, bf16[128,5120]{1,0:T(8,128)(2,1)S(1)} %get-tuple-element.38.refs_2_, ...), custom_call_target="tpu_custom_call" | custom-call | flops 1 | bytes 1 | tf_op jit(solution)/shard_map/pallas_call | solution.py:243
  9.6 0.8 %shard_map.53 = (f32[4,136,128]{2,1,0:T(8,128)S(1)}, f32[4,136,128]{2,1,0:T(8,128)S(1)}, f32[17,8,128]{2,1,0:T(8,128)S(1)}) custom-call(f32[17,8,128]{2,1,0:T(8,128)S(1)} %get-tuple-element.41.refs_0_, bf16[128,2560]{1,0:T(8,128)(2,1)S(1)} %get-tuple-element.37.refs_1_, bf16[128,5120]{1,0:T(8,128)(2,1)S(1)} %get-tuple-element.38.refs_2_, ...), custom_call_target="tpu_custom_call" | custom-call | flops 1 | bytes 1 | tf_op jit(solution)/shard_map/pallas_call | solution.py:243
  10.5 0.1 collective-permute-start.2
  10.5 3.4 %collective-permute-done.6.refs_3_ = f32[4,112,128]{2,1,0:T(8,128)S(1)} collective-permute-done((f32[4,112,128]{2,1,0:T(8,128)S(1)}, f32[4,112,128]{2,1,0:T(8,128)S(1)}, u32[]{:S(2)}, u32[]{:S(2)}) %collective-permute-start.6) | collective-permute-done | bytes 229408 | tf_op jit(solution)/shard_map/ppermute | solution.py:452
  14.0 0.1 shard_map.55
  14.0 2.4 %collective-permute-start.7 = (f32[2,128,128]{2,1,0:T(8,128)S(1)}, f32[2,128,128]{2,1,0:T(8,128)S(1)}, u32[]{:S(2)}, u32[]{:S(2)}) collective-permute-start(f32[2,128,128]{2,1,0:T(8,128)S(1)} %get-tuple-element.57), channel_id=1, source_target_pairs={{0,4},{1,3},{2,6},{3,1},{4,0},{5,7},{6,2},{7,5},{8,12},{9,11},{10,... | collective-permute-start | bytes 393224 | tf_op jit(solution)/shard_map/ppermute | solution.py:452
  16.4 0.6 %collective-permute-start.8 = (f32[2,112,128]{2,1,0:T(8,128)S(1)}, f32[2,112,128]{2,1,0:T(8,128)S(1)}, u32[]{:S(2)}, u32[]{:S(2)}) collective-permute-start(f32[2,112,128]{2,1,0:T(8,128)S(1)} %get-tuple-element.58), channel_id=1, source_target_pairs={{0,2},{1,5},{2,0},{3,7},{4,6},{5,1},{6,4},{7,3},{8,10},{9,13},{10,... | collective-permute-start | bytes 344072 | tf_op jit(solution)/shard_map/ppermute | solution.py:452
  17.0 0.9 %collective-permute-start.9 = (f32[2,128]{1,0:T(2,128)S(1)}, f32[2,128]{1,0:T(2,128)S(1)}, u32[]{:S(2)}, u32[]{:S(2)}) collective-permute-start(f32[2,128]{1,0:T(2,128)S(1)} %fusion.refs_4_), channel_id=1, source_target_pairs={{0,6},{1,7},{2,4},{3,5},{4,2},{5,3},{6,0},{7,1},{8,14},{9,15},{10,... | collective-permute-start | bytes 3080 | tf_op jit(solution)/shard_map/ppermute | solution.py:452
  17.9 0.7 %collective-permute-done.refs_2_ = f32[4,136,128]{2,1,0:T(8,128)S(1)} collective-permute-done((f32[4,136,128]{2,1,0:T(8,128)S(1)}, f32[4,136,128]{2,1,0:T(8,128)S(1)}, u32[]{:S(2)}, u32[]{:S(2)}) %collective-permute-start) | collective-permute-done | bytes 278560 | tf_op jit(solution)/shard_map/ppermute | solution.py:452
  18.6 0.2 collective-permute-done.1.refs_3_
  18.9 2.6 %collective-permute-start.3 = (f32[2,136,128]{2,1,0:T(8,128)S(1)}, f32[2,136,128]{2,1,0:T(8,128)S(1)}, u32[]{:S(2)}, u32[]{:S(2)}) collective-permute-start(f32[2,136,128]{2,1,0:T(8,128)S(1)} %get-tuple-element.49), channel_id=1, source_target_pairs={{0,4},{1,3},{2,6},{3,1},{4,0},{5,7},{6,2},{7,5},{8,12},{9,11},{10,... | collective-permute-start | bytes 417800 | tf_op jit(solution)/shard_map/ppermute | solution.py:452
  21.5 1.5 %collective-permute-start.4 = (f32[2,136,128]{2,1,0:T(8,128)S(1)}, f32[2,136,128]{2,1,0:T(8,128)S(1)}, u32[]{:S(2)}, u32[]{:S(2)}) collective-permute-start(f32[2,136,128]{2,1,0:T(8,128)S(1)} %get-tuple-element.50), channel_id=1, source_target_pairs={{0,2},{1,5},{2,0},{3,7},{4,6},{5,1},{6,4},{7,3},{8,10},{9,13},{10,... | collective-permute-start | bytes 417800 | tf_op jit(solution)/shard_map/ppermute | solution.py:452
  23.1 2.7 %collective-permute-start.11 = (f32[1,240,128]{2,1,0:T(8,128)S(1)}, f32[1,240,128]{2,1,0:T(8,128)S(1)}, u32[]{:S(2)}, u32[]{:S(2)}) collective-permute-start(f32[1,240,128]{2,1,0:T(8,128)S(1)} %get-tuple-element.65), channel_id=1, source_target_pairs={{0,8},{1,9},{2,10},{3,11},{4,12},{5,13},{6,14},{7,15},{8,0},{9,1},... | collective-permute-start | bytes 368648 | tf_op jit(solution)/shard_map/ppermute | solution.py:452
  25.7 1.4 %collective-permute-done.3.refs_2_ = f32[2,136,128]{2,1,0:T(8,128)S(1)} collective-permute-done((f32[2,136,128]{2,1,0:T(8,128)S(1)}, f32[2,136,128]{2,1,0:T(8,128)S(1)}, u32[]{:S(2)}, u32[]{:S(2)}) %collective-permute-start.3) | collective-permute-done | bytes 139296 | tf_op jit(solution)/shard_map/ppermute | solution.py:452
  27.1 2.1 %collective-permute-start.10 = (f32[1,272,128]{2,1,0:T(8,128)S(1)}, f32[1,272,128]{2,1,0:T(8,128)S(1)}, u32[]{:S(2)}, u32[]{:S(2)}) collective-permute-start(f32[1,272,128]{2,1,0:T(8,128)S(1)} %get-tuple-element.62), channel_id=1, source_target_pairs={{0,8},{1,9},{2,10},{3,11},{4,12},{5,13},{6,14},{7,15},{8,0},{9,1},... | collective-permute-start | bytes 417800 | tf_op jit(solution)/shard_map/ppermute | solution.py:452
  29.2 5.7 %collective-permute-done.11.refs_2_ = f32[1,240,128]{2,1,0:T(8,128)S(1)} collective-permute-done((f32[1,240,128]{2,1,0:T(8,128)S(1)}, f32[1,240,128]{2,1,0:T(8,128)S(1)}, u32[]{:S(2)}, u32[]{:S(2)}) %collective-permute-start.11) | collective-permute-done | bytes 122912 | tf_op jit(solution)/shard_map/ppermute | solution.py:452
  34.9 0.3 shard_map.58
  35.2 2.3 %collective-permute-done.10.refs_2_ = f32[1,272,128]{2,1,0:T(8,128)S(1)} collective-permute-done((f32[1,272,128]{2,1,0:T(8,128)S(1)}, f32[1,272,128]{2,1,0:T(8,128)S(1)}, u32[]{:S(2)}, u32[]{:S(2)}) %collective-permute-start.10) | collective-permute-done | bytes 139296 | tf_op jit(solution)/shard_map/ppermute | solution.py:452
  37.5 1.1 %shard_map.59 = (f32[320,128]{1,0:T(8,128)}, f32[640,128]{1,0:T(8,128)}) custom-call(f32[1,136,128]{2,1,0:T(8,128)S(1)} %get-tuple-element.60.refs_0_, f32[1,136,128]{2,1,0:T(8,128)S(1)} %get-tuple-element.61.refs_1_, f32[1,272,128]{2,1,0:T(8,128)S(1)} %collective-permute-done.10.refs_2_, f32[320,128]{1,0:T(8,128)S(1)} %get-tuple-element.66.refs_3_, ...), custom_call_target="tpu_custom_call" | custom-call | tf_op jit(solution)/shard_map/pallas_call | solution.py:433
  (12 shorter events, 0.2 us)
Async XLA Ops:
  3.1 10.8 %collective-permute-start.5 = (f32[4,128,128]{2,1,0:T(8,128)S(1)}, f32[4,128,128]{2,1,0:T(8,128)S(1)}, u32[]{:S(2)}, u32[]{:S(2)}) collective-permute-start(f32[4,128,128]{2,1,0:T(8,128)S(1)} %get-tuple-element.53), channel_id=1, source_target_pairs={{0,2},{1,5},{2,0},{3,7},{4,6},{5,1},{6,4},{7,3},{8,10},{9,13},{10,... | collective-permute-start | bytes 786440 | tf_op jit(solution)/shard_map/ppermute | solution.py:452
  6.1 7.8 %collective-permute-start.6 = (f32[4,112,128]{2,1,0:T(8,128)S(1)}, f32[4,112,128]{2,1,0:T(8,128)S(1)}, u32[]{:S(2)}, u32[]{:S(2)}) collective-permute-start(f32[4,112,128]{2,1,0:T(8,128)S(1)} %get-tuple-element.54), channel_id=1, source_target_pairs={{0,4},{1,3},{2,6},{3,1},{4,0},{5,7},{6,2},{7,5},{8,12},{9,11},{10,... | collective-permute-start | bytes 688136 | tf_op jit(solution)/shard_map/ppermute | solution.py:452
  8.5 10.1 %collective-permute-start = (f32[4,136,128]{2,1,0:T(8,128)S(1)}, f32[4,136,128]{2,1,0:T(8,128)S(1)}, u32[]{:S(2)}, u32[]{:S(2)}) collective-permute-start(f32[4,136,128]{2,1,0:T(8,128)S(1)} %get-tuple-element.44), channel_id=1, source_target_pairs={{0,2},{1,5},{2,0},{3,7},{4,6},{5,1},{6,4},{7,3},{8,10},{9,13},{10,... | collective-permute-start | bytes 835592 | tf_op jit(solution)/shard_map/ppermute | solution.py:452
  9.1 9.8 %collective-permute-start.1 = (f32[4,136,128]{2,1,0:T(8,128)S(1)}, f32[4,136,128]{2,1,0:T(8,128)S(1)}, u32[]{:S(2)}, u32[]{:S(2)}) collective-permute-start(f32[4,136,128]{2,1,0:T(8,128)S(1)} %get-tuple-element.45), channel_id=1, source_target_pairs={{0,4},{1,3},{2,6},{3,1},{4,0},{5,7},{6,2},{7,5},{8,12},{9,11},{10,... | collective-permute-start | bytes 835592 | tf_op jit(solution)/shard_map/ppermute | solution.py:452
  10.5 6.6 %collective-permute-start.2 = (f32[2,128]{1,0:T(2,128)S(1)}, f32[2,128]{1,0:T(2,128)S(1)}, u32[]{:S(2)}, u32[]{:S(2)}) collective-permute-start(f32[2,128]{1,0:T(2,128)S(1)} %slice_bitcast_fusion), channel_id=1, source_target_pairs={{0,1},{1,0},{2,3},{3,2},{4,5},{5,4},{6,7},{7,6},{8,9},{9,8},{10,11... | collective-permute-start | bytes 3080 | tf_op jit(solution)/shard_map/ppermute | solution.py:452
  14.0 9.0 %collective-permute-start.7 = (f32[2,128,128]{2,1,0:T(8,128)S(1)}, f32[2,128,128]{2,1,0:T(8,128)S(1)}, u32[]{:S(2)}, u32[]{:S(2)}) collective-permute-start(f32[2,128,128]{2,1,0:T(8,128)S(1)} %get-tuple-element.57), channel_id=1, source_target_pairs={{0,4},{1,3},{2,6},{3,1},{4,0},{5,7},{6,2},{7,5},{8,12},{9,11},{10,... | collective-permute-start | bytes 393224 | tf_op jit(solution)/shard_map/ppermute | solution.py:452
  16.4 6.6 %collective-permute-start.8 = (f32[2,112,128]{2,1,0:T(8,128)S(1)}, f32[2,112,128]{2,1,0:T(8,128)S(1)}, u32[]{:S(2)}, u32[]{:S(2)}) collective-permute-start(f32[2,112,128]{2,1,0:T(8,128)S(1)} %get-tuple-element.58), channel_id=1, source_target_pairs={{0,2},{1,5},{2,0},{3,7},{4,6},{5,1},{6,4},{7,3},{8,10},{9,13},{10,... | collective-permute-start | bytes 344072 | tf_op jit(solution)/shard_map/ppermute | solution.py:452
  17.0 6.0 %collective-permute-start.9 = (f32[2,128]{1,0:T(2,128)S(1)}, f32[2,128]{1,0:T(2,128)S(1)}, u32[]{:S(2)}, u32[]{:S(2)}) collective-permute-start(f32[2,128]{1,0:T(2,128)S(1)} %fusion.refs_4_), channel_id=1, source_target_pairs={{0,6},{1,7},{2,4},{3,5},{4,2},{5,3},{6,0},{7,1},{8,14},{9,15},{10,... | collective-permute-start | bytes 3080 | tf_op jit(solution)/shard_map/ppermute | solution.py:452
  18.9 8.2 %collective-permute-start.3 = (f32[2,136,128]{2,1,0:T(8,128)S(1)}, f32[2,136,128]{2,1,0:T(8,128)S(1)}, u32[]{:S(2)}, u32[]{:S(2)}) collective-permute-start(f32[2,136,128]{2,1,0:T(8,128)S(1)} %get-tuple-element.49), channel_id=1, source_target_pairs={{0,4},{1,3},{2,6},{3,1},{4,0},{5,7},{6,2},{7,5},{8,12},{9,11},{10,... | collective-permute-start | bytes 417800 | tf_op jit(solution)/shard_map/ppermute | solution.py:452
  21.5 5.6 %collective-permute-start.4 = (f32[2,136,128]{2,1,0:T(8,128)S(1)}, f32[2,136,128]{2,1,0:T(8,128)S(1)}, u32[]{:S(2)}, u32[]{:S(2)}) collective-permute-start(f32[2,136,128]{2,1,0:T(8,128)S(1)} %get-tuple-element.50), channel_id=1, source_target_pairs={{0,2},{1,5},{2,0},{3,7},{4,6},{5,1},{6,4},{7,3},{8,10},{9,13},{10,... | collective-permute-start | bytes 417800 | tf_op jit(solution)/shard_map/ppermute | solution.py:452
  23.1 11.9 %collective-permute-start.11 = (f32[1,240,128]{2,1,0:T(8,128)S(1)}, f32[1,240,128]{2,1,0:T(8,128)S(1)}, u32[]{:S(2)}, u32[]{:S(2)}) collective-permute-start(f32[1,240,128]{2,1,0:T(8,128)S(1)} %get-tuple-element.65), channel_id=1, source_target_pairs={{0,8},{1,9},{2,10},{3,11},{4,12},{5,13},{6,14},{7,15},{8,0},{9,1},... | collective-permute-start | bytes 368648 | tf_op jit(solution)/shard_map/ppermute | solution.py:452
  27.1 10.4 %collective-permute-start.10 = (f32[1,272,128]{2,1,0:T(8,128)S(1)}, f32[1,272,128]{2,1,0:T(8,128)S(1)}, u32[]{:S(2)}, u32[]{:S(2)}) collective-permute-start(f32[1,272,128]{2,1,0:T(8,128)S(1)} %get-tuple-element.62), channel_id=1, source_target_pairs={{0,8},{1,9},{2,10},{3,11},{4,12},{5,13},{6,14},{7,15},{8,0},{9,1},... | collective-permute-start | bytes 417800 | tf_op jit(solution)/shard_map/ppermute | solution.py:452

commit v11 on v10

--- a/solution.py
+++ b/solution.py
@@ -104,35 +104,66 @@
 LOADS = 4
 
 
-def pack_body(pieces, items, count_a, count_g, fresh, *refs):
+def pack_body(pieces, items, count_a, count_g, call, *refs):
     n = len(items)
-    if fresh:
-        arrays, outs, (notes, *held), sems = refs[:3], refs[3 : 3 + n], refs[3 + n : -1], refs[-1]
-    else:
-        notes_in, held, outs, notes = refs[0], refs[1:4], refs[4 : 4 + n], refs[-1]
+    refs = list(refs)
+
+    def pop(count):
+        taken = refs[:count]
+        del refs[:count]
+        return taken
+
+    notes_in = pop(call > 0)
+    arrays = pop(3)
+    outs, (notes,) = pop(n), pop(1)
+    held = pop(1) if call == 0 else arrays[:1] + pop(2) if call == 1 else arrays
+    columns, sems = (pop(2) if call == 0 else None), (pop(1) if call < 2 else None)
+    fresh = call == 0
+    notes_in = notes_in[0] if notes_in else None
     full, half = split_rows(count_a)
     slots = SLOTS // 2
-
-    def copies(i):
+    split = [(i, k, first, slot) for i, (k, first) in enumerate(items) for slot in range(slots)]
+
+    def whole(i):
         rows = arrays[i].shape[0] // LOADS
-        parts = [slice(part * rows, (part + 1) * rows) for part in range(LOADS)]
         return [
-            pltpu.make_async_copy(arrays[i].at[part], held[i].at[part], sems.at[i, part_no])
-            for part_no, part in enumerate(parts)
+            pltpu.make_async_copy(
+                arrays[i].at[part * rows : (part + 1) * rows],
+                held[i].at[part * rows : (part + 1) * rows],
+                sems[0].at[i, part],
+            )
+            for part in range(LOADS)
         ]
 
-    waiting = [0, 1, 2] if fresh else []
-    for i in waiting:
-        for copy in copies(i):
-            copy.start()
-
-    def arrive(upto):
-        while waiting and waiting[0] <= upto:
-            for copy in copies(waiting.pop(0)):
-                copy.wait()
+    def own_columns():
+        found = []
+        for i, k, first, slot in split:
+            g_blocks, kind = pieces[k][2:]
+            if g_blocks:
+                start = slot_owner(first + slot, KINDS[kind]) * count_g + g_blocks[0] * B
+                size = len(g_blocks) * B
+                for m in (0, 1):
+                    src = arrays[1 + m].at[:, pl.ds(pl.multiple_of(start, B), size)]
+                    dst = columns[m].at[i * slots + slot, :, :size]
+                    sem = sems[0].at[1 + m, i * slots + slot]
+                    found.append(pltpu.make_async_copy(src, dst, sem))
+        return found
+
+    early = whole(0) if call == 0 else []
+    late = own_columns() if call == 0 else whole(1) + whole(2) if call == 1 else []
+    for copy in early + late:
+        copy.start()
 
     def read(i, start):
         return held[i][:, pl.ds(pl.multiple_of(start, B), B)]
+
+    def read_g(i, k, first, slot, b):
+        _, _, g_blocks, kind = pieces[k]
+        if call == 0:
+            part = slice((b - g_blocks[0]) * B, (b - g_blocks[0] + 1) * B)
+            return [columns[m][i * slots + slot, :, part] for m in (0, 1)]
+        start = slot_owner(first + slot, KINDS[kind]) * count_g + b * B
+        return [read(1, start), read(2, start)]
 
     row, col = iotas(H)
     low = col < row
@@ -191,33 +222,31 @@
             at = at + quarter * 3 // 2
         return at
 
-    def g_parts(out, k, first, slot, index, at):
+    def g_parts(i, k, first, slot, index, at):
         _, _, g_blocks, kind = pieces[k]
-        owner = slot_owner(first + slot, KINDS[kind])
         here = kind * SLOTS + first + slot
         for b in g_blocks:
-            start = owner * count_g + b * B
-            value = read(1, start).astype(jnp.float32)
-            grad = read(2, start).astype(jnp.float32)
+            value, grad = (part.astype(jnp.float32) for part in read_g(i, k, first, slot, b))
             block = cov((grad * gelu_slope(value)).astype(jnp.bfloat16))
-            out[slot, at : at + H, :] = fold(block, here, next(index), 1)
+            outs[i][slot, at : at + H, :] = fold(block, here, next(index), 1)
             at = at + H
         return at
 
-    arrive(0)
+    for copy in early:
+        copy.wait()
     begun = []
-    for out, (k, first) in zip(outs, items):
-        for slot in range(slots):
-            here = pieces[k][3] * SLOTS + first + slot
-            if here not in tiles:
-                tiles[here] = jnp.zeros((EDGE, B), jnp.float32) if fresh else notes_in[here]
-            index = corner_indices(pieces, k)
-            begun.append((out, k, first, slot, index, a_parts(out, k, first, slot, index)))
-    arrive(2)
-    for out, k, first, slot, index, at in begun:
-        at = g_parts(out, k, first, slot, index, at)
+    for i, k, first, slot in split:
+        here = pieces[k][3] * SLOTS + first + slot
+        if here not in tiles:
+            tiles[here] = jnp.zeros((EDGE, B), jnp.float32) if fresh else notes_in[here]
+        index = corner_indices(pieces, k)
+        begun.append((index, a_parts(outs[i], k, first, slot, index)))
+    for copy in late:
+        copy.wait()
+    for (i, k, first, slot), (index, at) in zip(split, begun):
+        at = g_parts(i, k, first, slot, index, at)
         if has_edge(pieces, k):
-            out[slot, at:, :] = tiles[pieces[k][3] * SLOTS + first + slot]
+            outs[i][slot, at:, :] = tiles[pieces[k][3] * SLOTS + first + slot]
 
     for slot in range(NOTES):
         if slot in tiles:
@@ -229,23 +258,31 @@
     notes[NOTES] = tile if fresh else notes_in[NOTES] + tile
 
 
-def pack(arrays, pieces, items, count_a, count_g, notes):
-    fresh = notes is None
+def pack(arrays, pieces, items, count_a, count_g, call, notes):
+    slots = SLOTS // 2
     out_shape = [
-        jax.ShapeDtypeStruct((SLOTS // 2, piece_rows(pieces, k), B), jnp.float32)
-        for k, _ in items
+        jax.ShapeDtypeStruct((slots, piece_rows(pieces, k), B), jnp.float32) for k, _ in items
     ]
     out_shape.append(jax.ShapeDtypeStruct((NOTES + 1, EDGE, B), jnp.float32))
-    if fresh:
-        out_shape += [jax.ShapeDtypeStruct(array.shape, array.dtype) for array in arrays]
-    args = arrays if fresh else (notes, *arrays)
-    space = pltpu.HBM if fresh else pltpu.VMEM
+    moved = arrays[:1] if call == 0 else arrays[1:] if call == 1 else ()
+    out_shape += [jax.ShapeDtypeStruct(array.shape, array.dtype) for array in moved]
+    scratch = []
+    if call == 0:
+        width = max(len(pieces[k][2]) for k, _ in items) * B
+        shape = (len(items) * slots, arrays[1].shape[0], max(width, B))
+        scratch += [pltpu.VMEM(shape, arrays[1].dtype)] * 2
+    if call < 2:
+        scratch.append(pltpu.SemaphoreType.DMA((3, max(LOADS, len(items) * slots))))
+    spaces = [pltpu.HBM] * 3 if call == 0 else [pltpu.VMEM] + [pltpu.HBM] * 2
+    spaces = [pltpu.VMEM] * 3 if call > 1 else spaces
+    args = [*([notes] if call else []), *arrays]
+    spaces = [pltpu.VMEM] * (call > 0) + spaces
     outs = pl.pallas_call(
-        functools.partial(pack_body, pieces, items, count_a, count_g, fresh),
-        in_specs=[pl.BlockSpec(memory_space=space)] * len(args),
+        functools.partial(pack_body, pieces, items, count_a, count_g, call),
+        in_specs=[pl.BlockSpec(memory_space=space) for space in spaces],
         out_specs=[pl.BlockSpec(memory_space=pltpu.VMEM)] * len(out_shape),
         out_shape=out_shape,
-        scratch_shapes=[pltpu.SemaphoreType.DMA((len(arrays), LOADS))] * fresh,
+        scratch_shapes=scratch,
         compiler_params=pltpu.CompilerParams(vmem_limit_bytes=32 * 2**20),
         cost_estimate=pl.CostEstimate(flops=1, bytes_accessed=1, transcendentals=0),
     )(*args)
@@ -304,15 +341,14 @@
     return jnp.concatenate([folded] * (B // folded.shape[0]), axis=0).T
 
 
-def unfold(folded, put):
+def unfold(folded):
     row, col = iotas(H)
     turned = turn(folded)
     last = pltpu.roll(jnp.where(col < row, folded, turned[:H]), H, 1)
-    put(0, jnp.where(col < row, turned[:H], folded))
-    put(H, jnp.where(col < H, turned[H:], last))
-
-
-def unfold_half(square, rest, odd, put):
+    return jnp.where(col < row, turned[:H], folded), jnp.where(col < H, turned[H:], last)
+
+
+def unfold_half(square, rest, odd):
     quarter = H // 2
     row, col = iotas(quarter)
     turned = turn(square)
@@ -321,7 +357,7 @@
     lower = jnp.where(col < quarter, turned[quarter:H], last)
     rest = jnp.concatenate([rest, pltpu.roll(rest, H, 1)], axis=0)
     part = jnp.concatenate([upper, jnp.where(col < H, lower, rest)], axis=0)
-    put(0, jnp.where(odd == 1, pltpu.roll(part, H, 1), part))
+    return (jnp.where(odd == 1, pltpu.roll(part, H, 1), part),)
 
 
 def places(pieces, ks, count_a):
@@ -344,7 +380,7 @@
     return {k: sum(rows[:i]) for i, k in enumerate(ks)}
 
 
-def unfold_body(pieces, ks, count_a, total, owns, got, outs):
+def unfolded(pieces, ks, count_a, total, owns, got):
     odd = lax.axis_index("dp") & 1
     at = dict.fromkeys(ks, 0)
     begins = row_begins(pieces, ks)
@@ -356,30 +392,29 @@
         begin = begin + begins[k]
         return mean_of(mine + got[0, begin : begin + rows, :], total)
 
-    for k, which, start, rows, _ in places(pieces, ks, count_a):
-        def put(offset, value):
-            outs[which][pl.ds(start + offset, value.shape[0]), :] = value
-
+    for place in places(pieces, ks, count_a):
+        k, _, _, rows, _ = place
         if rows == H:
-            unfold(take(k, H), put)
+            yield place, unfold(take(k, H))
         else:
-            unfold_half(take(k, H // 2), take(k, H // 4), odd, put)
+            yield place, unfold_half(take(k, H // 2), take(k, H // 4), odd)
 
 
 def early_body(pieces, ks, count_a, total, *refs):
     n = len(ks)
-    unfold_body(pieces, ks, count_a, total, refs[:n], refs[n], refs[n + 1 :])
+    owns, got, outs = refs[:n], refs[n], refs[n + 1 :]
+    for (_, which, start, _, _), halves in unfolded(pieces, ks, count_a, total, owns, got):
+        for i, value in enumerate(halves):
+            outs[which][pl.ds(start + i * H, H), :] = value
 
 
 def finish_body(pieces, early, late, count_a, total, *refs):
     n = len(late)
-    owns, got, (early_a, early_g, a_ref, g_ref) = refs[:n], refs[n], refs[n + 1 :]
-    outs = (a_ref, g_ref)
-    full, half = split_rows(count_a)
+    owns, got, firsts, outs = refs[:n], refs[n], refs[n + 1 : n + 3], refs[n + 3 : n + 5]
+    made, sem = refs[n + 5 : n + 7], refs[n + 7]
+    _, half = split_rows(count_a)
     odd = lax.axis_index("dp") & half
     row, col = iotas(H)
-
-    unfold_body(pieces, late, count_a, total, owns, got, outs)
 
     edges = {}
     for k, own in zip(late, owns):
@@ -395,22 +430,40 @@
         line = index // 2
         return edges[kind][0 if index % 2 == natural else 1][line : line + 1]
 
-    for ks in (early, late):
-        ins = (early_a, early_g) if ks is early else outs
-        for k, which, start, rows, index in places(pieces, ks, count_a):
-            src, out, shift, kind = ins[which], outs[which], shifts[which], pieces[k][3]
-            here = pl.ds(start, H)
-            if rows == H:
-                low = pl.ds(start + H, H)
-                out[here, :] = src[here, :] + jnp.where(col == row, shift, 0.0)
-                value = corner(kind, index, 0) + shift
-                out[low, :] = jnp.where(col == row + H, value, src[low, :])
-            else:
-                value = src[here, :] + jnp.where(col == row + odd * H, shift, 0.0)
-                line = corner(kind, index, 1)
-                line = jnp.where(odd == 1, pltpu.roll(line, H, 1), line) + shift
-                last = jnp.logical_and(col == row + odd * H, row >= H // 2)
-                out[here, :] = jnp.where(last, line, value)
+    copies = []
+
+    def give(place, halves):
+        k, which, start, rows, index = place
+        shift, kind = shifts[which], pieces[k][3]
+        if rows == H:
+            top, bottom = halves
+            top = top + jnp.where(col == row, shift, 0.0)
+            bottom = jnp.where(col == row + H, corner(kind, index, 0) + shift, bottom)
+            halves = (top, bottom)
+        else:
+            line = corner(kind, index, 1)
+            line = jnp.where(odd == 1, pltpu.roll(line, H, 1), line) + shift
+            diagonal = col == row + odd * H
+            value = halves[0] + jnp.where(diagonal, shift, 0.0)
+            last = jnp.logical_and(diagonal, row >= H // 2)
+            halves = (jnp.where(last, line, value),)
+        for i, value in enumerate(halves):
+            made[which][pl.ds(start + i * H, H), :] = value
+        part = pl.ds(start, len(halves) * H)
+        copy = pltpu.make_async_copy(
+            made[which].at[part], outs[which].at[part], sem.at[len(copies)]
+        )
+        copy.start()
+        copies.append(copy)
+
+    for place in places(pieces, early, count_a):
+        _, which, start, rows, _ = place
+        count = 2 if rows == H else 1
+        give(place, [firsts[which][pl.ds(start + i * H, H), :] for i in range(count)])
+    for place, halves in unfolded(pieces, late, count_a, total, owns, got):
+        give(place, halves)
+    for copy in copies:
+        copy.wait()
 
 
 def unfold_early(pieces, ks, owns, got, count_a, count_g, total):
@@ -430,13 +483,19 @@
 
 def finish(pieces, early, late, owns, got, first, count_a, count_g, total):
     args = (*owns, got, *first)
+    parts = sum(len(a_blocks) + a_half + len(g_blocks) for a_blocks, a_half, g_blocks, _ in pieces)
     return pl.pallas_call(
         functools.partial(finish_body, pieces, early, late, count_a, total),
         in_specs=[pl.BlockSpec(memory_space=pltpu.VMEM)] * len(args),
-        out_specs=[pl.BlockSpec(memory_space=pltpu.VMEM)] * 2,
+        out_specs=[pl.BlockSpec(memory_space=pltpu.HBM)] * 2,
         out_shape=[
             jax.ShapeDtypeStruct((count_a, B), jnp.float32),
             jax.ShapeDtypeStruct((count_g, B), jnp.float32),
+        ],
+        scratch_shapes=[
+            pltpu.VMEM((count_a, B), jnp.float32),
+            pltpu.VMEM((count_g, B), jnp.float32),
+            pltpu.SemaphoreType.DMA((parts,)),
         ],
         compiler_params=pltpu.CompilerParams(vmem_limit_bytes=32 * 2**20),
     )(*args)
@@ -478,11 +537,11 @@
     early, late = (0, 2), (1, 3)
     keeps, gots, notes = {}, {}, None
 
-    def pack_next(first, ks):
+    def pack_next(call, first, ks):
         nonlocal notes, arrays
         items = tuple((k, first) for k in ks)
-        parts, notes, held = pack(arrays, pieces, items, count_a, count_g, notes)
-        arrays = held or arrays
+        parts, notes, held = pack(arrays, pieces, items, count_a, count_g, call, notes)
+        arrays = (*arrays[:call], *held, *arrays[call + len(held) :])
         return dict(zip(ks, parts))
 
     def exchange(parts, stage):
@@ -501,10 +560,10 @@
             exchange(dict(zip(ks, parts)), stage)
         return others
 
-    exchange(pack_next(send, early), 0)
-    exchange(pack_next(send, late), 0)
-    keeps.update(pack_next(keep, early))
-    keeps.update(pack_next(keep, late))
+    exchange(pack_next(0, send, early), 0)
+    exchange(pack_next(1, send, late), 0)
+    keeps.update(pack_next(2, keep, early))
+    keeps.update(pack_next(3, keep, late))
 
     trace = notes[NOTES, :2, :]
     trace = trace + swap(trace, lambda i, j: (i, j ^ 1))

time: 38.7 us -> 38.2 us (0.987)
  starting transfers between devices: 18 us -> 15.6 us
  Pallas kernels: 6.19 us -> 7.74 us
    ppermute x12, starting transfers between devices: 18 us -> 15.6 us  [swap(): return lax.ppermute(value, ('dp', 'tensor'), pairs)]
    pallas_call x4, Pallas kernels: 4.61 us -> 6.24 us  [pack(): pl.pallas_call(functools.partial(pack_body, pieces, items, count_a, count...]
  transfers between devices with their start and end apart: 12 -> 12, of which waited for: 6 -> 6; matrix products, arithmetic and copies ran while one was open for 0% -> 0% of each run, Pallas kernels for 7% -> 12%
where the time goes in v11:
time: 38.2 us; the launch traced here: 38 us
  starting transfers between devices  15.6 us (41%)
  waiting for transfers between devices  14 us (37%)
  Pallas kernels  7.74 us (20%)
  between operations  0.72 us (2%)
    ppermute x12, starting transfers between devices, swap(): return lax.ppermute(value, ('dp', 'tensor'), pairs)  15.6 us
    ppermute x12, waiting for transfers between devices, swap(): return lax.ppermute(value, ('dp', 'tensor'), pairs)  14 us
    pallas_call x4, Pallas kernels, pack(): pl.pallas_call(functools.partial(pack_body, pieces, items, count_a, count...  6.24 us
    pallas_call x1, Pallas kernels, finish(): pl.pallas_call(functools.partial(finish_body, pieces, early, late, count_...  1.03 us
  transfers between devices with their start and end apart: 12, of which 6 were waited for; matrix products, arithmetic and copies ran while one was open for 0% of the time, Pallas kernels for 12%

profile of v11, /device:TPU:0, one launch (start us, length us, event | category | flops | bytes accessed | tf_op | source)
XLA Modules:
  0.0 38.0 jit_solution(2760113066773052377)
XLA Ops:
  0.6 2.3 %shard_map.50 = (f32[4,128,128]{2,1,0:T(8,128)S(1)}, f32[4,112,128]{2,1,0:T(8,128)S(1)}, f32[17,8,128]{2,1,0:T(8,128)S(1)}, bf16[128,2560]{1,0:T(8,128)(2,1)S(1)}) custom-call(bf16[128,2560]{1,0:T(8,128)(2,1)} %refs_0_.1, bf16[128,5120]{1,0:T(8,128)(2,1)} %refs_2_.3, bf16[128,5120]{1,0:T(8,128)(2,1)} %refs_3_.1), custom_call_target="tpu_custom_call" | custom-call | flops 1 | bytes 1 | tf_op jit(solution)/shard_map/pallas_call | solution.py:280
  2.9 3.0 %collective-permute-start.5 = (f32[4,128,128]{2,1,0:T(8,128)S(1)}, f32[4,128,128]{2,1,0:T(8,128)S(1)}, u32[]{:S(2)}, u32[]{:S(2)}) collective-permute-start(f32[4,128,128]{2,1,0:T(8,128)S(1)} %get-tuple-element.53), channel_id=1, source_target_pairs={{0,2},{1,5},{2,0},{3,7},{4,6},{5,1},{6,4},{7,3},{8,10},{9,13},{10,... | collective-permute-start | bytes 786440 | tf_op jit(solution)/shard_map/ppermute | solution.py:511
  5.9 1.6 %collective-permute-start.6 = (f32[4,112,128]{2,1,0:T(8,128)S(1)}, f32[4,112,128]{2,1,0:T(8,128)S(1)}, u32[]{:S(2)}, u32[]{:S(2)}) collective-permute-start(f32[4,112,128]{2,1,0:T(8,128)S(1)} %get-tuple-element.54), channel_id=1, source_target_pairs={{0,4},{1,3},{2,6},{3,1},{4,0},{5,7},{6,2},{7,5},{8,12},{9,11},{10,... | collective-permute-start | bytes 688136 | tf_op jit(solution)/shard_map/ppermute | solution.py:511
  7.5 2.7 %shard_map.51 = (f32[4,136,128]{2,1,0:T(8,128)S(1)}, f32[4,136,128]{2,1,0:T(8,128)S(1)}, f32[17,8,128]{2,1,0:T(8,128)S(1)}, bf16[128,5120]{1,0:T(8,128)(2,1)S(1)}, bf16[128,5120]{1,0:T(8,128)(2,1)S(1)}) custom-call(f32[17,8,128]{2,1,0:T(8,128)S(1)} %get-tuple-element.36.refs_0_, bf16[128,2560]{1,0:T(8,128)(2,1)S(1)} %get-tuple-element.37.refs_1_, ...), custom_call_target="tpu_custom_call" | custom-call | flops 1 | bytes 1 | tf_op jit(solution)/shard_map/pallas_call | solution.py:280
  10.2 0.6 %collective-permute-start = (f32[4,136,128]{2,1,0:T(8,128)S(1)}, f32[4,136,128]{2,1,0:T(8,128)S(1)}, u32[]{:S(2)}, u32[]{:S(2)}) collective-permute-start(f32[4,136,128]{2,1,0:T(8,128)S(1)} %get-tuple-element.44), channel_id=1, source_target_pairs={{0,2},{1,5},{2,0},{3,7},{4,6},{5,1},{6,4},{7,3},{8,10},{9,13},{10,... | collective-permute-start | bytes 835592 | tf_op jit(solution)/shard_map/ppermute | solution.py:511
  10.8 0.5 %shard_map.52 = (f32[4,128,128]{2,1,0:T(8,128)S(1)}, f32[4,112,128]{2,1,0:T(8,128)S(1)}, f32[17,8,128]{2,1,0:T(8,128)S(1)}) custom-call(f32[17,8,128]{2,1,0:T(8,128)S(1)} %get-tuple-element.38.refs_0_, bf16[128,2560]{1,0:T(8,128)(2,1)S(1)} %get-tuple-element.37.refs_1_, bf16[128,5120]{1,0:T(8,128)(2,1)S(1)} %get-tuple-element.39.refs_2_, ...), custom_call_target="tpu_custom_call" | custom-call | flops 1 | bytes 1 | tf_op jit(solution)/shard_map/pallas_call | solution.py:280
  11.3 0.8 %shard_map.53 = (f32[4,136,128]{2,1,0:T(8,128)S(1)}, f32[4,136,128]{2,1,0:T(8,128)S(1)}, f32[17,8,128]{2,1,0:T(8,128)S(1)}) custom-call(f32[17,8,128]{2,1,0:T(8,128)S(1)} %get-tuple-element.41.refs_0_, bf16[128,2560]{1,0:T(8,128)(2,1)S(1)} %get-tuple-element.37.refs_1_, bf16[128,5120]{1,0:T(8,128)(2,1)S(1)} %get-tuple-element.39.refs_2_, ...), custom_call_target="tpu_custom_call" | custom-call | flops 1 | bytes 1 | tf_op jit(solution)/shard_map/pallas_call | solution.py:280
  12.1 0.1 collective-permute-start.2
  12.2 0.1 collective-permute-done.6.refs_3_
  12.3 0.2 collective-permute-done.5.refs_2_
  12.4 0.1 shard_map.55
  12.5 2.4 %collective-permute-start.7 = (f32[2,128,128]{2,1,0:T(8,128)S(1)}, f32[2,128,128]{2,1,0:T(8,128)S(1)}, u32[]{:S(2)}, u32[]{:S(2)}) collective-permute-start(f32[2,128,128]{2,1,0:T(8,128)S(1)} %get-tuple-element.57), channel_id=1, source_target_pairs={{0,4},{1,3},{2,6},{3,1},{4,0},{5,7},{6,2},{7,5},{8,12},{9,11},{10,... | collective-permute-start | bytes 393224 | tf_op jit(solution)/shard_map/ppermute | solution.py:511
  14.9 1.8 %collective-permute-start.8 = (f32[2,112,128]{2,1,0:T(8,128)S(1)}, f32[2,112,128]{2,1,0:T(8,128)S(1)}, u32[]{:S(2)}, u32[]{:S(2)}) collective-permute-start(f32[2,112,128]{2,1,0:T(8,128)S(1)} %get-tuple-element.58), channel_id=1, source_target_pairs={{0,2},{1,5},{2,0},{3,7},{4,6},{5,1},{6,4},{7,3},{8,10},{9,13},{10,... | collective-permute-start | bytes 344072 | tf_op jit(solution)/shard_map/ppermute | solution.py:511
  16.7 3.1 %collective-permute-done.refs_2_ = f32[4,136,128]{2,1,0:T(8,128)S(1)} collective-permute-done((f32[4,136,128]{2,1,0:T(8,128)S(1)}, f32[4,136,128]{2,1,0:T(8,128)S(1)}, u32[]{:S(2)}, u32[]{:S(2)}) %collective-permute-start) | collective-permute-done | bytes 278560 | tf_op jit(solution)/shard_map/ppermute | solution.py:511
  19.8 0.1 shard_map.54
  19.9 0.8 %collective-permute-start.3 = (f32[2,136,128]{2,1,0:T(8,128)S(1)}, f32[2,136,128]{2,1,0:T(8,128)S(1)}, u32[]{:S(2)}, u32[]{:S(2)}) collective-permute-start(f32[2,136,128]{2,1,0:T(8,128)S(1)} %get-tuple-element.49), channel_id=1, source_target_pairs={{0,4},{1,3},{2,6},{3,1},{4,0},{5,7},{6,2},{7,5},{8,12},{9,11},{10,... | collective-permute-start | bytes 417800 | tf_op jit(solution)/shard_map/ppermute | solution.py:511
  20.7 1.8 %collective-permute-start.4 = (f32[2,136,128]{2,1,0:T(8,128)S(1)}, f32[2,136,128]{2,1,0:T(8,128)S(1)}, u32[]{:S(2)}, u32[]{:S(2)}) collective-permute-start(f32[2,136,128]{2,1,0:T(8,128)S(1)} %get-tuple-element.50), channel_id=1, source_target_pairs={{0,2},{1,5},{2,0},{3,7},{4,6},{5,1},{6,4},{7,3},{8,10},{9,13},{10,... | collective-permute-start | bytes 417800 | tf_op jit(solution)/shard_map/ppermute | solution.py:511
  22.6 2.7 %collective-permute-start.11 = (f32[1,240,128]{2,1,0:T(8,128)S(1)}, f32[1,240,128]{2,1,0:T(8,128)S(1)}, u32[]{:S(2)}, u32[]{:S(2)}) collective-permute-start(f32[1,240,128]{2,1,0:T(8,128)S(1)} %get-tuple-element.65), channel_id=1, source_target_pairs={{0,8},{1,9},{2,10},{3,11},{4,12},{5,13},{6,14},{7,15},{8,0},{9,1},... | collective-permute-start | bytes 368648 | tf_op jit(solution)/shard_map/ppermute | solution.py:511
  25.2 3.0 %collective-permute-done.3.refs_2_ = f32[2,136,128]{2,1,0:T(8,128)S(1)} collective-permute-done((f32[2,136,128]{2,1,0:T(8,128)S(1)}, f32[2,136,128]{2,1,0:T(8,128)S(1)}, u32[]{:S(2)}, u32[]{:S(2)}) %collective-permute-start.3) | collective-permute-done | bytes 139296 | tf_op jit(solution)/shard_map/ppermute | solution.py:511
  28.3 0.8 %collective-permute-start.10 = (f32[1,272,128]{2,1,0:T(8,128)S(1)}, f32[1,272,128]{2,1,0:T(8,128)S(1)}, u32[]{:S(2)}, u32[]{:S(2)}) collective-permute-start(f32[1,272,128]{2,1,0:T(8,128)S(1)} %get-tuple-element.62), channel_id=1, source_target_pairs={{0,8},{1,9},{2,10},{3,11},{4,12},{5,13},{6,14},{7,15},{8,0},{9,1},... | collective-permute-start | bytes 417800 | tf_op jit(solution)/shard_map/ppermute | solution.py:511
  29.1 5.1 %collective-permute-done.11.refs_2_ = f32[1,240,128]{2,1,0:T(8,128)S(1)} collective-permute-done((f32[1,240,128]{2,1,0:T(8,128)S(1)}, f32[1,240,128]{2,1,0:T(8,128)S(1)}, u32[]{:S(2)}, u32[]{:S(2)}) %collective-permute-start.11) | collective-permute-done | bytes 122912 | tf_op jit(solution)/shard_map/ppermute | solution.py:511
  34.2 0.3 shard_map.58
  34.5 2.5 %collective-permute-done.10.refs_2_ = f32[1,272,128]{2,1,0:T(8,128)S(1)} collective-permute-done((f32[1,272,128]{2,1,0:T(8,128)S(1)}, f32[1,272,128]{2,1,0:T(8,128)S(1)}, u32[]{:S(2)}, u32[]{:S(2)}) %collective-permute-start.10) | collective-permute-done | bytes 139296 | tf_op jit(solution)/shard_map/ppermute | solution.py:511
  37.0 1.0 %shard_map.59 = (f32[320,128]{1,0:T(8,128)}, f32[640,128]{1,0:T(8,128)}) custom-call(f32[1,136,128]{2,1,0:T(8,128)S(1)} %get-tuple-element.60.refs_0_, f32[1,136,128]{2,1,0:T(8,128)S(1)} %get-tuple-element.61.refs_1_, f32[1,272,128]{2,1,0:T(8,128)S(1)} %collective-permute-done.10.refs_2_, f32[320,128]{1,0:T(8,128)S(1)} %get-tuple-element.66.refs_3_, ...), custom_call_target="tpu_custom_call" | custom-call | tf_op jit(solution)/shard_map/pallas_call | solution.py:487
  (12 shorter events, 0.1 us)
Async XLA Ops:
  2.9 9.5 %collective-permute-start.5 = (f32[4,128,128]{2,1,0:T(8,128)S(1)}, f32[4,128,128]{2,1,0:T(8,128)S(1)}, u32[]{:S(2)}, u32[]{:S(2)}) collective-permute-start(f32[4,128,128]{2,1,0:T(8,128)S(1)} %get-tuple-element.53), channel_id=1, source_target_pairs={{0,2},{1,5},{2,0},{3,7},{4,6},{5,1},{6,4},{7,3},{8,10},{9,13},{10,... | collective-permute-start | bytes 786440 | tf_op jit(solution)/shard_map/ppermute | solution.py:511
  5.9 6.4 %collective-permute-start.6 = (f32[4,112,128]{2,1,0:T(8,128)S(1)}, f32[4,112,128]{2,1,0:T(8,128)S(1)}, u32[]{:S(2)}, u32[]{:S(2)}) collective-permute-start(f32[4,112,128]{2,1,0:T(8,128)S(1)} %get-tuple-element.54), channel_id=1, source_target_pairs={{0,4},{1,3},{2,6},{3,1},{4,0},{5,7},{6,2},{7,5},{8,12},{9,11},{10,... | collective-permute-start | bytes 688136 | tf_op jit(solution)/shard_map/ppermute | solution.py:511
  10.2 9.7 %collective-permute-start = (f32[4,136,128]{2,1,0:T(8,128)S(1)}, f32[4,136,128]{2,1,0:T(8,128)S(1)}, u32[]{:S(2)}, u32[]{:S(2)}) collective-permute-start(f32[4,136,128]{2,1,0:T(8,128)S(1)} %get-tuple-element.44), channel_id=1, source_target_pairs={{0,2},{1,5},{2,0},{3,7},{4,6},{5,1},{6,4},{7,3},{8,10},{9,13},{10,... | collective-permute-start | bytes 835592 | tf_op jit(solution)/shard_map/ppermute | solution.py:511
  10.8 9.1 %collective-permute-start.1 = (f32[4,136,128]{2,1,0:T(8,128)S(1)}, f32[4,136,128]{2,1,0:T(8,128)S(1)}, u32[]{:S(2)}, u32[]{:S(2)}) collective-permute-start(f32[4,136,128]{2,1,0:T(8,128)S(1)} %get-tuple-element.45), channel_id=1, source_target_pairs={{0,4},{1,3},{2,6},{3,1},{4,0},{5,7},{6,2},{7,5},{8,12},{9,11},{10,... | collective-permute-start | bytes 835592 | tf_op jit(solution)/shard_map/ppermute | solution.py:511
  12.1 4.6 %collective-permute-start.2 = (f32[2,128]{1,0:T(2,128)S(1)}, f32[2,128]{1,0:T(2,128)S(1)}, u32[]{:S(2)}, u32[]{:S(2)}) collective-permute-start(f32[2,128]{1,0:T(2,128)S(1)} %slice_bitcast_fusion), channel_id=1, source_target_pairs={{0,1},{1,0},{2,3},{3,2},{4,5},{5,4},{6,7},{7,6},{8,9},{9,8},{10,11... | collective-permute-start | bytes 3080 | tf_op jit(solution)/shard_map/ppermute | solution.py:511
  12.5 10.0 %collective-permute-start.7 = (f32[2,128,128]{2,1,0:T(8,128)S(1)}, f32[2,128,128]{2,1,0:T(8,128)S(1)}, u32[]{:S(2)}, u32[]{:S(2)}) collective-permute-start(f32[2,128,128]{2,1,0:T(8,128)S(1)} %get-tuple-element.57), channel_id=1, source_target_pairs={{0,4},{1,3},{2,6},{3,1},{4,0},{5,7},{6,2},{7,5},{8,12},{9,11},{10,... | collective-permute-start | bytes 393224 | tf_op jit(solution)/shard_map/ppermute | solution.py:511
  14.9 7.6 %collective-permute-start.8 = (f32[2,112,128]{2,1,0:T(8,128)S(1)}, f32[2,112,128]{2,1,0:T(8,128)S(1)}, u32[]{:S(2)}, u32[]{:S(2)}) collective-permute-start(f32[2,112,128]{2,1,0:T(8,128)S(1)} %get-tuple-element.58), channel_id=1, source_target_pairs={{0,2},{1,5},{2,0},{3,7},{4,6},{5,1},{6,4},{7,3},{8,10},{9,13},{10,... | collective-permute-start | bytes 344072 | tf_op jit(solution)/shard_map/ppermute | solution.py:511
  16.7 5.8 %collective-permute-start.9 = (f32[2,128]{1,0:T(2,128)S(1)}, f32[2,128]{1,0:T(2,128)S(1)}, u32[]{:S(2)}, u32[]{:S(2)}) collective-permute-start(f32[2,128]{1,0:T(2,128)S(1)} %fusion.refs_4_), channel_id=1, source_target_pairs={{0,6},{1,7},{2,4},{3,5},{4,2},{5,3},{6,0},{7,1},{8,14},{9,15},{10,... | collective-permute-start | bytes 3080 | tf_op jit(solution)/shard_map/ppermute | solution.py:511
  19.9 8.4 %collective-permute-start.3 = (f32[2,136,128]{2,1,0:T(8,128)S(1)}, f32[2,136,128]{2,1,0:T(8,128)S(1)}, u32[]{:S(2)}, u32[]{:S(2)}) collective-permute-start(f32[2,136,128]{2,1,0:T(8,128)S(1)} %get-tuple-element.49), channel_id=1, source_target_pairs={{0,4},{1,3},{2,6},{3,1},{4,0},{5,7},{6,2},{7,5},{8,12},{9,11},{10,... | collective-permute-start | bytes 417800 | tf_op jit(solution)/shard_map/ppermute | solution.py:511
  20.7 7.5 %collective-permute-start.4 = (f32[2,136,128]{2,1,0:T(8,128)S(1)}, f32[2,136,128]{2,1,0:T(8,128)S(1)}, u32[]{:S(2)}, u32[]{:S(2)}) collective-permute-start(f32[2,136,128]{2,1,0:T(8,128)S(1)} %get-tuple-element.50), channel_id=1, source_target_pairs={{0,2},{1,5},{2,0},{3,7},{4,6},{5,1},{6,4},{7,3},{8,10},{9,13},{10,... | collective-permute-start | bytes 417800 | tf_op jit(solution)/shard_map/ppermute | solution.py:511
  22.6 11.6 %collective-permute-start.11 = (f32[1,240,128]{2,1,0:T(8,128)S(1)}, f32[1,240,128]{2,1,0:T(8,128)S(1)}, u32[]{:S(2)}, u32[]{:S(2)}) collective-permute-start(f32[1,240,128]{2,1,0:T(8,128)S(1)} %get-tuple-element.65), channel_id=1, source_target_pairs={{0,8},{1,9},{2,10},{3,11},{4,12},{5,13},{6,14},{7,15},{8,0},{9,1},... | collective-permute-start | bytes 368648 | tf_op jit(solution)/shard_map/ppermute | solution.py:511
  28.3 8.7 %collective-permute-start.10 = (f32[1,272,128]{2,1,0:T(8,128)S(1)}, f32[1,272,128]{2,1,0:T(8,128)S(1)}, u32[]{:S(2)}, u32[]{:S(2)}) collective-permute-start(f32[1,272,128]{2,1,0:T(8,128)S(1)} %get-tuple-element.62), channel_id=1, source_target_pairs={{0,8},{1,9},{2,10},{3,11},{4,12},{5,13},{6,14},{7,15},{8,0},{9,1},... | collective-permute-start | bytes 417800 | tf_op jit(solution)/shard_map/ppermute | solution.py:511

commit v12 on v11

--- a/solution.py
+++ b/solution.py
@@ -522,12 +522,12 @@
     count_g = saved_pre.shape[1] // dp
     full_a, half_a = split_rows(count_a)
     full_g, _ = split_rows(count_g)
-    some = 1 + (full_g - 1) // 2
+    some, more = (full_a + 1) // 2, full_g // 2
     pieces = (
-        (tuple(range(full_a)), 0, (), 0),
-        ((), 0, tuple(range(1, some)), 0),
-        ((), half_a, (0,), 1),
-        ((), 0, tuple(range(some, full_g)), 1),
+        (tuple(range(some, full_a)), half_a, (), 0),
+        ((), 0, tuple(range(more)), 0),
+        (tuple(range(some)), 0, (), 1),
+        ((), 0, tuple(range(more, full_g)), 1),
     )
     arrays = tuple(
         pltpu.with_memory_space_constraint(array, pltpu.HBM)
@@ -585,7 +585,7 @@
 
 def fits(count_a, count_g):
     (full_a, half_a), full_g = split_rows(count_a), count_g // B
-    if count_a % H or count_g % B or full_a < 1 or full_g < 3:
+    if count_a % H or count_g % B or full_a + half_a < 2 or full_g < 2:
         return False
     return full_a + half_a + full_g <= 2 * (EDGE - 2)
 

time: 38.2 us -> 37.5 us (0.982)
  waiting for transfers between devices: 14 us -> 13.1 us
  starting transfers between devices: 15.6 us -> 16 us
    ppermute x12, waiting for transfers between devices: 14 us -> 13.1 us  [swap(): return lax.ppermute(value, ('dp', 'tensor'), pairs)]
    ppermute x12, starting transfers between devices: 15.6 us -> 16 us  [swap(): return lax.ppermute(value, ('dp', 'tensor'), pairs)]
  transfers between devices with their start and end apart: 12 -> 12, of which waited for: 6 -> 5; matrix products, arithmetic and copies ran while one was open for 0% -> 0% of each run, Pallas kernels for 12% -> 12%
where the time goes in v12:
time: 37.5 us; the launch traced here: 37.3 us
  starting transfers between devices  16 us (43%)
  waiting for transfers between devices  13.1 us (35%)
  Pallas kernels  7.56 us (20%)
  between operations  0.72 us (2%)
    ppermute x12, starting transfers between devices, swap(): return lax.ppermute(value, ('dp', 'tensor'), pairs)  16 us
    ppermute x12, waiting for transfers between devices, swap(): return lax.ppermute(value, ('dp', 'tensor'), pairs)  13.1 us
    pallas_call x4, Pallas kernels, pack(): pl.pallas_call(functools.partial(pack_body, pieces, items, count_a, count...  6.02 us
    pallas_call x1, Pallas kernels, finish(): pl.pallas_call(functools.partial(finish_body, pieces, early, late, count_...  1.11 us
  transfers between devices with their start and end apart: 12, of which 5 were waited for; matrix products, arithmetic and copies ran while one was open for 0% of the time, Pallas kernels for 12%

profile of v12, /device:TPU:0, one launch (start us, length us, event | category | flops | bytes accessed | tf_op | source)
XLA Modules:
  0.0 37.3 jit_solution(12208090305991365682)
XLA Ops:
  0.6 1.8 %shard_map.50 = (f32[4,112,128]{2,1,0:T(8,128)S(1)}, f32[4,64,128]{2,1,0:T(8,128)S(1)}, f32[17,8,128]{2,1,0:T(8,128)S(1)}, bf16[128,2560]{1,0:T(8,128)(2,1)S(1)}) custom-call(bf16[128,2560]{1,0:T(8,128)(2,1)} %refs_0_.1, bf16[128,5120]{1,0:T(8,128)(2,1)} %refs_2_.3, bf16[128,5120]{1,0:T(8,128)(2,1)} %refs_3_.1), custom_call_target="tpu_custom_call" | custom-call | flops 1 | bytes 1 | tf_op jit(solution)/shard_map/pallas_call | solution.py:280
  2.5 3.0 %collective-permute-start.5 = (f32[4,112,128]{2,1,0:T(8,128)S(1)}, f32[4,112,128]{2,1,0:T(8,128)S(1)}, u32[]{:S(2)}, u32[]{:S(2)}) collective-permute-start(f32[4,112,128]{2,1,0:T(8,128)S(1)} %get-tuple-element.53), channel_id=1, source_target_pairs={{0,2},{1,5},{2,0},{3,7},{4,6},{5,1},{6,4},{7,3},{8,10},{9,13},{10,... | collective-permute-start | bytes 688136 | tf_op jit(solution)/shard_map/ppermute | solution.py:511
  5.5 1.6 %collective-permute-start.6 = (f32[4,64,128]{2,1,0:T(8,128)S(1)}, f32[4,64,128]{2,1,0:T(8,128)S(1)}, u32[]{:S(2)}, u32[]{:S(2)}) collective-permute-start(f32[4,64,128]{2,1,0:T(8,128)S(1)} %get-tuple-element.54), channel_id=1, source_target_pairs={{0,4},{1,3},{2,6},{3,1},{4,0},{5,7},{6,2},{7,5},{8,12},{9,11},{10,... | collective-permute-start | bytes 393224 | tf_op jit(solution)/shard_map/ppermute | solution.py:511
  7.0 2.8 %shard_map.51 = (f32[4,136,128]{2,1,0:T(8,128)S(1)}, f32[4,200,128]{2,1,0:T(8,128)S(1)}, f32[17,8,128]{2,1,0:T(8,128)S(1)}, bf16[128,5120]{1,0:T(8,128)(2,1)S(1)}, bf16[128,5120]{1,0:T(8,128)(2,1)S(1)}) custom-call(f32[17,8,128]{2,1,0:T(8,128)S(1)} %get-tuple-element.36.refs_0_, bf16[128,2560]{1,0:T(8,128)(2,1)S(1)} %get-tuple-element.37.refs_1_, ...), custom_call_target="tpu_custom_call" | custom-call | flops 1 | bytes 1 | tf_op jit(solution)/shard_map/pallas_call | solution.py:280
  9.8 0.5 %collective-permute-start.1 = (f32[4,200,128]{2,1,0:T(8,128)S(1)}, f32[4,200,128]{2,1,0:T(8,128)S(1)}, u32[]{:S(2)}, u32[]{:S(2)}) collective-permute-start(f32[4,200,128]{2,1,0:T(8,128)S(1)} %get-tuple-element.45), channel_id=1, source_target_pairs={{0,4},{1,3},{2,6},{3,1},{4,0},{5,7},{6,2},{7,5},{8,12},{9,11},{10,... | collective-permute-start | bytes 1228808 | tf_op jit(solution)/shard_map/ppermute | solution.py:511
  10.4 0.2 collective-permute-start
  10.5 0.4 %shard_map.52 = (f32[4,112,128]{2,1,0:T(8,128)S(1)}, f32[4,64,128]{2,1,0:T(8,128)S(1)}, f32[17,8,128]{2,1,0:T(8,128)S(1)}) custom-call(f32[17,8,128]{2,1,0:T(8,128)S(1)} %get-tuple-element.38.refs_0_, bf16[128,2560]{1,0:T(8,128)(2,1)S(1)} %get-tuple-element.37.refs_1_, bf16[128,5120]{1,0:T(8,128)(2,1)S(1)} %get-tuple-element.39.refs_2_, ...), custom_call_target="tpu_custom_call" | custom-call | flops 1 | bytes 1 | tf_op jit(solution)/shard_map/pallas_call | solution.py:280
  11.0 1.0 %shard_map.53 = (f32[4,136,128]{2,1,0:T(8,128)S(1)}, f32[4,200,128]{2,1,0:T(8,128)S(1)}, f32[17,8,128]{2,1,0:T(8,128)S(1)}) custom-call(f32[17,8,128]{2,1,0:T(8,128)S(1)} %get-tuple-element.41.refs_0_, bf16[128,2560]{1,0:T(8,128)(2,1)S(1)} %get-tuple-element.37.refs_1_, bf16[128,5120]{1,0:T(8,128)(2,1)S(1)} %get-tuple-element.39.refs_2_, ...), custom_call_target="tpu_custom_call" | custom-call | flops 1 | bytes 1 | tf_op jit(solution)/shard_map/pallas_call | solution.py:280
  11.9 0.1 collective-permute-start.2
  12.1 2.0 %collective-permute-start.7 = (f32[2,112,128]{2,1,0:T(8,128)S(1)}, f32[2,112,128]{2,1,0:T(8,128)S(1)}, u32[]{:S(2)}, u32[]{:S(2)}) collective-permute-start(f32[2,112,128]{2,1,0:T(8,128)S(1)} %get-tuple-element.57), channel_id=1, source_target_pairs={{0,4},{1,3},{2,6},{3,1},{4,0},{5,7},{6,2},{7,5},{8,12},{9,11},{10,... | collective-permute-start | bytes 344072 | tf_op jit(solution)/shard_map/ppermute | solution.py:511
  14.1 1.5 %collective-permute-start.8 = (f32[2,64,128]{2,1,0:T(8,128)S(1)}, f32[2,64,128]{2,1,0:T(8,128)S(1)}, u32[]{:S(2)}, u32[]{:S(2)}) collective-permute-start(f32[2,64,128]{2,1,0:T(8,128)S(1)} %get-tuple-element.58), channel_id=1, source_target_pairs={{0,2},{1,5},{2,0},{3,7},{4,6},{5,1},{6,4},{7,3},{8,10},{9,13},{10,... | collective-permute-start | bytes 196616 | tf_op jit(solution)/shard_map/ppermute | solution.py:511
  15.6 0.4 %collective-permute-start.9 = (f32[2,128]{1,0:T(2,128)S(1)}, f32[2,128]{1,0:T(2,128)S(1)}, u32[]{:S(2)}, u32[]{:S(2)}) collective-permute-start(f32[2,128]{1,0:T(2,128)S(1)} %fusion.refs_4_), channel_id=1, source_target_pairs={{0,6},{1,7},{2,4},{3,5},{4,2},{5,3},{6,0},{7,1},{8,14},{9,15},{10,... | collective-permute-start | bytes 3080 | tf_op jit(solution)/shard_map/ppermute | solution.py:511
  16.0 3.9 %collective-permute-done.refs_2_ = f32[4,136,128]{2,1,0:T(8,128)S(1)} collective-permute-done((f32[4,136,128]{2,1,0:T(8,128)S(1)}, f32[4,136,128]{2,1,0:T(8,128)S(1)}, u32[]{:S(2)}, u32[]{:S(2)}) %collective-permute-start) | collective-permute-done | bytes 278560 | tf_op jit(solution)/shard_map/ppermute | solution.py:511
  20.0 0.2 collective-permute-done.1.refs_3_
  20.1 0.1 shard_map.54
  20.2 1.6 %collective-permute-start.4 = (f32[2,200,128]{2,1,0:T(8,128)S(1)}, f32[2,200,128]{2,1,0:T(8,128)S(1)}, u32[]{:S(2)}, u32[]{:S(2)}) collective-permute-start(f32[2,200,128]{2,1,0:T(8,128)S(1)} %get-tuple-element.50), channel_id=1, source_target_pairs={{0,2},{1,5},{2,0},{3,7},{4,6},{5,1},{6,4},{7,3},{8,10},{9,13},{10,... | collective-permute-start | bytes 614408 | tf_op jit(solution)/shard_map/ppermute | solution.py:511
  21.8 0.5 %collective-permute-start.3 = (f32[2,136,128]{2,1,0:T(8,128)S(1)}, f32[2,136,128]{2,1,0:T(8,128)S(1)}, u32[]{:S(2)}, u32[]{:S(2)}) collective-permute-start(f32[2,136,128]{2,1,0:T(8,128)S(1)} %get-tuple-element.49), channel_id=1, source_target_pairs={{0,4},{1,3},{2,6},{3,1},{4,0},{5,7},{6,2},{7,5},{8,12},{9,11},{10,... | collective-permute-start | bytes 417800 | tf_op jit(solution)/shard_map/ppermute | solution.py:511
  22.2 0.1 collective-permute-done.9.refs_5_
  22.3 2.7 %collective-permute-start.11 = (f32[1,176,128]{2,1,0:T(8,128)S(1)}, f32[1,176,128]{2,1,0:T(8,128)S(1)}, u32[]{:S(2)}, u32[]{:S(2)}) collective-permute-start(f32[1,176,128]{2,1,0:T(8,128)S(1)} %get-tuple-element.65), channel_id=1, source_target_pairs={{0,8},{1,9},{2,10},{3,11},{4,12},{5,13},{6,14},{7,15},{8,0},{9,1},... | collective-permute-start | bytes 270344 | tf_op jit(solution)/shard_map/ppermute | solution.py:511
  25.0 3.3 %collective-permute-done.3.refs_2_ = f32[2,136,128]{2,1,0:T(8,128)S(1)} collective-permute-done((f32[2,136,128]{2,1,0:T(8,128)S(1)}, f32[2,136,128]{2,1,0:T(8,128)S(1)}, u32[]{:S(2)}, u32[]{:S(2)}) %collective-permute-start.3) | collective-permute-done | bytes 139296 | tf_op jit(solution)/shard_map/ppermute | solution.py:511
  28.3 2.0 %collective-permute-start.10 = (f32[1,336,128]{2,1,0:T(8,128)S(1)}, f32[1,336,128]{2,1,0:T(8,128)S(1)}, u32[]{:S(2)}, u32[]{:S(2)}) collective-permute-start(f32[1,336,128]{2,1,0:T(8,128)S(1)} %get-tuple-element.62), channel_id=1, source_target_pairs={{0,8},{1,9},{2,10},{3,11},{4,12},{5,13},{6,14},{7,15},{8,0},{9,1},... | collective-permute-start | bytes 516104 | tf_op jit(solution)/shard_map/ppermute | solution.py:511
  30.3 0.2 shard_map.58
  30.6 5.6 %collective-permute-done.10.refs_2_ = f32[1,336,128]{2,1,0:T(8,128)S(1)} collective-permute-done((f32[1,336,128]{2,1,0:T(8,128)S(1)}, f32[1,336,128]{2,1,0:T(8,128)S(1)}, u32[]{:S(2)}, u32[]{:S(2)}) %collective-permute-start.10) | collective-permute-done | bytes 172064 | tf_op jit(solution)/shard_map/ppermute | solution.py:511
  36.2 1.1 %shard_map.59 = (f32[320,128]{1,0:T(8,128)}, f32[640,128]{1,0:T(8,128)}) custom-call(f32[1,136,128]{2,1,0:T(8,128)S(1)} %get-tuple-element.60.refs_0_, f32[1,200,128]{2,1,0:T(8,128)S(1)} %get-tuple-element.61.refs_1_, f32[1,336,128]{2,1,0:T(8,128)S(1)} %collective-permute-done.10.refs_2_, f32[320,128]{1,0:T(8,128)S(1)} %get-tuple-element.66.refs_3_, ...), custom_call_target="tpu_custom_call" | custom-call | tf_op jit(solution)/shard_map/pallas_call | solution.py:487
  (12 shorter events, 0.1 us)
Async XLA Ops:
  2.5 9.6 %collective-permute-start.5 = (f32[4,112,128]{2,1,0:T(8,128)S(1)}, f32[4,112,128]{2,1,0:T(8,128)S(1)}, u32[]{:S(2)}, u32[]{:S(2)}) collective-permute-start(f32[4,112,128]{2,1,0:T(8,128)S(1)} %get-tuple-element.53), channel_id=1, source_target_pairs={{0,2},{1,5},{2,0},{3,7},{4,6},{5,1},{6,4},{7,3},{8,10},{9,13},{10,... | collective-permute-start | bytes 688136 | tf_op jit(solution)/shard_map/ppermute | solution.py:511
  5.5 6.6 %collective-permute-start.6 = (f32[4,64,128]{2,1,0:T(8,128)S(1)}, f32[4,64,128]{2,1,0:T(8,128)S(1)}, u32[]{:S(2)}, u32[]{:S(2)}) collective-permute-start(f32[4,64,128]{2,1,0:T(8,128)S(1)} %get-tuple-element.54), channel_id=1, source_target_pairs={{0,4},{1,3},{2,6},{3,1},{4,0},{5,7},{6,2},{7,5},{8,12},{9,11},{10,... | collective-permute-start | bytes 393224 | tf_op jit(solution)/shard_map/ppermute | solution.py:511
  9.8 10.3 %collective-permute-start.1 = (f32[4,200,128]{2,1,0:T(8,128)S(1)}, f32[4,200,128]{2,1,0:T(8,128)S(1)}, u32[]{:S(2)}, u32[]{:S(2)}) collective-permute-start(f32[4,200,128]{2,1,0:T(8,128)S(1)} %get-tuple-element.45), channel_id=1, source_target_pairs={{0,4},{1,3},{2,6},{3,1},{4,0},{5,7},{6,2},{7,5},{8,12},{9,11},{10,... | collective-permute-start | bytes 1228808 | tf_op jit(solution)/shard_map/ppermute | solution.py:511
  10.4 9.6 %collective-permute-start = (f32[4,136,128]{2,1,0:T(8,128)S(1)}, f32[4,136,128]{2,1,0:T(8,128)S(1)}, u32[]{:S(2)}, u32[]{:S(2)}) collective-permute-start(f32[4,136,128]{2,1,0:T(8,128)S(1)} %get-tuple-element.44), channel_id=1, source_target_pairs={{0,2},{1,5},{2,0},{3,7},{4,6},{5,1},{6,4},{7,3},{8,10},{9,13},{10,... | collective-permute-start | bytes 835592 | tf_op jit(solution)/shard_map/ppermute | solution.py:511
  11.9 3.7 %collective-permute-start.2 = (f32[2,128]{1,0:T(2,128)S(1)}, f32[2,128]{1,0:T(2,128)S(1)}, u32[]{:S(2)}, u32[]{:S(2)}) collective-permute-start(f32[2,128]{1,0:T(2,128)S(1)} %slice_bitcast_fusion), channel_id=1, source_target_pairs={{0,1},{1,0},{2,3},{3,2},{4,5},{5,4},{6,7},{7,6},{8,9},{9,8},{10,11... | collective-permute-start | bytes 3080 | tf_op jit(solution)/shard_map/ppermute | solution.py:511
  12.1 10.2 %collective-permute-start.7 = (f32[2,112,128]{2,1,0:T(8,128)S(1)}, f32[2,112,128]{2,1,0:T(8,128)S(1)}, u32[]{:S(2)}, u32[]{:S(2)}) collective-permute-start(f32[2,112,128]{2,1,0:T(8,128)S(1)} %get-tuple-element.57), channel_id=1, source_target_pairs={{0,4},{1,3},{2,6},{3,1},{4,0},{5,7},{6,2},{7,5},{8,12},{9,11},{10,... | collective-permute-start | bytes 344072 | tf_op jit(solution)/shard_map/ppermute | solution.py:511
  14.1 8.2 %collective-permute-start.8 = (f32[2,64,128]{2,1,0:T(8,128)S(1)}, f32[2,64,128]{2,1,0:T(8,128)S(1)}, u32[]{:S(2)}, u32[]{:S(2)}) collective-permute-start(f32[2,64,128]{2,1,0:T(8,128)S(1)} %get-tuple-element.58), channel_id=1, source_target_pairs={{0,2},{1,5},{2,0},{3,7},{4,6},{5,1},{6,4},{7,3},{8,10},{9,13},{10,... | collective-permute-start | bytes 196616 | tf_op jit(solution)/shard_map/ppermute | solution.py:511
  15.6 6.7 %collective-permute-start.9 = (f32[2,128]{1,0:T(2,128)S(1)}, f32[2,128]{1,0:T(2,128)S(1)}, u32[]{:S(2)}, u32[]{:S(2)}) collective-permute-start(f32[2,128]{1,0:T(2,128)S(1)} %fusion.refs_4_), channel_id=1, source_target_pairs={{0,6},{1,7},{2,4},{3,5},{4,2},{5,3},{6,0},{7,1},{8,14},{9,15},{10,... | collective-permute-start | bytes 3080 | tf_op jit(solution)/shard_map/ppermute | solution.py:511
  20.2 8.1 %collective-permute-start.4 = (f32[2,200,128]{2,1,0:T(8,128)S(1)}, f32[2,200,128]{2,1,0:T(8,128)S(1)}, u32[]{:S(2)}, u32[]{:S(2)}) collective-permute-start(f32[2,200,128]{2,1,0:T(8,128)S(1)} %get-tuple-element.50), channel_id=1, source_target_pairs={{0,2},{1,5},{2,0},{3,7},{4,6},{5,1},{6,4},{7,3},{8,10},{9,13},{10,... | collective-permute-start | bytes 614408 | tf_op jit(solution)/shard_map/ppermute | solution.py:511
  21.8 6.5 %collective-permute-start.3 = (f32[2,136,128]{2,1,0:T(8,128)S(1)}, f32[2,136,128]{2,1,0:T(8,128)S(1)}, u32[]{:S(2)}, u32[]{:S(2)}) collective-permute-start(f32[2,136,128]{2,1,0:T(8,128)S(1)} %get-tuple-element.49), channel_id=1, source_target_pairs={{0,4},{1,3},{2,6},{3,1},{4,0},{5,7},{6,2},{7,5},{8,12},{9,11},{10,... | collective-permute-start | bytes 417800 | tf_op jit(solution)/shard_map/ppermute | solution.py:511
  22.3 8.0 %collective-permute-start.11 = (f32[1,176,128]{2,1,0:T(8,128)S(1)}, f32[1,176,128]{2,1,0:T(8,128)S(1)}, u32[]{:S(2)}, u32[]{:S(2)}) collective-permute-start(f32[1,176,128]{2,1,0:T(8,128)S(1)} %get-tuple-element.65), channel_id=1, source_target_pairs={{0,8},{1,9},{2,10},{3,11},{4,12},{5,13},{6,14},{7,15},{8,0},{9,1},... | collective-permute-start | bytes 270344 | tf_op jit(solution)/shard_map/ppermute | solution.py:511
  28.3 7.9 %collective-permute-start.10 = (f32[1,336,128]{2,1,0:T(8,128)S(1)}, f32[1,336,128]{2,1,0:T(8,128)S(1)}, u32[]{:S(2)}, u32[]{:S(2)}) collective-permute-start(f32[1,336,128]{2,1,0:T(8,128)S(1)} %get-tuple-element.62), channel_id=1, source_target_pairs={{0,8},{1,9},{2,10},{3,11},{4,12},{5,13},{6,14},{7,15},{8,0},{9,1},... | collective-permute-start | bytes 516104 | tf_op jit(solution)/shard_map/ppermute | solution.py:511

commit v13 on v12

--- a/solution.py
+++ b/solution.py
@@ -102,68 +102,31 @@
 
 
 LOADS = 4
-
-
-def pack_body(pieces, items, count_a, count_g, call, *refs):
+FIRST = 4 * 10**9
+
+
+def pack_body(pieces, items, count_a, count_g, fresh, *refs):
     n = len(items)
-    refs = list(refs)
-
-    def pop(count):
-        taken = refs[:count]
-        del refs[:count]
-        return taken
-
-    notes_in = pop(call > 0)
-    arrays = pop(3)
-    outs, (notes,) = pop(n), pop(1)
-    held = pop(1) if call == 0 else arrays[:1] + pop(2) if call == 1 else arrays
-    columns, sems = (pop(2) if call == 0 else None), (pop(1) if call < 2 else None)
-    fresh = call == 0
-    notes_in = notes_in[0] if notes_in else None
+    if fresh:
+        (a_hbm, *outs), (notes, a_held, sems) = refs[: n + 1], refs[n + 1 :]
+        rows = a_hbm.shape[0] // LOADS
+        parts = [slice(part * rows, (part + 1) * rows) for part in range(LOADS)]
+        copies = [
+            pltpu.make_async_copy(a_hbm.at[part], a_held.at[part], sems.at[i])
+            for i, part in enumerate(parts)
+        ]
+        for copy in copies:
+            copy.start()
+        held = (a_held,)
+    else:
+        copies = []
+        notes_in, held, outs, notes = refs[0], refs[1:4], refs[4 : 4 + n], refs[4 + n]
     full, half = split_rows(count_a)
     slots = SLOTS // 2
     split = [(i, k, first, slot) for i, (k, first) in enumerate(items) for slot in range(slots)]
 
-    def whole(i):
-        rows = arrays[i].shape[0] // LOADS
-        return [
-            pltpu.make_async_copy(
-                arrays[i].at[part * rows : (part + 1) * rows],
-                held[i].at[part * rows : (part + 1) * rows],
-                sems[0].at[i, part],
-            )
-            for part in range(LOADS)
-        ]
-
-    def own_columns():
-        found = []
-        for i, k, first, slot in split:
-            g_blocks, kind = pieces[k][2:]
-            if g_blocks:
-                start = slot_owner(first + slot, KINDS[kind]) * count_g + g_blocks[0] * B
-                size = len(g_blocks) * B
-                for m in (0, 1):
-                    src = arrays[1 + m].at[:, pl.ds(pl.multiple_of(start, B), size)]
-                    dst = columns[m].at[i * slots + slot, :, :size]
-                    sem = sems[0].at[1 + m, i * slots + slot]
-                    found.append(pltpu.make_async_copy(src, dst, sem))
-        return found
-
-    early = whole(0) if call == 0 else []
-    late = own_columns() if call == 0 else whole(1) + whole(2) if call == 1 else []
-    for copy in early + late:
-        copy.start()
-
     def read(i, start):
         return held[i][:, pl.ds(pl.multiple_of(start, B), B)]
-
-    def read_g(i, k, first, slot, b):
-        _, _, g_blocks, kind = pieces[k]
-        if call == 0:
-            part = slice((b - g_blocks[0]) * B, (b - g_blocks[0] + 1) * B)
-            return [columns[m][i * slots + slot, :, part] for m in (0, 1)]
-        start = slot_owner(first + slot, KINDS[kind]) * count_g + b * B
-        return [read(1, start), read(2, start)]
 
     row, col = iotas(H)
     low = col < row
@@ -222,31 +185,29 @@
             at = at + quarter * 3 // 2
         return at
 
-    def g_parts(i, k, first, slot, index, at):
+    def g_parts(out, k, first, slot, index, at):
         _, _, g_blocks, kind = pieces[k]
         here = kind * SLOTS + first + slot
+        owner = slot_owner(first + slot, KINDS[kind])
         for b in g_blocks:
-            value, grad = (part.astype(jnp.float32) for part in read_g(i, k, first, slot, b))
+            start = owner * count_g + b * B
+            value, grad = read(1, start).astype(jnp.float32), read(2, start).astype(jnp.float32)
             block = cov((grad * gelu_slope(value)).astype(jnp.bfloat16))
-            outs[i][slot, at : at + H, :] = fold(block, here, next(index), 1)
+            out[slot, at : at + H, :] = fold(block, here, next(index), 1)
             at = at + H
         return at
 
-    for copy in early:
+    for copy in copies:
         copy.wait()
-    begun = []
     for i, k, first, slot in split:
         here = pieces[k][3] * SLOTS + first + slot
         if here not in tiles:
             tiles[here] = jnp.zeros((EDGE, B), jnp.float32) if fresh else notes_in[here]
         index = corner_indices(pieces, k)
-        begun.append((index, a_parts(outs[i], k, first, slot, index)))
-    for copy in late:
-        copy.wait()
-    for (i, k, first, slot), (index, at) in zip(split, begun):
-        at = g_parts(i, k, first, slot, index, at)
+        at = a_parts(outs[i], k, first, slot, index)
+        at = g_parts(outs[i], k, first, slot, index, at)
         if has_edge(pieces, k):
-            outs[i][slot, at:, :] = tiles[pieces[k][3] * SLOTS + first + slot]
+            outs[i][slot, at:, :] = tiles[here]
 
     for slot in range(NOTES):
         if slot in tiles:
@@ -258,33 +219,29 @@
     notes[NOTES] = tile if fresh else notes_in[NOTES] + tile
 
 
-def pack(arrays, pieces, items, count_a, count_g, call, notes):
+def pack(arrays, pieces, items, count_a, count_g, notes):
     slots = SLOTS // 2
+    fresh = notes is None
     out_shape = [
         jax.ShapeDtypeStruct((slots, piece_rows(pieces, k), B), jnp.float32) for k, _ in items
     ]
     out_shape.append(jax.ShapeDtypeStruct((NOTES + 1, EDGE, B), jnp.float32))
-    moved = arrays[:1] if call == 0 else arrays[1:] if call == 1 else ()
-    out_shape += [jax.ShapeDtypeStruct(array.shape, array.dtype) for array in moved]
-    scratch = []
-    if call == 0:
-        width = max(len(pieces[k][2]) for k, _ in items) * B
-        shape = (len(items) * slots, arrays[1].shape[0], max(width, B))
-        scratch += [pltpu.VMEM(shape, arrays[1].dtype)] * 2
-    if call < 2:
-        scratch.append(pltpu.SemaphoreType.DMA((3, max(LOADS, len(items) * slots))))
-    spaces = [pltpu.HBM] * 3 if call == 0 else [pltpu.VMEM] + [pltpu.HBM] * 2
-    spaces = [pltpu.VMEM] * 3 if call > 1 else spaces
-    args = [*([notes] if call else []), *arrays]
-    spaces = [pltpu.VMEM] * (call > 0) + spaces
+    if fresh:
+        args = [pltpu.with_memory_space_constraint(arrays[0], pltpu.HBM)]
+        out_shape.append(jax.ShapeDtypeStruct(arrays[0].shape, arrays[0].dtype))
+    else:
+        args = [notes, *arrays]
+    space = pltpu.HBM if fresh else pltpu.VMEM
     outs = pl.pallas_call(
-        functools.partial(pack_body, pieces, items, count_a, count_g, call),
-        in_specs=[pl.BlockSpec(memory_space=space) for space in spaces],
+        functools.partial(pack_body, pieces, items, count_a, count_g, fresh),
+        in_specs=[pl.BlockSpec(memory_space=space)] * len(args),
         out_specs=[pl.BlockSpec(memory_space=pltpu.VMEM)] * len(out_shape),
         out_shape=out_shape,
-        scratch_shapes=scratch,
+        scratch_shapes=[pltpu.SemaphoreType.DMA((LOADS,))] * fresh,
         compiler_params=pltpu.CompilerParams(vmem_limit_bytes=32 * 2**20),
-        cost_estimate=pl.CostEstimate(flops=1, bytes_accessed=1, transcendentals=0),
+        cost_estimate=pl.CostEstimate(
+            flops=FIRST if fresh else 1, bytes_accessed=1, transcendentals=0
+        ),
     )(*args)
     n = len(items)
     return outs[:n], outs[n], outs[n + 1 :]
@@ -529,19 +486,16 @@
         (tuple(range(some)), 0, (), 1),
         ((), 0, tuple(range(more, full_g)), 1),
     )
-    arrays = tuple(
-        pltpu.with_memory_space_constraint(array, pltpu.HBM)
-        for array in (saved_input, saved_pre, grad_act)
-    )
+    arrays = (saved_input, saved_pre, grad_act)
     keep, send = 0, SLOTS // 2
     early, late = (0, 2), (1, 3)
     keeps, gots, notes = {}, {}, None
 
-    def pack_next(call, first, ks):
+    def pack_next(first, ks):
         nonlocal notes, arrays
         items = tuple((k, first) for k in ks)
-        parts, notes, held = pack(arrays, pieces, items, count_a, count_g, call, notes)
-        arrays = (*arrays[:call], *held, *arrays[call + len(held) :])
+        parts, notes, held = pack(arrays, pieces, items, count_a, count_g, notes)
+        arrays = (*held, *arrays[len(held) :])
         return dict(zip(ks, parts))
 
     def exchange(parts, stage):
@@ -560,10 +514,10 @@
             exchange(dict(zip(ks, parts)), stage)
         return others
 
-    exchange(pack_next(0, send, early), 0)
-    exchange(pack_next(1, send, late), 0)
-    keeps.update(pack_next(2, keep, early))
-    keeps.update(pack_next(3, keep, late))
+    exchange(pack_next(send, early), 0)
+    exchange(pack_next(send, late), 0)
+    keeps.update(pack_next(keep, early))
+    keeps.update(pack_next(keep, late))
 
     trace = notes[NOTES, :2, :]
     trace = trace + swap(trace, lambda i, j: (i, j ^ 1))

time: 37.5 us -> 38.4 us (1.024)
  Pallas kernels: 7.56 us -> 5.65 us
  starting transfers between devices: 16 us -> 17.6 us
  waiting for transfers between devices: 13.1 us -> 13.9 us
    pallas_call x4, Pallas kernels: 6.02 us -> 4.11 us  [pack(): pl.pallas_call(functools.partial(pack_body, pieces, items, count_a, count...]
    ppermute x12, starting transfers between devices: 16 us -> 17.6 us  [swap(): return lax.ppermute(value, ('dp', 'tensor'), pairs)]
    ppermute x12, waiting for transfers between devices: 13.1 us -> 13.9 us  [swap(): return lax.ppermute(value, ('dp', 'tensor'), pairs)]
  transfers between devices with their start and end apart: 12 -> 12, of which waited for: 5 -> 6; matrix products, arithmetic and copies ran while one was open for 0% -> 0% of each run, Pallas kernels for 12% -> 7%
where the time goes in v13:
time: 38.4 us; the launch traced here: 37.9 us
  starting transfers between devices  17.6 us (46%)
  waiting for transfers between devices  13.9 us (36%)
  Pallas kernels  5.65 us (15%)
  between operations  0.72 us (2%)
    ppermute x12, starting transfers between devices, swap(): return lax.ppermute(value, ('dp', 'tensor'), pairs)  17.6 us
    ppermute x12, waiting for transfers between devices, swap(): return lax.ppermute(value, ('dp', 'tensor'), pairs)  13.9 us
    pallas_call x4, Pallas kernels, pack(): pl.pallas_call(functools.partial(pack_body, pieces, items, count_a, count...  4.11 us
    pallas_call x1, Pallas kernels, finish(): pl.pallas_call(functools.partial(finish_body, pieces, early, late, count_...  1.11 us
  transfers between devices with their start and end apart: 12, of which 6 were waited for; matrix products, arithmetic and copies ran while one was open for 0% of the time, Pallas kernels for 7%

profile of v13, /device:TPU:0, one launch (start us, length us, event | category | flops | bytes accessed | tf_op | source)
XLA Modules:
  0.0 37.9 jit_solution(16988634768036083223)
XLA Ops:
  0.6 1.8 %shard_map.50 = (f32[4,112,128]{2,1,0:T(8,128)S(1)}, f32[4,64,128]{2,1,0:T(8,128)S(1)}, f32[17,8,128]{2,1,0:T(8,128)S(1)}, bf16[128,2560]{1,0:T(8,128)(2,1)S(1)}) custom-call(bf16[128,2560]{1,0:T(8,128)(2,1)} %refs_0_.1), custom_call_target="tpu_custom_call" | custom-call | flops 4000000000 | bytes 1 | tf_op jit(solution)/shard_map/pallas_call | solution.py:235
  2.4 3.0 %collective-permute-start.5 = (f32[4,112,128]{2,1,0:T(8,128)S(1)}, f32[4,112,128]{2,1,0:T(8,128)S(1)}, u32[]{:S(2)}, u32[]{:S(2)}) collective-permute-start(f32[4,112,128]{2,1,0:T(8,128)S(1)} %get-tuple-element.49), channel_id=1, source_target_pairs={{0,2},{1,5},{2,0},{3,7},{4,6},{5,1},{6,4},{7,3},{8,10},{9,13},{10,... | collective-permute-start | bytes 688136 | tf_op jit(solution)/shard_map/ppermute | solution.py:468
  5.4 1.6 %collective-permute-start.6 = (f32[4,64,128]{2,1,0:T(8,128)S(1)}, f32[4,64,128]{2,1,0:T(8,128)S(1)}, u32[]{:S(2)}, u32[]{:S(2)}) collective-permute-start(f32[4,64,128]{2,1,0:T(8,128)S(1)} %get-tuple-element.50), channel_id=1, source_target_pairs={{0,4},{1,3},{2,6},{3,1},{4,0},{5,7},{6,2},{7,5},{8,12},{9,11},{10,... | collective-permute-start | bytes 393224 | tf_op jit(solution)/shard_map/ppermute | solution.py:468
  7.0 0.9 %shard_map.51 = (f32[4,136,128]{2,1,0:T(8,128)S(1)}, f32[4,200,128]{2,1,0:T(8,128)S(1)}, f32[17,8,128]{2,1,0:T(8,128)S(1)}) custom-call(f32[17,8,128]{2,1,0:T(8,128)S(1)} %get-tuple-element.34.refs_0_, bf16[128,2560]{1,0:T(8,128)(2,1)S(1)} %get-tuple-element.35.refs_1_, bf16[128,5120]{1,0:T(8,128)(2,1)S(1)} %copy-done, bf16[128,5120]{1,0:T(8,128)(2,1)S(1)} %copy-done.1), custom_call_target="tpu_custom_call" | custom-call | flops 1 | bytes 1 | tf_op jit(solution)/shard_map/pallas_call | solution.py:235
  8.0 0.6 %collective-permute-start = (f32[4,136,128]{2,1,0:T(8,128)S(1)}, f32[4,136,128]{2,1,0:T(8,128)S(1)}, u32[]{:S(2)}, u32[]{:S(2)}) collective-permute-start(f32[4,136,128]{2,1,0:T(8,128)S(1)} %get-tuple-element.40), channel_id=1, source_target_pairs={{0,2},{1,5},{2,0},{3,7},{4,6},{5,1},{6,4},{7,3},{8,10},{9,13},{10,... | collective-permute-start | bytes 835592 | tf_op jit(solution)/shard_map/ppermute | solution.py:468
  8.6 0.4 %shard_map.52 = (f32[4,112,128]{2,1,0:T(8,128)S(1)}, f32[4,64,128]{2,1,0:T(8,128)S(1)}, f32[17,8,128]{2,1,0:T(8,128)S(1)}) custom-call(f32[17,8,128]{2,1,0:T(8,128)S(1)} %get-tuple-element.36.refs_0_, bf16[128,2560]{1,0:T(8,128)(2,1)S(1)} %get-tuple-element.35.refs_1_, bf16[128,5120]{1,0:T(8,128)(2,1)S(1)} %copy-done, bf16[128,5120]{1,0:T(8,128)(2,1)S(1)} %copy-done.1), custom_call_target="tpu_custom_call" | custom-call | flops 1 | bytes 1 | tf_op jit(solution)/shard_map/pallas_call | solution.py:235
  9.0 0.9 %shard_map.53 = (f32[4,136,128]{2,1,0:T(8,128)S(1)}, f32[4,200,128]{2,1,0:T(8,128)S(1)}, f32[17,8,128]{2,1,0:T(8,128)S(1)}) custom-call(f32[17,8,128]{2,1,0:T(8,128)S(1)} %get-tuple-element.37.refs_0_, bf16[128,2560]{1,0:T(8,128)(2,1)S(1)} %get-tuple-element.35.refs_1_, bf16[128,5120]{1,0:T(8,128)(2,1)S(1)} %copy-done, bf16[128,5120]{1,0:T(8,128)(2,1)S(1)} %copy-done.1), custom_call_target="tpu_custom_call" | custom-call | flops 1 | bytes 1 | tf_op jit(solution)/shard_map/pallas_call | solution.py:235
  10.0 0.1 collective-permute-start.2
  10.1 0.9 %collective-permute-done.6.refs_3_ = f32[4,64,128]{2,1,0:T(8,128)S(1)} collective-permute-done((f32[4,64,128]{2,1,0:T(8,128)S(1)}, f32[4,64,128]{2,1,0:T(8,128)S(1)}, u32[]{:S(2)}, u32[]{:S(2)}) %collective-permute-start.6) | collective-permute-done | bytes 131104 | tf_op jit(solution)/shard_map/ppermute | solution.py:468
  11.0 0.3 collective-permute-done.5.refs_2_
  11.3 2.5 %collective-permute-start.8 = (f32[2,64,128]{2,1,0:T(8,128)S(1)}, f32[2,64,128]{2,1,0:T(8,128)S(1)}, u32[]{:S(2)}, u32[]{:S(2)}) collective-permute-start(f32[2,64,128]{2,1,0:T(8,128)S(1)} %get-tuple-element.54), channel_id=1, source_target_pairs={{0,2},{1,5},{2,0},{3,7},{4,6},{5,1},{6,4},{7,3},{8,10},{9,13},{10,... | collective-permute-start | bytes 196616 | tf_op jit(solution)/shard_map/ppermute | solution.py:468
  13.9 0.9 %collective-permute-start.7 = (f32[2,112,128]{2,1,0:T(8,128)S(1)}, f32[2,112,128]{2,1,0:T(8,128)S(1)}, u32[]{:S(2)}, u32[]{:S(2)}) collective-permute-start(f32[2,112,128]{2,1,0:T(8,128)S(1)} %get-tuple-element.53), channel_id=1, source_target_pairs={{0,4},{1,3},{2,6},{3,1},{4,0},{5,7},{6,2},{7,5},{8,12},{9,11},{10,... | collective-permute-start | bytes 344072 | tf_op jit(solution)/shard_map/ppermute | solution.py:468
  14.8 0.6 %collective-permute-start.9 = (f32[2,128]{1,0:T(2,128)S(1)}, f32[2,128]{1,0:T(2,128)S(1)}, u32[]{:S(2)}, u32[]{:S(2)}) collective-permute-start(f32[2,128]{1,0:T(2,128)S(1)} %fusion.refs_4_), channel_id=1, source_target_pairs={{0,6},{1,7},{2,4},{3,5},{4,2},{5,3},{6,0},{7,1},{8,14},{9,15},{10,... | collective-permute-start | bytes 3080 | tf_op jit(solution)/shard_map/ppermute | solution.py:468
  15.4 2.2 %collective-permute-done.refs_2_ = f32[4,136,128]{2,1,0:T(8,128)S(1)} collective-permute-done((f32[4,136,128]{2,1,0:T(8,128)S(1)}, f32[4,136,128]{2,1,0:T(8,128)S(1)}, u32[]{:S(2)}, u32[]{:S(2)}) %collective-permute-start) | collective-permute-done | bytes 278560 | tf_op jit(solution)/shard_map/ppermute | solution.py:468
  17.6 0.9 %collective-permute-done.1.refs_3_ = f32[4,200,128]{2,1,0:T(8,128)S(1)} collective-permute-done((f32[4,200,128]{2,1,0:T(8,128)S(1)}, f32[4,200,128]{2,1,0:T(8,128)S(1)}, u32[]{:S(2)}, u32[]{:S(2)}) %collective-permute-start.1) | collective-permute-done | bytes 409632 | tf_op jit(solution)/shard_map/ppermute | solution.py:468
  18.5 0.1 shard_map.54
  18.6 1.5 %collective-permute-start.3 = (f32[2,136,128]{2,1,0:T(8,128)S(1)}, f32[2,136,128]{2,1,0:T(8,128)S(1)}, u32[]{:S(2)}, u32[]{:S(2)}) collective-permute-start(f32[2,136,128]{2,1,0:T(8,128)S(1)} %get-tuple-element.45), channel_id=1, source_target_pairs={{0,4},{1,3},{2,6},{3,1},{4,0},{5,7},{6,2},{7,5},{8,12},{9,11},{10,... | collective-permute-start | bytes 417800 | tf_op jit(solution)/shard_map/ppermute | solution.py:468
  20.0 1.5 %collective-permute-start.4 = (f32[2,200,128]{2,1,0:T(8,128)S(1)}, f32[2,200,128]{2,1,0:T(8,128)S(1)}, u32[]{:S(2)}, u32[]{:S(2)}) collective-permute-start(f32[2,200,128]{2,1,0:T(8,128)S(1)} %get-tuple-element.46), channel_id=1, source_target_pairs={{0,2},{1,5},{2,0},{3,7},{4,6},{5,1},{6,4},{7,3},{8,10},{9,13},{10,... | collective-permute-start | bytes 614408 | tf_op jit(solution)/shard_map/ppermute | solution.py:468
  21.6 2.7 %collective-permute-start.11 = (f32[1,176,128]{2,1,0:T(8,128)S(1)}, f32[1,176,128]{2,1,0:T(8,128)S(1)}, u32[]{:S(2)}, u32[]{:S(2)}) collective-permute-start(f32[1,176,128]{2,1,0:T(8,128)S(1)} %get-tuple-element.61), channel_id=1, source_target_pairs={{0,8},{1,9},{2,10},{3,11},{4,12},{5,13},{6,14},{7,15},{8,0},{9,1},... | collective-permute-start | bytes 270344 | tf_op jit(solution)/shard_map/ppermute | solution.py:468
  24.2 1.6 %collective-permute-done.4.refs_3_ = f32[2,200,128]{2,1,0:T(8,128)S(1)} collective-permute-done((f32[2,200,128]{2,1,0:T(8,128)S(1)}, f32[2,200,128]{2,1,0:T(8,128)S(1)}, u32[]{:S(2)}, u32[]{:S(2)}) %collective-permute-start.4) | collective-permute-done | bytes 204832 | tf_op jit(solution)/shard_map/ppermute | solution.py:468
  25.9 2.7 %collective-permute-start.10 = (f32[1,336,128]{2,1,0:T(8,128)S(1)}, f32[1,336,128]{2,1,0:T(8,128)S(1)}, u32[]{:S(2)}, u32[]{:S(2)}) collective-permute-start(f32[1,336,128]{2,1,0:T(8,128)S(1)} %get-tuple-element.58), channel_id=1, source_target_pairs={{0,8},{1,9},{2,10},{3,11},{4,12},{5,13},{6,14},{7,15},{8,0},{9,1},... | collective-permute-start | bytes 516104 | tf_op jit(solution)/shard_map/ppermute | solution.py:468
  28.5 0.2 shard_map.58
  28.8 8.1 %collective-permute-done.10.refs_2_ = f32[1,336,128]{2,1,0:T(8,128)S(1)} collective-permute-done((f32[1,336,128]{2,1,0:T(8,128)S(1)}, f32[1,336,128]{2,1,0:T(8,128)S(1)}, u32[]{:S(2)}, u32[]{:S(2)}) %collective-permute-start.10) | collective-permute-done | bytes 172064 | tf_op jit(solution)/shard_map/ppermute | solution.py:468
  36.8 1.1 %shard_map.59 = (f32[320,128]{1,0:T(8,128)}, f32[640,128]{1,0:T(8,128)}) custom-call(f32[1,136,128]{2,1,0:T(8,128)S(1)} %get-tuple-element.56.refs_0_, f32[1,200,128]{2,1,0:T(8,128)S(1)} %get-tuple-element.57.refs_1_, f32[1,336,128]{2,1,0:T(8,128)S(1)} %collective-permute-done.10.refs_2_, f32[320,128]{1,0:T(8,128)S(1)} %get-tuple-element.62.refs_3_, ...), custom_call_target="tpu_custom_call" | custom-call | tf_op jit(solution)/shard_map/pallas_call | solution.py:444
  (16 shorter events, 0.2 us)
Async XLA Ops:
  0.6 6.4 %copy-start.1 = (bf16[128,5120]{1,0:T(8,128)(2,1)S(1)}, bf16[128,5120]{1,0:T(8,128)(2,1)}, u32[]{:S(2)}) copy-start(bf16[128,5120]{1,0:T(8,128)(2,1)} %refs_3_.5) | copy-start | bytes 3932164
  0.6 6.4 %copy-start = (bf16[128,5120]{1,0:T(8,128)(2,1)S(1)}, bf16[128,5120]{1,0:T(8,128)(2,1)}, u32[]{:S(2)}) copy-start(bf16[128,5120]{1,0:T(8,128)(2,1)} %refs_2_.5) | copy-start | bytes 3932164
  2.4 8.8 %collective-permute-start.5 = (f32[4,112,128]{2,1,0:T(8,128)S(1)}, f32[4,112,128]{2,1,0:T(8,128)S(1)}, u32[]{:S(2)}, u32[]{:S(2)}) collective-permute-start(f32[4,112,128]{2,1,0:T(8,128)S(1)} %get-tuple-element.49), channel_id=1, source_target_pairs={{0,2},{1,5},{2,0},{3,7},{4,6},{5,1},{6,4},{7,3},{8,10},{9,13},{10,... | collective-permute-start | bytes 688136 | tf_op jit(solution)/shard_map/ppermute | solution.py:468
  5.4 5.5 %collective-permute-start.6 = (f32[4,64,128]{2,1,0:T(8,128)S(1)}, f32[4,64,128]{2,1,0:T(8,128)S(1)}, u32[]{:S(2)}, u32[]{:S(2)}) collective-permute-start(f32[4,64,128]{2,1,0:T(8,128)S(1)} %get-tuple-element.50), channel_id=1, source_target_pairs={{0,4},{1,3},{2,6},{3,1},{4,0},{5,7},{6,2},{7,5},{8,12},{9,11},{10,... | collective-permute-start | bytes 393224 | tf_op jit(solution)/shard_map/ppermute | solution.py:468
  8.0 9.7 %collective-permute-start = (f32[4,136,128]{2,1,0:T(8,128)S(1)}, f32[4,136,128]{2,1,0:T(8,128)S(1)}, u32[]{:S(2)}, u32[]{:S(2)}) collective-permute-start(f32[4,136,128]{2,1,0:T(8,128)S(1)} %get-tuple-element.40), channel_id=1, source_target_pairs={{0,2},{1,5},{2,0},{3,7},{4,6},{5,1},{6,4},{7,3},{8,10},{9,13},{10,... | collective-permute-start | bytes 835592 | tf_op jit(solution)/shard_map/ppermute | solution.py:468
  8.6 9.9 %collective-permute-start.1 = (f32[4,200,128]{2,1,0:T(8,128)S(1)}, f32[4,200,128]{2,1,0:T(8,128)S(1)}, u32[]{:S(2)}, u32[]{:S(2)}) collective-permute-start(f32[4,200,128]{2,1,0:T(8,128)S(1)} %get-tuple-element.41), channel_id=1, source_target_pairs={{0,4},{1,3},{2,6},{3,1},{4,0},{5,7},{6,2},{7,5},{8,12},{9,11},{10,... | collective-permute-start | bytes 1228808 | tf_op jit(solution)/shard_map/ppermute | solution.py:468
  10.0 4.8 %collective-permute-start.2 = (f32[2,128]{1,0:T(2,128)S(1)}, f32[2,128]{1,0:T(2,128)S(1)}, u32[]{:S(2)}, u32[]{:S(2)}) collective-permute-start(f32[2,128]{1,0:T(2,128)S(1)} %slice_bitcast_fusion), channel_id=1, source_target_pairs={{0,1},{1,0},{2,3},{3,2},{4,5},{5,4},{6,7},{7,6},{8,9},{9,8},{10,11... | collective-permute-start | bytes 3080 | tf_op jit(solution)/shard_map/ppermute | solution.py:468
  11.3 10.2 %collective-permute-start.8 = (f32[2,64,128]{2,1,0:T(8,128)S(1)}, f32[2,64,128]{2,1,0:T(8,128)S(1)}, u32[]{:S(2)}, u32[]{:S(2)}) collective-permute-start(f32[2,64,128]{2,1,0:T(8,128)S(1)} %get-tuple-element.54), channel_id=1, source_target_pairs={{0,2},{1,5},{2,0},{3,7},{4,6},{5,1},{6,4},{7,3},{8,10},{9,13},{10,... | collective-permute-start | bytes 196616 | tf_op jit(solution)/shard_map/ppermute | solution.py:468
  13.9 7.7 %collective-permute-start.7 = (f32[2,112,128]{2,1,0:T(8,128)S(1)}, f32[2,112,128]{2,1,0:T(8,128)S(1)}, u32[]{:S(2)}, u32[]{:S(2)}) collective-permute-start(f32[2,112,128]{2,1,0:T(8,128)S(1)} %get-tuple-element.53), channel_id=1, source_target_pairs={{0,4},{1,3},{2,6},{3,1},{4,0},{5,7},{6,2},{7,5},{8,12},{9,11},{10,... | collective-permute-start | bytes 344072 | tf_op jit(solution)/shard_map/ppermute | solution.py:468
  14.8 6.7 %collective-permute-start.9 = (f32[2,128]{1,0:T(2,128)S(1)}, f32[2,128]{1,0:T(2,128)S(1)}, u32[]{:S(2)}, u32[]{:S(2)}) collective-permute-start(f32[2,128]{1,0:T(2,128)S(1)} %fusion.refs_4_), channel_id=1, source_target_pairs={{0,6},{1,7},{2,4},{3,5},{4,2},{5,3},{6,0},{7,1},{8,14},{9,15},{10,... | collective-permute-start | bytes 3080 | tf_op jit(solution)/shard_map/ppermute | solution.py:468
  18.6 5.7 %collective-permute-start.3 = (f32[2,136,128]{2,1,0:T(8,128)S(1)}, f32[2,136,128]{2,1,0:T(8,128)S(1)}, u32[]{:S(2)}, u32[]{:S(2)}) collective-permute-start(f32[2,136,128]{2,1,0:T(8,128)S(1)} %get-tuple-element.45), channel_id=1, source_target_pairs={{0,4},{1,3},{2,6},{3,1},{4,0},{5,7},{6,2},{7,5},{8,12},{9,11},{10,... | collective-permute-start | bytes 417800 | tf_op jit(solution)/shard_map/ppermute | solution.py:468
  20.0 5.8 %collective-permute-start.4 = (f32[2,200,128]{2,1,0:T(8,128)S(1)}, f32[2,200,128]{2,1,0:T(8,128)S(1)}, u32[]{:S(2)}, u32[]{:S(2)}) collective-permute-start(f32[2,200,128]{2,1,0:T(8,128)S(1)} %get-tuple-element.46), channel_id=1, source_target_pairs={{0,2},{1,5},{2,0},{3,7},{4,6},{5,1},{6,4},{7,3},{8,10},{9,13},{10,... | collective-permute-start | bytes 614408 | tf_op jit(solution)/shard_map/ppermute | solution.py:468
  21.6 6.9 %collective-permute-start.11 = (f32[1,176,128]{2,1,0:T(8,128)S(1)}, f32[1,176,128]{2,1,0:T(8,128)S(1)}, u32[]{:S(2)}, u32[]{:S(2)}) collective-permute-start(f32[1,176,128]{2,1,0:T(8,128)S(1)} %get-tuple-element.61), channel_id=1, source_target_pairs={{0,8},{1,9},{2,10},{3,11},{4,12},{5,13},{6,14},{7,15},{8,0},{9,1},... | collective-permute-start | bytes 270344 | tf_op jit(solution)/shard_map/ppermute | solution.py:468
  25.9 11.0 %collective-permute-start.10 = (f32[1,336,128]{2,1,0:T(8,128)S(1)}, f32[1,336,128]{2,1,0:T(8,128)S(1)}, u32[]{:S(2)}, u32[]{:S(2)}) collective-permute-start(f32[1,336,128]{2,1,0:T(8,128)S(1)} %get-tuple-element.58), channel_id=1, source_target_pairs={{0,8},{1,9},{2,10},{3,11},{4,12},{5,13},{6,14},{7,15},{8,0},{9,1},... | collective-permute-start | bytes 516104 | tf_op jit(solution)/shard_map/ppermute | solution.py:468

commit v14 on v13

--- a/solution.py
+++ b/solution.py
@@ -479,12 +479,12 @@
     count_g = saved_pre.shape[1] // dp
     full_a, half_a = split_rows(count_a)
     full_g, _ = split_rows(count_g)
-    some, more = (full_a + 1) // 2, full_g // 2
+    some = 1 + (full_g - 1) // 2
     pieces = (
-        (tuple(range(some, full_a)), half_a, (), 0),
-        ((), 0, tuple(range(more)), 0),
-        (tuple(range(some)), 0, (), 1),
-        ((), 0, tuple(range(more, full_g)), 1),
+        (tuple(range(full_a)), 0, (), 0),
+        ((), 0, tuple(range(1, some)), 0),
+        ((), half_a, (0,), 1),
+        ((), 0, tuple(range(some, full_g)), 1),
     )
     arrays = (saved_input, saved_pre, grad_act)
     keep, send = 0, SLOTS // 2
@@ -514,7 +514,8 @@
             exchange(dict(zip(ks, parts)), stage)
         return others
 
-    exchange(pack_next(send, early), 0)
+    exchange(pack_next(send, early[:1]), 0)
+    exchange(pack_next(send, early[1:]), 0)
     exchange(pack_next(send, late), 0)
     keeps.update(pack_next(keep, early))
     keeps.update(pack_next(keep, late))
@@ -539,7 +540,7 @@
 
 def fits(count_a, count_g):
     (full_a, half_a), full_g = split_rows(count_a), count_g // B
-    if count_a % H or count_g % B or full_a + half_a < 2 or full_g < 2:
+    if count_a % H or count_g % B or full_a < 1 or full_g < 3:
         return False
     return full_a + half_a + full_g <= 2 * (EDGE - 2)
 

time: 38.4 us -> 37.8 us (0.984)
  starting transfers between devices: 17.6 us -> 15.4 us
  waiting for transfers between devices: 13.9 us -> 15.8 us
    ppermute x12, starting transfers between devices: 17.6 us -> 15.4 us  [swap(): return lax.ppermute(value, ('dp', 'tensor'), pairs)]
    ppermute x12, waiting for transfers between devices: 13.9 us -> 15.8 us  [swap(): return lax.ppermute(value, ('dp', 'tensor'), pairs)]
    pallas_call x4 -> x5, Pallas kernels: 4.11 us -> 4.25 us  [pack(): pl.pallas_call(functools.partial(pack_body, pieces, items, count_a, count...]
  transfers between devices with their start and end apart: 12 -> 12, of which waited for: 6 -> 6; matrix products, arithmetic and copies ran while one was open for 0% -> 0% of each run, Pallas kernels for 7% -> 8%
where the time goes in v14:
time: 37.8 us; the launch traced here: 37.7 us
  waiting for transfers between devices  15.8 us (42%)
  starting transfers between devices  15.4 us (41%)
  Pallas kernels  5.76 us (15%)
  between operations  0.73 us (2%)
    ppermute x12, waiting for transfers between devices, swap(): return lax.ppermute(value, ('dp', 'tensor'), pairs)  15.8 us
    ppermute x12, starting transfers between devices, swap(): return lax.ppermute(value, ('dp', 'tensor'), pairs)  15.4 us
    pallas_call x5, Pallas kernels, pack(): pl.pallas_call(functools.partial(pack_body, pieces, items, count_a, count...  4.25 us
    pallas_call x1, Pallas kernels, finish(): pl.pallas_call(functools.partial(finish_body, pieces, early, late, count_...  1.03 us
  transfers between devices with their start and end apart: 12, of which 6 were waited for; matrix products, arithmetic and copies ran while one was open for 0% of the time, Pallas kernels for 8%

profile of v14, /device:TPU:0, one launch (start us, length us, event | category | flops | bytes accessed | tf_op | source)
XLA Modules:
  0.0 37.7 jit_solution(12441189126532295787)
XLA Ops:
  0.6 1.7 %shard_map.50 = (f32[4,128,128]{2,1,0:T(8,128)S(1)}, f32[17,8,128]{2,1,0:T(8,128)S(1)}, bf16[128,2560]{1,0:T(8,128)(2,1)S(1)}) custom-call(bf16[128,2560]{1,0:T(8,128)(2,1)} %refs_0_.1), custom_call_target="tpu_custom_call" | custom-call | flops 4000000000 | bytes 1 | tf_op jit(solution)/shard_map/pallas_call | solution.py:235
  2.3 3.0 %collective-permute-start.5 = (f32[4,128,128]{2,1,0:T(8,128)S(1)}, f32[4,128,128]{2,1,0:T(8,128)S(1)}, u32[]{:S(2)}, u32[]{:S(2)}) collective-permute-start(f32[4,128,128]{2,1,0:T(8,128)S(1)} %get-tuple-element.51), channel_id=1, source_target_pairs={{0,2},{1,5},{2,0},{3,7},{4,6},{5,1},{6,4},{7,3},{8,10},{9,13},{10,... | collective-permute-start | bytes 786440 | tf_op jit(solution)/shard_map/ppermute | solution.py:468
  5.3 0.4 %shard_map.51 = (f32[4,112,128]{2,1,0:T(8,128)S(1)}, f32[17,8,128]{2,1,0:T(8,128)S(1)}) custom-call(f32[17,8,128]{2,1,0:T(8,128)S(1)} %get-tuple-element.35.refs_0_, bf16[128,2560]{1,0:T(8,128)(2,1)S(1)} %get-tuple-element.36.refs_1_, bf16[128,5120]{1,0:T(8,128)(2,1)S(1)} %copy-done, bf16[128,5120]{1,0:T(8,128)(2,1)S(1)} %copy-done.1), custom_call_target="tpu_custom_call" | custom-call | flops 1 | bytes 1 | tf_op jit(solution)/shard_map/pallas_call | solution.py:235
  5.8 1.6 %collective-permute-start.6 = (f32[4,112,128]{2,1,0:T(8,128)S(1)}, f32[4,112,128]{2,1,0:T(8,128)S(1)}, u32[]{:S(2)}, u32[]{:S(2)}) collective-permute-start(f32[4,112,128]{2,1,0:T(8,128)S(1)} %get-tuple-element.52), channel_id=1, source_target_pairs={{0,4},{1,3},{2,6},{3,1},{4,0},{5,7},{6,2},{7,5},{8,12},{9,11},{10,... | collective-permute-start | bytes 688136 | tf_op jit(solution)/shard_map/ppermute | solution.py:468
  7.4 0.8 %shard_map.52 = (f32[4,136,128]{2,1,0:T(8,128)S(1)}, f32[4,136,128]{2,1,0:T(8,128)S(1)}, f32[17,8,128]{2,1,0:T(8,128)S(1)}) custom-call(f32[17,8,128]{2,1,0:T(8,128)S(1)} %get-tuple-element.37.refs_0_, bf16[128,2560]{1,0:T(8,128)(2,1)S(1)} %get-tuple-element.36.refs_1_, bf16[128,5120]{1,0:T(8,128)(2,1)S(1)} %copy-done, bf16[128,5120]{1,0:T(8,128)(2,1)S(1)} %copy-done.1), custom_call_target="tpu_custom_call" | custom-call | flops 1 | bytes 1 | tf_op jit(solution)/shard_map/pallas_call | solution.py:235
  8.2 0.6 %collective-permute-start = (f32[4,136,128]{2,1,0:T(8,128)S(1)}, f32[4,136,128]{2,1,0:T(8,128)S(1)}, u32[]{:S(2)}, u32[]{:S(2)}) collective-permute-start(f32[4,136,128]{2,1,0:T(8,128)S(1)} %get-tuple-element.42), channel_id=1, source_target_pairs={{0,2},{1,5},{2,0},{3,7},{4,6},{5,1},{6,4},{7,3},{8,10},{9,13},{10,... | collective-permute-start | bytes 835592 | tf_op jit(solution)/shard_map/ppermute | solution.py:468
  8.8 0.2 collective-permute-start.1
  9.0 0.5 %shard_map.53 = (f32[4,128,128]{2,1,0:T(8,128)S(1)}, f32[4,112,128]{2,1,0:T(8,128)S(1)}, f32[17,8,128]{2,1,0:T(8,128)S(1)}) custom-call(f32[17,8,128]{2,1,0:T(8,128)S(1)} %get-tuple-element.38.refs_0_, bf16[128,2560]{1,0:T(8,128)(2,1)S(1)} %get-tuple-element.36.refs_1_, bf16[128,5120]{1,0:T(8,128)(2,1)S(1)} %copy-done, bf16[128,5120]{1,0:T(8,128)(2,1)S(1)} %copy-done.1), custom_call_target="tpu_custom_call" | custom-call | flops 1 | bytes 1 | tf_op jit(solution)/shard_map/pallas_call | solution.py:235
  9.5 0.8 %shard_map.54 = (f32[4,136,128]{2,1,0:T(8,128)S(1)}, f32[4,136,128]{2,1,0:T(8,128)S(1)}, f32[17,8,128]{2,1,0:T(8,128)S(1)}) custom-call(f32[17,8,128]{2,1,0:T(8,128)S(1)} %get-tuple-element.39.refs_0_, bf16[128,2560]{1,0:T(8,128)(2,1)S(1)} %get-tuple-element.36.refs_1_, bf16[128,5120]{1,0:T(8,128)(2,1)S(1)} %copy-done, bf16[128,5120]{1,0:T(8,128)(2,1)S(1)} %copy-done.1), custom_call_target="tpu_custom_call" | custom-call | flops 1 | bytes 1 | tf_op jit(solution)/shard_map/pallas_call | solution.py:235
  10.4 3.2 %collective-permute-done.6.refs_3_ = f32[4,112,128]{2,1,0:T(8,128)S(1)} collective-permute-done((f32[4,112,128]{2,1,0:T(8,128)S(1)}, f32[4,112,128]{2,1,0:T(8,128)S(1)}, u32[]{:S(2)}, u32[]{:S(2)}) %collective-permute-start.6) | collective-permute-done | bytes 229408 | tf_op jit(solution)/shard_map/ppermute | solution.py:468
  13.7 1.1 %collective-permute-start.8 = (f32[2,112,128]{2,1,0:T(8,128)S(1)}, f32[2,112,128]{2,1,0:T(8,128)S(1)}, u32[]{:S(2)}, u32[]{:S(2)}) collective-permute-start(f32[2,112,128]{2,1,0:T(8,128)S(1)} %get-tuple-element.56), channel_id=1, source_target_pairs={{0,2},{1,5},{2,0},{3,7},{4,6},{5,1},{6,4},{7,3},{8,10},{9,13},{10,... | collective-permute-start | bytes 344072 | tf_op jit(solution)/shard_map/ppermute | solution.py:468
  14.8 1.9 %collective-permute-start.7 = (f32[2,128,128]{2,1,0:T(8,128)S(1)}, f32[2,128,128]{2,1,0:T(8,128)S(1)}, u32[]{:S(2)}, u32[]{:S(2)}) collective-permute-start(f32[2,128,128]{2,1,0:T(8,128)S(1)} %get-tuple-element.55), channel_id=1, source_target_pairs={{0,4},{1,3},{2,6},{3,1},{4,0},{5,7},{6,2},{7,5},{8,12},{9,11},{10,... | collective-permute-start | bytes 393224 | tf_op jit(solution)/shard_map/ppermute | solution.py:468
  16.7 0.9 %collective-permute-start.9 = (f32[2,128]{1,0:T(2,128)S(1)}, f32[2,128]{1,0:T(2,128)S(1)}, u32[]{:S(2)}, u32[]{:S(2)}) collective-permute-start(f32[2,128]{1,0:T(2,128)S(1)} %fusion.refs_4_), channel_id=1, source_target_pairs={{0,6},{1,7},{2,4},{3,5},{4,2},{5,3},{6,0},{7,1},{8,14},{9,15},{10,... | collective-permute-start | bytes 3080 | tf_op jit(solution)/shard_map/ppermute | solution.py:468
  17.6 0.3 collective-permute-done.refs_2_
  17.9 1.2 %collective-permute-done.1.refs_3_ = f32[4,136,128]{2,1,0:T(8,128)S(1)} collective-permute-done((f32[4,136,128]{2,1,0:T(8,128)S(1)}, f32[4,136,128]{2,1,0:T(8,128)S(1)}, u32[]{:S(2)}, u32[]{:S(2)}) %collective-permute-start.1) | collective-permute-done | bytes 278560 | tf_op jit(solution)/shard_map/ppermute | solution.py:468
  19.2 1.5 %collective-permute-start.3 = (f32[2,136,128]{2,1,0:T(8,128)S(1)}, f32[2,136,128]{2,1,0:T(8,128)S(1)}, u32[]{:S(2)}, u32[]{:S(2)}) collective-permute-start(f32[2,136,128]{2,1,0:T(8,128)S(1)} %get-tuple-element.47), channel_id=1, source_target_pairs={{0,4},{1,3},{2,6},{3,1},{4,0},{5,7},{6,2},{7,5},{8,12},{9,11},{10,... | collective-permute-start | bytes 417800 | tf_op jit(solution)/shard_map/ppermute | solution.py:468
  20.6 1.5 %collective-permute-start.4 = (f32[2,136,128]{2,1,0:T(8,128)S(1)}, f32[2,136,128]{2,1,0:T(8,128)S(1)}, u32[]{:S(2)}, u32[]{:S(2)}) collective-permute-start(f32[2,136,128]{2,1,0:T(8,128)S(1)} %get-tuple-element.48), channel_id=1, source_target_pairs={{0,2},{1,5},{2,0},{3,7},{4,6},{5,1},{6,4},{7,3},{8,10},{9,13},{10,... | collective-permute-start | bytes 417800 | tf_op jit(solution)/shard_map/ppermute | solution.py:468
  22.2 2.7 %collective-permute-start.11 = (f32[1,240,128]{2,1,0:T(8,128)S(1)}, f32[1,240,128]{2,1,0:T(8,128)S(1)}, u32[]{:S(2)}, u32[]{:S(2)}) collective-permute-start(f32[1,240,128]{2,1,0:T(8,128)S(1)} %get-tuple-element.63), channel_id=1, source_target_pairs={{0,8},{1,9},{2,10},{3,11},{4,12},{5,13},{6,14},{7,15},{8,0},{9,1},... | collective-permute-start | bytes 368648 | tf_op jit(solution)/shard_map/ppermute | solution.py:468
  24.8 3.1 %collective-permute-done.3.refs_2_ = f32[2,136,128]{2,1,0:T(8,128)S(1)} collective-permute-done((f32[2,136,128]{2,1,0:T(8,128)S(1)}, f32[2,136,128]{2,1,0:T(8,128)S(1)}, u32[]{:S(2)}, u32[]{:S(2)}) %collective-permute-start.3) | collective-permute-done | bytes 139296 | tf_op jit(solution)/shard_map/ppermute | solution.py:468
  28.0 0.4 %collective-permute-start.10 = (f32[1,272,128]{2,1,0:T(8,128)S(1)}, f32[1,272,128]{2,1,0:T(8,128)S(1)}, u32[]{:S(2)}, u32[]{:S(2)}) collective-permute-start(f32[1,272,128]{2,1,0:T(8,128)S(1)} %get-tuple-element.60), channel_id=1, source_target_pairs={{0,8},{1,9},{2,10},{3,11},{4,12},{5,13},{6,14},{7,15},{8,0},{9,1},... | collective-permute-start | bytes 417800 | tf_op jit(solution)/shard_map/ppermute | solution.py:468
  28.4 5.3 %collective-permute-done.11.refs_2_ = f32[1,240,128]{2,1,0:T(8,128)S(1)} collective-permute-done((f32[1,240,128]{2,1,0:T(8,128)S(1)}, f32[1,240,128]{2,1,0:T(8,128)S(1)}, u32[]{:S(2)}, u32[]{:S(2)}) %collective-permute-start.11) | collective-permute-done | bytes 122912 | tf_op jit(solution)/shard_map/ppermute | solution.py:468
  33.6 0.3 shard_map.59
  33.9 2.7 %collective-permute-done.10.refs_2_ = f32[1,272,128]{2,1,0:T(8,128)S(1)} collective-permute-done((f32[1,272,128]{2,1,0:T(8,128)S(1)}, f32[1,272,128]{2,1,0:T(8,128)S(1)}, u32[]{:S(2)}, u32[]{:S(2)}) %collective-permute-start.10) | collective-permute-done | bytes 139296 | tf_op jit(solution)/shard_map/ppermute | solution.py:468
  36.6 1.0 %shard_map.60 = (f32[320,128]{1,0:T(8,128)}, f32[640,128]{1,0:T(8,128)}) custom-call(f32[1,136,128]{2,1,0:T(8,128)S(1)} %get-tuple-element.58.refs_0_, f32[1,136,128]{2,1,0:T(8,128)S(1)} %get-tuple-element.59.refs_1_, f32[1,272,128]{2,1,0:T(8,128)S(1)} %collective-permute-done.10.refs_2_, f32[320,128]{1,0:T(8,128)S(1)} %get-tuple-element.64.refs_3_, ...), custom_call_target="tpu_custom_call" | custom-call | tf_op jit(solution)/shard_map/pallas_call | solution.py:444
  (17 shorter events, 0.3 us)
Async XLA Ops:
  0.6 4.7 %copy-start.1 = (bf16[128,5120]{1,0:T(8,128)(2,1)S(1)}, bf16[128,5120]{1,0:T(8,128)(2,1)}, u32[]{:S(2)}) copy-start(bf16[128,5120]{1,0:T(8,128)(2,1)} %refs_3_.7) | copy-start | bytes 3932164
  0.6 4.7 %copy-start = (bf16[128,5120]{1,0:T(8,128)(2,1)S(1)}, bf16[128,5120]{1,0:T(8,128)(2,1)}, u32[]{:S(2)}) copy-start(bf16[128,5120]{1,0:T(8,128)(2,1)} %refs_2_.7) | copy-start | bytes 3932164
  2.3 11.3 %collective-permute-start.5 = (f32[4,128,128]{2,1,0:T(8,128)S(1)}, f32[4,128,128]{2,1,0:T(8,128)S(1)}, u32[]{:S(2)}, u32[]{:S(2)}) collective-permute-start(f32[4,128,128]{2,1,0:T(8,128)S(1)} %get-tuple-element.51), channel_id=1, source_target_pairs={{0,2},{1,5},{2,0},{3,7},{4,6},{5,1},{6,4},{7,3},{8,10},{9,13},{10,... | collective-permute-start | bytes 786440 | tf_op jit(solution)/shard_map/ppermute | solution.py:468
  5.8 7.8 %collective-permute-start.6 = (f32[4,112,128]{2,1,0:T(8,128)S(1)}, f32[4,112,128]{2,1,0:T(8,128)S(1)}, u32[]{:S(2)}, u32[]{:S(2)}) collective-permute-start(f32[4,112,128]{2,1,0:T(8,128)S(1)} %get-tuple-element.52), channel_id=1, source_target_pairs={{0,4},{1,3},{2,6},{3,1},{4,0},{5,7},{6,2},{7,5},{8,12},{9,11},{10,... | collective-permute-start | bytes 688136 | tf_op jit(solution)/shard_map/ppermute | solution.py:468
  8.2 9.7 %collective-permute-start = (f32[4,136,128]{2,1,0:T(8,128)S(1)}, f32[4,136,128]{2,1,0:T(8,128)S(1)}, u32[]{:S(2)}, u32[]{:S(2)}) collective-permute-start(f32[4,136,128]{2,1,0:T(8,128)S(1)} %get-tuple-element.42), channel_id=1, source_target_pairs={{0,2},{1,5},{2,0},{3,7},{4,6},{5,1},{6,4},{7,3},{8,10},{9,13},{10,... | collective-permute-start | bytes 835592 | tf_op jit(solution)/shard_map/ppermute | solution.py:468
  8.8 10.3 %collective-permute-start.1 = (f32[4,136,128]{2,1,0:T(8,128)S(1)}, f32[4,136,128]{2,1,0:T(8,128)S(1)}, u32[]{:S(2)}, u32[]{:S(2)}) collective-permute-start(f32[4,136,128]{2,1,0:T(8,128)S(1)} %get-tuple-element.43), channel_id=1, source_target_pairs={{0,4},{1,3},{2,6},{3,1},{4,0},{5,7},{6,2},{7,5},{8,12},{9,11},{10,... | collective-permute-start | bytes 835592 | tf_op jit(solution)/shard_map/ppermute | solution.py:468
  10.4 6.3 %collective-permute-start.2 = (f32[2,128]{1,0:T(2,128)S(1)}, f32[2,128]{1,0:T(2,128)S(1)}, u32[]{:S(2)}, u32[]{:S(2)}) collective-permute-start(f32[2,128]{1,0:T(2,128)S(1)} %slice_bitcast_fusion), channel_id=1, source_target_pairs={{0,1},{1,0},{2,3},{3,2},{4,5},{5,4},{6,7},{7,6},{8,9},{9,8},{10,11... | collective-permute-start | bytes 3080 | tf_op jit(solution)/shard_map/ppermute | solution.py:468
  13.7 8.4 %collective-permute-start.8 = (f32[2,112,128]{2,1,0:T(8,128)S(1)}, f32[2,112,128]{2,1,0:T(8,128)S(1)}, u32[]{:S(2)}, u32[]{:S(2)}) collective-permute-start(f32[2,112,128]{2,1,0:T(8,128)S(1)} %get-tuple-element.56), channel_id=1, source_target_pairs={{0,2},{1,5},{2,0},{3,7},{4,6},{5,1},{6,4},{7,3},{8,10},{9,13},{10,... | collective-permute-start | bytes 344072 | tf_op jit(solution)/shard_map/ppermute | solution.py:468
  14.8 7.3 %collective-permute-start.7 = (f32[2,128,128]{2,1,0:T(8,128)S(1)}, f32[2,128,128]{2,1,0:T(8,128)S(1)}, u32[]{:S(2)}, u32[]{:S(2)}) collective-permute-start(f32[2,128,128]{2,1,0:T(8,128)S(1)} %get-tuple-element.55), channel_id=1, source_target_pairs={{0,4},{1,3},{2,6},{3,1},{4,0},{5,7},{6,2},{7,5},{8,12},{9,11},{10,... | collective-permute-start | bytes 393224 | tf_op jit(solution)/shard_map/ppermute | solution.py:468
  16.7 5.5 %collective-permute-start.9 = (f32[2,128]{1,0:T(2,128)S(1)}, f32[2,128]{1,0:T(2,128)S(1)}, u32[]{:S(2)}, u32[]{:S(2)}) collective-permute-start(f32[2,128]{1,0:T(2,128)S(1)} %fusion.refs_4_), channel_id=1, source_target_pairs={{0,6},{1,7},{2,4},{3,5},{4,2},{5,3},{6,0},{7,1},{8,14},{9,15},{10,... | collective-permute-start | bytes 3080 | tf_op jit(solution)/shard_map/ppermute | solution.py:468
  19.2 8.8 %collective-permute-start.3 = (f32[2,136,128]{2,1,0:T(8,128)S(1)}, f32[2,136,128]{2,1,0:T(8,128)S(1)}, u32[]{:S(2)}, u32[]{:S(2)}) collective-permute-start(f32[2,136,128]{2,1,0:T(8,128)S(1)} %get-tuple-element.47), channel_id=1, source_target_pairs={{0,4},{1,3},{2,6},{3,1},{4,0},{5,7},{6,2},{7,5},{8,12},{9,11},{10,... | collective-permute-start | bytes 417800 | tf_op jit(solution)/shard_map/ppermute | solution.py:468
  20.6 7.3 %collective-permute-start.4 = (f32[2,136,128]{2,1,0:T(8,128)S(1)}, f32[2,136,128]{2,1,0:T(8,128)S(1)}, u32[]{:S(2)}, u32[]{:S(2)}) collective-permute-start(f32[2,136,128]{2,1,0:T(8,128)S(1)} %get-tuple-element.48), channel_id=1, source_target_pairs={{0,2},{1,5},{2,0},{3,7},{4,6},{5,1},{6,4},{7,3},{8,10},{9,13},{10,... | collective-permute-start | bytes 417800 | tf_op jit(solution)/shard_map/ppermute | solution.py:468
  22.2 11.5 %collective-permute-start.11 = (f32[1,240,128]{2,1,0:T(8,128)S(1)}, f32[1,240,128]{2,1,0:T(8,128)S(1)}, u32[]{:S(2)}, u32[]{:S(2)}) collective-permute-start(f32[1,240,128]{2,1,0:T(8,128)S(1)} %get-tuple-element.63), channel_id=1, source_target_pairs={{0,8},{1,9},{2,10},{3,11},{4,12},{5,13},{6,14},{7,15},{8,0},{9,1},... | collective-permute-start | bytes 368648 | tf_op jit(solution)/shard_map/ppermute | solution.py:468
  28.0 8.6 %collective-permute-start.10 = (f32[1,272,128]{2,1,0:T(8,128)S(1)}, f32[1,272,128]{2,1,0:T(8,128)S(1)}, u32[]{:S(2)}, u32[]{:S(2)}) collective-permute-start(f32[1,272,128]{2,1,0:T(8,128)S(1)} %get-tuple-element.60), channel_id=1, source_target_pairs={{0,8},{1,9},{2,10},{3,11},{4,12},{5,13},{6,14},{7,15},{8,0},{9,1},... | collective-permute-start | bytes 417800 | tf_op jit(solution)/shard_map/ppermute | solution.py:468

commit v15 on v13

--- a/solution.py
+++ b/solution.py
@@ -481,8 +481,8 @@
     full_g, _ = split_rows(count_g)
     some, more = (full_a + 1) // 2, full_g // 2
     pieces = (
-        (tuple(range(some, full_a)), half_a, (), 0),
-        ((), 0, tuple(range(more)), 0),
+        (tuple(range(some, full_a)), 0, (), 0),
+        ((), half_a, tuple(range(more)), 0),
         (tuple(range(some)), 0, (), 1),
         ((), 0, tuple(range(more, full_g)), 1),
     )
@@ -539,7 +539,7 @@
 
 def fits(count_a, count_g):
     (full_a, half_a), full_g = split_rows(count_a), count_g // B
-    if count_a % H or count_g % B or full_a + half_a < 2 or full_g < 2:
+    if count_a % H or count_g % B or full_a < 2 or full_g < 2:
         return False
     return full_a + half_a + full_g <= 2 * (EDGE - 2)
 

time: 38.4 us -> 39.9 us (1.039)
  waiting for transfers between devices: 13.9 us -> 17.4 us
  starting transfers between devices: 17.6 us -> 15.9 us
    ppermute x12, waiting for transfers between devices: 13.9 us -> 17.4 us  [swap(): return lax.ppermute(value, ('dp', 'tensor'), pairs)]
    ppermute x12, starting transfers between devices: 17.6 us -> 15.9 us  [swap(): return lax.ppermute(value, ('dp', 'tensor'), pairs)]
  transfers between devices with their start and end apart: 12 -> 12, of which waited for: 6 -> 5; matrix products, arithmetic and copies ran while one was open for 0% -> 0% of each run, Pallas kernels for 7% -> 7%
where the time goes in v15:
time: 39.9 us; the launch traced here: 39.8 us
  waiting for transfers between devices  17.4 us (44%)
  starting transfers between devices  15.9 us (40%)
  Pallas kernels  5.77 us (14%)
  between operations  0.73 us (2%)
    ppermute x12, waiting for transfers between devices, swap(): return lax.ppermute(value, ('dp', 'tensor'), pairs)  17.4 us
    ppermute x12, starting transfers between devices, swap(): return lax.ppermute(value, ('dp', 'tensor'), pairs)  15.9 us
    pallas_call x4, Pallas kernels, pack(): pl.pallas_call(functools.partial(pack_body, pieces, items, count_a, count...  4.32 us
    pallas_call x1, Pallas kernels, finish(): pl.pallas_call(functools.partial(finish_body, pieces, early, late, count_...  1.11 us
  transfers between devices with their start and end apart: 12, of which 5 were waited for; matrix products, arithmetic and copies ran while one was open for 0% of the time, Pallas kernels for 7%

profile of v15, /device:TPU:0, one launch (start us, length us, event | category | flops | bytes accessed | tf_op | source)
XLA Modules:
  0.0 39.8 jit_solution(10233805148764547133)
XLA Ops:
  0.6 1.7 %shard_map.50 = (f32[4,64,128]{2,1,0:T(8,128)S(1)}, f32[4,64,128]{2,1,0:T(8,128)S(1)}, f32[17,8,128]{2,1,0:T(8,128)S(1)}, bf16[128,2560]{1,0:T(8,128)(2,1)S(1)}) custom-call(bf16[128,2560]{1,0:T(8,128)(2,1)} %refs_0_.1), custom_call_target="tpu_custom_call" | custom-call | flops 4000000000 | bytes 1 | tf_op jit(solution)/shard_map/pallas_call | solution.py:235
  2.3 3.0 %collective-permute-start.5 = (f32[4,64,128]{2,1,0:T(8,128)S(1)}, f32[4,64,128]{2,1,0:T(8,128)S(1)}, u32[]{:S(2)}, u32[]{:S(2)}) collective-permute-start(f32[4,64,128]{2,1,0:T(8,128)S(1)} %get-tuple-element.49), channel_id=1, source_target_pairs={{0,2},{1,5},{2,0},{3,7},{4,6},{5,1},{6,4},{7,3},{8,10},{9,13},{10,... | collective-permute-start | bytes 393224 | tf_op jit(solution)/shard_map/ppermute | solution.py:468
  5.3 1.6 %collective-permute-start.6 = (f32[4,64,128]{2,1,0:T(8,128)S(1)}, f32[4,64,128]{2,1,0:T(8,128)S(1)}, u32[]{:S(2)}, u32[]{:S(2)}) collective-permute-start(f32[4,64,128]{2,1,0:T(8,128)S(1)} %get-tuple-element.50), channel_id=1, source_target_pairs={{0,4},{1,3},{2,6},{3,1},{4,0},{5,7},{6,2},{7,5},{8,12},{9,11},{10,... | collective-permute-start | bytes 393224 | tf_op jit(solution)/shard_map/ppermute | solution.py:468
  6.9 1.2 %shard_map.51 = (f32[4,184,128]{2,1,0:T(8,128)S(1)}, f32[4,200,128]{2,1,0:T(8,128)S(1)}, f32[17,8,128]{2,1,0:T(8,128)S(1)}) custom-call(f32[17,8,128]{2,1,0:T(8,128)S(1)} %get-tuple-element.34.refs_0_, bf16[128,2560]{1,0:T(8,128)(2,1)S(1)} %get-tuple-element.35.refs_1_, bf16[128,5120]{1,0:T(8,128)(2,1)S(1)} %copy-done, bf16[128,5120]{1,0:T(8,128)(2,1)S(1)} %copy-done.1), custom_call_target="tpu_custom_call" | custom-call | flops 1 | bytes 1 | tf_op jit(solution)/shard_map/pallas_call | solution.py:235
  8.1 0.6 %collective-permute-start = (f32[4,184,128]{2,1,0:T(8,128)S(1)}, f32[4,184,128]{2,1,0:T(8,128)S(1)}, u32[]{:S(2)}, u32[]{:S(2)}) collective-permute-start(f32[4,184,128]{2,1,0:T(8,128)S(1)} %get-tuple-element.40), channel_id=1, source_target_pairs={{0,2},{1,5},{2,0},{3,7},{4,6},{5,1},{6,4},{7,3},{8,10},{9,13},{10,... | collective-permute-start | bytes 1130504 | tf_op jit(solution)/shard_map/ppermute | solution.py:468
  8.7 0.3 shard_map.52
  9.0 1.2 %shard_map.53 = (f32[4,184,128]{2,1,0:T(8,128)S(1)}, f32[4,200,128]{2,1,0:T(8,128)S(1)}, f32[17,8,128]{2,1,0:T(8,128)S(1)}) custom-call(f32[17,8,128]{2,1,0:T(8,128)S(1)} %get-tuple-element.37.refs_0_, bf16[128,2560]{1,0:T(8,128)(2,1)S(1)} %get-tuple-element.35.refs_1_, bf16[128,5120]{1,0:T(8,128)(2,1)S(1)} %copy-done, bf16[128,5120]{1,0:T(8,128)(2,1)S(1)} %copy-done.1), custom_call_target="tpu_custom_call" | custom-call | flops 1 | bytes 1 | tf_op jit(solution)/shard_map/pallas_call | solution.py:235
  10.2 0.1 collective-permute-start.2
  10.3 0.5 %collective-permute-done.6.refs_3_ = f32[4,64,128]{2,1,0:T(8,128)S(1)} collective-permute-done((f32[4,64,128]{2,1,0:T(8,128)S(1)}, f32[4,64,128]{2,1,0:T(8,128)S(1)}, u32[]{:S(2)}, u32[]{:S(2)}) %collective-permute-start.6) | collective-permute-done | bytes 131104 | tf_op jit(solution)/shard_map/ppermute | solution.py:468
  10.8 2.5 %collective-permute-start.7 = (f32[2,64,128]{2,1,0:T(8,128)S(1)}, f32[2,64,128]{2,1,0:T(8,128)S(1)}, u32[]{:S(2)}, u32[]{:S(2)}) collective-permute-start(f32[2,64,128]{2,1,0:T(8,128)S(1)} %get-tuple-element.53), channel_id=1, source_target_pairs={{0,4},{1,3},{2,6},{3,1},{4,0},{5,7},{6,2},{7,5},{8,12},{9,11},{10,... | collective-permute-start | bytes 196616 | tf_op jit(solution)/shard_map/ppermute | solution.py:468
  13.4 0.5 %collective-permute-start.8 = (f32[2,64,128]{2,1,0:T(8,128)S(1)}, f32[2,64,128]{2,1,0:T(8,128)S(1)}, u32[]{:S(2)}, u32[]{:S(2)}) collective-permute-start(f32[2,64,128]{2,1,0:T(8,128)S(1)} %get-tuple-element.54), channel_id=1, source_target_pairs={{0,2},{1,5},{2,0},{3,7},{4,6},{5,1},{6,4},{7,3},{8,10},{9,13},{10,... | collective-permute-start | bytes 196616 | tf_op jit(solution)/shard_map/ppermute | solution.py:468
  13.9 1.0 %collective-permute-start.9 = (f32[2,128]{1,0:T(2,128)S(1)}, f32[2,128]{1,0:T(2,128)S(1)}, u32[]{:S(2)}, u32[]{:S(2)}) collective-permute-start(f32[2,128]{1,0:T(2,128)S(1)} %fusion.refs_4_), channel_id=1, source_target_pairs={{0,6},{1,7},{2,4},{3,5},{4,2},{5,3},{6,0},{7,1},{8,14},{9,15},{10,... | collective-permute-start | bytes 3080 | tf_op jit(solution)/shard_map/ppermute | solution.py:468
  14.9 4.4 %collective-permute-done.refs_2_ = f32[4,184,128]{2,1,0:T(8,128)S(1)} collective-permute-done((f32[4,184,128]{2,1,0:T(8,128)S(1)}, f32[4,184,128]{2,1,0:T(8,128)S(1)}, u32[]{:S(2)}, u32[]{:S(2)}) %collective-permute-start) | collective-permute-done | bytes 376864 | tf_op jit(solution)/shard_map/ppermute | solution.py:468
  19.3 0.1 collective-permute-done.1.refs_3_
  19.4 0.1 shard_map.54
  19.5 1.6 %collective-permute-start.3 = (f32[2,184,128]{2,1,0:T(8,128)S(1)}, f32[2,184,128]{2,1,0:T(8,128)S(1)}, u32[]{:S(2)}, u32[]{:S(2)}) collective-permute-start(f32[2,184,128]{2,1,0:T(8,128)S(1)} %get-tuple-element.45), channel_id=1, source_target_pairs={{0,4},{1,3},{2,6},{3,1},{4,0},{5,7},{6,2},{7,5},{8,12},{9,11},{10,... | collective-permute-start | bytes 565256 | tf_op jit(solution)/shard_map/ppermute | solution.py:468
  21.2 0.4 %collective-permute-start.4 = (f32[2,200,128]{2,1,0:T(8,128)S(1)}, f32[2,200,128]{2,1,0:T(8,128)S(1)}, u32[]{:S(2)}, u32[]{:S(2)}) collective-permute-start(f32[2,200,128]{2,1,0:T(8,128)S(1)} %get-tuple-element.46), channel_id=1, source_target_pairs={{0,2},{1,5},{2,0},{3,7},{4,6},{5,1},{6,4},{7,3},{8,10},{9,13},{10,... | collective-permute-start | bytes 614408 | tf_op jit(solution)/shard_map/ppermute | solution.py:468
  21.6 2.7 %collective-permute-start.11 = (f32[1,128,128]{2,1,0:T(8,128)S(1)}, f32[1,128,128]{2,1,0:T(8,128)S(1)}, u32[]{:S(2)}, u32[]{:S(2)}) collective-permute-start(f32[1,128,128]{2,1,0:T(8,128)S(1)} %get-tuple-element.61), channel_id=1, source_target_pairs={{0,8},{1,9},{2,10},{3,11},{4,12},{5,13},{6,14},{7,15},{8,0},{9,1},... | collective-permute-start | bytes 196616 | tf_op jit(solution)/shard_map/ppermute | solution.py:468
  24.4 3.7 %collective-permute-done.3.refs_2_ = f32[2,184,128]{2,1,0:T(8,128)S(1)} collective-permute-done((f32[2,184,128]{2,1,0:T(8,128)S(1)}, f32[2,184,128]{2,1,0:T(8,128)S(1)}, u32[]{:S(2)}, u32[]{:S(2)}) %collective-permute-start.3) | collective-permute-done | bytes 188448 | tf_op jit(solution)/shard_map/ppermute | solution.py:468
  28.1 0.1 shard_map.57
  28.2 1.7 %collective-permute-start.10 = (f32[1,384,128]{2,1,0:T(8,128)S(1)}, f32[1,384,128]{2,1,0:T(8,128)S(1)}, u32[]{:S(2)}, u32[]{:S(2)}) collective-permute-start(f32[1,384,128]{2,1,0:T(8,128)S(1)} %get-tuple-element.58), channel_id=1, source_target_pairs={{0,8},{1,9},{2,10},{3,11},{4,12},{5,13},{6,14},{7,15},{8,0},{9,1},... | collective-permute-start | bytes 589832 | tf_op jit(solution)/shard_map/ppermute | solution.py:468
  29.9 0.2 shard_map.58
  30.0 8.7 %collective-permute-done.10.refs_2_ = f32[1,384,128]{2,1,0:T(8,128)S(1)} collective-permute-done((f32[1,384,128]{2,1,0:T(8,128)S(1)}, f32[1,384,128]{2,1,0:T(8,128)S(1)}, u32[]{:S(2)}, u32[]{:S(2)}) %collective-permute-start.10) | collective-permute-done | bytes 196640 | tf_op jit(solution)/shard_map/ppermute | solution.py:468
  38.7 1.1 %shard_map.59 = (f32[320,128]{1,0:T(8,128)}, f32[640,128]{1,0:T(8,128)}) custom-call(f32[1,184,128]{2,1,0:T(8,128)S(1)} %get-tuple-element.56.refs_0_, f32[1,200,128]{2,1,0:T(8,128)S(1)} %get-tuple-element.57.refs_1_, f32[1,384,128]{2,1,0:T(8,128)S(1)} %collective-permute-done.10.refs_2_, f32[320,128]{1,0:T(8,128)S(1)} %get-tuple-element.62.refs_3_, ...), custom_call_target="tpu_custom_call" | custom-call | tf_op jit(solution)/shard_map/pallas_call | solution.py:444
  (16 shorter events, 0.1 us)
Async XLA Ops:
  0.6 6.3 %copy-start.1 = (bf16[128,5120]{1,0:T(8,128)(2,1)S(1)}, bf16[128,5120]{1,0:T(8,128)(2,1)}, u32[]{:S(2)}) copy-start(bf16[128,5120]{1,0:T(8,128)(2,1)} %refs_3_.5) | copy-start | bytes 3932164
  0.6 6.3 %copy-start = (bf16[128,5120]{1,0:T(8,128)(2,1)S(1)}, bf16[128,5120]{1,0:T(8,128)(2,1)}, u32[]{:S(2)}) copy-start(bf16[128,5120]{1,0:T(8,128)(2,1)} %refs_2_.5) | copy-start | bytes 3932164
  2.3 8.0 %collective-permute-start.5 = (f32[4,64,128]{2,1,0:T(8,128)S(1)}, f32[4,64,128]{2,1,0:T(8,128)S(1)}, u32[]{:S(2)}, u32[]{:S(2)}) collective-permute-start(f32[4,64,128]{2,1,0:T(8,128)S(1)} %get-tuple-element.49), channel_id=1, source_target_pairs={{0,2},{1,5},{2,0},{3,7},{4,6},{5,1},{6,4},{7,3},{8,10},{9,13},{10,... | collective-permute-start | bytes 393224 | tf_op jit(solution)/shard_map/ppermute | solution.py:468
  5.3 5.5 %collective-permute-start.6 = (f32[4,64,128]{2,1,0:T(8,128)S(1)}, f32[4,64,128]{2,1,0:T(8,128)S(1)}, u32[]{:S(2)}, u32[]{:S(2)}) collective-permute-start(f32[4,64,128]{2,1,0:T(8,128)S(1)} %get-tuple-element.50), channel_id=1, source_target_pairs={{0,4},{1,3},{2,6},{3,1},{4,0},{5,7},{6,2},{7,5},{8,12},{9,11},{10,... | collective-permute-start | bytes 393224 | tf_op jit(solution)/shard_map/ppermute | solution.py:468
  8.1 11.2 %collective-permute-start = (f32[4,184,128]{2,1,0:T(8,128)S(1)}, f32[4,184,128]{2,1,0:T(8,128)S(1)}, u32[]{:S(2)}, u32[]{:S(2)}) collective-permute-start(f32[4,184,128]{2,1,0:T(8,128)S(1)} %get-tuple-element.40), channel_id=1, source_target_pairs={{0,2},{1,5},{2,0},{3,7},{4,6},{5,1},{6,4},{7,3},{8,10},{9,13},{10,... | collective-permute-start | bytes 1130504 | tf_op jit(solution)/shard_map/ppermute | solution.py:468
  8.7 10.8 %collective-permute-start.1 = (f32[4,200,128]{2,1,0:T(8,128)S(1)}, f32[4,200,128]{2,1,0:T(8,128)S(1)}, u32[]{:S(2)}, u32[]{:S(2)}) collective-permute-start(f32[4,200,128]{2,1,0:T(8,128)S(1)} %get-tuple-element.41), channel_id=1, source_target_pairs={{0,4},{1,3},{2,6},{3,1},{4,0},{5,7},{6,2},{7,5},{8,12},{9,11},{10,... | collective-permute-start | bytes 1228808 | tf_op jit(solution)/shard_map/ppermute | solution.py:468
  10.2 3.7 %collective-permute-start.2 = (f32[2,128]{1,0:T(2,128)S(1)}, f32[2,128]{1,0:T(2,128)S(1)}, u32[]{:S(2)}, u32[]{:S(2)}) collective-permute-start(f32[2,128]{1,0:T(2,128)S(1)} %slice_bitcast_fusion), channel_id=1, source_target_pairs={{0,1},{1,0},{2,3},{3,2},{4,5},{5,4},{6,7},{7,6},{8,9},{9,8},{10,11... | collective-permute-start | bytes 3080 | tf_op jit(solution)/shard_map/ppermute | solution.py:468
  10.8 10.8 %collective-permute-start.7 = (f32[2,64,128]{2,1,0:T(8,128)S(1)}, f32[2,64,128]{2,1,0:T(8,128)S(1)}, u32[]{:S(2)}, u32[]{:S(2)}) collective-permute-start(f32[2,64,128]{2,1,0:T(8,128)S(1)} %get-tuple-element.53), channel_id=1, source_target_pairs={{0,4},{1,3},{2,6},{3,1},{4,0},{5,7},{6,2},{7,5},{8,12},{9,11},{10,... | collective-permute-start | bytes 196616 | tf_op jit(solution)/shard_map/ppermute | solution.py:468
  13.4 8.2 %collective-permute-start.8 = (f32[2,64,128]{2,1,0:T(8,128)S(1)}, f32[2,64,128]{2,1,0:T(8,128)S(1)}, u32[]{:S(2)}, u32[]{:S(2)}) collective-permute-start(f32[2,64,128]{2,1,0:T(8,128)S(1)} %get-tuple-element.54), channel_id=1, source_target_pairs={{0,2},{1,5},{2,0},{3,7},{4,6},{5,1},{6,4},{7,3},{8,10},{9,13},{10,... | collective-permute-start | bytes 196616 | tf_op jit(solution)/shard_map/ppermute | solution.py:468
  13.9 7.7 %collective-permute-start.9 = (f32[2,128]{1,0:T(2,128)S(1)}, f32[2,128]{1,0:T(2,128)S(1)}, u32[]{:S(2)}, u32[]{:S(2)}) collective-permute-start(f32[2,128]{1,0:T(2,128)S(1)} %fusion.refs_4_), channel_id=1, source_target_pairs={{0,6},{1,7},{2,4},{3,5},{4,2},{5,3},{6,0},{7,1},{8,14},{9,15},{10,... | collective-permute-start | bytes 3080 | tf_op jit(solution)/shard_map/ppermute | solution.py:468
  19.5 8.6 %collective-permute-start.3 = (f32[2,184,128]{2,1,0:T(8,128)S(1)}, f32[2,184,128]{2,1,0:T(8,128)S(1)}, u32[]{:S(2)}, u32[]{:S(2)}) collective-permute-start(f32[2,184,128]{2,1,0:T(8,128)S(1)} %get-tuple-element.45), channel_id=1, source_target_pairs={{0,4},{1,3},{2,6},{3,1},{4,0},{5,7},{6,2},{7,5},{8,12},{9,11},{10,... | collective-permute-start | bytes 565256 | tf_op jit(solution)/shard_map/ppermute | solution.py:468
  21.2 6.9 %collective-permute-start.4 = (f32[2,200,128]{2,1,0:T(8,128)S(1)}, f32[2,200,128]{2,1,0:T(8,128)S(1)}, u32[]{:S(2)}, u32[]{:S(2)}) collective-permute-start(f32[2,200,128]{2,1,0:T(8,128)S(1)} %get-tuple-element.46), channel_id=1, source_target_pairs={{0,2},{1,5},{2,0},{3,7},{4,6},{5,1},{6,4},{7,3},{8,10},{9,13},{10,... | collective-permute-start | bytes 614408 | tf_op jit(solution)/shard_map/ppermute | solution.py:468
  21.6 8.2 %collective-permute-start.11 = (f32[1,128,128]{2,1,0:T(8,128)S(1)}, f32[1,128,128]{2,1,0:T(8,128)S(1)}, u32[]{:S(2)}, u32[]{:S(2)}) collective-permute-start(f32[1,128,128]{2,1,0:T(8,128)S(1)} %get-tuple-element.61), channel_id=1, source_target_pairs={{0,8},{1,9},{2,10},{3,11},{4,12},{5,13},{6,14},{7,15},{8,0},{9,1},... | collective-permute-start | bytes 196616 | tf_op jit(solution)/shard_map/ppermute | solution.py:468
  28.2 10.5 %collective-permute-start.10 = (f32[1,384,128]{2,1,0:T(8,128)S(1)}, f32[1,384,128]{2,1,0:T(8,128)S(1)}, u32[]{:S(2)}, u32[]{:S(2)}) collective-permute-start(f32[1,384,128]{2,1,0:T(8,128)S(1)} %get-tuple-element.58), channel_id=1, source_target_pairs={{0,8},{1,9},{2,10},{3,11},{4,12},{5,13},{6,14},{7,15},{8,0},{9,1},... | collective-permute-start | bytes 589832 | tf_op jit(solution)/shard_map/ppermute | solution.py:468

commit v16 on v14

--- a/solution.py
+++ b/solution.py
@@ -479,12 +479,12 @@
     count_g = saved_pre.shape[1] // dp
     full_a, half_a = split_rows(count_a)
     full_g, _ = split_rows(count_g)
-    some = 1 + (full_g - 1) // 2
+    some, more = full_g // 2, full_g - full_g // 4
     pieces = (
         (tuple(range(full_a)), 0, (), 0),
-        ((), 0, tuple(range(1, some)), 0),
-        ((), half_a, (0,), 1),
-        ((), 0, tuple(range(some, full_g)), 1),
+        ((), 0, tuple(range(some, more)), 0),
+        ((), half_a, tuple(range(some)), 1),
+        ((), 0, tuple(range(more, full_g)), 1),
     )
     arrays = (saved_input, saved_pre, grad_act)
     keep, send = 0, SLOTS // 2
@@ -540,7 +540,7 @@
 
 def fits(count_a, count_g):
     (full_a, half_a), full_g = split_rows(count_a), count_g // B
-    if count_a % H or count_g % B or full_a < 1 or full_g < 3:
+    if count_a % H or count_g % B or full_a < 1 or full_g < 4:
         return False
     return full_a + half_a + full_g <= 2 * (EDGE - 2)
 

time: 37.8 us -> 41.2 us (1.090)
  starting transfers between devices: 15.4 us -> 18.5 us
    ppermute x12, starting transfers between devices: 15.4 us -> 18.5 us  [swap(): return lax.ppermute(value, ('dp', 'tensor'), pairs)]
  transfers between devices with their start and end apart: 12 -> 12, of which waited for: 6 -> 6; matrix products, arithmetic and copies ran while one was open for 0% -> 0% of each run, Pallas kernels for 8% -> 7%
where the time goes in v16:
time: 41.2 us; the launch traced here: 41 us
  starting transfers between devices  18.5 us (45%)
  waiting for transfers between devices  15.4 us (37%)
  Pallas kernels  6.04 us (15%)
  between operations  0.74 us (2%)
    ppermute x12, starting transfers between devices, swap(): return lax.ppermute(value, ('dp', 'tensor'), pairs)  18.5 us
    ppermute x12, waiting for transfers between devices, swap(): return lax.ppermute(value, ('dp', 'tensor'), pairs)  15.4 us
    pallas_call x5, Pallas kernels, pack(): pl.pallas_call(functools.partial(pack_body, pieces, items, count_a, count...  4.48 us
    pallas_call x1, Pallas kernels, finish(): pl.pallas_call(functools.partial(finish_body, pieces, early, late, count_...  1.03 us
  transfers between devices with their start and end apart: 12, of which 6 were waited for; matrix products, arithmetic and copies ran while one was open for 0% of the time, Pallas kernels for 7%

profile of v16, /device:TPU:0, one launch (start us, length us, event | category | flops | bytes accessed | tf_op | source)
XLA Modules:
  0.0 41.0 jit_solution(1116194147055193334)
XLA Ops:
  0.6 1.7 %shard_map.50 = (f32[4,128,128]{2,1,0:T(8,128)S(1)}, f32[17,8,128]{2,1,0:T(8,128)S(1)}, bf16[128,2560]{1,0:T(8,128)(2,1)S(1)}) custom-call(bf16[128,2560]{1,0:T(8,128)(2,1)} %refs_0_.1), custom_call_target="tpu_custom_call" | custom-call | flops 4000000000 | bytes 1 | tf_op jit(solution)/shard_map/pallas_call | solution.py:235
  2.4 0.3 copy-done
  2.7 0.6 %shard_map.51 = (f32[4,176,128]{2,1,0:T(8,128)S(1)}, f32[17,8,128]{2,1,0:T(8,128)S(1)}) custom-call(f32[17,8,128]{2,1,0:T(8,128)S(1)} %get-tuple-element.35.refs_0_, bf16[128,2560]{1,0:T(8,128)(2,1)S(1)} %get-tuple-element.36.refs_1_, bf16[128,5120]{1,0:T(8,128)(2,1)S(1)} %copy-done, bf16[128,5120]{1,0:T(8,128)(2,1)S(1)} %copy-done.1), custom_call_target="tpu_custom_call" | custom-call | flops 1 | bytes 1 | tf_op jit(solution)/shard_map/pallas_call | solution.py:235
  3.2 3.1 %collective-permute-start.6 = (f32[4,176,128]{2,1,0:T(8,128)S(1)}, f32[4,176,128]{2,1,0:T(8,128)S(1)}, u32[]{:S(2)}, u32[]{:S(2)}) collective-permute-start(f32[4,176,128]{2,1,0:T(8,128)S(1)} %get-tuple-element.52), channel_id=1, source_target_pairs={{0,4},{1,3},{2,6},{3,1},{4,0},{5,7},{6,2},{7,5},{8,12},{9,11},{10,... | collective-permute-start | bytes 1081352 | tf_op jit(solution)/shard_map/ppermute | solution.py:468
  6.3 1.5 %collective-permute-start.5 = (f32[4,128,128]{2,1,0:T(8,128)S(1)}, f32[4,128,128]{2,1,0:T(8,128)S(1)}, u32[]{:S(2)}, u32[]{:S(2)}) collective-permute-start(f32[4,128,128]{2,1,0:T(8,128)S(1)} %get-tuple-element.51), channel_id=1, source_target_pairs={{0,2},{1,5},{2,0},{3,7},{4,6},{5,1},{6,4},{7,3},{8,10},{9,13},{10,... | collective-permute-start | bytes 786440 | tf_op jit(solution)/shard_map/ppermute | solution.py:468
  7.8 0.7 %shard_map.52 = (f32[4,136,128]{2,1,0:T(8,128)S(1)}, f32[4,72,128]{2,1,0:T(8,128)S(1)}, f32[17,8,128]{2,1,0:T(8,128)S(1)}) custom-call(f32[17,8,128]{2,1,0:T(8,128)S(1)} %get-tuple-element.37.refs_0_, bf16[128,2560]{1,0:T(8,128)(2,1)S(1)} %get-tuple-element.36.refs_1_, bf16[128,5120]{1,0:T(8,128)(2,1)S(1)} %copy-done, bf16[128,5120]{1,0:T(8,128)(2,1)S(1)} %copy-done.1), custom_call_target="tpu_custom_call" | custom-call | flops 1 | bytes 1 | tf_op jit(solution)/shard_map/pallas_call | solution.py:235
  8.5 0.9 %shard_map.53 = (f32[4,128,128]{2,1,0:T(8,128)S(1)}, f32[4,176,128]{2,1,0:T(8,128)S(1)}, f32[17,8,128]{2,1,0:T(8,128)S(1)}) custom-call(f32[17,8,128]{2,1,0:T(8,128)S(1)} %get-tuple-element.38.refs_0_, bf16[128,2560]{1,0:T(8,128)(2,1)S(1)} %get-tuple-element.36.refs_1_, bf16[128,5120]{1,0:T(8,128)(2,1)S(1)} %copy-done, bf16[128,5120]{1,0:T(8,128)(2,1)S(1)} %copy-done.1), custom_call_target="tpu_custom_call" | custom-call | flops 1 | bytes 1 | tf_op jit(solution)/shard_map/pallas_call | solution.py:235
  9.4 0.7 %shard_map.54 = (f32[4,136,128]{2,1,0:T(8,128)S(1)}, f32[4,72,128]{2,1,0:T(8,128)S(1)}, f32[17,8,128]{2,1,0:T(8,128)S(1)}) custom-call(f32[17,8,128]{2,1,0:T(8,128)S(1)} %get-tuple-element.39.refs_0_, bf16[128,2560]{1,0:T(8,128)(2,1)S(1)} %get-tuple-element.36.refs_1_, bf16[128,5120]{1,0:T(8,128)(2,1)S(1)} %copy-done, bf16[128,5120]{1,0:T(8,128)(2,1)S(1)} %copy-done.1), custom_call_target="tpu_custom_call" | custom-call | flops 1 | bytes 1 | tf_op jit(solution)/shard_map/pallas_call | solution.py:235
  10.1 0.6 %collective-permute-start = (f32[4,136,128]{2,1,0:T(8,128)S(1)}, f32[4,136,128]{2,1,0:T(8,128)S(1)}, u32[]{:S(2)}, u32[]{:S(2)}) collective-permute-start(f32[4,136,128]{2,1,0:T(8,128)S(1)} %get-tuple-element.42), channel_id=1, source_target_pairs={{0,2},{1,5},{2,0},{3,7},{4,6},{5,1},{6,4},{7,3},{8,10},{9,13},{10,... | collective-permute-start | bytes 835592 | tf_op jit(solution)/shard_map/ppermute | solution.py:468
  10.7 2.8 %collective-permute-done.5.refs_2_ = f32[4,128,128]{2,1,0:T(8,128)S(1)} collective-permute-done((f32[4,128,128]{2,1,0:T(8,128)S(1)}, f32[4,128,128]{2,1,0:T(8,128)S(1)}, u32[]{:S(2)}, u32[]{:S(2)}) %collective-permute-start.5) | collective-permute-done | bytes 262176 | tf_op jit(solution)/shard_map/ppermute | solution.py:468
  13.6 1.5 %collective-permute-done.6.refs_3_ = f32[4,176,128]{2,1,0:T(8,128)S(1)} collective-permute-done((f32[4,176,128]{2,1,0:T(8,128)S(1)}, f32[4,176,128]{2,1,0:T(8,128)S(1)}, u32[]{:S(2)}, u32[]{:S(2)}) %collective-permute-start.6) | collective-permute-done | bytes 360480 | tf_op jit(solution)/shard_map/ppermute | solution.py:468
  15.2 2.5 %collective-permute-start.7 = (f32[2,128,128]{2,1,0:T(8,128)S(1)}, f32[2,128,128]{2,1,0:T(8,128)S(1)}, u32[]{:S(2)}, u32[]{:S(2)}) collective-permute-start(f32[2,128,128]{2,1,0:T(8,128)S(1)} %get-tuple-element.55), channel_id=1, source_target_pairs={{0,4},{1,3},{2,6},{3,1},{4,0},{5,7},{6,2},{7,5},{8,12},{9,11},{10,... | collective-permute-start | bytes 393224 | tf_op jit(solution)/shard_map/ppermute | solution.py:468
  17.7 1.5 %collective-permute-start.8 = (f32[2,176,128]{2,1,0:T(8,128)S(1)}, f32[2,176,128]{2,1,0:T(8,128)S(1)}, u32[]{:S(2)}, u32[]{:S(2)}) collective-permute-start(f32[2,176,128]{2,1,0:T(8,128)S(1)} %get-tuple-element.56), channel_id=1, source_target_pairs={{0,2},{1,5},{2,0},{3,7},{4,6},{5,1},{6,4},{7,3},{8,10},{9,13},{10,... | collective-permute-start | bytes 540680 | tf_op jit(solution)/shard_map/ppermute | solution.py:468
  19.2 1.9 %collective-permute-start.1 = (f32[4,72,128]{2,1,0:T(8,128)S(1)}, f32[4,72,128]{2,1,0:T(8,128)S(1)}, u32[]{:S(2)}, u32[]{:S(2)}) collective-permute-start(f32[4,72,128]{2,1,0:T(8,128)S(1)} %get-tuple-element.43), channel_id=1, source_target_pairs={{0,4},{1,3},{2,6},{3,1},{4,0},{5,7},{6,2},{7,5},{8,12},{9,11},{10,... | collective-permute-start | bytes 442376 | tf_op jit(solution)/shard_map/ppermute | solution.py:468
  21.1 2.5 %collective-permute-done.9.refs_5_ = f32[2,128]{1,0:T(2,128)S(1)} collective-permute-done((f32[2,128]{1,0:T(2,128)S(1)}, f32[2,128]{1,0:T(2,128)S(1)}, u32[]{:S(2)}, u32[]{:S(2)}) %collective-permute-start.9) | collective-permute-done | bytes 1056 | tf_op jit(solution)/shard_map/ppermute | solution.py:468
  23.7 2.7 %collective-permute-start.11 = (f32[1,304,128]{2,1,0:T(8,128)S(1)}, f32[1,304,128]{2,1,0:T(8,128)S(1)}, u32[]{:S(2)}, u32[]{:S(2)}) collective-permute-start(f32[1,304,128]{2,1,0:T(8,128)S(1)} %get-tuple-element.63), channel_id=1, source_target_pairs={{0,8},{1,9},{2,10},{3,11},{4,12},{5,13},{6,14},{7,15},{8,0},{9,1},... | collective-permute-start | bytes 466952 | tf_op jit(solution)/shard_map/ppermute | solution.py:468
  26.4 1.0 %collective-permute-start.3 = (f32[2,136,128]{2,1,0:T(8,128)S(1)}, f32[2,136,128]{2,1,0:T(8,128)S(1)}, u32[]{:S(2)}, u32[]{:S(2)}) collective-permute-start(f32[2,136,128]{2,1,0:T(8,128)S(1)} %get-tuple-element.47), channel_id=1, source_target_pairs={{0,4},{1,3},{2,6},{3,1},{4,0},{5,7},{6,2},{7,5},{8,12},{9,11},{10,... | collective-permute-start | bytes 417800 | tf_op jit(solution)/shard_map/ppermute | solution.py:468
  27.4 1.8 %collective-permute-start.4 = (f32[2,72,128]{2,1,0:T(8,128)S(1)}, f32[2,72,128]{2,1,0:T(8,128)S(1)}, u32[]{:S(2)}, u32[]{:S(2)}) collective-permute-start(f32[2,72,128]{2,1,0:T(8,128)S(1)} %get-tuple-element.48), channel_id=1, source_target_pairs={{0,2},{1,5},{2,0},{3,7},{4,6},{5,1},{6,4},{7,3},{8,10},{9,13},{10,... | collective-permute-start | bytes 221192 | tf_op jit(solution)/shard_map/ppermute | solution.py:468
  29.2 2.6 %collective-permute-done.4.refs_3_ = f32[2,72,128]{2,1,0:T(8,128)S(1)} collective-permute-done((f32[2,72,128]{2,1,0:T(8,128)S(1)}, f32[2,72,128]{2,1,0:T(8,128)S(1)}, u32[]{:S(2)}, u32[]{:S(2)}) %collective-permute-start.4) | collective-permute-done | bytes 73760 | tf_op jit(solution)/shard_map/ppermute | solution.py:468
  31.8 1.4 %collective-permute-done.3.refs_2_ = f32[2,136,128]{2,1,0:T(8,128)S(1)} collective-permute-done((f32[2,136,128]{2,1,0:T(8,128)S(1)}, f32[2,136,128]{2,1,0:T(8,128)S(1)}, u32[]{:S(2)}, u32[]{:S(2)}) %collective-permute-start.3) | collective-permute-done | bytes 139296 | tf_op jit(solution)/shard_map/ppermute | solution.py:468
  33.2 1.9 %collective-permute-start.10 = (f32[1,208,128]{2,1,0:T(8,128)S(1)}, f32[1,208,128]{2,1,0:T(8,128)S(1)}, u32[]{:S(2)}, u32[]{:S(2)}) collective-permute-start(f32[1,208,128]{2,1,0:T(8,128)S(1)} %get-tuple-element.60), channel_id=1, source_target_pairs={{0,8},{1,9},{2,10},{3,11},{4,12},{5,13},{6,14},{7,15},{8,0},{9,1},... | collective-permute-start | bytes 319496 | tf_op jit(solution)/shard_map/ppermute | solution.py:468
  35.0 0.3 shard_map.59
  35.4 4.6 %collective-permute-done.10.refs_2_ = f32[1,208,128]{2,1,0:T(8,128)S(1)} collective-permute-done((f32[1,208,128]{2,1,0:T(8,128)S(1)}, f32[1,208,128]{2,1,0:T(8,128)S(1)}, u32[]{:S(2)}, u32[]{:S(2)}) %collective-permute-start.10) | collective-permute-done | bytes 106528 | tf_op jit(solution)/shard_map/ppermute | solution.py:468
  40.0 1.0 %shard_map.60 = (f32[320,128]{1,0:T(8,128)}, f32[640,128]{1,0:T(8,128)}) custom-call(f32[1,136,128]{2,1,0:T(8,128)S(1)} %get-tuple-element.58.refs_0_, f32[1,72,128]{2,1,0:T(8,128)S(1)} %get-tuple-element.59.refs_1_, f32[1,208,128]{2,1,0:T(8,128)S(1)} %collective-permute-done.10.refs_2_, f32[320,128]{1,0:T(8,128)S(1)} %get-tuple-element.64.refs_3_, ...), custom_call_target="tpu_custom_call" | custom-call | tf_op jit(solution)/shard_map/pallas_call | solution.py:444
  (17 shorter events, 0.3 us)
Async XLA Ops:
  0.6 1.7 %copy-start.1 = (bf16[128,5120]{1,0:T(8,128)(2,1)S(1)}, bf16[128,5120]{1,0:T(8,128)(2,1)}, u32[]{:S(2)}) copy-start(bf16[128,5120]{1,0:T(8,128)(2,1)} %refs_3_.7) | copy-start | bytes 3932164
  0.6 2.0 %copy-start = (bf16[128,5120]{1,0:T(8,128)(2,1)S(1)}, bf16[128,5120]{1,0:T(8,128)(2,1)}, u32[]{:S(2)}) copy-start(bf16[128,5120]{1,0:T(8,128)(2,1)} %refs_2_.7) | copy-start | bytes 3932164
  3.2 11.9 %collective-permute-start.6 = (f32[4,176,128]{2,1,0:T(8,128)S(1)}, f32[4,176,128]{2,1,0:T(8,128)S(1)}, u32[]{:S(2)}, u32[]{:S(2)}) collective-permute-start(f32[4,176,128]{2,1,0:T(8,128)S(1)} %get-tuple-element.52), channel_id=1, source_target_pairs={{0,4},{1,3},{2,6},{3,1},{4,0},{5,7},{6,2},{7,5},{8,12},{9,11},{10,... | collective-permute-start | bytes 1081352 | tf_op jit(solution)/shard_map/ppermute | solution.py:468
  6.3 7.3 %collective-permute-start.5 = (f32[4,128,128]{2,1,0:T(8,128)S(1)}, f32[4,128,128]{2,1,0:T(8,128)S(1)}, u32[]{:S(2)}, u32[]{:S(2)}) collective-permute-start(f32[4,128,128]{2,1,0:T(8,128)S(1)} %get-tuple-element.51), channel_id=1, source_target_pairs={{0,2},{1,5},{2,0},{3,7},{4,6},{5,1},{6,4},{7,3},{8,10},{9,13},{10,... | collective-permute-start | bytes 786440 | tf_op jit(solution)/shard_map/ppermute | solution.py:468
  10.1 9.1 %collective-permute-start.2 = (f32[2,128]{1,0:T(2,128)S(1)}, f32[2,128]{1,0:T(2,128)S(1)}, u32[]{:S(2)}, u32[]{:S(2)}) collective-permute-start(f32[2,128]{1,0:T(2,128)S(1)} %slice_bitcast_fusion), channel_id=1, source_target_pairs={{0,1},{1,0},{2,3},{3,2},{4,5},{5,4},{6,7},{7,6},{8,9},{9,8},{10,11... | collective-permute-start | bytes 3080 | tf_op jit(solution)/shard_map/ppermute | solution.py:468
  10.1 16.3 %collective-permute-start = (f32[4,136,128]{2,1,0:T(8,128)S(1)}, f32[4,136,128]{2,1,0:T(8,128)S(1)}, u32[]{:S(2)}, u32[]{:S(2)}) collective-permute-start(f32[4,136,128]{2,1,0:T(8,128)S(1)} %get-tuple-element.42), channel_id=1, source_target_pairs={{0,2},{1,5},{2,0},{3,7},{4,6},{5,1},{6,4},{7,3},{8,10},{9,13},{10,... | collective-permute-start | bytes 835592 | tf_op jit(solution)/shard_map/ppermute | solution.py:468
  15.2 8.5 %collective-permute-start.7 = (f32[2,128,128]{2,1,0:T(8,128)S(1)}, f32[2,128,128]{2,1,0:T(8,128)S(1)}, u32[]{:S(2)}, u32[]{:S(2)}) collective-permute-start(f32[2,128,128]{2,1,0:T(8,128)S(1)} %get-tuple-element.55), channel_id=1, source_target_pairs={{0,4},{1,3},{2,6},{3,1},{4,0},{5,7},{6,2},{7,5},{8,12},{9,11},{10,... | collective-permute-start | bytes 393224 | tf_op jit(solution)/shard_map/ppermute | solution.py:468
  17.7 6.0 %collective-permute-start.8 = (f32[2,176,128]{2,1,0:T(8,128)S(1)}, f32[2,176,128]{2,1,0:T(8,128)S(1)}, u32[]{:S(2)}, u32[]{:S(2)}) collective-permute-start(f32[2,176,128]{2,1,0:T(8,128)S(1)} %get-tuple-element.56), channel_id=1, source_target_pairs={{0,2},{1,5},{2,0},{3,7},{4,6},{5,1},{6,4},{7,3},{8,10},{9,13},{10,... | collective-permute-start | bytes 540680 | tf_op jit(solution)/shard_map/ppermute | solution.py:468
  19.2 4.5 %collective-permute-start.9 = (f32[2,128]{1,0:T(2,128)S(1)}, f32[2,128]{1,0:T(2,128)S(1)}, u32[]{:S(2)}, u32[]{:S(2)}) collective-permute-start(f32[2,128]{1,0:T(2,128)S(1)} %fusion.refs_4_), channel_id=1, source_target_pairs={{0,6},{1,7},{2,4},{3,5},{4,2},{5,3},{6,0},{7,1},{8,14},{9,15},{10,... | collective-permute-start | bytes 3080 | tf_op jit(solution)/shard_map/ppermute | solution.py:468
  19.2 7.2 %collective-permute-start.1 = (f32[4,72,128]{2,1,0:T(8,128)S(1)}, f32[4,72,128]{2,1,0:T(8,128)S(1)}, u32[]{:S(2)}, u32[]{:S(2)}) collective-permute-start(f32[4,72,128]{2,1,0:T(8,128)S(1)} %get-tuple-element.43), channel_id=1, source_target_pairs={{0,4},{1,3},{2,6},{3,1},{4,0},{5,7},{6,2},{7,5},{8,12},{9,11},{10,... | collective-permute-start | bytes 442376 | tf_op jit(solution)/shard_map/ppermute | solution.py:468
  23.7 11.3 %collective-permute-start.11 = (f32[1,304,128]{2,1,0:T(8,128)S(1)}, f32[1,304,128]{2,1,0:T(8,128)S(1)}, u32[]{:S(2)}, u32[]{:S(2)}) collective-permute-start(f32[1,304,128]{2,1,0:T(8,128)S(1)} %get-tuple-element.63), channel_id=1, source_target_pairs={{0,8},{1,9},{2,10},{3,11},{4,12},{5,13},{6,14},{7,15},{8,0},{9,1},... | collective-permute-start | bytes 466952 | tf_op jit(solution)/shard_map/ppermute | solution.py:468
  26.4 6.7 %collective-permute-start.3 = (f32[2,136,128]{2,1,0:T(8,128)S(1)}, f32[2,136,128]{2,1,0:T(8,128)S(1)}, u32[]{:S(2)}, u32[]{:S(2)}) collective-permute-start(f32[2,136,128]{2,1,0:T(8,128)S(1)} %get-tuple-element.47), channel_id=1, source_target_pairs={{0,4},{1,3},{2,6},{3,1},{4,0},{5,7},{6,2},{7,5},{8,12},{9,11},{10,... | collective-permute-start | bytes 417800 | tf_op jit(solution)/shard_map/ppermute | solution.py:468
  27.4 4.4 %collective-permute-start.4 = (f32[2,72,128]{2,1,0:T(8,128)S(1)}, f32[2,72,128]{2,1,0:T(8,128)S(1)}, u32[]{:S(2)}, u32[]{:S(2)}) collective-permute-start(f32[2,72,128]{2,1,0:T(8,128)S(1)} %get-tuple-element.48), channel_id=1, source_target_pairs={{0,2},{1,5},{2,0},{3,7},{4,6},{5,1},{6,4},{7,3},{8,10},{9,13},{10,... | collective-permute-start | bytes 221192 | tf_op jit(solution)/shard_map/ppermute | solution.py:468
  33.2 6.8 %collective-permute-start.10 = (f32[1,208,128]{2,1,0:T(8,128)S(1)}, f32[1,208,128]{2,1,0:T(8,128)S(1)}, u32[]{:S(2)}, u32[]{:S(2)}) collective-permute-start(f32[1,208,128]{2,1,0:T(8,128)S(1)} %get-tuple-element.60), channel_id=1, source_target_pairs={{0,8},{1,9},{2,10},{3,11},{4,12},{5,13},{6,14},{7,15},{8,0},{9,1},... | collective-permute-start | bytes 319496 | tf_op jit(solution)/shard_map/ppermute | solution.py:468

commit v17 on v14

--- a/solution.py
+++ b/solution.py
@@ -59,7 +59,7 @@
 EDGE = 8
 SLOTS = 8
 X, NEAR, FAR = 0, 1, 2
-KINDS = (((X, NEAR, FAR), (NEAR, X, FAR)), ((NEAR, X, FAR), (X, NEAR, FAR)))
+KINDS = (((X, NEAR, FAR), (X, NEAR, FAR)), ((NEAR, X, FAR), (NEAR, X, FAR)))
 NOTES = len(KINDS) * SLOTS
 
 WEIGHTS = {((0, 2), 2): 2 * 10**9}

time: 37.8 us -> 36.7 us (0.971)
  waiting for transfers between devices: 15.8 us -> 13.5 us
  starting transfers between devices: 15.4 us -> 16.5 us
    ppermute x12, waiting for transfers between devices: 15.8 us -> 13.5 us  [swap(): return lax.ppermute(value, ('dp', 'tensor'), pairs)]
    ppermute x12, starting transfers between devices: 15.4 us -> 16.5 us  [swap(): return lax.ppermute(value, ('dp', 'tensor'), pairs)]
  transfers between devices with their start and end apart: 12 -> 12, of which waited for: 6 -> 9; matrix products, arithmetic and copies ran while one was open for 0% -> 0% of each run, Pallas kernels for 8% -> 8%
where the time goes in v17:
time: 36.7 us; the launch traced here: 36.6 us
  starting transfers between devices  16.5 us (45%)
  waiting for transfers between devices  13.5 us (37%)
  Pallas kernels  5.76 us (16%)
  between operations  0.73 us (2%)
    ppermute x12, starting transfers between devices, swap(): return lax.ppermute(value, ('dp', 'tensor'), pairs)  16.5 us
    ppermute x12, waiting for transfers between devices, swap(): return lax.ppermute(value, ('dp', 'tensor'), pairs)  13.5 us
    pallas_call x5, Pallas kernels, pack(): pl.pallas_call(functools.partial(pack_body, pieces, items, count_a, count...  4.25 us
    pallas_call x1, Pallas kernels, finish(): pl.pallas_call(functools.partial(finish_body, pieces, early, late, count_...  1.03 us
  transfers between devices with their start and end apart: 12, of which 9 were waited for; matrix products, arithmetic and copies ran while one was open for 0% of the time, Pallas kernels for 8%

profile of v17, /device:TPU:0, one launch (start us, length us, event | category | flops | bytes accessed | tf_op | source)
XLA Modules:
  0.0 36.6 jit_solution(4649352530575634490)
XLA Ops:
  0.6 1.7 %shard_map.50 = (f32[4,128,128]{2,1,0:T(8,128)S(1)}, f32[17,8,128]{2,1,0:T(8,128)S(1)}, bf16[128,2560]{1,0:T(8,128)(2,1)S(1)}) custom-call(bf16[128,2560]{1,0:T(8,128)(2,1)} %refs_0_.1), custom_call_target="tpu_custom_call" | custom-call | flops 4000000000 | bytes 1 | tf_op jit(solution)/shard_map/pallas_call | solution.py:235
  2.3 3.0 %collective-permute-start.5 = (f32[4,128,128]{2,1,0:T(8,128)S(1)}, f32[4,128,128]{2,1,0:T(8,128)S(1)}, u32[]{:S(2)}, u32[]{:S(2)}) collective-permute-start(f32[4,128,128]{2,1,0:T(8,128)S(1)} %get-tuple-element.51), channel_id=1, source_target_pairs={{0,2},{1,3},{2,0},{3,1},{4,6},{5,7},{6,4},{7,5},{8,10},{9,11},{10,... | collective-permute-start | bytes 786440 | tf_op jit(solution)/shard_map/ppermute | solution.py:468
  5.3 0.4 %shard_map.51 = (f32[4,112,128]{2,1,0:T(8,128)S(1)}, f32[17,8,128]{2,1,0:T(8,128)S(1)}) custom-call(f32[17,8,128]{2,1,0:T(8,128)S(1)} %get-tuple-element.35.refs_0_, bf16[128,2560]{1,0:T(8,128)(2,1)S(1)} %get-tuple-element.36.refs_1_, bf16[128,5120]{1,0:T(8,128)(2,1)S(1)} %copy-done, bf16[128,5120]{1,0:T(8,128)(2,1)S(1)} %copy-done.1), custom_call_target="tpu_custom_call" | custom-call | flops 1 | bytes 1 | tf_op jit(solution)/shard_map/pallas_call | solution.py:235
  5.8 1.6 %collective-permute-start.6 = (f32[4,112,128]{2,1,0:T(8,128)S(1)}, f32[4,112,128]{2,1,0:T(8,128)S(1)}, u32[]{:S(2)}, u32[]{:S(2)}) collective-permute-start(f32[4,112,128]{2,1,0:T(8,128)S(1)} %get-tuple-element.52), channel_id=1, source_target_pairs={{0,4},{1,5},{2,6},{3,7},{4,0},{5,1},{6,2},{7,3},{8,12},{9,13},{10,... | collective-permute-start | bytes 688136 | tf_op jit(solution)/shard_map/ppermute | solution.py:468
  7.4 0.8 %shard_map.52 = (f32[4,136,128]{2,1,0:T(8,128)S(1)}, f32[4,136,128]{2,1,0:T(8,128)S(1)}, f32[17,8,128]{2,1,0:T(8,128)S(1)}) custom-call(f32[17,8,128]{2,1,0:T(8,128)S(1)} %get-tuple-element.37.refs_0_, bf16[128,2560]{1,0:T(8,128)(2,1)S(1)} %get-tuple-element.36.refs_1_, bf16[128,5120]{1,0:T(8,128)(2,1)S(1)} %copy-done, bf16[128,5120]{1,0:T(8,128)(2,1)S(1)} %copy-done.1), custom_call_target="tpu_custom_call" | custom-call | flops 1 | bytes 1 | tf_op jit(solution)/shard_map/pallas_call | solution.py:235
  8.2 0.6 %collective-permute-start = (f32[4,136,128]{2,1,0:T(8,128)S(1)}, f32[4,136,128]{2,1,0:T(8,128)S(1)}, u32[]{:S(2)}, u32[]{:S(2)}) collective-permute-start(f32[4,136,128]{2,1,0:T(8,128)S(1)} %get-tuple-element.42), channel_id=1, source_target_pairs={{0,2},{1,3},{2,0},{3,1},{4,6},{5,7},{6,4},{7,5},{8,10},{9,11},{10,... | collective-permute-start | bytes 835592 | tf_op jit(solution)/shard_map/ppermute | solution.py:468
  9.0 0.5 %shard_map.53 = (f32[4,128,128]{2,1,0:T(8,128)S(1)}, f32[4,112,128]{2,1,0:T(8,128)S(1)}, f32[17,8,128]{2,1,0:T(8,128)S(1)}) custom-call(f32[17,8,128]{2,1,0:T(8,128)S(1)} %get-tuple-element.38.refs_0_, bf16[128,2560]{1,0:T(8,128)(2,1)S(1)} %get-tuple-element.36.refs_1_, bf16[128,5120]{1,0:T(8,128)(2,1)S(1)} %copy-done, bf16[128,5120]{1,0:T(8,128)(2,1)S(1)} %copy-done.1), custom_call_target="tpu_custom_call" | custom-call | flops 1 | bytes 1 | tf_op jit(solution)/shard_map/pallas_call | solution.py:235
  9.5 0.8 %shard_map.54 = (f32[4,136,128]{2,1,0:T(8,128)S(1)}, f32[4,136,128]{2,1,0:T(8,128)S(1)}, f32[17,8,128]{2,1,0:T(8,128)S(1)}) custom-call(f32[17,8,128]{2,1,0:T(8,128)S(1)} %get-tuple-element.39.refs_0_, bf16[128,2560]{1,0:T(8,128)(2,1)S(1)} %get-tuple-element.36.refs_1_, bf16[128,5120]{1,0:T(8,128)(2,1)S(1)} %copy-done, bf16[128,5120]{1,0:T(8,128)(2,1)S(1)} %copy-done.1), custom_call_target="tpu_custom_call" | custom-call | flops 1 | bytes 1 | tf_op jit(solution)/shard_map/pallas_call | solution.py:235
  10.4 4.0 %collective-permute-done.6.refs_3_ = f32[4,112,128]{2,1,0:T(8,128)S(1)} collective-permute-done((f32[4,112,128]{2,1,0:T(8,128)S(1)}, f32[4,112,128]{2,1,0:T(8,128)S(1)}, u32[]{:S(2)}, u32[]{:S(2)}) %collective-permute-start.6) | collective-permute-done | bytes 229408 | tf_op jit(solution)/shard_map/ppermute | solution.py:468
  14.7 1.9 %collective-permute-start.7 = (f32[2,128,128]{2,1,0:T(8,128)S(1)}, f32[2,128,128]{2,1,0:T(8,128)S(1)}, u32[]{:S(2)}, u32[]{:S(2)}) collective-permute-start(f32[2,128,128]{2,1,0:T(8,128)S(1)} %get-tuple-element.55), channel_id=1, source_target_pairs={{0,4},{1,5},{2,6},{3,7},{4,0},{5,1},{6,2},{7,3},{8,12},{9,13},{10,... | collective-permute-start | bytes 393224 | tf_op jit(solution)/shard_map/ppermute | solution.py:468
  16.7 1.4 %collective-permute-start.9 = (f32[2,128]{1,0:T(2,128)S(1)}, f32[2,128]{1,0:T(2,128)S(1)}, u32[]{:S(2)}, u32[]{:S(2)}) collective-permute-start(f32[2,128]{1,0:T(2,128)S(1)} %fusion.refs_4_), channel_id=1, source_target_pairs={{0,6},{1,7},{2,4},{3,5},{4,2},{5,3},{6,0},{7,1},{8,14},{9,15},{10,... | collective-permute-start | bytes 3080 | tf_op jit(solution)/shard_map/ppermute | solution.py:468
  18.0 0.4 %collective-permute-done.refs_2_ = f32[4,136,128]{2,1,0:T(8,128)S(1)} collective-permute-done((f32[4,136,128]{2,1,0:T(8,128)S(1)}, f32[4,136,128]{2,1,0:T(8,128)S(1)}, u32[]{:S(2)}, u32[]{:S(2)}) %collective-permute-start) | collective-permute-done | bytes 278560 | tf_op jit(solution)/shard_map/ppermute | solution.py:468
  18.4 1.9 %collective-permute-done.1.refs_3_ = f32[4,136,128]{2,1,0:T(8,128)S(1)} collective-permute-done((f32[4,136,128]{2,1,0:T(8,128)S(1)}, f32[4,136,128]{2,1,0:T(8,128)S(1)}, u32[]{:S(2)}, u32[]{:S(2)}) %collective-permute-start.1) | collective-permute-done | bytes 278560 | tf_op jit(solution)/shard_map/ppermute | solution.py:468
  20.4 1.6 %collective-permute-start.3 = (f32[2,136,128]{2,1,0:T(8,128)S(1)}, f32[2,136,128]{2,1,0:T(8,128)S(1)}, u32[]{:S(2)}, u32[]{:S(2)}) collective-permute-start(f32[2,136,128]{2,1,0:T(8,128)S(1)} %get-tuple-element.47), channel_id=1, source_target_pairs={{0,4},{1,5},{2,6},{3,7},{4,0},{5,1},{6,2},{7,3},{8,12},{9,13},{10,... | collective-permute-start | bytes 417800 | tf_op jit(solution)/shard_map/ppermute | solution.py:468
  22.0 0.5 %collective-permute-start.4 = (f32[2,136,128]{2,1,0:T(8,128)S(1)}, f32[2,136,128]{2,1,0:T(8,128)S(1)}, u32[]{:S(2)}, u32[]{:S(2)}) collective-permute-start(f32[2,136,128]{2,1,0:T(8,128)S(1)} %get-tuple-element.48), channel_id=1, source_target_pairs={{0,2},{1,3},{2,0},{3,1},{4,6},{5,7},{6,4},{7,5},{8,10},{9,11},{10,... | collective-permute-start | bytes 417800 | tf_op jit(solution)/shard_map/ppermute | solution.py:468
  22.8 0.3 collective-permute-done.7.refs_2_
  23.1 2.7 %collective-permute-start.11 = (f32[1,240,128]{2,1,0:T(8,128)S(1)}, f32[1,240,128]{2,1,0:T(8,128)S(1)}, u32[]{:S(2)}, u32[]{:S(2)}) collective-permute-start(f32[1,240,128]{2,1,0:T(8,128)S(1)} %get-tuple-element.63), channel_id=1, source_target_pairs={{0,8},{1,9},{2,10},{3,11},{4,12},{5,13},{6,14},{7,15},{8,0},{9,1},... | collective-permute-start | bytes 368648 | tf_op jit(solution)/shard_map/ppermute | solution.py:468
  25.8 1.0 %collective-permute-done.3.refs_2_ = f32[2,136,128]{2,1,0:T(8,128)S(1)} collective-permute-done((f32[2,136,128]{2,1,0:T(8,128)S(1)}, f32[2,136,128]{2,1,0:T(8,128)S(1)}, u32[]{:S(2)}, u32[]{:S(2)}) %collective-permute-start.3) | collective-permute-done | bytes 139296 | tf_op jit(solution)/shard_map/ppermute | solution.py:468
  26.8 0.3 collective-permute-done.4.refs_3_
  27.1 2.7 %collective-permute-start.10 = (f32[1,272,128]{2,1,0:T(8,128)S(1)}, f32[1,272,128]{2,1,0:T(8,128)S(1)}, u32[]{:S(2)}, u32[]{:S(2)}) collective-permute-start(f32[1,272,128]{2,1,0:T(8,128)S(1)} %get-tuple-element.60), channel_id=1, source_target_pairs={{0,8},{1,9},{2,10},{3,11},{4,12},{5,13},{6,14},{7,15},{8,0},{9,1},... | collective-permute-start | bytes 417800 | tf_op jit(solution)/shard_map/ppermute | solution.py:468
  29.8 4.3 %collective-permute-done.11.refs_2_ = f32[1,240,128]{2,1,0:T(8,128)S(1)} collective-permute-done((f32[1,240,128]{2,1,0:T(8,128)S(1)}, f32[1,240,128]{2,1,0:T(8,128)S(1)}, u32[]{:S(2)}, u32[]{:S(2)}) %collective-permute-start.11) | collective-permute-done | bytes 122912 | tf_op jit(solution)/shard_map/ppermute | solution.py:468
  34.0 0.3 shard_map.59
  34.3 1.2 %collective-permute-done.10.refs_2_ = f32[1,272,128]{2,1,0:T(8,128)S(1)} collective-permute-done((f32[1,272,128]{2,1,0:T(8,128)S(1)}, f32[1,272,128]{2,1,0:T(8,128)S(1)}, u32[]{:S(2)}, u32[]{:S(2)}) %collective-permute-start.10) | collective-permute-done | bytes 139296 | tf_op jit(solution)/shard_map/ppermute | solution.py:468
  35.5 1.0 %shard_map.60 = (f32[320,128]{1,0:T(8,128)}, f32[640,128]{1,0:T(8,128)}) custom-call(f32[1,136,128]{2,1,0:T(8,128)S(1)} %get-tuple-element.58.refs_0_, f32[1,136,128]{2,1,0:T(8,128)S(1)} %get-tuple-element.59.refs_1_, f32[1,272,128]{2,1,0:T(8,128)S(1)} %collective-permute-done.10.refs_2_, f32[320,128]{1,0:T(8,128)S(1)} %get-tuple-element.64.refs_3_, ...), custom_call_target="tpu_custom_call" | custom-call | tf_op jit(solution)/shard_map/pallas_call | solution.py:444
  (17 shorter events, 0.9 us)
Async XLA Ops:
  0.6 4.7 %copy-start.1 = (bf16[128,5120]{1,0:T(8,128)(2,1)S(1)}, bf16[128,5120]{1,0:T(8,128)(2,1)}, u32[]{:S(2)}) copy-start(bf16[128,5120]{1,0:T(8,128)(2,1)} %refs_3_.7) | copy-start | bytes 3932164
  0.6 4.7 %copy-start = (bf16[128,5120]{1,0:T(8,128)(2,1)S(1)}, bf16[128,5120]{1,0:T(8,128)(2,1)}, u32[]{:S(2)}) copy-start(bf16[128,5120]{1,0:T(8,128)(2,1)} %refs_2_.7) | copy-start | bytes 3932164
  2.3 12.1 %collective-permute-start.5 = (f32[4,128,128]{2,1,0:T(8,128)S(1)}, f32[4,128,128]{2,1,0:T(8,128)S(1)}, u32[]{:S(2)}, u32[]{:S(2)}) collective-permute-start(f32[4,128,128]{2,1,0:T(8,128)S(1)} %get-tuple-element.51), channel_id=1, source_target_pairs={{0,2},{1,3},{2,0},{3,1},{4,6},{5,7},{6,4},{7,5},{8,10},{9,11},{10,... | collective-permute-start | bytes 786440 | tf_op jit(solution)/shard_map/ppermute | solution.py:468
  5.8 8.6 %collective-permute-start.6 = (f32[4,112,128]{2,1,0:T(8,128)S(1)}, f32[4,112,128]{2,1,0:T(8,128)S(1)}, u32[]{:S(2)}, u32[]{:S(2)}) collective-permute-start(f32[4,112,128]{2,1,0:T(8,128)S(1)} %get-tuple-element.52), channel_id=1, source_target_pairs={{0,4},{1,5},{2,6},{3,7},{4,0},{5,1},{6,2},{7,3},{8,12},{9,13},{10,... | collective-permute-start | bytes 688136 | tf_op jit(solution)/shard_map/ppermute | solution.py:468
  8.2 10.2 %collective-permute-start = (f32[4,136,128]{2,1,0:T(8,128)S(1)}, f32[4,136,128]{2,1,0:T(8,128)S(1)}, u32[]{:S(2)}, u32[]{:S(2)}) collective-permute-start(f32[4,136,128]{2,1,0:T(8,128)S(1)} %get-tuple-element.42), channel_id=1, source_target_pairs={{0,2},{1,3},{2,0},{3,1},{4,6},{5,7},{6,4},{7,5},{8,10},{9,11},{10,... | collective-permute-start | bytes 835592 | tf_op jit(solution)/shard_map/ppermute | solution.py:468
  8.8 11.5 %collective-permute-start.1 = (f32[4,136,128]{2,1,0:T(8,128)S(1)}, f32[4,136,128]{2,1,0:T(8,128)S(1)}, u32[]{:S(2)}, u32[]{:S(2)}) collective-permute-start(f32[4,136,128]{2,1,0:T(8,128)S(1)} %get-tuple-element.43), channel_id=1, source_target_pairs={{0,4},{1,5},{2,6},{3,7},{4,0},{5,1},{6,2},{7,3},{8,12},{9,13},{10,... | collective-permute-start | bytes 835592 | tf_op jit(solution)/shard_map/ppermute | solution.py:468
  10.4 6.3 %collective-permute-start.2 = (f32[2,128]{1,0:T(2,128)S(1)}, f32[2,128]{1,0:T(2,128)S(1)}, u32[]{:S(2)}, u32[]{:S(2)}) collective-permute-start(f32[2,128]{1,0:T(2,128)S(1)} %slice_bitcast_fusion), channel_id=1, source_target_pairs={{0,1},{1,0},{2,3},{3,2},{4,5},{5,4},{6,7},{7,6},{8,9},{9,8},{10,11... | collective-permute-start | bytes 3080 | tf_op jit(solution)/shard_map/ppermute | solution.py:468
  14.5 8.3 %collective-permute-start.8 = (f32[2,112,128]{2,1,0:T(8,128)S(1)}, f32[2,112,128]{2,1,0:T(8,128)S(1)}, u32[]{:S(2)}, u32[]{:S(2)}) collective-permute-start(f32[2,112,128]{2,1,0:T(8,128)S(1)} %get-tuple-element.56), channel_id=1, source_target_pairs={{0,2},{1,3},{2,0},{3,1},{4,6},{5,7},{6,4},{7,5},{8,10},{9,11},{10,... | collective-permute-start | bytes 344072 | tf_op jit(solution)/shard_map/ppermute | solution.py:468
  14.7 8.4 %collective-permute-start.7 = (f32[2,128,128]{2,1,0:T(8,128)S(1)}, f32[2,128,128]{2,1,0:T(8,128)S(1)}, u32[]{:S(2)}, u32[]{:S(2)}) collective-permute-start(f32[2,128,128]{2,1,0:T(8,128)S(1)} %get-tuple-element.55), channel_id=1, source_target_pairs={{0,4},{1,5},{2,6},{3,7},{4,0},{5,1},{6,2},{7,3},{8,12},{9,13},{10,... | collective-permute-start | bytes 393224 | tf_op jit(solution)/shard_map/ppermute | solution.py:468
  16.7 6.1 %collective-permute-start.9 = (f32[2,128]{1,0:T(2,128)S(1)}, f32[2,128]{1,0:T(2,128)S(1)}, u32[]{:S(2)}, u32[]{:S(2)}) collective-permute-start(f32[2,128]{1,0:T(2,128)S(1)} %fusion.refs_4_), channel_id=1, source_target_pairs={{0,6},{1,7},{2,4},{3,5},{4,2},{5,3},{6,0},{7,1},{8,14},{9,15},{10,... | collective-permute-start | bytes 3080 | tf_op jit(solution)/shard_map/ppermute | solution.py:468
  20.4 6.4 %collective-permute-start.3 = (f32[2,136,128]{2,1,0:T(8,128)S(1)}, f32[2,136,128]{2,1,0:T(8,128)S(1)}, u32[]{:S(2)}, u32[]{:S(2)}) collective-permute-start(f32[2,136,128]{2,1,0:T(8,128)S(1)} %get-tuple-element.47), channel_id=1, source_target_pairs={{0,4},{1,5},{2,6},{3,7},{4,0},{5,1},{6,2},{7,3},{8,12},{9,13},{10,... | collective-permute-start | bytes 417800 | tf_op jit(solution)/shard_map/ppermute | solution.py:468
  22.0 5.1 %collective-permute-start.4 = (f32[2,136,128]{2,1,0:T(8,128)S(1)}, f32[2,136,128]{2,1,0:T(8,128)S(1)}, u32[]{:S(2)}, u32[]{:S(2)}) collective-permute-start(f32[2,136,128]{2,1,0:T(8,128)S(1)} %get-tuple-element.48), channel_id=1, source_target_pairs={{0,2},{1,3},{2,0},{3,1},{4,6},{5,7},{6,4},{7,5},{8,10},{9,11},{10,... | collective-permute-start | bytes 417800 | tf_op jit(solution)/shard_map/ppermute | solution.py:468
  23.1 10.9 %collective-permute-start.11 = (f32[1,240,128]{2,1,0:T(8,128)S(1)}, f32[1,240,128]{2,1,0:T(8,128)S(1)}, u32[]{:S(2)}, u32[]{:S(2)}) collective-permute-start(f32[1,240,128]{2,1,0:T(8,128)S(1)} %get-tuple-element.63), channel_id=1, source_target_pairs={{0,8},{1,9},{2,10},{3,11},{4,12},{5,13},{6,14},{7,15},{8,0},{9,1},... | collective-permute-start | bytes 368648 | tf_op jit(solution)/shard_map/ppermute | solution.py:468
  27.1 8.4 %collective-permute-start.10 = (f32[1,272,128]{2,1,0:T(8,128)S(1)}, f32[1,272,128]{2,1,0:T(8,128)S(1)}, u32[]{:S(2)}, u32[]{:S(2)}) collective-permute-start(f32[1,272,128]{2,1,0:T(8,128)S(1)} %get-tuple-element.60), channel_id=1, source_target_pairs={{0,8},{1,9},{2,10},{3,11},{4,12},{5,13},{6,14},{7,15},{8,0},{9,1},... | collective-permute-start | bytes 417800 | tf_op jit(solution)/shard_map/ppermute | solution.py:468

commit v18 on v17

--- a/solution.py
+++ b/solution.py
@@ -525,8 +525,8 @@
     across = swap(trace, lambda i, j: (i ^ (1 << X) ^ (1 << NEAR), j))
     halve_pair(early, 1)
     halve_pair(late, 1, terms=(trace,), put=(0, 1))
-    (trace,) = halve_pair(early, 2, terms=(trace, across))
-    halve_pair(late, 2, terms=(trace,), came=(0, 1), put=(0, 1))
+    halve_pair(early, 2)
+    halve_pair(late, 2, terms=(trace, across), came=(0, 1), put=(0, 1))
 
     def both(ks):
         return [keeps[k] for k in ks], gots[ks]

time: 36.7 us -> 39.1 us (1.065)
  waiting for transfers between devices: 13.5 us -> 18.4 us
  starting transfers between devices: 16.5 us -> 14.1 us
    ppermute x12, waiting for transfers between devices: 13.5 us -> 18.4 us  [swap(): return lax.ppermute(value, ('dp', 'tensor'), pairs)]
    ppermute x12, starting transfers between devices: 16.5 us -> 14.1 us  [swap(): return lax.ppermute(value, ('dp', 'tensor'), pairs)]
  transfers between devices with their start and end apart: 12 -> 12, of which waited for: 9 -> 6; matrix products, arithmetic and copies ran while one was open for 0% -> 0% of each run, Pallas kernels for 8% -> 8%
where the time goes in v18:
time: 39.1 us; the launch traced here: 38.9 us
  waiting for transfers between devices  18.4 us (47%)
  starting transfers between devices  14.1 us (36%)
  Pallas kernels  5.77 us (15%)
  between operations  0.72 us (2%)
    ppermute x12, waiting for transfers between devices, swap(): return lax.ppermute(value, ('dp', 'tensor'), pairs)  18.4 us
    ppermute x12, starting transfers between devices, swap(): return lax.ppermute(value, ('dp', 'tensor'), pairs)  14.1 us
    pallas_call x5, Pallas kernels, pack(): pl.pallas_call(functools.partial(pack_body, pieces, items, count_a, count...  4.25 us
    pallas_call x1, Pallas kernels, finish(): pl.pallas_call(functools.partial(finish_body, pieces, early, late, count_...  1.03 us
  transfers between devices with their start and end apart: 12, of which 6 were waited for; matrix products, arithmetic and copies ran while one was open for 0% of the time, Pallas kernels for 8%

profile of v18, /device:TPU:0, one launch (start us, length us, event | category | flops | bytes accessed | tf_op | source)
XLA Modules:
  0.0 38.9 jit_solution(11426167400243514709)
XLA Ops:
  0.6 1.7 %shard_map.50 = (f32[4,128,128]{2,1,0:T(8,128)S(1)}, f32[17,8,128]{2,1,0:T(8,128)S(1)}, bf16[128,2560]{1,0:T(8,128)(2,1)S(1)}) custom-call(bf16[128,2560]{1,0:T(8,128)(2,1)} %refs_0_.1), custom_call_target="tpu_custom_call" | custom-call | flops 4000000000 | bytes 1 | tf_op jit(solution)/shard_map/pallas_call | solution.py:235
  2.3 3.0 %collective-permute-start.7 = (f32[4,128,128]{2,1,0:T(8,128)S(1)}, f32[4,128,128]{2,1,0:T(8,128)S(1)}, u32[]{:S(2)}, u32[]{:S(2)}) collective-permute-start(f32[4,128,128]{2,1,0:T(8,128)S(1)} %get-tuple-element.53), channel_id=1, source_target_pairs={{0,2},{1,3},{2,0},{3,1},{4,6},{5,7},{6,4},{7,5},{8,10},{9,11},{10,... | collective-permute-start | bytes 786440 | tf_op jit(solution)/shard_map/ppermute | solution.py:468
  5.3 0.4 %shard_map.51 = (f32[4,112,128]{2,1,0:T(8,128)S(1)}, f32[17,8,128]{2,1,0:T(8,128)S(1)}) custom-call(f32[17,8,128]{2,1,0:T(8,128)S(1)} %get-tuple-element.34.refs_0_, bf16[128,2560]{1,0:T(8,128)(2,1)S(1)} %get-tuple-element.35.refs_1_, bf16[128,5120]{1,0:T(8,128)(2,1)S(1)} %copy-done, bf16[128,5120]{1,0:T(8,128)(2,1)S(1)} %copy-done.1), custom_call_target="tpu_custom_call" | custom-call | flops 1 | bytes 1 | tf_op jit(solution)/shard_map/pallas_call | solution.py:235
  5.8 1.6 %collective-permute-start.8 = (f32[4,112,128]{2,1,0:T(8,128)S(1)}, f32[4,112,128]{2,1,0:T(8,128)S(1)}, u32[]{:S(2)}, u32[]{:S(2)}) collective-permute-start(f32[4,112,128]{2,1,0:T(8,128)S(1)} %get-tuple-element.54), channel_id=1, source_target_pairs={{0,4},{1,5},{2,6},{3,7},{4,0},{5,1},{6,2},{7,3},{8,12},{9,13},{10,... | collective-permute-start | bytes 688136 | tf_op jit(solution)/shard_map/ppermute | solution.py:468
  7.4 0.8 %shard_map.52 = (f32[4,136,128]{2,1,0:T(8,128)S(1)}, f32[4,136,128]{2,1,0:T(8,128)S(1)}, f32[17,8,128]{2,1,0:T(8,128)S(1)}) custom-call(f32[17,8,128]{2,1,0:T(8,128)S(1)} %get-tuple-element.36.refs_0_, bf16[128,2560]{1,0:T(8,128)(2,1)S(1)} %get-tuple-element.35.refs_1_, bf16[128,5120]{1,0:T(8,128)(2,1)S(1)} %copy-done, bf16[128,5120]{1,0:T(8,128)(2,1)S(1)} %copy-done.1), custom_call_target="tpu_custom_call" | custom-call | flops 1 | bytes 1 | tf_op jit(solution)/shard_map/pallas_call | solution.py:235
  8.2 0.6 %collective-permute-start = (f32[4,136,128]{2,1,0:T(8,128)S(1)}, f32[4,136,128]{2,1,0:T(8,128)S(1)}, u32[]{:S(2)}, u32[]{:S(2)}) collective-permute-start(f32[4,136,128]{2,1,0:T(8,128)S(1)} %get-tuple-element.41), channel_id=1, source_target_pairs={{0,2},{1,3},{2,0},{3,1},{4,6},{5,7},{6,4},{7,5},{8,10},{9,11},{10,... | collective-permute-start | bytes 835592 | tf_op jit(solution)/shard_map/ppermute | solution.py:468
  8.8 0.2 collective-permute-start.1
  9.0 0.5 %shard_map.53 = (f32[4,128,128]{2,1,0:T(8,128)S(1)}, f32[4,112,128]{2,1,0:T(8,128)S(1)}, f32[17,8,128]{2,1,0:T(8,128)S(1)}) custom-call(f32[17,8,128]{2,1,0:T(8,128)S(1)} %get-tuple-element.37.refs_0_, bf16[128,2560]{1,0:T(8,128)(2,1)S(1)} %get-tuple-element.35.refs_1_, bf16[128,5120]{1,0:T(8,128)(2,1)S(1)} %copy-done, bf16[128,5120]{1,0:T(8,128)(2,1)S(1)} %copy-done.1), custom_call_target="tpu_custom_call" | custom-call | flops 1 | bytes 1 | tf_op jit(solution)/shard_map/pallas_call | solution.py:235
  9.5 0.8 %shard_map.54 = (f32[4,136,128]{2,1,0:T(8,128)S(1)}, f32[4,136,128]{2,1,0:T(8,128)S(1)}, f32[17,8,128]{2,1,0:T(8,128)S(1)}) custom-call(f32[17,8,128]{2,1,0:T(8,128)S(1)} %get-tuple-element.38.refs_0_, bf16[128,2560]{1,0:T(8,128)(2,1)S(1)} %get-tuple-element.35.refs_1_, bf16[128,5120]{1,0:T(8,128)(2,1)S(1)} %copy-done, bf16[128,5120]{1,0:T(8,128)(2,1)S(1)} %copy-done.1), custom_call_target="tpu_custom_call" | custom-call | flops 1 | bytes 1 | tf_op jit(solution)/shard_map/pallas_call | solution.py:235
  10.4 4.0 %collective-permute-done.8.refs_3_ = f32[4,112,128]{2,1,0:T(8,128)S(1)} collective-permute-done((f32[4,112,128]{2,1,0:T(8,128)S(1)}, f32[4,112,128]{2,1,0:T(8,128)S(1)}, u32[]{:S(2)}, u32[]{:S(2)}) %collective-permute-start.8) | collective-permute-done | bytes 229408 | tf_op jit(solution)/shard_map/ppermute | solution.py:468
  14.5 1.6 %collective-permute-start.9 = (f32[2,128,128]{2,1,0:T(8,128)S(1)}, f32[2,128,128]{2,1,0:T(8,128)S(1)}, u32[]{:S(2)}, u32[]{:S(2)}) collective-permute-start(f32[2,128,128]{2,1,0:T(8,128)S(1)} %get-tuple-element.57), channel_id=1, source_target_pairs={{0,4},{1,5},{2,6},{3,7},{4,0},{5,1},{6,2},{7,3},{8,12},{9,13},{10,... | collective-permute-start | bytes 393224 | tf_op jit(solution)/shard_map/ppermute | solution.py:468
  16.1 0.5 %collective-permute-start.10 = (f32[2,112,128]{2,1,0:T(8,128)S(1)}, f32[2,112,128]{2,1,0:T(8,128)S(1)}, u32[]{:S(2)}, u32[]{:S(2)}) collective-permute-start(f32[2,112,128]{2,1,0:T(8,128)S(1)} %get-tuple-element.58), channel_id=1, source_target_pairs={{0,2},{1,3},{2,0},{3,1},{4,6},{5,7},{6,4},{7,5},{8,10},{9,11},{10,... | collective-permute-start | bytes 344072 | tf_op jit(solution)/shard_map/ppermute | solution.py:468
  16.7 1.8 %collective-permute-done.refs_2_ = f32[4,136,128]{2,1,0:T(8,128)S(1)} collective-permute-done((f32[4,136,128]{2,1,0:T(8,128)S(1)}, f32[4,136,128]{2,1,0:T(8,128)S(1)}, u32[]{:S(2)}, u32[]{:S(2)}) %collective-permute-start) | collective-permute-done | bytes 278560 | tf_op jit(solution)/shard_map/ppermute | solution.py:468
  18.4 1.9 %collective-permute-done.1.refs_3_ = f32[4,136,128]{2,1,0:T(8,128)S(1)} collective-permute-done((f32[4,136,128]{2,1,0:T(8,128)S(1)}, f32[4,136,128]{2,1,0:T(8,128)S(1)}, u32[]{:S(2)}, u32[]{:S(2)}) %collective-permute-start.1) | collective-permute-done | bytes 278560 | tf_op jit(solution)/shard_map/ppermute | solution.py:468
  20.4 1.6 %collective-permute-start.3 = (f32[2,136,128]{2,1,0:T(8,128)S(1)}, f32[2,136,128]{2,1,0:T(8,128)S(1)}, u32[]{:S(2)}, u32[]{:S(2)}) collective-permute-start(f32[2,136,128]{2,1,0:T(8,128)S(1)} %get-tuple-element.46), channel_id=1, source_target_pairs={{0,4},{1,5},{2,6},{3,7},{4,0},{5,1},{6,2},{7,3},{8,12},{9,13},{10,... | collective-permute-start | bytes 417800 | tf_op jit(solution)/shard_map/ppermute | solution.py:468
  22.0 0.5 %collective-permute-start.4 = (f32[2,136,128]{2,1,0:T(8,128)S(1)}, f32[2,136,128]{2,1,0:T(8,128)S(1)}, u32[]{:S(2)}, u32[]{:S(2)}) collective-permute-start(f32[2,136,128]{2,1,0:T(8,128)S(1)} %get-tuple-element.47), channel_id=1, source_target_pairs={{0,2},{1,3},{2,0},{3,1},{4,6},{5,7},{6,4},{7,5},{8,10},{9,11},{10,... | collective-permute-start | bytes 417800 | tf_op jit(solution)/shard_map/ppermute | solution.py:468
  22.5 0.5 %collective-permute-done.9.refs_2_ = f32[2,128,128]{2,1,0:T(8,128)S(1)} collective-permute-done((f32[2,128,128]{2,1,0:T(8,128)S(1)}, f32[2,128,128]{2,1,0:T(8,128)S(1)}, u32[]{:S(2)}, u32[]{:S(2)}) %collective-permute-start.9) | collective-permute-done | bytes 131104 | tf_op jit(solution)/shard_map/ppermute | solution.py:468
  23.1 2.7 %collective-permute-start.11 = (f32[1,240,128]{2,1,0:T(8,128)S(1)}, f32[1,240,128]{2,1,0:T(8,128)S(1)}, u32[]{:S(2)}, u32[]{:S(2)}) collective-permute-start(f32[1,240,128]{2,1,0:T(8,128)S(1)} %get-tuple-element.61), channel_id=1, source_target_pairs={{0,8},{1,9},{2,10},{3,11},{4,12},{5,13},{6,14},{7,15},{8,0},{9,1},... | collective-permute-start | bytes 368648 | tf_op jit(solution)/shard_map/ppermute | solution.py:468
  25.8 1.3 %collective-permute-start.5 = (f32[2,128]{1,0:T(2,128)S(1)}, f32[2,128]{1,0:T(2,128)S(1)}, u32[]{:S(2)}, u32[]{:S(2)}) collective-permute-start(f32[2,128]{1,0:T(2,128)S(1)} %fusion.refs_4_), channel_id=1, source_target_pairs={{0,6},{1,7},{2,4},{3,5},{4,2},{5,3},{6,0},{7,1},{8,14},{9,15},{10,... | collective-permute-start | bytes 3080 | tf_op jit(solution)/shard_map/ppermute | solution.py:468
  27.1 3.3 %collective-permute-done.5.refs_5_ = f32[2,128]{1,0:T(2,128)S(1)} collective-permute-done((f32[2,128]{1,0:T(2,128)S(1)}, f32[2,128]{1,0:T(2,128)S(1)}, u32[]{:S(2)}, u32[]{:S(2)}) %collective-permute-start.5) | collective-permute-done | bytes 1056 | tf_op jit(solution)/shard_map/ppermute | solution.py:468
  30.4 0.3 collective-permute-start.6
  30.7 0.3 shard_map.59
  31.0 6.9 %collective-permute-done.6.refs_2_ = f32[1,272,128]{2,1,0:T(8,128)S(1)} collective-permute-done((f32[1,272,128]{2,1,0:T(8,128)S(1)}, f32[1,272,128]{2,1,0:T(8,128)S(1)}, u32[]{:S(2)}, u32[]{:S(2)}) %collective-permute-start.6) | collective-permute-done | bytes 139296 | tf_op jit(solution)/shard_map/ppermute | solution.py:468
  37.9 1.0 %shard_map.60 = (f32[320,128]{1,0:T(8,128)}, f32[640,128]{1,0:T(8,128)}) custom-call(f32[1,136,128]{2,1,0:T(8,128)S(1)} %get-tuple-element.48.refs_0_, f32[1,136,128]{2,1,0:T(8,128)S(1)} %get-tuple-element.49.refs_1_, f32[1,272,128]{2,1,0:T(8,128)S(1)} %collective-permute-done.6.refs_2_, f32[320,128]{1,0:T(8,128)S(1)} %get-tuple-element.62.refs_3_, ...), custom_call_target="tpu_custom_call" | custom-call | tf_op jit(solution)/shard_map/pallas_call | solution.py:444
  (17 shorter events, 0.3 us)
Async XLA Ops:
  0.6 4.7 %copy-start = (bf16[128,5120]{1,0:T(8,128)(2,1)S(1)}, bf16[128,5120]{1,0:T(8,128)(2,1)}, u32[]{:S(2)}) copy-start(bf16[128,5120]{1,0:T(8,128)(2,1)} %refs_2_.7) | copy-start | bytes 3932164
  0.6 4.7 %copy-start.1 = (bf16[128,5120]{1,0:T(8,128)(2,1)S(1)}, bf16[128,5120]{1,0:T(8,128)(2,1)}, u32[]{:S(2)}) copy-start(bf16[128,5120]{1,0:T(8,128)(2,1)} %refs_3_.7) | copy-start | bytes 3932164
  2.3 12.1 %collective-permute-start.7 = (f32[4,128,128]{2,1,0:T(8,128)S(1)}, f32[4,128,128]{2,1,0:T(8,128)S(1)}, u32[]{:S(2)}, u32[]{:S(2)}) collective-permute-start(f32[4,128,128]{2,1,0:T(8,128)S(1)} %get-tuple-element.53), channel_id=1, source_target_pairs={{0,2},{1,3},{2,0},{3,1},{4,6},{5,7},{6,4},{7,5},{8,10},{9,11},{10,... | collective-permute-start | bytes 786440 | tf_op jit(solution)/shard_map/ppermute | solution.py:468
  5.8 8.6 %collective-permute-start.8 = (f32[4,112,128]{2,1,0:T(8,128)S(1)}, f32[4,112,128]{2,1,0:T(8,128)S(1)}, u32[]{:S(2)}, u32[]{:S(2)}) collective-permute-start(f32[4,112,128]{2,1,0:T(8,128)S(1)} %get-tuple-element.54), channel_id=1, source_target_pairs={{0,4},{1,5},{2,6},{3,7},{4,0},{5,1},{6,2},{7,3},{8,12},{9,13},{10,... | collective-permute-start | bytes 688136 | tf_op jit(solution)/shard_map/ppermute | solution.py:468
  8.2 10.2 %collective-permute-start = (f32[4,136,128]{2,1,0:T(8,128)S(1)}, f32[4,136,128]{2,1,0:T(8,128)S(1)}, u32[]{:S(2)}, u32[]{:S(2)}) collective-permute-start(f32[4,136,128]{2,1,0:T(8,128)S(1)} %get-tuple-element.41), channel_id=1, source_target_pairs={{0,2},{1,3},{2,0},{3,1},{4,6},{5,7},{6,4},{7,5},{8,10},{9,11},{10,... | collective-permute-start | bytes 835592 | tf_op jit(solution)/shard_map/ppermute | solution.py:468
  8.8 11.5 %collective-permute-start.1 = (f32[4,136,128]{2,1,0:T(8,128)S(1)}, f32[4,136,128]{2,1,0:T(8,128)S(1)}, u32[]{:S(2)}, u32[]{:S(2)}) collective-permute-start(f32[4,136,128]{2,1,0:T(8,128)S(1)} %get-tuple-element.42), channel_id=1, source_target_pairs={{0,4},{1,5},{2,6},{3,7},{4,0},{5,1},{6,2},{7,3},{8,12},{9,13},{10,... | collective-permute-start | bytes 835592 | tf_op jit(solution)/shard_map/ppermute | solution.py:468
  10.4 6.3 %collective-permute-start.2 = (f32[2,128]{1,0:T(2,128)S(1)}, f32[2,128]{1,0:T(2,128)S(1)}, u32[]{:S(2)}, u32[]{:S(2)}) collective-permute-start(f32[2,128]{1,0:T(2,128)S(1)} %slice_bitcast_fusion), channel_id=1, source_target_pairs={{0,1},{1,0},{2,3},{3,2},{4,5},{5,4},{6,7},{7,6},{8,9},{9,8},{10,11... | collective-permute-start | bytes 3080 | tf_op jit(solution)/shard_map/ppermute | solution.py:468
  14.5 8.6 %collective-permute-start.9 = (f32[2,128,128]{2,1,0:T(8,128)S(1)}, f32[2,128,128]{2,1,0:T(8,128)S(1)}, u32[]{:S(2)}, u32[]{:S(2)}) collective-permute-start(f32[2,128,128]{2,1,0:T(8,128)S(1)} %get-tuple-element.57), channel_id=1, source_target_pairs={{0,4},{1,5},{2,6},{3,7},{4,0},{5,1},{6,2},{7,3},{8,12},{9,13},{10,... | collective-permute-start | bytes 393224 | tf_op jit(solution)/shard_map/ppermute | solution.py:468
  16.1 6.4 %collective-permute-start.10 = (f32[2,112,128]{2,1,0:T(8,128)S(1)}, f32[2,112,128]{2,1,0:T(8,128)S(1)}, u32[]{:S(2)}, u32[]{:S(2)}) collective-permute-start(f32[2,112,128]{2,1,0:T(8,128)S(1)} %get-tuple-element.58), channel_id=1, source_target_pairs={{0,2},{1,3},{2,0},{3,1},{4,6},{5,7},{6,4},{7,5},{8,10},{9,11},{10,... | collective-permute-start | bytes 344072 | tf_op jit(solution)/shard_map/ppermute | solution.py:468
  20.4 10.0 %collective-permute-start.3 = (f32[2,136,128]{2,1,0:T(8,128)S(1)}, f32[2,136,128]{2,1,0:T(8,128)S(1)}, u32[]{:S(2)}, u32[]{:S(2)}) collective-permute-start(f32[2,136,128]{2,1,0:T(8,128)S(1)} %get-tuple-element.46), channel_id=1, source_target_pairs={{0,4},{1,5},{2,6},{3,7},{4,0},{5,1},{6,2},{7,3},{8,12},{9,13},{10,... | collective-permute-start | bytes 417800 | tf_op jit(solution)/shard_map/ppermute | solution.py:468
  22.0 8.3 %collective-permute-start.4 = (f32[2,136,128]{2,1,0:T(8,128)S(1)}, f32[2,136,128]{2,1,0:T(8,128)S(1)}, u32[]{:S(2)}, u32[]{:S(2)}) collective-permute-start(f32[2,136,128]{2,1,0:T(8,128)S(1)} %get-tuple-element.47), channel_id=1, source_target_pairs={{0,2},{1,3},{2,0},{3,1},{4,6},{5,7},{6,4},{7,5},{8,10},{9,11},{10,... | collective-permute-start | bytes 417800 | tf_op jit(solution)/shard_map/ppermute | solution.py:468
  23.1 7.6 %collective-permute-start.11 = (f32[1,240,128]{2,1,0:T(8,128)S(1)}, f32[1,240,128]{2,1,0:T(8,128)S(1)}, u32[]{:S(2)}, u32[]{:S(2)}) collective-permute-start(f32[1,240,128]{2,1,0:T(8,128)S(1)} %get-tuple-element.61), channel_id=1, source_target_pairs={{0,8},{1,9},{2,10},{3,11},{4,12},{5,13},{6,14},{7,15},{8,0},{9,1},... | collective-permute-start | bytes 368648 | tf_op jit(solution)/shard_map/ppermute | solution.py:468
  25.8 4.6 %collective-permute-start.5 = (f32[2,128]{1,0:T(2,128)S(1)}, f32[2,128]{1,0:T(2,128)S(1)}, u32[]{:S(2)}, u32[]{:S(2)}) collective-permute-start(f32[2,128]{1,0:T(2,128)S(1)} %fusion.refs_4_), channel_id=1, source_target_pairs={{0,6},{1,7},{2,4},{3,5},{4,2},{5,3},{6,0},{7,1},{8,14},{9,15},{10,... | collective-permute-start | bytes 3080 | tf_op jit(solution)/shard_map/ppermute | solution.py:468
  30.4 7.5 %collective-permute-start.6 = (f32[1,272,128]{2,1,0:T(8,128)S(1)}, f32[1,272,128]{2,1,0:T(8,128)S(1)}, u32[]{:S(2)}, u32[]{:S(2)}) collective-permute-start(f32[1,272,128]{2,1,0:T(8,128)S(1)} %get-tuple-element.50), channel_id=1, source_target_pairs={{0,8},{1,9},{2,10},{3,11},{4,12},{5,13},{6,14},{7,15},{8,0},{9,1},... | collective-permute-start | bytes 417800 | tf_op jit(solution)/shard_map/ppermute | solution.py:468

commit v19 on v17

--- a/solution.py
+++ b/solution.py
@@ -59,7 +59,7 @@
 EDGE = 8
 SLOTS = 8
 X, NEAR, FAR = 0, 1, 2
-KINDS = (((X, NEAR, FAR), (X, NEAR, FAR)), ((NEAR, X, FAR), (NEAR, X, FAR)))
+KINDS = (((NEAR, X, FAR), (NEAR, X, FAR)), ((X, NEAR, FAR), (X, NEAR, FAR)))
 NOTES = len(KINDS) * SLOTS
 
 WEIGHTS = {((0, 2), 2): 2 * 10**9}

time: 36.7 us -> 36.7 us (level)
  starting transfers between devices: 16.5 us -> 17 us
  waiting for transfers between devices: 13.5 us -> 13.1 us
    ppermute x12, waiting for transfers between devices: 13.5 us -> 13.1 us  [swap(): return lax.ppermute(value, ('dp', 'tensor'), pairs)]
    ppermute x12, starting transfers between devices: 16.5 us -> 17 us  [swap(): return lax.ppermute(value, ('dp', 'tensor'), pairs)]
  transfers between devices with their start and end apart: 12 -> 12, of which waited for: 9 -> 7; matrix products, arithmetic and copies ran while one was open for 0% -> 0% of each run, Pallas kernels for 8% -> 8%
where the time goes in v19:
time: 36.7 us; the launch traced here: 36.5 us
  starting transfers between devices  17 us (46%)
  waiting for transfers between devices  13.1 us (36%)
  Pallas kernels  5.76 us (16%)
  between operations  0.73 us (2%)
    ppermute x12, starting transfers between devices, swap(): return lax.ppermute(value, ('dp', 'tensor'), pairs)  17 us
    ppermute x12, waiting for transfers between devices, swap(): return lax.ppermute(value, ('dp', 'tensor'), pairs)  13.1 us
    pallas_call x5, Pallas kernels, pack(): pl.pallas_call(functools.partial(pack_body, pieces, items, count_a, count...  4.25 us
    pallas_call x1, Pallas kernels, finish(): pl.pallas_call(functools.partial(finish_body, pieces, early, late, count_...  1.03 us
  transfers between devices with their start and end apart: 12, of which 7 were waited for; matrix products, arithmetic and copies ran while one was open for 0% of the time, Pallas kernels for 8%

profile of v19, /device:TPU:0, one launch (start us, length us, event | category | flops | bytes accessed | tf_op | source)
XLA Modules:
  0.0 36.5 jit_solution(15323984519351264937)
XLA Ops:
  0.6 1.7 %shard_map.50 = (f32[4,128,128]{2,1,0:T(8,128)S(1)}, f32[17,8,128]{2,1,0:T(8,128)S(1)}, bf16[128,2560]{1,0:T(8,128)(2,1)S(1)}) custom-call(bf16[128,2560]{1,0:T(8,128)(2,1)} %refs_0_.1), custom_call_target="tpu_custom_call" | custom-call | flops 4000000000 | bytes 1 | tf_op jit(solution)/shard_map/pallas_call | solution.py:235
  2.3 3.1 %collective-permute-start.5 = (f32[4,128,128]{2,1,0:T(8,128)S(1)}, f32[4,128,128]{2,1,0:T(8,128)S(1)}, u32[]{:S(2)}, u32[]{:S(2)}) collective-permute-start(f32[4,128,128]{2,1,0:T(8,128)S(1)} %get-tuple-element.51), channel_id=1, source_target_pairs={{0,4},{1,5},{2,6},{3,7},{4,0},{5,1},{6,2},{7,3},{8,12},{9,13},{10,... | collective-permute-start | bytes 786440 | tf_op jit(solution)/shard_map/ppermute | solution.py:468
  5.4 0.4 %shard_map.51 = (f32[4,112,128]{2,1,0:T(8,128)S(1)}, f32[17,8,128]{2,1,0:T(8,128)S(1)}) custom-call(f32[17,8,128]{2,1,0:T(8,128)S(1)} %get-tuple-element.35.refs_0_, bf16[128,2560]{1,0:T(8,128)(2,1)S(1)} %get-tuple-element.36.refs_1_, bf16[128,5120]{1,0:T(8,128)(2,1)S(1)} %copy-done, bf16[128,5120]{1,0:T(8,128)(2,1)S(1)} %copy-done.1), custom_call_target="tpu_custom_call" | custom-call | flops 1 | bytes 1 | tf_op jit(solution)/shard_map/pallas_call | solution.py:235
  5.9 1.6 %collective-permute-start.6 = (f32[4,112,128]{2,1,0:T(8,128)S(1)}, f32[4,112,128]{2,1,0:T(8,128)S(1)}, u32[]{:S(2)}, u32[]{:S(2)}) collective-permute-start(f32[4,112,128]{2,1,0:T(8,128)S(1)} %get-tuple-element.52), channel_id=1, source_target_pairs={{0,2},{1,3},{2,0},{3,1},{4,6},{5,7},{6,4},{7,5},{8,10},{9,11},{10,... | collective-permute-start | bytes 688136 | tf_op jit(solution)/shard_map/ppermute | solution.py:468
  7.4 0.8 %shard_map.52 = (f32[4,136,128]{2,1,0:T(8,128)S(1)}, f32[4,136,128]{2,1,0:T(8,128)S(1)}, f32[17,8,128]{2,1,0:T(8,128)S(1)}) custom-call(f32[17,8,128]{2,1,0:T(8,128)S(1)} %get-tuple-element.37.refs_0_, bf16[128,2560]{1,0:T(8,128)(2,1)S(1)} %get-tuple-element.36.refs_1_, bf16[128,5120]{1,0:T(8,128)(2,1)S(1)} %copy-done, bf16[128,5120]{1,0:T(8,128)(2,1)S(1)} %copy-done.1), custom_call_target="tpu_custom_call" | custom-call | flops 1 | bytes 1 | tf_op jit(solution)/shard_map/pallas_call | solution.py:235
  8.2 0.5 %collective-permute-start = (f32[4,136,128]{2,1,0:T(8,128)S(1)}, f32[4,136,128]{2,1,0:T(8,128)S(1)}, u32[]{:S(2)}, u32[]{:S(2)}) collective-permute-start(f32[4,136,128]{2,1,0:T(8,128)S(1)} %get-tuple-element.42), channel_id=1, source_target_pairs={{0,4},{1,5},{2,6},{3,7},{4,0},{5,1},{6,2},{7,3},{8,12},{9,13},{10,... | collective-permute-start | bytes 835592 | tf_op jit(solution)/shard_map/ppermute | solution.py:468
  8.8 0.3 collective-permute-start.1
  9.1 0.5 %shard_map.53 = (f32[4,128,128]{2,1,0:T(8,128)S(1)}, f32[4,112,128]{2,1,0:T(8,128)S(1)}, f32[17,8,128]{2,1,0:T(8,128)S(1)}) custom-call(f32[17,8,128]{2,1,0:T(8,128)S(1)} %get-tuple-element.38.refs_0_, bf16[128,2560]{1,0:T(8,128)(2,1)S(1)} %get-tuple-element.36.refs_1_, bf16[128,5120]{1,0:T(8,128)(2,1)S(1)} %copy-done, bf16[128,5120]{1,0:T(8,128)(2,1)S(1)} %copy-done.1), custom_call_target="tpu_custom_call" | custom-call | flops 1 | bytes 1 | tf_op jit(solution)/shard_map/pallas_call | solution.py:235
  9.6 0.8 %shard_map.54 = (f32[4,136,128]{2,1,0:T(8,128)S(1)}, f32[4,136,128]{2,1,0:T(8,128)S(1)}, f32[17,8,128]{2,1,0:T(8,128)S(1)}) custom-call(f32[17,8,128]{2,1,0:T(8,128)S(1)} %get-tuple-element.39.refs_0_, bf16[128,2560]{1,0:T(8,128)(2,1)S(1)} %get-tuple-element.36.refs_1_, bf16[128,5120]{1,0:T(8,128)(2,1)S(1)} %copy-done, bf16[128,5120]{1,0:T(8,128)(2,1)S(1)} %copy-done.1), custom_call_target="tpu_custom_call" | custom-call | flops 1 | bytes 1 | tf_op jit(solution)/shard_map/pallas_call | solution.py:235
  10.5 4.0 %collective-permute-done.6.refs_3_ = f32[4,112,128]{2,1,0:T(8,128)S(1)} collective-permute-done((f32[4,112,128]{2,1,0:T(8,128)S(1)}, f32[4,112,128]{2,1,0:T(8,128)S(1)}, u32[]{:S(2)}, u32[]{:S(2)}) %collective-permute-start.6) | collective-permute-done | bytes 229408 | tf_op jit(solution)/shard_map/ppermute | solution.py:468
  14.8 1.7 %collective-permute-start.7 = (f32[2,128,128]{2,1,0:T(8,128)S(1)}, f32[2,128,128]{2,1,0:T(8,128)S(1)}, u32[]{:S(2)}, u32[]{:S(2)}) collective-permute-start(f32[2,128,128]{2,1,0:T(8,128)S(1)} %get-tuple-element.55), channel_id=1, source_target_pairs={{0,2},{1,3},{2,0},{3,1},{4,6},{5,7},{6,4},{7,5},{8,10},{9,11},{10,... | collective-permute-start | bytes 393224 | tf_op jit(solution)/shard_map/ppermute | solution.py:468
  16.6 1.6 %collective-permute-start.9 = (f32[2,128]{1,0:T(2,128)S(1)}, f32[2,128]{1,0:T(2,128)S(1)}, u32[]{:S(2)}, u32[]{:S(2)}) collective-permute-start(f32[2,128]{1,0:T(2,128)S(1)} %fusion.refs_4_), channel_id=1, source_target_pairs={{0,6},{1,7},{2,4},{3,5},{4,2},{5,3},{6,0},{7,1},{8,14},{9,15},{10,... | collective-permute-start | bytes 3080 | tf_op jit(solution)/shard_map/ppermute | solution.py:468
  18.1 0.4 %collective-permute-done.refs_2_ = f32[4,136,128]{2,1,0:T(8,128)S(1)} collective-permute-done((f32[4,136,128]{2,1,0:T(8,128)S(1)}, f32[4,136,128]{2,1,0:T(8,128)S(1)}, u32[]{:S(2)}, u32[]{:S(2)}) %collective-permute-start) | collective-permute-done | bytes 278560 | tf_op jit(solution)/shard_map/ppermute | solution.py:468
  18.5 1.9 %collective-permute-done.1.refs_3_ = f32[4,136,128]{2,1,0:T(8,128)S(1)} collective-permute-done((f32[4,136,128]{2,1,0:T(8,128)S(1)}, f32[4,136,128]{2,1,0:T(8,128)S(1)}, u32[]{:S(2)}, u32[]{:S(2)}) %collective-permute-start.1) | collective-permute-done | bytes 278560 | tf_op jit(solution)/shard_map/ppermute | solution.py:468
  20.5 1.6 %collective-permute-start.3 = (f32[2,136,128]{2,1,0:T(8,128)S(1)}, f32[2,136,128]{2,1,0:T(8,128)S(1)}, u32[]{:S(2)}, u32[]{:S(2)}) collective-permute-start(f32[2,136,128]{2,1,0:T(8,128)S(1)} %get-tuple-element.47), channel_id=1, source_target_pairs={{0,2},{1,3},{2,0},{3,1},{4,6},{5,7},{6,4},{7,5},{8,10},{9,11},{10,... | collective-permute-start | bytes 417800 | tf_op jit(solution)/shard_map/ppermute | solution.py:468
  22.0 0.5 %collective-permute-start.4 = (f32[2,136,128]{2,1,0:T(8,128)S(1)}, f32[2,136,128]{2,1,0:T(8,128)S(1)}, u32[]{:S(2)}, u32[]{:S(2)}) collective-permute-start(f32[2,136,128]{2,1,0:T(8,128)S(1)} %get-tuple-element.48), channel_id=1, source_target_pairs={{0,4},{1,5},{2,6},{3,7},{4,0},{5,1},{6,2},{7,3},{8,12},{9,13},{10,... | collective-permute-start | bytes 417800 | tf_op jit(solution)/shard_map/ppermute | solution.py:468
  22.5 0.7 %collective-permute-done.7.refs_2_ = f32[2,128,128]{2,1,0:T(8,128)S(1)} collective-permute-done((f32[2,128,128]{2,1,0:T(8,128)S(1)}, f32[2,128,128]{2,1,0:T(8,128)S(1)}, u32[]{:S(2)}, u32[]{:S(2)}) %collective-permute-start.7) | collective-permute-done | bytes 131104 | tf_op jit(solution)/shard_map/ppermute | solution.py:468
  23.2 2.7 %collective-permute-start.11 = (f32[1,240,128]{2,1,0:T(8,128)S(1)}, f32[1,240,128]{2,1,0:T(8,128)S(1)}, u32[]{:S(2)}, u32[]{:S(2)}) collective-permute-start(f32[1,240,128]{2,1,0:T(8,128)S(1)} %get-tuple-element.63), channel_id=1, source_target_pairs={{0,8},{1,9},{2,10},{3,11},{4,12},{5,13},{6,14},{7,15},{8,0},{9,1},... | collective-permute-start | bytes 368648 | tf_op jit(solution)/shard_map/ppermute | solution.py:468
  25.9 1.5 %collective-permute-done.4.refs_3_ = f32[2,136,128]{2,1,0:T(8,128)S(1)} collective-permute-done((f32[2,136,128]{2,1,0:T(8,128)S(1)}, f32[2,136,128]{2,1,0:T(8,128)S(1)}, u32[]{:S(2)}, u32[]{:S(2)}) %collective-permute-start.4) | collective-permute-done | bytes 139296 | tf_op jit(solution)/shard_map/ppermute | solution.py:468
  27.5 3.2 %collective-permute-start.10 = (f32[1,272,128]{2,1,0:T(8,128)S(1)}, f32[1,272,128]{2,1,0:T(8,128)S(1)}, u32[]{:S(2)}, u32[]{:S(2)}) collective-permute-start(f32[1,272,128]{2,1,0:T(8,128)S(1)} %get-tuple-element.60), channel_id=1, source_target_pairs={{0,8},{1,9},{2,10},{3,11},{4,12},{5,13},{6,14},{7,15},{8,0},{9,1},... | collective-permute-start | bytes 417800 | tf_op jit(solution)/shard_map/ppermute | solution.py:468
  30.6 1.9 %collective-permute-done.11.refs_2_ = f32[1,240,128]{2,1,0:T(8,128)S(1)} collective-permute-done((f32[1,240,128]{2,1,0:T(8,128)S(1)}, f32[1,240,128]{2,1,0:T(8,128)S(1)}, u32[]{:S(2)}, u32[]{:S(2)}) %collective-permute-start.11) | collective-permute-done | bytes 122912 | tf_op jit(solution)/shard_map/ppermute | solution.py:468
  32.5 0.3 shard_map.59
  32.8 2.7 %collective-permute-done.10.refs_2_ = f32[1,272,128]{2,1,0:T(8,128)S(1)} collective-permute-done((f32[1,272,128]{2,1,0:T(8,128)S(1)}, f32[1,272,128]{2,1,0:T(8,128)S(1)}, u32[]{:S(2)}, u32[]{:S(2)}) %collective-permute-start.10) | collective-permute-done | bytes 139296 | tf_op jit(solution)/shard_map/ppermute | solution.py:468
  35.5 1.0 %shard_map.60 = (f32[320,128]{1,0:T(8,128)}, f32[640,128]{1,0:T(8,128)}) custom-call(f32[1,136,128]{2,1,0:T(8,128)S(1)} %get-tuple-element.58.refs_0_, f32[1,136,128]{2,1,0:T(8,128)S(1)} %get-tuple-element.59.refs_1_, f32[1,272,128]{2,1,0:T(8,128)S(1)} %collective-permute-done.10.refs_2_, f32[320,128]{1,0:T(8,128)S(1)} %get-tuple-element.64.refs_3_, ...), custom_call_target="tpu_custom_call" | custom-call | tf_op jit(solution)/shard_map/pallas_call | solution.py:444
  (17 shorter events, 0.6 us)
Async XLA Ops:
  0.6 4.8 %copy-start.1 = (bf16[128,5120]{1,0:T(8,128)(2,1)S(1)}, bf16[128,5120]{1,0:T(8,128)(2,1)}, u32[]{:S(2)}) copy-start(bf16[128,5120]{1,0:T(8,128)(2,1)} %refs_3_.7) | copy-start | bytes 3932164
  0.6 4.8 %copy-start = (bf16[128,5120]{1,0:T(8,128)(2,1)S(1)}, bf16[128,5120]{1,0:T(8,128)(2,1)}, u32[]{:S(2)}) copy-start(bf16[128,5120]{1,0:T(8,128)(2,1)} %refs_2_.7) | copy-start | bytes 3932164
  2.3 12.1 %collective-permute-start.5 = (f32[4,128,128]{2,1,0:T(8,128)S(1)}, f32[4,128,128]{2,1,0:T(8,128)S(1)}, u32[]{:S(2)}, u32[]{:S(2)}) collective-permute-start(f32[4,128,128]{2,1,0:T(8,128)S(1)} %get-tuple-element.51), channel_id=1, source_target_pairs={{0,4},{1,5},{2,6},{3,7},{4,0},{5,1},{6,2},{7,3},{8,12},{9,13},{10,... | collective-permute-start | bytes 786440 | tf_op jit(solution)/shard_map/ppermute | solution.py:468
  5.9 8.6 %collective-permute-start.6 = (f32[4,112,128]{2,1,0:T(8,128)S(1)}, f32[4,112,128]{2,1,0:T(8,128)S(1)}, u32[]{:S(2)}, u32[]{:S(2)}) collective-permute-start(f32[4,112,128]{2,1,0:T(8,128)S(1)} %get-tuple-element.52), channel_id=1, source_target_pairs={{0,2},{1,3},{2,0},{3,1},{4,6},{5,7},{6,4},{7,5},{8,10},{9,11},{10,... | collective-permute-start | bytes 688136 | tf_op jit(solution)/shard_map/ppermute | solution.py:468
  8.2 10.3 %collective-permute-start = (f32[4,136,128]{2,1,0:T(8,128)S(1)}, f32[4,136,128]{2,1,0:T(8,128)S(1)}, u32[]{:S(2)}, u32[]{:S(2)}) collective-permute-start(f32[4,136,128]{2,1,0:T(8,128)S(1)} %get-tuple-element.42), channel_id=1, source_target_pairs={{0,4},{1,5},{2,6},{3,7},{4,0},{5,1},{6,2},{7,3},{8,12},{9,13},{10,... | collective-permute-start | bytes 835592 | tf_op jit(solution)/shard_map/ppermute | solution.py:468
  8.8 11.6 %collective-permute-start.1 = (f32[4,136,128]{2,1,0:T(8,128)S(1)}, f32[4,136,128]{2,1,0:T(8,128)S(1)}, u32[]{:S(2)}, u32[]{:S(2)}) collective-permute-start(f32[4,136,128]{2,1,0:T(8,128)S(1)} %get-tuple-element.43), channel_id=1, source_target_pairs={{0,2},{1,3},{2,0},{3,1},{4,6},{5,7},{6,4},{7,5},{8,10},{9,11},{10,... | collective-permute-start | bytes 835592 | tf_op jit(solution)/shard_map/ppermute | solution.py:468
  10.4 6.1 %collective-permute-start.2 = (f32[2,128]{1,0:T(2,128)S(1)}, f32[2,128]{1,0:T(2,128)S(1)}, u32[]{:S(2)}, u32[]{:S(2)}) collective-permute-start(f32[2,128]{1,0:T(2,128)S(1)} %slice_bitcast_fusion), channel_id=1, source_target_pairs={{0,1},{1,0},{2,3},{3,2},{4,5},{5,4},{6,7},{7,6},{8,9},{9,8},{10,11... | collective-permute-start | bytes 3080 | tf_op jit(solution)/shard_map/ppermute | solution.py:468
  14.6 8.0 %collective-permute-start.8 = (f32[2,112,128]{2,1,0:T(8,128)S(1)}, f32[2,112,128]{2,1,0:T(8,128)S(1)}, u32[]{:S(2)}, u32[]{:S(2)}) collective-permute-start(f32[2,112,128]{2,1,0:T(8,128)S(1)} %get-tuple-element.56), channel_id=1, source_target_pairs={{0,4},{1,5},{2,6},{3,7},{4,0},{5,1},{6,2},{7,3},{8,12},{9,13},{10,... | collective-permute-start | bytes 344072 | tf_op jit(solution)/shard_map/ppermute | solution.py:468
  14.8 8.4 %collective-permute-start.7 = (f32[2,128,128]{2,1,0:T(8,128)S(1)}, f32[2,128,128]{2,1,0:T(8,128)S(1)}, u32[]{:S(2)}, u32[]{:S(2)}) collective-permute-start(f32[2,128,128]{2,1,0:T(8,128)S(1)} %get-tuple-element.55), channel_id=1, source_target_pairs={{0,2},{1,3},{2,0},{3,1},{4,6},{5,7},{6,4},{7,5},{8,10},{9,11},{10,... | collective-permute-start | bytes 393224 | tf_op jit(solution)/shard_map/ppermute | solution.py:468
  16.6 6.0 %collective-permute-start.9 = (f32[2,128]{1,0:T(2,128)S(1)}, f32[2,128]{1,0:T(2,128)S(1)}, u32[]{:S(2)}, u32[]{:S(2)}) collective-permute-start(f32[2,128]{1,0:T(2,128)S(1)} %fusion.refs_4_), channel_id=1, source_target_pairs={{0,6},{1,7},{2,4},{3,5},{4,2},{5,3},{6,0},{7,1},{8,14},{9,15},{10,... | collective-permute-start | bytes 3080 | tf_op jit(solution)/shard_map/ppermute | solution.py:468
  20.5 5.4 %collective-permute-start.3 = (f32[2,136,128]{2,1,0:T(8,128)S(1)}, f32[2,136,128]{2,1,0:T(8,128)S(1)}, u32[]{:S(2)}, u32[]{:S(2)}) collective-permute-start(f32[2,136,128]{2,1,0:T(8,128)S(1)} %get-tuple-element.47), channel_id=1, source_target_pairs={{0,2},{1,3},{2,0},{3,1},{4,6},{5,7},{6,4},{7,5},{8,10},{9,11},{10,... | collective-permute-start | bytes 417800 | tf_op jit(solution)/shard_map/ppermute | solution.py:468
  22.0 5.4 %collective-permute-start.4 = (f32[2,136,128]{2,1,0:T(8,128)S(1)}, f32[2,136,128]{2,1,0:T(8,128)S(1)}, u32[]{:S(2)}, u32[]{:S(2)}) collective-permute-start(f32[2,136,128]{2,1,0:T(8,128)S(1)} %get-tuple-element.48), channel_id=1, source_target_pairs={{0,4},{1,5},{2,6},{3,7},{4,0},{5,1},{6,2},{7,3},{8,12},{9,13},{10,... | collective-permute-start | bytes 417800 | tf_op jit(solution)/shard_map/ppermute | solution.py:468
  23.2 9.3 %collective-permute-start.11 = (f32[1,240,128]{2,1,0:T(8,128)S(1)}, f32[1,240,128]{2,1,0:T(8,128)S(1)}, u32[]{:S(2)}, u32[]{:S(2)}) collective-permute-start(f32[1,240,128]{2,1,0:T(8,128)S(1)} %get-tuple-element.63), channel_id=1, source_target_pairs={{0,8},{1,9},{2,10},{3,11},{4,12},{5,13},{6,14},{7,15},{8,0},{9,1},... | collective-permute-start | bytes 368648 | tf_op jit(solution)/shard_map/ppermute | solution.py:468
  27.5 8.1 %collective-permute-start.10 = (f32[1,272,128]{2,1,0:T(8,128)S(1)}, f32[1,272,128]{2,1,0:T(8,128)S(1)}, u32[]{:S(2)}, u32[]{:S(2)}) collective-permute-start(f32[1,272,128]{2,1,0:T(8,128)S(1)} %get-tuple-element.60), channel_id=1, source_target_pairs={{0,8},{1,9},{2,10},{3,11},{4,12},{5,13},{6,14},{7,15},{8,0},{9,1},... | collective-permute-start | bytes 417800 | tf_op jit(solution)/shard_map/ppermute | solution.py:468

commit v20 on v17

--- a/solution.py
+++ b/solution.py
@@ -101,26 +101,16 @@
     return pl.ds(start if isinstance(start, int) else pl.multiple_of(start, B), size)
 
 
-LOADS = 4
 FIRST = 4 * 10**9
 
 
 def pack_body(pieces, items, count_a, count_g, fresh, *refs):
     n = len(items)
     if fresh:
-        (a_hbm, *outs), (notes, a_held, sems) = refs[: n + 1], refs[n + 1 :]
-        rows = a_hbm.shape[0] // LOADS
-        parts = [slice(part * rows, (part + 1) * rows) for part in range(LOADS)]
-        copies = [
-            pltpu.make_async_copy(a_hbm.at[part], a_held.at[part], sems.at[i])
-            for i, part in enumerate(parts)
-        ]
-        for copy in copies:
-            copy.start()
-        held = (a_held,)
+        held, refs = refs[:1], refs[1:]
     else:
-        copies = []
-        notes_in, held, outs, notes = refs[0], refs[1:4], refs[4 : 4 + n], refs[4 + n]
+        notes_in, held, refs = refs[0], refs[1:4], refs[4:]
+    outs, notes = refs[:n], refs[n]
     full, half = split_rows(count_a)
     slots = SLOTS // 2
     split = [(i, k, first, slot) for i, (k, first) in enumerate(items) for slot in range(slots)]
@@ -197,8 +187,6 @@
             at = at + H
         return at
 
-    for copy in copies:
-        copy.wait()
     for i, k, first, slot in split:
         here = pieces[k][3] * SLOTS + first + slot
         if here not in tiles:
@@ -226,25 +214,19 @@
         jax.ShapeDtypeStruct((slots, piece_rows(pieces, k), B), jnp.float32) for k, _ in items
     ]
     out_shape.append(jax.ShapeDtypeStruct((NOTES + 1, EDGE, B), jnp.float32))
-    if fresh:
-        args = [pltpu.with_memory_space_constraint(arrays[0], pltpu.HBM)]
-        out_shape.append(jax.ShapeDtypeStruct(arrays[0].shape, arrays[0].dtype))
-    else:
-        args = [notes, *arrays]
-    space = pltpu.HBM if fresh else pltpu.VMEM
+    args = arrays[:1] if fresh else [notes, *arrays]
     outs = pl.pallas_call(
         functools.partial(pack_body, pieces, items, count_a, count_g, fresh),
-        in_specs=[pl.BlockSpec(memory_space=space)] * len(args),
+        in_specs=[pl.BlockSpec(memory_space=pltpu.VMEM)] * len(args),
         out_specs=[pl.BlockSpec(memory_space=pltpu.VMEM)] * len(out_shape),
         out_shape=out_shape,
-        scratch_shapes=[pltpu.SemaphoreType.DMA((LOADS,))] * fresh,
         compiler_params=pltpu.CompilerParams(vmem_limit_bytes=32 * 2**20),
         cost_estimate=pl.CostEstimate(
             flops=FIRST if fresh else 1, bytes_accessed=1, transcendentals=0
         ),
     )(*args)
     n = len(items)
-    return outs[:n], outs[n], outs[n + 1 :]
+    return outs[:n], outs[n]
 
 
 def halve_body(n, terms, came, put, merged, *refs):
@@ -492,10 +474,9 @@
     keeps, gots, notes = {}, {}, None
 
     def pack_next(first, ks):
-        nonlocal notes, arrays
+        nonlocal notes
         items = tuple((k, first) for k in ks)
-        parts, notes, held = pack(arrays, pieces, items, count_a, count_g, notes)
-        arrays = (*held, *arrays[len(held) :])
+        parts, notes = pack(arrays, pieces, items, count_a, count_g, notes)
         return dict(zip(ks, parts))
 
     def exchange(parts, stage):

time: 36.7 us -> 37.2 us (1.014)
  Pallas kernels: 5.76 us -> 4.4 us
  starting transfers between devices: 16.5 us -> 17.7 us
  local copies, waits for them, and re-layouts: 0.01 us -> 1.19 us
  waiting for transfers between devices: 13.5 us -> 13 us
    pallas_call x5, Pallas kernels: 4.25 us -> 2.91 us  [pack(): pl.pallas_call(functools.partial(pack_body, pieces, items, count_a, count...]
    unnamed x4 -> x6, local copies, waits for them, and re-layouts: 0.01 us -> 1.19 us
    ppermute x12, starting transfers between devices: 16.5 us -> 17.7 us  [swap(): return lax.ppermute(value, ('dp', 'tensor'), pairs)]
    ppermute x12, waiting for transfers between devices: 13.5 us -> 13 us  [swap(): return lax.ppermute(value, ('dp', 'tensor'), pairs)]
  transfers between devices with their start and end apart: 12 -> 12, of which waited for: 9 -> 8; matrix products, arithmetic and copies ran while one was open for 0% -> 0% of each run, Pallas kernels for 8% -> 8%
where the time goes in v20:
time: 37.2 us; the launch traced here: 37 us
  starting transfers between devices  17.7 us (48%)
  waiting for transfers between devices  13 us (35%)
  Pallas kernels  4.4 us (12%)
  local copies, waits for them, and re-layouts  1.19 us (3%)
  between operations  0.73 us (2%)
    ppermute x12, starting transfers between devices, swap(): return lax.ppermute(value, ('dp', 'tensor'), pairs)  17.7 us
    ppermute x12, waiting for transfers between devices, swap(): return lax.ppermute(value, ('dp', 'tensor'), pairs)  13 us
    pallas_call x5, Pallas kernels, pack(): pl.pallas_call(functools.partial(pack_body, pieces, items, count_a, count...  2.91 us
    unnamed x6, local copies, waits for them, and re-layouts  1.19 us
    pallas_call x1, Pallas kernels, finish(): pl.pallas_call(functools.partial(finish_body, pieces, early, late, count_...  1.03 us
  transfers between devices with their start and end apart: 12, of which 8 were waited for; matrix products, arithmetic and copies ran while one was open for 0% of the time, Pallas kernels for 8%

profile of v20, /device:TPU:0, one launch (start us, length us, event | category | flops | bytes accessed | tf_op | source)
XLA Modules:
  0.0 37.0 jit_solution(4419934210166755607)
XLA Ops:
  0.6 1.2 %copy-done.2 = bf16[128,2560]{1,0:T(8,128)(2,1)S(1)} copy-done((bf16[128,2560]{1,0:T(8,128)(2,1)S(1)}, bf16[128,2560]{1,0:T(8,128)(2,1)}, u32[]{:S(2)}) %copy-start.2) | copy-done | bytes 655384
  2.2 3.0 %collective-permute-start.5 = (f32[4,128,128]{2,1,0:T(8,128)S(1)}, f32[4,128,128]{2,1,0:T(8,128)S(1)}, u32[]{:S(2)}, u32[]{:S(2)}) collective-permute-start(f32[4,128,128]{2,1,0:T(8,128)S(1)} %get-tuple-element.49), channel_id=1, source_target_pairs={{0,2},{1,3},{2,0},{3,1},{4,6},{5,7},{6,4},{7,5},{8,10},{9,11},{10,... | collective-permute-start | bytes 786440 | tf_op jit(solution)/shard_map/ppermute | solution.py:450
  5.2 0.4 %shard_map.51 = (f32[4,112,128]{2,1,0:T(8,128)S(1)}, f32[17,8,128]{2,1,0:T(8,128)S(1)}) custom-call(f32[17,8,128]{2,1,0:T(8,128)S(1)} %get-tuple-element.34.refs_0_, bf16[128,2560]{1,0:T(8,128)(2,1)S(1)} %copy-done.2, bf16[128,5120]{1,0:T(8,128)(2,1)S(1)} %copy-done, bf16[128,5120]{1,0:T(8,128)(2,1)S(1)} %copy-done.1), custom_call_target="tpu_custom_call" | custom-call | flops 1 | bytes 1 | tf_op jit(solution)/shard_map/pallas_call | solution.py:218
  5.6 1.6 %collective-permute-start.6 = (f32[4,112,128]{2,1,0:T(8,128)S(1)}, f32[4,112,128]{2,1,0:T(8,128)S(1)}, u32[]{:S(2)}, u32[]{:S(2)}) collective-permute-start(f32[4,112,128]{2,1,0:T(8,128)S(1)} %get-tuple-element.50), channel_id=1, source_target_pairs={{0,4},{1,5},{2,6},{3,7},{4,0},{5,1},{6,2},{7,3},{8,12},{9,13},{10,... | collective-permute-start | bytes 688136 | tf_op jit(solution)/shard_map/ppermute | solution.py:450
  7.3 0.8 %shard_map.52 = (f32[4,136,128]{2,1,0:T(8,128)S(1)}, f32[4,136,128]{2,1,0:T(8,128)S(1)}, f32[17,8,128]{2,1,0:T(8,128)S(1)}) custom-call(f32[17,8,128]{2,1,0:T(8,128)S(1)} %get-tuple-element.35.refs_0_, bf16[128,2560]{1,0:T(8,128)(2,1)S(1)} %copy-done.2, bf16[128,5120]{1,0:T(8,128)(2,1)S(1)} %copy-done, bf16[128,5120]{1,0:T(8,128)(2,1)S(1)} %copy-done.1), custom_call_target="tpu_custom_call" | custom-call | flops 1 | bytes 1 | tf_op jit(solution)/shard_map/pallas_call | solution.py:218
  8.1 1.0 %collective-permute-start = (f32[4,136,128]{2,1,0:T(8,128)S(1)}, f32[4,136,128]{2,1,0:T(8,128)S(1)}, u32[]{:S(2)}, u32[]{:S(2)}) collective-permute-start(f32[4,136,128]{2,1,0:T(8,128)S(1)} %get-tuple-element.40), channel_id=1, source_target_pairs={{0,2},{1,3},{2,0},{3,1},{4,6},{5,7},{6,4},{7,5},{8,10},{9,11},{10,... | collective-permute-start | bytes 835592 | tf_op jit(solution)/shard_map/ppermute | solution.py:450
  9.1 0.4 %collective-permute-start.1 = (f32[4,136,128]{2,1,0:T(8,128)S(1)}, f32[4,136,128]{2,1,0:T(8,128)S(1)}, u32[]{:S(2)}, u32[]{:S(2)}) collective-permute-start(f32[4,136,128]{2,1,0:T(8,128)S(1)} %get-tuple-element.41), channel_id=1, source_target_pairs={{0,4},{1,5},{2,6},{3,7},{4,0},{5,1},{6,2},{7,3},{8,12},{9,13},{10,... | collective-permute-start | bytes 835592 | tf_op jit(solution)/shard_map/ppermute | solution.py:450
  9.6 0.5 %shard_map.53 = (f32[4,128,128]{2,1,0:T(8,128)S(1)}, f32[4,112,128]{2,1,0:T(8,128)S(1)}, f32[17,8,128]{2,1,0:T(8,128)S(1)}) custom-call(f32[17,8,128]{2,1,0:T(8,128)S(1)} %get-tuple-element.36.refs_0_, bf16[128,2560]{1,0:T(8,128)(2,1)S(1)} %copy-done.2, bf16[128,5120]{1,0:T(8,128)(2,1)S(1)} %copy-done, bf16[128,5120]{1,0:T(8,128)(2,1)S(1)} %copy-done.1), custom_call_target="tpu_custom_call" | custom-call | flops 1 | bytes 1 | tf_op jit(solution)/shard_map/pallas_call | solution.py:218
  10.1 0.8 %shard_map.54 = (f32[4,136,128]{2,1,0:T(8,128)S(1)}, f32[4,136,128]{2,1,0:T(8,128)S(1)}, f32[17,8,128]{2,1,0:T(8,128)S(1)}) custom-call(f32[17,8,128]{2,1,0:T(8,128)S(1)} %get-tuple-element.37.refs_0_, bf16[128,2560]{1,0:T(8,128)(2,1)S(1)} %copy-done.2, bf16[128,5120]{1,0:T(8,128)(2,1)S(1)} %copy-done, bf16[128,5120]{1,0:T(8,128)(2,1)S(1)} %copy-done.1), custom_call_target="tpu_custom_call" | custom-call | flops 1 | bytes 1 | tf_op jit(solution)/shard_map/pallas_call | solution.py:218
  11.0 3.2 %collective-permute-done.6.refs_3_ = f32[4,112,128]{2,1,0:T(8,128)S(1)} collective-permute-done((f32[4,112,128]{2,1,0:T(8,128)S(1)}, f32[4,112,128]{2,1,0:T(8,128)S(1)}, u32[]{:S(2)}, u32[]{:S(2)}) %collective-permute-start.6) | collective-permute-done | bytes 229408 | tf_op jit(solution)/shard_map/ppermute | solution.py:450
  14.3 1.0 %collective-permute-start.8 = (f32[2,112,128]{2,1,0:T(8,128)S(1)}, f32[2,112,128]{2,1,0:T(8,128)S(1)}, u32[]{:S(2)}, u32[]{:S(2)}) collective-permute-start(f32[2,112,128]{2,1,0:T(8,128)S(1)} %get-tuple-element.54), channel_id=1, source_target_pairs={{0,2},{1,3},{2,0},{3,1},{4,6},{5,7},{6,4},{7,5},{8,10},{9,11},{10,... | collective-permute-start | bytes 344072 | tf_op jit(solution)/shard_map/ppermute | solution.py:450
  15.3 1.6 %collective-permute-start.7 = (f32[2,128,128]{2,1,0:T(8,128)S(1)}, f32[2,128,128]{2,1,0:T(8,128)S(1)}, u32[]{:S(2)}, u32[]{:S(2)}) collective-permute-start(f32[2,128,128]{2,1,0:T(8,128)S(1)} %get-tuple-element.53), channel_id=1, source_target_pairs={{0,4},{1,5},{2,6},{3,7},{4,0},{5,1},{6,2},{7,3},{8,12},{9,13},{10,... | collective-permute-start | bytes 393224 | tf_op jit(solution)/shard_map/ppermute | solution.py:450
  16.9 1.0 %collective-permute-start.9 = (f32[2,128]{1,0:T(2,128)S(1)}, f32[2,128]{1,0:T(2,128)S(1)}, u32[]{:S(2)}, u32[]{:S(2)}) collective-permute-start(f32[2,128]{1,0:T(2,128)S(1)} %fusion.refs_4_), channel_id=1, source_target_pairs={{0,6},{1,7},{2,4},{3,5},{4,2},{5,3},{6,0},{7,1},{8,14},{9,15},{10,... | collective-permute-start | bytes 3080 | tf_op jit(solution)/shard_map/ppermute | solution.py:450
  17.9 0.4 %collective-permute-done.refs_2_ = f32[4,136,128]{2,1,0:T(8,128)S(1)} collective-permute-done((f32[4,136,128]{2,1,0:T(8,128)S(1)}, f32[4,136,128]{2,1,0:T(8,128)S(1)}, u32[]{:S(2)}, u32[]{:S(2)}) %collective-permute-start) | collective-permute-done | bytes 278560 | tf_op jit(solution)/shard_map/ppermute | solution.py:450
  18.3 1.9 %collective-permute-done.1.refs_3_ = f32[4,136,128]{2,1,0:T(8,128)S(1)} collective-permute-done((f32[4,136,128]{2,1,0:T(8,128)S(1)}, f32[4,136,128]{2,1,0:T(8,128)S(1)}, u32[]{:S(2)}, u32[]{:S(2)}) %collective-permute-start.1) | collective-permute-done | bytes 278560 | tf_op jit(solution)/shard_map/ppermute | solution.py:450
  20.2 1.6 %collective-permute-start.3 = (f32[2,136,128]{2,1,0:T(8,128)S(1)}, f32[2,136,128]{2,1,0:T(8,128)S(1)}, u32[]{:S(2)}, u32[]{:S(2)}) collective-permute-start(f32[2,136,128]{2,1,0:T(8,128)S(1)} %get-tuple-element.45), channel_id=1, source_target_pairs={{0,4},{1,5},{2,6},{3,7},{4,0},{5,1},{6,2},{7,3},{8,12},{9,13},{10,... | collective-permute-start | bytes 417800 | tf_op jit(solution)/shard_map/ppermute | solution.py:450
  21.9 1.0 %collective-permute-start.4 = (f32[2,136,128]{2,1,0:T(8,128)S(1)}, f32[2,136,128]{2,1,0:T(8,128)S(1)}, u32[]{:S(2)}, u32[]{:S(2)}) collective-permute-start(f32[2,136,128]{2,1,0:T(8,128)S(1)} %get-tuple-element.46), channel_id=1, source_target_pairs={{0,2},{1,3},{2,0},{3,1},{4,6},{5,7},{6,4},{7,5},{8,10},{9,11},{10,... | collective-permute-start | bytes 417800 | tf_op jit(solution)/shard_map/ppermute | solution.py:450
  22.8 0.5 %collective-permute-done.9.refs_5_ = f32[2,128]{1,0:T(2,128)S(1)} collective-permute-done((f32[2,128]{1,0:T(2,128)S(1)}, f32[2,128]{1,0:T(2,128)S(1)}, u32[]{:S(2)}, u32[]{:S(2)}) %collective-permute-start.9) | collective-permute-done | bytes 1056 | tf_op jit(solution)/shard_map/ppermute | solution.py:450
  23.4 2.7 %collective-permute-start.11 = (f32[1,240,128]{2,1,0:T(8,128)S(1)}, f32[1,240,128]{2,1,0:T(8,128)S(1)}, u32[]{:S(2)}, u32[]{:S(2)}) collective-permute-start(f32[1,240,128]{2,1,0:T(8,128)S(1)} %get-tuple-element.61), channel_id=1, source_target_pairs={{0,8},{1,9},{2,10},{3,11},{4,12},{5,13},{6,14},{7,15},{8,0},{9,1},... | collective-permute-start | bytes 368648 | tf_op jit(solution)/shard_map/ppermute | solution.py:450
  26.0 0.6 %collective-permute-done.3.refs_2_ = f32[2,136,128]{2,1,0:T(8,128)S(1)} collective-permute-done((f32[2,136,128]{2,1,0:T(8,128)S(1)}, f32[2,136,128]{2,1,0:T(8,128)S(1)}, u32[]{:S(2)}, u32[]{:S(2)}) %collective-permute-start.3) | collective-permute-done | bytes 139296 | tf_op jit(solution)/shard_map/ppermute | solution.py:450
  26.9 2.7 %collective-permute-start.10 = (f32[1,272,128]{2,1,0:T(8,128)S(1)}, f32[1,272,128]{2,1,0:T(8,128)S(1)}, u32[]{:S(2)}, u32[]{:S(2)}) collective-permute-start(f32[1,272,128]{2,1,0:T(8,128)S(1)} %get-tuple-element.58), channel_id=1, source_target_pairs={{0,8},{1,9},{2,10},{3,11},{4,12},{5,13},{6,14},{7,15},{8,0},{9,1},... | collective-permute-start | bytes 417800 | tf_op jit(solution)/shard_map/ppermute | solution.py:450
  29.6 4.9 %collective-permute-done.11.refs_2_ = f32[1,240,128]{2,1,0:T(8,128)S(1)} collective-permute-done((f32[1,240,128]{2,1,0:T(8,128)S(1)}, f32[1,240,128]{2,1,0:T(8,128)S(1)}, u32[]{:S(2)}, u32[]{:S(2)}) %collective-permute-start.11) | collective-permute-done | bytes 122912 | tf_op jit(solution)/shard_map/ppermute | solution.py:450
  34.8 1.2 %collective-permute-done.10.refs_2_ = f32[1,272,128]{2,1,0:T(8,128)S(1)} collective-permute-done((f32[1,272,128]{2,1,0:T(8,128)S(1)}, f32[1,272,128]{2,1,0:T(8,128)S(1)}, u32[]{:S(2)}, u32[]{:S(2)}) %collective-permute-start.10) | collective-permute-done | bytes 139296 | tf_op jit(solution)/shard_map/ppermute | solution.py:450
  36.0 1.0 %shard_map.60 = (f32[320,128]{1,0:T(8,128)}, f32[640,128]{1,0:T(8,128)}) custom-call(f32[1,136,128]{2,1,0:T(8,128)S(1)} %get-tuple-element.56.refs_0_, f32[1,136,128]{2,1,0:T(8,128)S(1)} %get-tuple-element.57.refs_1_, f32[1,272,128]{2,1,0:T(8,128)S(1)} %collective-permute-done.10.refs_2_, f32[320,128]{1,0:T(8,128)S(1)} %get-tuple-element.62.refs_3_, ...), custom_call_target="tpu_custom_call" | custom-call | tf_op jit(solution)/shard_map/pallas_call | solution.py:426
  (19 shorter events, 1.2 us)
Async XLA Ops:
  0.6 4.6 %copy-start.1 = (bf16[128,5120]{1,0:T(8,128)(2,1)S(1)}, bf16[128,5120]{1,0:T(8,128)(2,1)}, u32[]{:S(2)}) copy-start(bf16[128,5120]{1,0:T(8,128)(2,1)} %refs_3_.7) | copy-start | bytes 3932164
  0.6 1.2 %copy-start.2 = (bf16[128,2560]{1,0:T(8,128)(2,1)S(1)}, bf16[128,2560]{1,0:T(8,128)(2,1)}, u32[]{:S(2)}) copy-start(bf16[128,2560]{1,0:T(8,128)(2,1)} %refs_1_.7) | copy-start | bytes 1966084
  1.8 3.4 %copy-start = (bf16[128,5120]{1,0:T(8,128)(2,1)S(1)}, bf16[128,5120]{1,0:T(8,128)(2,1)}, u32[]{:S(2)}) copy-start(bf16[128,5120]{1,0:T(8,128)(2,1)} %refs_2_.7) | copy-start | bytes 3932164
  2.2 12.1 %collective-permute-start.5 = (f32[4,128,128]{2,1,0:T(8,128)S(1)}, f32[4,128,128]{2,1,0:T(8,128)S(1)}, u32[]{:S(2)}, u32[]{:S(2)}) collective-permute-start(f32[4,128,128]{2,1,0:T(8,128)S(1)} %get-tuple-element.49), channel_id=1, source_target_pairs={{0,2},{1,3},{2,0},{3,1},{4,6},{5,7},{6,4},{7,5},{8,10},{9,11},{10,... | collective-permute-start | bytes 786440 | tf_op jit(solution)/shard_map/ppermute | solution.py:450
  5.6 8.6 %collective-permute-start.6 = (f32[4,112,128]{2,1,0:T(8,128)S(1)}, f32[4,112,128]{2,1,0:T(8,128)S(1)}, u32[]{:S(2)}, u32[]{:S(2)}) collective-permute-start(f32[4,112,128]{2,1,0:T(8,128)S(1)} %get-tuple-element.50), channel_id=1, source_target_pairs={{0,4},{1,5},{2,6},{3,7},{4,0},{5,1},{6,2},{7,3},{8,12},{9,13},{10,... | collective-permute-start | bytes 688136 | tf_op jit(solution)/shard_map/ppermute | solution.py:450
  8.1 10.2 %collective-permute-start = (f32[4,136,128]{2,1,0:T(8,128)S(1)}, f32[4,136,128]{2,1,0:T(8,128)S(1)}, u32[]{:S(2)}, u32[]{:S(2)}) collective-permute-start(f32[4,136,128]{2,1,0:T(8,128)S(1)} %get-tuple-element.40), channel_id=1, source_target_pairs={{0,2},{1,3},{2,0},{3,1},{4,6},{5,7},{6,4},{7,5},{8,10},{9,11},{10,... | collective-permute-start | bytes 835592 | tf_op jit(solution)/shard_map/ppermute | solution.py:450
  9.1 11.0 %collective-permute-start.1 = (f32[4,136,128]{2,1,0:T(8,128)S(1)}, f32[4,136,128]{2,1,0:T(8,128)S(1)}, u32[]{:S(2)}, u32[]{:S(2)}) collective-permute-start(f32[4,136,128]{2,1,0:T(8,128)S(1)} %get-tuple-element.41), channel_id=1, source_target_pairs={{0,4},{1,5},{2,6},{3,7},{4,0},{5,1},{6,2},{7,3},{8,12},{9,13},{10,... | collective-permute-start | bytes 835592 | tf_op jit(solution)/shard_map/ppermute | solution.py:450
  10.9 5.9 %collective-permute-start.2 = (f32[2,128]{1,0:T(2,128)S(1)}, f32[2,128]{1,0:T(2,128)S(1)}, u32[]{:S(2)}, u32[]{:S(2)}) collective-permute-start(f32[2,128]{1,0:T(2,128)S(1)} %slice_bitcast_fusion), channel_id=1, source_target_pairs={{0,1},{1,0},{2,3},{3,2},{4,5},{5,4},{6,7},{7,6},{8,9},{9,8},{10,11... | collective-permute-start | bytes 3080 | tf_op jit(solution)/shard_map/ppermute | solution.py:450
  14.3 9.0 %collective-permute-start.8 = (f32[2,112,128]{2,1,0:T(8,128)S(1)}, f32[2,112,128]{2,1,0:T(8,128)S(1)}, u32[]{:S(2)}, u32[]{:S(2)}) collective-permute-start(f32[2,112,128]{2,1,0:T(8,128)S(1)} %get-tuple-element.54), channel_id=1, source_target_pairs={{0,2},{1,3},{2,0},{3,1},{4,6},{5,7},{6,4},{7,5},{8,10},{9,11},{10,... | collective-permute-start | bytes 344072 | tf_op jit(solution)/shard_map/ppermute | solution.py:450
  15.3 8.0 %collective-permute-start.7 = (f32[2,128,128]{2,1,0:T(8,128)S(1)}, f32[2,128,128]{2,1,0:T(8,128)S(1)}, u32[]{:S(2)}, u32[]{:S(2)}) collective-permute-start(f32[2,128,128]{2,1,0:T(8,128)S(1)} %get-tuple-element.53), channel_id=1, source_target_pairs={{0,4},{1,5},{2,6},{3,7},{4,0},{5,1},{6,2},{7,3},{8,12},{9,13},{10,... | collective-permute-start | bytes 393224 | tf_op jit(solution)/shard_map/ppermute | solution.py:450
  16.9 6.5 %collective-permute-start.9 = (f32[2,128]{1,0:T(2,128)S(1)}, f32[2,128]{1,0:T(2,128)S(1)}, u32[]{:S(2)}, u32[]{:S(2)}) collective-permute-start(f32[2,128]{1,0:T(2,128)S(1)} %fusion.refs_4_), channel_id=1, source_target_pairs={{0,6},{1,7},{2,4},{3,5},{4,2},{5,3},{6,0},{7,1},{8,14},{9,15},{10,... | collective-permute-start | bytes 3080 | tf_op jit(solution)/shard_map/ppermute | solution.py:450
  20.2 6.4 %collective-permute-start.3 = (f32[2,136,128]{2,1,0:T(8,128)S(1)}, f32[2,136,128]{2,1,0:T(8,128)S(1)}, u32[]{:S(2)}, u32[]{:S(2)}) collective-permute-start(f32[2,136,128]{2,1,0:T(8,128)S(1)} %get-tuple-element.45), channel_id=1, source_target_pairs={{0,4},{1,5},{2,6},{3,7},{4,0},{5,1},{6,2},{7,3},{8,12},{9,13},{10,... | collective-permute-start | bytes 417800 | tf_op jit(solution)/shard_map/ppermute | solution.py:450
  21.9 5.1 %collective-permute-start.4 = (f32[2,136,128]{2,1,0:T(8,128)S(1)}, f32[2,136,128]{2,1,0:T(8,128)S(1)}, u32[]{:S(2)}, u32[]{:S(2)}) collective-permute-start(f32[2,136,128]{2,1,0:T(8,128)S(1)} %get-tuple-element.46), channel_id=1, source_target_pairs={{0,2},{1,3},{2,0},{3,1},{4,6},{5,7},{6,4},{7,5},{8,10},{9,11},{10,... | collective-permute-start | bytes 417800 | tf_op jit(solution)/shard_map/ppermute | solution.py:450
  23.4 11.1 %collective-permute-start.11 = (f32[1,240,128]{2,1,0:T(8,128)S(1)}, f32[1,240,128]{2,1,0:T(8,128)S(1)}, u32[]{:S(2)}, u32[]{:S(2)}) collective-permute-start(f32[1,240,128]{2,1,0:T(8,128)S(1)} %get-tuple-element.61), channel_id=1, source_target_pairs={{0,8},{1,9},{2,10},{3,11},{4,12},{5,13},{6,14},{7,15},{8,0},{9,1},... | collective-permute-start | bytes 368648 | tf_op jit(solution)/shard_map/ppermute | solution.py:450
  26.9 9.0 %collective-permute-start.10 = (f32[1,272,128]{2,1,0:T(8,128)S(1)}, f32[1,272,128]{2,1,0:T(8,128)S(1)}, u32[]{:S(2)}, u32[]{:S(2)}) collective-permute-start(f32[1,272,128]{2,1,0:T(8,128)S(1)} %get-tuple-element.58), channel_id=1, source_target_pairs={{0,8},{1,9},{2,10},{3,11},{4,12},{5,13},{6,14},{7,15},{8,0},{9,1},... | collective-permute-start | bytes 417800 | tf_op jit(solution)/shard_map/ppermute | solution.py:450

commit v21 on v17

--- a/solution.py
+++ b/solution.py
@@ -62,7 +62,7 @@
 KINDS = (((X, NEAR, FAR), (X, NEAR, FAR)), ((NEAR, X, FAR), (NEAR, X, FAR)))
 NOTES = len(KINDS) * SLOTS
 
-WEIGHTS = {((0, 2), 2): 2 * 10**9}
+WEIGHTS = {((0, 1), 2): 2 * 10**9}
 
 
 def split_rows(count):
@@ -247,10 +247,12 @@
     return outs[:n], outs[n], outs[n + 1 :]
 
 
-def halve_body(n, terms, came, put, merged, *refs):
+def halve_body(n, terms, came, put, merged, passed, *refs):
     keeps, gots, refs = refs[:n], refs[n : 2 * n], refs[2 * n :]
-    terms, kept, refs = refs[:terms], refs[terms : terms + n], refs[terms + n :]
+    terms, refs = refs[:terms], refs[terms + passed :]
+    kept, refs = refs[:n], refs[n:]
     sent, sums = (refs[:1], refs[1:]) if merged else (refs[:n], refs[n:])
+    sums = sums[passed:]
     if merged:
         ends = [sum(ref.shape[1] for ref in kept[: k + 1]) for k in range(n)]
         sent = [
@@ -272,18 +274,21 @@
             sent[k][0, rows - 2 :, :] = value
 
 
-def halve(keeps, gots, terms=(), came=(), put=(), merged=False, weight=1):
+def halve(keeps, gots, terms=(), came=(), put=(), merged=False, passes=(), weight=1):
     n = len(keeps)
     emit = bool(terms) and not put
-    args = [*keeps, *gots, *terms]
+    args = [*keeps, *gots, *terms, *passes]
+    first = len(args) - len(passes)
     kept = [(keep.shape[0] // 2, *keep.shape[1:]) for keep in keeps]
     sent = [(kept[0][0], sum(shape[1] for shape in kept), B)] if merged else kept
-    shapes = [*kept, *sent, *([(2, B)] * emit)]
+    shapes = [*kept, *sent, *(array.shape for array in passes), *([(2, B)] * emit)]
+    last = n + len(sent)
     outs = pl.pallas_call(
-        functools.partial(halve_body, n, len(terms), came, put, merged),
+        functools.partial(halve_body, n, len(terms), came, put, merged, len(passes)),
         in_specs=[pl.BlockSpec(memory_space=pltpu.VMEM)] * len(args),
         out_specs=[pl.BlockSpec(memory_space=pltpu.VMEM)] * len(shapes),
         out_shape=[jax.ShapeDtypeStruct(shape, jnp.float32) for shape in shapes],
+        input_output_aliases={first + i: last + i for i in range(len(passes))},
         compiler_params=pltpu.CompilerParams(vmem_limit_bytes=32 * 2**20),
         cost_estimate=pl.CostEstimate(flops=weight, bytes_accessed=1, transcendentals=0),
     )(*args)
@@ -365,10 +370,10 @@
             outs[which][pl.ds(start + i * H, H), :] = value
 
 
-def finish_body(pieces, early, late, count_a, total, *refs):
+def finish_body(pieces, befores, late, count_a, total, *refs):
     n = len(late)
-    owns, got, firsts, outs = refs[:n], refs[n], refs[n + 1 : n + 3], refs[n + 3 : n + 5]
-    made, sem = refs[n + 5 : n + 7], refs[n + 7]
+    owns, got, firsts, refs = refs[:n], refs[n], refs[n + 1 : -5], refs[-5:]
+    outs, made, sem = refs[:2], refs[2:4], refs[4]
     _, half = split_rows(count_a)
     odd = lax.axis_index("dp") & half
     row, col = iotas(H)
@@ -413,10 +418,11 @@
         copy.start()
         copies.append(copy)
 
-    for place in places(pieces, early, count_a):
-        _, which, start, rows, _ = place
-        count = 2 if rows == H else 1
-        give(place, [firsts[which][pl.ds(start + i * H, H), :] for i in range(count)])
+    for number, ks in enumerate(befores):
+        for place in places(pieces, ks, count_a):
+            _, which, start, rows, _ = place
+            ref, count = firsts[2 * number + which], 2 if rows == H else 1
+            give(place, [ref[pl.ds(start + i * H, H), :] for i in range(count)])
     for place, halves in unfolded(pieces, late, count_a, total, owns, got):
         give(place, halves)
     for copy in copies:
@@ -438,11 +444,11 @@
     )(*args)
 
 
-def finish(pieces, early, late, owns, got, first, count_a, count_g, total):
+def finish(pieces, befores, late, owns, got, first, count_a, count_g, total):
     args = (*owns, got, *first)
     parts = sum(len(a_blocks) + a_half + len(g_blocks) for a_blocks, a_half, g_blocks, _ in pieces)
     return pl.pallas_call(
-        functools.partial(finish_body, pieces, early, late, count_a, total),
+        functools.partial(finish_body, pieces, befores, late, count_a, total),
         in_specs=[pl.BlockSpec(memory_space=pltpu.VMEM)] * len(args),
         out_specs=[pl.BlockSpec(memory_space=pltpu.HBM)] * 2,
         out_shape=[
@@ -479,16 +485,19 @@
     count_g = saved_pre.shape[1] // dp
     full_a, half_a = split_rows(count_a)
     full_g, _ = split_rows(count_g)
-    some = 1 + (full_g - 1) // 2
+    cuts = [0] + [1 + (full_g - 1) * i // 4 for i in range(5)]
+    blocks = [tuple(range(begin, end)) for begin, end in zip(cuts, cuts[1:])]
     pieces = (
         (tuple(range(full_a)), 0, (), 0),
-        ((), 0, tuple(range(1, some)), 0),
-        ((), half_a, (0,), 1),
-        ((), 0, tuple(range(some, full_g)), 1),
+        ((), half_a, blocks[0], 1),
+        ((), 0, blocks[1], 0),
+        ((), 0, blocks[2], 1),
+        ((), 0, blocks[3], 0),
+        ((), 0, blocks[4], 1),
     )
     arrays = (saved_input, saved_pre, grad_act)
     keep, send = 0, SLOTS // 2
-    early, late = (0, 2), (1, 3)
+    early, middle, late = (0, 1), (2, 3), (4, 5)
     keeps, gots, notes = {}, {}, None
 
     def pack_next(first, ks):
@@ -516,31 +525,38 @@
 
     exchange(pack_next(send, early[:1]), 0)
     exchange(pack_next(send, early[1:]), 0)
-    exchange(pack_next(send, late), 0)
+    exchange(pack_next(send, middle), 0)
+    waiting = pack_next(send, late)
     keeps.update(pack_next(keep, early))
+    keeps.update(pack_next(keep, middle))
     keeps.update(pack_next(keep, late))
 
     trace = notes[NOTES, :2, :]
     trace = trace + swap(trace, lambda i, j: (i, j ^ 1))
     across = swap(trace, lambda i, j: (i ^ (1 << X) ^ (1 << NEAR), j))
-    halve_pair(early, 1)
+    parts = halve_pair(early, 1, passes=tuple(waiting.values()))
+    exchange(dict(zip(waiting, parts)), 0)
+    halve_pair(middle, 1)
     halve_pair(late, 1, terms=(trace,), put=(0, 1))
     (trace,) = halve_pair(early, 2, terms=(trace, across))
+    halve_pair(middle, 2)
     halve_pair(late, 2, terms=(trace,), came=(0, 1), put=(0, 1))
 
     def both(ks):
         return [keeps[k] for k in ks], gots[ks]
 
-    first = unfold_early(pieces, early, *both(early), count_a, count_g, total)
+    befores, first = (early, middle), []
+    for ks in befores:
+        first += unfold_early(pieces, ks, *both(ks), count_a, count_g, total)
     a_factor, g_factor = finish(
-        pieces, early, late, *both(late), first, count_a, count_g, total
+        pieces, befores, late, *both(late), first, count_a, count_g, total
     )
     return a_factor[None], g_factor[None]
 
 
 def fits(count_a, count_g):
     (full_a, half_a), full_g = split_rows(count_a), count_g // B
-    if count_a % H or count_g % B or full_a < 1 or full_g < 3:
+    if count_a % H or count_g % B or full_a < 1 or full_g < 5:
         return False
     return full_a + half_a + full_g <= 2 * (EDGE - 2)
 

time: 36.7 us -> 45.1 us (1.23)
  starting transfers between devices: 16.5 us -> 21.2 us
  waiting for transfers between devices: 13.5 us -> 16.5 us
  Pallas kernels: 5.76 us -> 6.44 us
    ppermute x12 -> x17, starting transfers between devices: 16.5 us -> 21.2 us  [swap(): return lax.ppermute(value, ('dp', 'tensor'), pairs)]
    ppermute x12 -> x17, waiting for transfers between devices: 13.5 us -> 16.5 us  [swap(): return lax.ppermute(value, ('dp', 'tensor'), pairs)]
    pallas_call x5 -> x7, Pallas kernels: 4.25 us -> 4.81 us  [pack(): pl.pallas_call(functools.partial(pack_body, pieces, items, count_a, count...]
  transfers between devices with their start and end apart: 12 -> 17, of which waited for: 9 -> 7; matrix products, arithmetic and copies ran while one was open for 0% -> 0% of each run, Pallas kernels for 8% -> 8%
where the time goes in v21:
time: 45.1 us; the launch traced here: 45 us
  starting transfers between devices  21.2 us (47%)
  waiting for transfers between devices  16.5 us (37%)
  Pallas kernels  6.44 us (14%)
  between operations  0.79 us (2%)
    ppermute x17, starting transfers between devices, swap(): return lax.ppermute(value, ('dp', 'tensor'), pairs)  21.2 us
    ppermute x17, waiting for transfers between devices, swap(): return lax.ppermute(value, ('dp', 'tensor'), pairs)  16.5 us
    pallas_call x7, Pallas kernels, pack(): pl.pallas_call(functools.partial(pack_body, pieces, items, count_a, count...  4.81 us
    pallas_call x1, Pallas kernels, finish(): pl.pallas_call(functools.partial(finish_body, pieces, befores, late, coun...  1.02 us
  transfers between devices with their start and end apart: 17, of which 7 were waited for; matrix products, arithmetic and copies ran while one was open for 0% of the time, Pallas kernels for 8%

profile of v21, /device:TPU:0, one launch (start us, length us, event | category | flops | bytes accessed | tf_op | source)
XLA Modules:
  0.0 45.0 jit_solution(10902655933038050171)
XLA Ops:
  0.6 1.7 %shard_map.50 = (f32[4,128,128]{2,1,0:T(8,128)S(1)}, f32[17,8,128]{2,1,0:T(8,128)S(1)}, bf16[128,2560]{1,0:T(8,128)(2,1)S(1)}) custom-call(bf16[128,2560]{1,0:T(8,128)(2,1)} %refs_0_.1), custom_call_target="tpu_custom_call" | custom-call | flops 4000000000 | bytes 1 | tf_op jit(solution)/shard_map/pallas_call | solution.py:235
  2.3 3.0 %collective-permute-start = (f32[4,128,128]{2,1,0:T(8,128)S(1)}, f32[4,128,128]{2,1,0:T(8,128)S(1)}, u32[]{:S(2)}, u32[]{:S(2)}) collective-permute-start(f32[4,128,128]{2,1,0:T(8,128)S(1)} %get-tuple-element.63), channel_id=1, source_target_pairs={{0,2},{1,3},{2,0},{3,1},{4,6},{5,7},{6,4},{7,5},{8,10},{9,11},{10,... | collective-permute-start | bytes 786440 | tf_op jit(solution)/shard_map/ppermute | solution.py:474
  5.8 1.6 %collective-permute-start.1 = (f32[4,112,128]{2,1,0:T(8,128)S(1)}, f32[4,112,128]{2,1,0:T(8,128)S(1)}, u32[]{:S(2)}, u32[]{:S(2)}) collective-permute-start(f32[4,112,128]{2,1,0:T(8,128)S(1)} %get-tuple-element.64), channel_id=1, source_target_pairs={{0,4},{1,5},{2,6},{3,7},{4,0},{5,1},{6,2},{7,3},{8,12},{9,13},{10,... | collective-permute-start | bytes 688136 | tf_op jit(solution)/shard_map/ppermute | solution.py:474
  7.4 0.5 %shard_map.52 = (f32[4,64,128]{2,1,0:T(8,128)S(1)}, f32[4,64,128]{2,1,0:T(8,128)S(1)}, f32[17,8,128]{2,1,0:T(8,128)S(1)}) custom-call(f32[17,8,128]{2,1,0:T(8,128)S(1)} %get-tuple-element.54.refs_0_, bf16[128,2560]{1,0:T(8,128)(2,1)S(1)} %get-tuple-element.53.refs_1_, bf16[128,5120]{1,0:T(8,128)(2,1)S(1)} %copy-done, bf16[128,5120]{1,0:T(8,128)(2,1)S(1)} %copy-done.1), custom_call_target="tpu_custom_call" | custom-call | flops 1 | bytes 1 | tf_op jit(solution)/shard_map/pallas_call | solution.py:235
  8.0 0.6 %collective-permute-start.12 = (f32[4,64,128]{2,1,0:T(8,128)S(1)}, f32[4,64,128]{2,1,0:T(8,128)S(1)}, u32[]{:S(2)}, u32[]{:S(2)}) collective-permute-start(f32[4,64,128]{2,1,0:T(8,128)S(1)} %get-tuple-element.89), channel_id=1, source_target_pairs={{0,2},{1,3},{2,0},{3,1},{4,6},{5,7},{6,4},{7,5},{8,10},{9,11},{10,... | collective-permute-start | bytes 393224 | tf_op jit(solution)/shard_map/ppermute | solution.py:474
  8.7 0.5 %shard_map.53 = (f32[4,72,128]{2,1,0:T(8,128)S(1)}, f32[4,72,128]{2,1,0:T(8,128)S(1)}, f32[17,8,128]{2,1,0:T(8,128)S(1)}) custom-call(f32[17,8,128]{2,1,0:T(8,128)S(1)} %get-tuple-element.55.refs_0_, bf16[128,2560]{1,0:T(8,128)(2,1)S(1)} %get-tuple-element.53.refs_1_, bf16[128,5120]{1,0:T(8,128)(2,1)S(1)} %copy-done, bf16[128,5120]{1,0:T(8,128)(2,1)S(1)} %copy-done.1), custom_call_target="tpu_custom_call" | custom-call | flops 1 | bytes 1 | tf_op jit(solution)/shard_map/pallas_call | solution.py:235
  9.3 0.5 %shard_map.54 = (f32[4,128,128]{2,1,0:T(8,128)S(1)}, f32[4,112,128]{2,1,0:T(8,128)S(1)}, f32[17,8,128]{2,1,0:T(8,128)S(1)}) custom-call(f32[17,8,128]{2,1,0:T(8,128)S(1)} %get-tuple-element.56.refs_0_, bf16[128,2560]{1,0:T(8,128)(2,1)S(1)} %get-tuple-element.53.refs_1_, bf16[128,5120]{1,0:T(8,128)(2,1)S(1)} %copy-done, bf16[128,5120]{1,0:T(8,128)(2,1)S(1)} %copy-done.1), custom_call_target="tpu_custom_call" | custom-call | flops 1 | bytes 1 | tf_op jit(solution)/shard_map/pallas_call | solution.py:235
  9.8 0.5 %shard_map.55 = (f32[4,64,128]{2,1,0:T(8,128)S(1)}, f32[4,64,128]{2,1,0:T(8,128)S(1)}, f32[17,8,128]{2,1,0:T(8,128)S(1)}) custom-call(f32[17,8,128]{2,1,0:T(8,128)S(1)} %get-tuple-element.57.refs_0_, bf16[128,2560]{1,0:T(8,128)(2,1)S(1)} %get-tuple-element.53.refs_1_, bf16[128,5120]{1,0:T(8,128)(2,1)S(1)} %copy-done, bf16[128,5120]{1,0:T(8,128)(2,1)S(1)} %copy-done.1), custom_call_target="tpu_custom_call" | custom-call | flops 1 | bytes 1 | tf_op jit(solution)/shard_map/pallas_call | solution.py:235
  10.4 0.5 %shard_map.56 = (f32[4,72,128]{2,1,0:T(8,128)S(1)}, f32[4,72,128]{2,1,0:T(8,128)S(1)}, f32[17,8,128]{2,1,0:T(8,128)S(1)}) custom-call(f32[17,8,128]{2,1,0:T(8,128)S(1)} %get-tuple-element.58.refs_0_, bf16[128,2560]{1,0:T(8,128)(2,1)S(1)} %get-tuple-element.53.refs_1_, bf16[128,5120]{1,0:T(8,128)(2,1)S(1)} %copy-done, bf16[128,5120]{1,0:T(8,128)(2,1)S(1)} %copy-done.1), custom_call_target="tpu_custom_call" | custom-call | flops 1 | bytes 1 | tf_op jit(solution)/shard_map/pallas_call | solution.py:235
  11.0 3.5 %collective-permute-done.12.refs_2_ = f32[4,64,128]{2,1,0:T(8,128)S(1)} collective-permute-done((f32[4,64,128]{2,1,0:T(8,128)S(1)}, f32[4,64,128]{2,1,0:T(8,128)S(1)}, u32[]{:S(2)}, u32[]{:S(2)}) %collective-permute-start.12) | collective-permute-done | bytes 131104 | tf_op jit(solution)/shard_map/ppermute | solution.py:474
  14.5 1.3 %collective-permute-done.13.refs_3_ = f32[4,64,128]{2,1,0:T(8,128)S(1)} collective-permute-done((f32[4,64,128]{2,1,0:T(8,128)S(1)}, f32[4,64,128]{2,1,0:T(8,128)S(1)}, u32[]{:S(2)}, u32[]{:S(2)}) %collective-permute-start.13) | collective-permute-done | bytes 131104 | tf_op jit(solution)/shard_map/ppermute | solution.py:474
  15.8 1.6 %collective-permute-start.14 = (f32[2,64,128]{2,1,0:T(8,128)S(1)}, f32[2,64,128]{2,1,0:T(8,128)S(1)}, u32[]{:S(2)}, u32[]{:S(2)}) collective-permute-start(f32[2,64,128]{2,1,0:T(8,128)S(1)} %get-tuple-element.93), channel_id=1, source_target_pairs={{0,4},{1,5},{2,6},{3,7},{4,0},{5,1},{6,2},{7,3},{8,12},{9,13},{10,... | collective-permute-start | bytes 196616 | tf_op jit(solution)/shard_map/ppermute | solution.py:474
  17.4 0.5 %collective-permute-start.15 = (f32[2,64,128]{2,1,0:T(8,128)S(1)}, f32[2,64,128]{2,1,0:T(8,128)S(1)}, u32[]{:S(2)}, u32[]{:S(2)}) collective-permute-start(f32[2,64,128]{2,1,0:T(8,128)S(1)} %get-tuple-element.94), channel_id=1, source_target_pairs={{0,2},{1,3},{2,0},{3,1},{4,6},{5,7},{6,4},{7,5},{8,10},{9,11},{10,... | collective-permute-start | bytes 196616 | tf_op jit(solution)/shard_map/ppermute | solution.py:474
  18.5 1.5 %collective-permute-start.8 = (f32[2,112,128]{2,1,0:T(8,128)S(1)}, f32[2,112,128]{2,1,0:T(8,128)S(1)}, u32[]{:S(2)}, u32[]{:S(2)}) collective-permute-start(f32[2,112,128]{2,1,0:T(8,128)S(1)} %get-tuple-element.77), channel_id=1, source_target_pairs={{0,2},{1,3},{2,0},{3,1},{4,6},{5,7},{6,4},{7,5},{8,10},{9,11},{10,... | collective-permute-start | bytes 344072 | tf_op jit(solution)/shard_map/ppermute | solution.py:474
  20.0 1.6 %collective-permute-start.9 = (f32[2,128]{1,0:T(2,128)S(1)}, f32[2,128]{1,0:T(2,128)S(1)}, u32[]{:S(2)}, u32[]{:S(2)}) collective-permute-start(f32[2,128]{1,0:T(2,128)S(1)} %fusion.refs_4_), channel_id=1, source_target_pairs={{0,6},{1,7},{2,4},{3,5},{4,2},{5,3},{6,0},{7,1},{8,14},{9,15},{10,... | collective-permute-start | bytes 3080 | tf_op jit(solution)/shard_map/ppermute | solution.py:474
  21.7 2.7 %collective-permute-start.16 = (f32[1,128,128]{2,1,0:T(8,128)S(1)}, f32[1,128,128]{2,1,0:T(8,128)S(1)}, u32[]{:S(2)}, u32[]{:S(2)}) collective-permute-start(f32[1,128,128]{2,1,0:T(8,128)S(1)} %get-tuple-element.97), channel_id=1, source_target_pairs={{0,8},{1,9},{2,10},{3,11},{4,12},{5,13},{6,14},{7,15},{8,0},{9,1},... | collective-permute-start | bytes 196616 | tf_op jit(solution)/shard_map/ppermute | solution.py:474
  24.4 1.4 %collective-permute-start.2 = (f32[4,72,128]{2,1,0:T(8,128)S(1)}, f32[4,72,128]{2,1,0:T(8,128)S(1)}, u32[]{:S(2)}, u32[]{:S(2)}) collective-permute-start(f32[4,72,128]{2,1,0:T(8,128)S(1)} %get-tuple-element.67), channel_id=1, source_target_pairs={{0,2},{1,3},{2,0},{3,1},{4,6},{5,7},{6,4},{7,5},{8,10},{9,11},{10,... | collective-permute-start | bytes 442376 | tf_op jit(solution)/shard_map/ppermute | solution.py:474
  26.2 2.5 %collective-permute-start.11 = (f32[1,240,128]{2,1,0:T(8,128)S(1)}, f32[1,240,128]{2,1,0:T(8,128)S(1)}, u32[]{:S(2)}, u32[]{:S(2)}) collective-permute-start(f32[1,240,128]{2,1,0:T(8,128)S(1)} %get-tuple-element.84), channel_id=1, source_target_pairs={{0,8},{1,9},{2,10},{3,11},{4,12},{5,13},{6,14},{7,15},{8,0},{9,1},... | collective-permute-start | bytes 368648 | tf_op jit(solution)/shard_map/ppermute | solution.py:474
  28.8 0.7 %collective-permute-done.2.refs_2_ = f32[4,72,128]{2,1,0:T(8,128)S(1)} collective-permute-done((f32[4,72,128]{2,1,0:T(8,128)S(1)}, f32[4,72,128]{2,1,0:T(8,128)S(1)}, u32[]{:S(2)}, u32[]{:S(2)}) %collective-permute-start.2) | collective-permute-done | bytes 147488 | tf_op jit(solution)/shard_map/ppermute | solution.py:474
  29.5 4.2 %collective-permute-done.3.refs_3_ = f32[4,72,128]{2,1,0:T(8,128)S(1)} collective-permute-done((f32[4,72,128]{2,1,0:T(8,128)S(1)}, f32[4,72,128]{2,1,0:T(8,128)S(1)}, u32[]{:S(2)}, u32[]{:S(2)}) %collective-permute-start.3) | collective-permute-done | bytes 147488 | tf_op jit(solution)/shard_map/ppermute | solution.py:474
  34.1 4.5 %collective-permute-done.5.refs_2_ = f32[2,72,128]{2,1,0:T(8,128)S(1)} collective-permute-done((f32[2,72,128]{2,1,0:T(8,128)S(1)}, f32[2,72,128]{2,1,0:T(8,128)S(1)}, u32[]{:S(2)}, u32[]{:S(2)}) %collective-permute-start.5) | collective-permute-done | bytes 73760 | tf_op jit(solution)/shard_map/ppermute | solution.py:474
  38.6 2.8 %collective-permute-start.10 = (f32[1,144,128]{2,1,0:T(8,128)S(1)}, f32[1,144,128]{2,1,0:T(8,128)S(1)}, u32[]{:S(2)}, u32[]{:S(2)}) collective-permute-start(f32[1,144,128]{2,1,0:T(8,128)S(1)} %get-tuple-element.81), channel_id=1, source_target_pairs={{0,8},{1,9},{2,10},{3,11},{4,12},{5,13},{6,14},{7,15},{8,0},{9,1},... | collective-permute-start | bytes 221192 | tf_op jit(solution)/shard_map/ppermute | solution.py:474
  41.7 2.2 %collective-permute-done.10.refs_2_ = f32[1,144,128]{2,1,0:T(8,128)S(1)} collective-permute-done((f32[1,144,128]{2,1,0:T(8,128)S(1)}, f32[1,144,128]{2,1,0:T(8,128)S(1)}, u32[]{:S(2)}, u32[]{:S(2)}) %collective-permute-start.10) | collective-permute-done | bytes 73760 | tf_op jit(solution)/shard_map/ppermute | solution.py:474
  43.9 1.0 %shard_map.65 = (f32[320,128]{1,0:T(8,128)}, f32[640,128]{1,0:T(8,128)}) custom-call(f32[1,72,128]{2,1,0:T(8,128)S(1)} %get-tuple-element.79.refs_0_, f32[1,72,128]{2,1,0:T(8,128)S(1)} %get-tuple-element.80.refs_1_, f32[1,144,128]{2,1,0:T(8,128)S(1)} %collective-permute-done.10.refs_2_, f32[320,128]{1,0:T(8,128)S(1)} %get-tuple-element.85.refs_3_, ...), custom_call_target="tpu_custom_call" | custom-call | tf_op jit(solution)/shard_map/pallas_call | solution.py:450
  (32 shorter events, 2.5 us)
Async XLA Ops:
  0.6 4.7 %copy-start = (bf16[128,5120]{1,0:T(8,128)(2,1)S(1)}, bf16[128,5120]{1,0:T(8,128)(2,1)}, u32[]{:S(2)}) copy-start(bf16[128,5120]{1,0:T(8,128)(2,1)} %refs_2_.11) | copy-start | bytes 3932164
  0.6 4.7 %copy-start.1 = (bf16[128,5120]{1,0:T(8,128)(2,1)S(1)}, bf16[128,5120]{1,0:T(8,128)(2,1)}, u32[]{:S(2)}) copy-start(bf16[128,5120]{1,0:T(8,128)(2,1)} %refs_3_.11) | copy-start | bytes 3932164
  2.3 15.6 %collective-permute-start = (f32[4,128,128]{2,1,0:T(8,128)S(1)}, f32[4,128,128]{2,1,0:T(8,128)S(1)}, u32[]{:S(2)}, u32[]{:S(2)}) collective-permute-start(f32[4,128,128]{2,1,0:T(8,128)S(1)} %get-tuple-element.63), channel_id=1, source_target_pairs={{0,2},{1,3},{2,0},{3,1},{4,6},{5,7},{6,4},{7,5},{8,10},{9,11},{10,... | collective-permute-start | bytes 786440 | tf_op jit(solution)/shard_map/ppermute | solution.py:474
  5.8 12.2 %collective-permute-start.1 = (f32[4,112,128]{2,1,0:T(8,128)S(1)}, f32[4,112,128]{2,1,0:T(8,128)S(1)}, u32[]{:S(2)}, u32[]{:S(2)}) collective-permute-start(f32[4,112,128]{2,1,0:T(8,128)S(1)} %get-tuple-element.64), channel_id=1, source_target_pairs={{0,4},{1,5},{2,6},{3,7},{4,0},{5,1},{6,2},{7,3},{8,12},{9,13},{10,... | collective-permute-start | bytes 688136 | tf_op jit(solution)/shard_map/ppermute | solution.py:474
  8.0 6.5 %collective-permute-start.12 = (f32[4,64,128]{2,1,0:T(8,128)S(1)}, f32[4,64,128]{2,1,0:T(8,128)S(1)}, u32[]{:S(2)}, u32[]{:S(2)}) collective-permute-start(f32[4,64,128]{2,1,0:T(8,128)S(1)} %get-tuple-element.89), channel_id=1, source_target_pairs={{0,2},{1,3},{2,0},{3,1},{4,6},{5,7},{6,4},{7,5},{8,10},{9,11},{10,... | collective-permute-start | bytes 393224 | tf_op jit(solution)/shard_map/ppermute | solution.py:474
  8.6 7.2 %collective-permute-start.13 = (f32[4,64,128]{2,1,0:T(8,128)S(1)}, f32[4,64,128]{2,1,0:T(8,128)S(1)}, u32[]{:S(2)}, u32[]{:S(2)}) collective-permute-start(f32[4,64,128]{2,1,0:T(8,128)S(1)} %get-tuple-element.90), channel_id=1, source_target_pairs={{0,4},{1,5},{2,6},{3,7},{4,0},{5,1},{6,2},{7,3},{8,12},{9,13},{10,... | collective-permute-start | bytes 393224 | tf_op jit(solution)/shard_map/ppermute | solution.py:474
  10.9 9.1 %collective-permute-start.4 = (f32[2,128]{1,0:T(2,128)S(1)}, f32[2,128]{1,0:T(2,128)S(1)}, u32[]{:S(2)}, u32[]{:S(2)}) collective-permute-start(f32[2,128]{1,0:T(2,128)S(1)} %slice_bitcast_fusion), channel_id=1, source_target_pairs={{0,1},{1,0},{2,3},{3,2},{4,5},{5,4},{6,7},{7,6},{8,9},{9,8},{10,11... | collective-permute-start | bytes 3080 | tf_op jit(solution)/shard_map/ppermute | solution.py:474
  15.8 5.8 %collective-permute-start.14 = (f32[2,64,128]{2,1,0:T(8,128)S(1)}, f32[2,64,128]{2,1,0:T(8,128)S(1)}, u32[]{:S(2)}, u32[]{:S(2)}) collective-permute-start(f32[2,64,128]{2,1,0:T(8,128)S(1)} %get-tuple-element.93), channel_id=1, source_target_pairs={{0,4},{1,5},{2,6},{3,7},{4,0},{5,1},{6,2},{7,3},{8,12},{9,13},{10,... | collective-permute-start | bytes 196616 | tf_op jit(solution)/shard_map/ppermute | solution.py:474
  17.4 4.3 %collective-permute-start.15 = (f32[2,64,128]{2,1,0:T(8,128)S(1)}, f32[2,64,128]{2,1,0:T(8,128)S(1)}, u32[]{:S(2)}, u32[]{:S(2)}) collective-permute-start(f32[2,64,128]{2,1,0:T(8,128)S(1)} %get-tuple-element.94), channel_id=1, source_target_pairs={{0,2},{1,3},{2,0},{3,1},{4,6},{5,7},{6,4},{7,5},{8,10},{9,11},{10,... | collective-permute-start | bytes 196616 | tf_op jit(solution)/shard_map/ppermute | solution.py:474
  18.0 8.2 %collective-permute-start.7 = (f32[2,128,128]{2,1,0:T(8,128)S(1)}, f32[2,128,128]{2,1,0:T(8,128)S(1)}, u32[]{:S(2)}, u32[]{:S(2)}) collective-permute-start(f32[2,128,128]{2,1,0:T(8,128)S(1)} %get-tuple-element.76), channel_id=1, source_target_pairs={{0,4},{1,5},{2,6},{3,7},{4,0},{5,1},{6,2},{7,3},{8,12},{9,13},{10,... | collective-permute-start | bytes 393224 | tf_op jit(solution)/shard_map/ppermute | solution.py:474
  18.5 7.7 %collective-permute-start.8 = (f32[2,112,128]{2,1,0:T(8,128)S(1)}, f32[2,112,128]{2,1,0:T(8,128)S(1)}, u32[]{:S(2)}, u32[]{:S(2)}) collective-permute-start(f32[2,112,128]{2,1,0:T(8,128)S(1)} %get-tuple-element.77), channel_id=1, source_target_pairs={{0,2},{1,3},{2,0},{3,1},{4,6},{5,7},{6,4},{7,5},{8,10},{9,11},{10,... | collective-permute-start | bytes 344072 | tf_op jit(solution)/shard_map/ppermute | solution.py:474
  20.0 5.7 %collective-permute-start.9 = (f32[2,128]{1,0:T(2,128)S(1)}, f32[2,128]{1,0:T(2,128)S(1)}, u32[]{:S(2)}, u32[]{:S(2)}) collective-permute-start(f32[2,128]{1,0:T(2,128)S(1)} %fusion.refs_4_), channel_id=1, source_target_pairs={{0,6},{1,7},{2,4},{3,5},{4,2},{5,3},{6,0},{7,1},{8,14},{9,15},{10,... | collective-permute-start | bytes 3080 | tf_op jit(solution)/shard_map/ppermute | solution.py:474
  21.7 12.2 %collective-permute-start.16 = (f32[1,128,128]{2,1,0:T(8,128)S(1)}, f32[1,128,128]{2,1,0:T(8,128)S(1)}, u32[]{:S(2)}, u32[]{:S(2)}) collective-permute-start(f32[1,128,128]{2,1,0:T(8,128)S(1)} %get-tuple-element.97), channel_id=1, source_target_pairs={{0,8},{1,9},{2,10},{3,11},{4,12},{5,13},{6,14},{7,15},{8,0},{9,1},... | collective-permute-start | bytes 196616 | tf_op jit(solution)/shard_map/ppermute | solution.py:474
  24.4 5.1 %collective-permute-start.2 = (f32[4,72,128]{2,1,0:T(8,128)S(1)}, f32[4,72,128]{2,1,0:T(8,128)S(1)}, u32[]{:S(2)}, u32[]{:S(2)}) collective-permute-start(f32[4,72,128]{2,1,0:T(8,128)S(1)} %get-tuple-element.67), channel_id=1, source_target_pairs={{0,2},{1,3},{2,0},{3,1},{4,6},{5,7},{6,4},{7,5},{8,10},{9,11},{10,... | collective-permute-start | bytes 442376 | tf_op jit(solution)/shard_map/ppermute | solution.py:474
  25.7 8.0 %collective-permute-start.3 = (f32[4,72,128]{2,1,0:T(8,128)S(1)}, f32[4,72,128]{2,1,0:T(8,128)S(1)}, u32[]{:S(2)}, u32[]{:S(2)}) collective-permute-start(f32[4,72,128]{2,1,0:T(8,128)S(1)} %get-tuple-element.68), channel_id=1, source_target_pairs={{0,4},{1,5},{2,6},{3,7},{4,0},{5,1},{6,2},{7,3},{8,12},{9,13},{10,... | collective-permute-start | bytes 442376 | tf_op jit(solution)/shard_map/ppermute | solution.py:474
  26.2 15.2 %collective-permute-start.11 = (f32[1,240,128]{2,1,0:T(8,128)S(1)}, f32[1,240,128]{2,1,0:T(8,128)S(1)}, u32[]{:S(2)}, u32[]{:S(2)}) collective-permute-start(f32[1,240,128]{2,1,0:T(8,128)S(1)} %get-tuple-element.84), channel_id=1, source_target_pairs={{0,8},{1,9},{2,10},{3,11},{4,12},{5,13},{6,14},{7,15},{8,0},{9,1},... | collective-permute-start | bytes 368648 | tf_op jit(solution)/shard_map/ppermute | solution.py:474
  33.7 4.9 %collective-permute-start.5 = (f32[2,72,128]{2,1,0:T(8,128)S(1)}, f32[2,72,128]{2,1,0:T(8,128)S(1)}, u32[]{:S(2)}, u32[]{:S(2)}) collective-permute-start(f32[2,72,128]{2,1,0:T(8,128)S(1)} %get-tuple-element.72), channel_id=1, source_target_pairs={{0,4},{1,5},{2,6},{3,7},{4,0},{5,1},{6,2},{7,3},{8,12},{9,13},{10,... | collective-permute-start | bytes 221192 | tf_op jit(solution)/shard_map/ppermute | solution.py:474
  33.8 4.8 %collective-permute-start.6 = (f32[2,72,128]{2,1,0:T(8,128)S(1)}, f32[2,72,128]{2,1,0:T(8,128)S(1)}, u32[]{:S(2)}, u32[]{:S(2)}) collective-permute-start(f32[2,72,128]{2,1,0:T(8,128)S(1)} %get-tuple-element.73), channel_id=1, source_target_pairs={{0,2},{1,3},{2,0},{3,1},{4,6},{5,7},{6,4},{7,5},{8,10},{9,11},{10,... | collective-permute-start | bytes 221192 | tf_op jit(solution)/shard_map/ppermute | solution.py:474
  38.6 5.3 %collective-permute-start.10 = (f32[1,144,128]{2,1,0:T(8,128)S(1)}, f32[1,144,128]{2,1,0:T(8,128)S(1)}, u32[]{:S(2)}, u32[]{:S(2)}) collective-permute-start(f32[1,144,128]{2,1,0:T(8,128)S(1)} %get-tuple-element.81), channel_id=1, source_target_pairs={{0,8},{1,9},{2,10},{3,11},{4,12},{5,13},{6,14},{7,15},{8,0},{9,1},... | collective-permute-start | bytes 221192 | tf_op jit(solution)/shard_map/ppermute | solution.py:474

commit v22 on v19

--- a/solution.py
+++ b/solution.py
@@ -62,7 +62,7 @@
 KINDS = (((NEAR, X, FAR), (NEAR, X, FAR)), ((X, NEAR, FAR), (X, NEAR, FAR)))
 NOTES = len(KINDS) * SLOTS
 
-WEIGHTS = {((0, 2), 2): 2 * 10**9}
+WEIGHTS = {((0, 1), 2): 2 * 10**9}
 
 
 def split_rows(count):
@@ -482,13 +482,13 @@
     some = 1 + (full_g - 1) // 2
     pieces = (
         (tuple(range(full_a)), 0, (), 0),
-        ((), 0, tuple(range(1, some)), 0),
         ((), half_a, (0,), 1),
-        ((), 0, tuple(range(some, full_g)), 1),
+        ((), 0, tuple(range(1, some)), 1),
+        ((), 0, tuple(range(some, full_g)), 0),
     )
     arrays = (saved_input, saved_pre, grad_act)
     keep, send = 0, SLOTS // 2
-    early, late = (0, 2), (1, 3)
+    early, late = (0, 1), (2, 3)
     keeps, gots, notes = {}, {}, None
 
     def pack_next(first, ks):

time: 36.7 us -> 36.5 us (level)
  starting transfers between devices: 17 us -> 15.6 us
  waiting for transfers between devices: 13.1 us -> 14.3 us
    ppermute x12, starting transfers between devices: 17 us -> 15.6 us  [swap(): return lax.ppermute(value, ('dp', 'tensor'), pairs)]
    ppermute x12, waiting for transfers between devices: 13.1 us -> 14.3 us  [swap(): return lax.ppermute(value, ('dp', 'tensor'), pairs)]
  transfers between devices with their start and end apart: 12 -> 12, of which waited for: 7 -> 6; matrix products, arithmetic and copies ran while one was open for 0% -> 0% of each run, Pallas kernels for 8% -> 8%
where the time goes in v22:
time: 36.5 us; the launch traced here: 36.4 us
  starting transfers between devices  15.6 us (43%)
  waiting for transfers between devices  14.3 us (39%)
  Pallas kernels  5.76 us (16%)
  between operations  0.73 us (2%)
    ppermute x12, starting transfers between devices, swap(): return lax.ppermute(value, ('dp', 'tensor'), pairs)  15.6 us
    ppermute x12, waiting for transfers between devices, swap(): return lax.ppermute(value, ('dp', 'tensor'), pairs)  14.3 us
    pallas_call x5, Pallas kernels, pack(): pl.pallas_call(functools.partial(pack_body, pieces, items, count_a, count...  4.25 us
    pallas_call x1, Pallas kernels, finish(): pl.pallas_call(functools.partial(finish_body, pieces, early, late, count_...  1.03 us
  transfers between devices with their start and end apart: 12, of which 6 were waited for; matrix products, arithmetic and copies ran while one was open for 0% of the time, Pallas kernels for 8%

profile of v22, /device:TPU:0, one launch (start us, length us, event | category | flops | bytes accessed | tf_op | source)
XLA Modules:
  0.0 36.4 jit_solution(9728233070194521356)
XLA Ops:
  0.6 1.7 %shard_map.50 = (f32[4,128,128]{2,1,0:T(8,128)S(1)}, f32[17,8,128]{2,1,0:T(8,128)S(1)}, bf16[128,2560]{1,0:T(8,128)(2,1)S(1)}) custom-call(bf16[128,2560]{1,0:T(8,128)(2,1)} %refs_0_.1), custom_call_target="tpu_custom_call" | custom-call | flops 4000000000 | bytes 1 | tf_op jit(solution)/shard_map/pallas_call | solution.py:235
  2.3 3.1 %collective-permute-start.5 = (f32[4,128,128]{2,1,0:T(8,128)S(1)}, f32[4,128,128]{2,1,0:T(8,128)S(1)}, u32[]{:S(2)}, u32[]{:S(2)}) collective-permute-start(f32[4,128,128]{2,1,0:T(8,128)S(1)} %get-tuple-element.51), channel_id=1, source_target_pairs={{0,4},{1,5},{2,6},{3,7},{4,0},{5,1},{6,2},{7,3},{8,12},{9,13},{10,... | collective-permute-start | bytes 786440 | tf_op jit(solution)/shard_map/ppermute | solution.py:468
  5.4 0.4 %shard_map.51 = (f32[4,112,128]{2,1,0:T(8,128)S(1)}, f32[17,8,128]{2,1,0:T(8,128)S(1)}) custom-call(f32[17,8,128]{2,1,0:T(8,128)S(1)} %get-tuple-element.35.refs_0_, bf16[128,2560]{1,0:T(8,128)(2,1)S(1)} %get-tuple-element.36.refs_1_, bf16[128,5120]{1,0:T(8,128)(2,1)S(1)} %copy-done, bf16[128,5120]{1,0:T(8,128)(2,1)S(1)} %copy-done.1), custom_call_target="tpu_custom_call" | custom-call | flops 1 | bytes 1 | tf_op jit(solution)/shard_map/pallas_call | solution.py:235
  5.9 1.6 %collective-permute-start.6 = (f32[4,112,128]{2,1,0:T(8,128)S(1)}, f32[4,112,128]{2,1,0:T(8,128)S(1)}, u32[]{:S(2)}, u32[]{:S(2)}) collective-permute-start(f32[4,112,128]{2,1,0:T(8,128)S(1)} %get-tuple-element.52), channel_id=1, source_target_pairs={{0,2},{1,3},{2,0},{3,1},{4,6},{5,7},{6,4},{7,5},{8,10},{9,11},{10,... | collective-permute-start | bytes 688136 | tf_op jit(solution)/shard_map/ppermute | solution.py:468
  7.4 0.8 %shard_map.52 = (f32[4,136,128]{2,1,0:T(8,128)S(1)}, f32[4,136,128]{2,1,0:T(8,128)S(1)}, f32[17,8,128]{2,1,0:T(8,128)S(1)}) custom-call(f32[17,8,128]{2,1,0:T(8,128)S(1)} %get-tuple-element.37.refs_0_, bf16[128,2560]{1,0:T(8,128)(2,1)S(1)} %get-tuple-element.36.refs_1_, bf16[128,5120]{1,0:T(8,128)(2,1)S(1)} %copy-done, bf16[128,5120]{1,0:T(8,128)(2,1)S(1)} %copy-done.1), custom_call_target="tpu_custom_call" | custom-call | flops 1 | bytes 1 | tf_op jit(solution)/shard_map/pallas_call | solution.py:235
  8.2 0.6 %collective-permute-start = (f32[4,136,128]{2,1,0:T(8,128)S(1)}, f32[4,136,128]{2,1,0:T(8,128)S(1)}, u32[]{:S(2)}, u32[]{:S(2)}) collective-permute-start(f32[4,136,128]{2,1,0:T(8,128)S(1)} %get-tuple-element.42), channel_id=1, source_target_pairs={{0,2},{1,3},{2,0},{3,1},{4,6},{5,7},{6,4},{7,5},{8,10},{9,11},{10,... | collective-permute-start | bytes 835592 | tf_op jit(solution)/shard_map/ppermute | solution.py:468
  8.8 0.2 collective-permute-start.1
  9.1 0.5 %shard_map.53 = (f32[4,128,128]{2,1,0:T(8,128)S(1)}, f32[4,112,128]{2,1,0:T(8,128)S(1)}, f32[17,8,128]{2,1,0:T(8,128)S(1)}) custom-call(f32[17,8,128]{2,1,0:T(8,128)S(1)} %get-tuple-element.38.refs_0_, bf16[128,2560]{1,0:T(8,128)(2,1)S(1)} %get-tuple-element.36.refs_1_, bf16[128,5120]{1,0:T(8,128)(2,1)S(1)} %copy-done, bf16[128,5120]{1,0:T(8,128)(2,1)S(1)} %copy-done.1), custom_call_target="tpu_custom_call" | custom-call | flops 1 | bytes 1 | tf_op jit(solution)/shard_map/pallas_call | solution.py:235
  9.6 0.8 %shard_map.54 = (f32[4,136,128]{2,1,0:T(8,128)S(1)}, f32[4,136,128]{2,1,0:T(8,128)S(1)}, f32[17,8,128]{2,1,0:T(8,128)S(1)}) custom-call(f32[17,8,128]{2,1,0:T(8,128)S(1)} %get-tuple-element.39.refs_0_, bf16[128,2560]{1,0:T(8,128)(2,1)S(1)} %get-tuple-element.36.refs_1_, bf16[128,5120]{1,0:T(8,128)(2,1)S(1)} %copy-done, bf16[128,5120]{1,0:T(8,128)(2,1)S(1)} %copy-done.1), custom_call_target="tpu_custom_call" | custom-call | flops 1 | bytes 1 | tf_op jit(solution)/shard_map/pallas_call | solution.py:235
  10.5 4.0 %collective-permute-done.6.refs_3_ = f32[4,112,128]{2,1,0:T(8,128)S(1)} collective-permute-done((f32[4,112,128]{2,1,0:T(8,128)S(1)}, f32[4,112,128]{2,1,0:T(8,128)S(1)}, u32[]{:S(2)}, u32[]{:S(2)}) %collective-permute-start.6) | collective-permute-done | bytes 229408 | tf_op jit(solution)/shard_map/ppermute | solution.py:468
  14.6 0.3 collective-permute-start.8
  14.8 1.7 %collective-permute-start.7 = (f32[2,128,128]{2,1,0:T(8,128)S(1)}, f32[2,128,128]{2,1,0:T(8,128)S(1)}, u32[]{:S(2)}, u32[]{:S(2)}) collective-permute-start(f32[2,128,128]{2,1,0:T(8,128)S(1)} %get-tuple-element.55), channel_id=1, source_target_pairs={{0,2},{1,3},{2,0},{3,1},{4,6},{5,7},{6,4},{7,5},{8,10},{9,11},{10,... | collective-permute-start | bytes 393224 | tf_op jit(solution)/shard_map/ppermute | solution.py:468
  16.6 1.6 %collective-permute-start.9 = (f32[2,128]{1,0:T(2,128)S(1)}, f32[2,128]{1,0:T(2,128)S(1)}, u32[]{:S(2)}, u32[]{:S(2)}) collective-permute-start(f32[2,128]{1,0:T(2,128)S(1)} %fusion.refs_4_), channel_id=1, source_target_pairs={{0,6},{1,7},{2,4},{3,5},{4,2},{5,3},{6,0},{7,1},{8,14},{9,15},{10,... | collective-permute-start | bytes 3080 | tf_op jit(solution)/shard_map/ppermute | solution.py:468
  18.1 2.3 %collective-permute-done.refs_2_ = f32[4,136,128]{2,1,0:T(8,128)S(1)} collective-permute-done((f32[4,136,128]{2,1,0:T(8,128)S(1)}, f32[4,136,128]{2,1,0:T(8,128)S(1)}, u32[]{:S(2)}, u32[]{:S(2)}) %collective-permute-start) | collective-permute-done | bytes 278560 | tf_op jit(solution)/shard_map/ppermute | solution.py:468
  20.5 0.3 collective-permute-start.3
  20.8 1.7 %collective-permute-start.4 = (f32[2,136,128]{2,1,0:T(8,128)S(1)}, f32[2,136,128]{2,1,0:T(8,128)S(1)}, u32[]{:S(2)}, u32[]{:S(2)}) collective-permute-start(f32[2,136,128]{2,1,0:T(8,128)S(1)} %get-tuple-element.48), channel_id=1, source_target_pairs={{0,2},{1,3},{2,0},{3,1},{4,6},{5,7},{6,4},{7,5},{8,10},{9,11},{10,... | collective-permute-start | bytes 417800 | tf_op jit(solution)/shard_map/ppermute | solution.py:468
  22.5 0.1 collective-permute-done.7.refs_2_
  22.7 2.7 %collective-permute-start.11 = (f32[1,240,128]{2,1,0:T(8,128)S(1)}, f32[1,240,128]{2,1,0:T(8,128)S(1)}, u32[]{:S(2)}, u32[]{:S(2)}) collective-permute-start(f32[1,240,128]{2,1,0:T(8,128)S(1)} %get-tuple-element.63), channel_id=1, source_target_pairs={{0,8},{1,9},{2,10},{3,11},{4,12},{5,13},{6,14},{7,15},{8,0},{9,1},... | collective-permute-start | bytes 368648 | tf_op jit(solution)/shard_map/ppermute | solution.py:468
  25.4 1.8 %collective-permute-done.3.refs_2_ = f32[2,136,128]{2,1,0:T(8,128)S(1)} collective-permute-done((f32[2,136,128]{2,1,0:T(8,128)S(1)}, f32[2,136,128]{2,1,0:T(8,128)S(1)}, u32[]{:S(2)}, u32[]{:S(2)}) %collective-permute-start.3) | collective-permute-done | bytes 139296 | tf_op jit(solution)/shard_map/ppermute | solution.py:468
  27.2 1.7 %collective-permute-start.10 = (f32[1,272,128]{2,1,0:T(8,128)S(1)}, f32[1,272,128]{2,1,0:T(8,128)S(1)}, u32[]{:S(2)}, u32[]{:S(2)}) collective-permute-start(f32[1,272,128]{2,1,0:T(8,128)S(1)} %get-tuple-element.60), channel_id=1, source_target_pairs={{0,8},{1,9},{2,10},{3,11},{4,12},{5,13},{6,14},{7,15},{8,0},{9,1},... | collective-permute-start | bytes 417800 | tf_op jit(solution)/shard_map/ppermute | solution.py:468
  28.9 4.9 %collective-permute-done.11.refs_2_ = f32[1,240,128]{2,1,0:T(8,128)S(1)} collective-permute-done((f32[1,240,128]{2,1,0:T(8,128)S(1)}, f32[1,240,128]{2,1,0:T(8,128)S(1)}, u32[]{:S(2)}, u32[]{:S(2)}) %collective-permute-start.11) | collective-permute-done | bytes 122912 | tf_op jit(solution)/shard_map/ppermute | solution.py:468
  33.8 0.3 shard_map.59
  34.1 1.2 %collective-permute-done.10.refs_2_ = f32[1,272,128]{2,1,0:T(8,128)S(1)} collective-permute-done((f32[1,272,128]{2,1,0:T(8,128)S(1)}, f32[1,272,128]{2,1,0:T(8,128)S(1)}, u32[]{:S(2)}, u32[]{:S(2)}) %collective-permute-start.10) | collective-permute-done | bytes 139296 | tf_op jit(solution)/shard_map/ppermute | solution.py:468
  35.3 1.0 %shard_map.60 = (f32[320,128]{1,0:T(8,128)}, f32[640,128]{1,0:T(8,128)}) custom-call(f32[1,136,128]{2,1,0:T(8,128)S(1)} %get-tuple-element.58.refs_0_, f32[1,136,128]{2,1,0:T(8,128)S(1)} %get-tuple-element.59.refs_1_, f32[1,272,128]{2,1,0:T(8,128)S(1)} %collective-permute-done.10.refs_2_, f32[320,128]{1,0:T(8,128)S(1)} %get-tuple-element.64.refs_3_, ...), custom_call_target="tpu_custom_call" | custom-call | tf_op jit(solution)/shard_map/pallas_call | solution.py:444
  (17 shorter events, 0.3 us)
Async XLA Ops:
  0.6 4.8 %copy-start.1 = (bf16[128,5120]{1,0:T(8,128)(2,1)S(1)}, bf16[128,5120]{1,0:T(8,128)(2,1)}, u32[]{:S(2)}) copy-start(bf16[128,5120]{1,0:T(8,128)(2,1)} %refs_3_.7) | copy-start | bytes 3932164
  0.6 4.8 %copy-start = (bf16[128,5120]{1,0:T(8,128)(2,1)S(1)}, bf16[128,5120]{1,0:T(8,128)(2,1)}, u32[]{:S(2)}) copy-start(bf16[128,5120]{1,0:T(8,128)(2,1)} %refs_2_.7) | copy-start | bytes 3932164
  2.3 12.1 %collective-permute-start.5 = (f32[4,128,128]{2,1,0:T(8,128)S(1)}, f32[4,128,128]{2,1,0:T(8,128)S(1)}, u32[]{:S(2)}, u32[]{:S(2)}) collective-permute-start(f32[4,128,128]{2,1,0:T(8,128)S(1)} %get-tuple-element.51), channel_id=1, source_target_pairs={{0,4},{1,5},{2,6},{3,7},{4,0},{5,1},{6,2},{7,3},{8,12},{9,13},{10,... | collective-permute-start | bytes 786440 | tf_op jit(solution)/shard_map/ppermute | solution.py:468
  5.9 8.6 %collective-permute-start.6 = (f32[4,112,128]{2,1,0:T(8,128)S(1)}, f32[4,112,128]{2,1,0:T(8,128)S(1)}, u32[]{:S(2)}, u32[]{:S(2)}) collective-permute-start(f32[4,112,128]{2,1,0:T(8,128)S(1)} %get-tuple-element.52), channel_id=1, source_target_pairs={{0,2},{1,3},{2,0},{3,1},{4,6},{5,7},{6,4},{7,5},{8,10},{9,11},{10,... | collective-permute-start | bytes 688136 | tf_op jit(solution)/shard_map/ppermute | solution.py:468
  8.2 12.2 %collective-permute-start = (f32[4,136,128]{2,1,0:T(8,128)S(1)}, f32[4,136,128]{2,1,0:T(8,128)S(1)}, u32[]{:S(2)}, u32[]{:S(2)}) collective-permute-start(f32[4,136,128]{2,1,0:T(8,128)S(1)} %get-tuple-element.42), channel_id=1, source_target_pairs={{0,2},{1,3},{2,0},{3,1},{4,6},{5,7},{6,4},{7,5},{8,10},{9,11},{10,... | collective-permute-start | bytes 835592 | tf_op jit(solution)/shard_map/ppermute | solution.py:468
  8.8 11.6 %collective-permute-start.1 = (f32[4,136,128]{2,1,0:T(8,128)S(1)}, f32[4,136,128]{2,1,0:T(8,128)S(1)}, u32[]{:S(2)}, u32[]{:S(2)}) collective-permute-start(f32[4,136,128]{2,1,0:T(8,128)S(1)} %get-tuple-element.43), channel_id=1, source_target_pairs={{0,4},{1,5},{2,6},{3,7},{4,0},{5,1},{6,2},{7,3},{8,12},{9,13},{10,... | collective-permute-start | bytes 835592 | tf_op jit(solution)/shard_map/ppermute | solution.py:468
  10.4 6.1 %collective-permute-start.2 = (f32[2,128]{1,0:T(2,128)S(1)}, f32[2,128]{1,0:T(2,128)S(1)}, u32[]{:S(2)}, u32[]{:S(2)}) collective-permute-start(f32[2,128]{1,0:T(2,128)S(1)} %slice_bitcast_fusion), channel_id=1, source_target_pairs={{0,1},{1,0},{2,3},{3,2},{4,5},{5,4},{6,7},{7,6},{8,9},{9,8},{10,11... | collective-permute-start | bytes 3080 | tf_op jit(solution)/shard_map/ppermute | solution.py:468
  14.6 8.0 %collective-permute-start.8 = (f32[2,112,128]{2,1,0:T(8,128)S(1)}, f32[2,112,128]{2,1,0:T(8,128)S(1)}, u32[]{:S(2)}, u32[]{:S(2)}) collective-permute-start(f32[2,112,128]{2,1,0:T(8,128)S(1)} %get-tuple-element.56), channel_id=1, source_target_pairs={{0,4},{1,5},{2,6},{3,7},{4,0},{5,1},{6,2},{7,3},{8,12},{9,13},{10,... | collective-permute-start | bytes 344072 | tf_op jit(solution)/shard_map/ppermute | solution.py:468
  14.8 7.8 %collective-permute-start.7 = (f32[2,128,128]{2,1,0:T(8,128)S(1)}, f32[2,128,128]{2,1,0:T(8,128)S(1)}, u32[]{:S(2)}, u32[]{:S(2)}) collective-permute-start(f32[2,128,128]{2,1,0:T(8,128)S(1)} %get-tuple-element.55), channel_id=1, source_target_pairs={{0,2},{1,3},{2,0},{3,1},{4,6},{5,7},{6,4},{7,5},{8,10},{9,11},{10,... | collective-permute-start | bytes 393224 | tf_op jit(solution)/shard_map/ppermute | solution.py:468
  16.6 6.0 %collective-permute-start.9 = (f32[2,128]{1,0:T(2,128)S(1)}, f32[2,128]{1,0:T(2,128)S(1)}, u32[]{:S(2)}, u32[]{:S(2)}) collective-permute-start(f32[2,128]{1,0:T(2,128)S(1)} %fusion.refs_4_), channel_id=1, source_target_pairs={{0,6},{1,7},{2,4},{3,5},{4,2},{5,3},{6,0},{7,1},{8,14},{9,15},{10,... | collective-permute-start | bytes 3080 | tf_op jit(solution)/shard_map/ppermute | solution.py:468
  20.5 6.7 %collective-permute-start.3 = (f32[2,136,128]{2,1,0:T(8,128)S(1)}, f32[2,136,128]{2,1,0:T(8,128)S(1)}, u32[]{:S(2)}, u32[]{:S(2)}) collective-permute-start(f32[2,136,128]{2,1,0:T(8,128)S(1)} %get-tuple-element.47), channel_id=1, source_target_pairs={{0,4},{1,5},{2,6},{3,7},{4,0},{5,1},{6,2},{7,3},{8,12},{9,13},{10,... | collective-permute-start | bytes 417800 | tf_op jit(solution)/shard_map/ppermute | solution.py:468
  20.8 6.4 %collective-permute-start.4 = (f32[2,136,128]{2,1,0:T(8,128)S(1)}, f32[2,136,128]{2,1,0:T(8,128)S(1)}, u32[]{:S(2)}, u32[]{:S(2)}) collective-permute-start(f32[2,136,128]{2,1,0:T(8,128)S(1)} %get-tuple-element.48), channel_id=1, source_target_pairs={{0,2},{1,3},{2,0},{3,1},{4,6},{5,7},{6,4},{7,5},{8,10},{9,11},{10,... | collective-permute-start | bytes 417800 | tf_op jit(solution)/shard_map/ppermute | solution.py:468
  22.7 11.2 %collective-permute-start.11 = (f32[1,240,128]{2,1,0:T(8,128)S(1)}, f32[1,240,128]{2,1,0:T(8,128)S(1)}, u32[]{:S(2)}, u32[]{:S(2)}) collective-permute-start(f32[1,240,128]{2,1,0:T(8,128)S(1)} %get-tuple-element.63), channel_id=1, source_target_pairs={{0,8},{1,9},{2,10},{3,11},{4,12},{5,13},{6,14},{7,15},{8,0},{9,1},... | collective-permute-start | bytes 368648 | tf_op jit(solution)/shard_map/ppermute | solution.py:468
  27.2 8.1 %collective-permute-start.10 = (f32[1,272,128]{2,1,0:T(8,128)S(1)}, f32[1,272,128]{2,1,0:T(8,128)S(1)}, u32[]{:S(2)}, u32[]{:S(2)}) collective-permute-start(f32[1,272,128]{2,1,0:T(8,128)S(1)} %get-tuple-element.60), channel_id=1, source_target_pairs={{0,8},{1,9},{2,10},{3,11},{4,12},{5,13},{6,14},{7,15},{8,0},{9,1},... | collective-permute-start | bytes 417800 | tf_op jit(solution)/shard_map/ppermute | solution.py:468

commit v23 on v20

--- a/solution.py
+++ b/solution.py
@@ -59,10 +59,10 @@
 EDGE = 8
 SLOTS = 8
 X, NEAR, FAR = 0, 1, 2
-KINDS = (((X, NEAR, FAR), (X, NEAR, FAR)), ((NEAR, X, FAR), (NEAR, X, FAR)))
+KINDS = (((NEAR, X, FAR), (NEAR, X, FAR)), ((X, NEAR, FAR), (X, NEAR, FAR)))
 NOTES = len(KINDS) * SLOTS
 
-WEIGHTS = {((0, 2), 2): 2 * 10**9}
+WEIGHTS = {((0, 1), 2): 2 * 10**9}
 
 
 def split_rows(count):
@@ -464,13 +464,13 @@
     some = 1 + (full_g - 1) // 2
     pieces = (
         (tuple(range(full_a)), 0, (), 0),
-        ((), 0, tuple(range(1, some)), 0),
         ((), half_a, (0,), 1),
-        ((), 0, tuple(range(some, full_g)), 1),
+        ((), 0, tuple(range(1, some)), 1),
+        ((), 0, tuple(range(some, full_g)), 0),
     )
     arrays = (saved_input, saved_pre, grad_act)
     keep, send = 0, SLOTS // 2
-    early, late = (0, 2), (1, 3)
+    early, late = (0, 1), (2, 3)
     keeps, gots, notes = {}, {}, None
 
     def pack_next(first, ks):

time: 37.2 us -> 36.4 us (0.978)
  starting transfers between devices: 17.7 us -> 16.5 us
    ppermute x12, starting transfers between devices: 17.7 us -> 16.5 us  [swap(): return lax.ppermute(value, ('dp', 'tensor'), pairs)]
  transfers between devices with their start and end apart: 12 -> 12, of which waited for: 8 -> 5; matrix products, arithmetic and copies ran while one was open for 0% -> 0% of each run, Pallas kernels for 8% -> 8%
where the time goes in v23:
time: 36.4 us; the launch traced here: 36.2 us
  starting transfers between devices  16.5 us (45%)
  waiting for transfers between devices  13.3 us (37%)
  Pallas kernels  4.4 us (12%)
  local copies, waits for them, and re-layouts  1.19 us (3%)
  between operations  0.74 us (2%)
    ppermute x12, starting transfers between devices, swap(): return lax.ppermute(value, ('dp', 'tensor'), pairs)  16.5 us
    ppermute x12, waiting for transfers between devices, swap(): return lax.ppermute(value, ('dp', 'tensor'), pairs)  13.3 us
    pallas_call x5, Pallas kernels, pack(): pl.pallas_call(functools.partial(pack_body, pieces, items, count_a, count...  2.91 us
    unnamed x6, local copies, waits for them, and re-layouts  1.19 us
    pallas_call x1, Pallas kernels, finish(): pl.pallas_call(functools.partial(finish_body, pieces, early, late, count_...  1.03 us
  transfers between devices with their start and end apart: 12, of which 5 were waited for; matrix products, arithmetic and copies ran while one was open for 0% of the time, Pallas kernels for 8%

profile of v23, /device:TPU:0, one launch (start us, length us, event | category | flops | bytes accessed | tf_op | source)
XLA Modules:
  0.0 36.2 jit_solution(3255921832957620809)
XLA Ops:
  0.6 1.2 %copy-done.2 = bf16[128,2560]{1,0:T(8,128)(2,1)S(1)} copy-done((bf16[128,2560]{1,0:T(8,128)(2,1)S(1)}, bf16[128,2560]{1,0:T(8,128)(2,1)}, u32[]{:S(2)}) %copy-start.2) | copy-done | bytes 655384
  1.8 0.3 shard_map.50
  2.2 3.1 %collective-permute-start.5 = (f32[4,128,128]{2,1,0:T(8,128)S(1)}, f32[4,128,128]{2,1,0:T(8,128)S(1)}, u32[]{:S(2)}, u32[]{:S(2)}) collective-permute-start(f32[4,128,128]{2,1,0:T(8,128)S(1)} %get-tuple-element.49), channel_id=1, source_target_pairs={{0,4},{1,5},{2,6},{3,7},{4,0},{5,1},{6,2},{7,3},{8,12},{9,13},{10,... | collective-permute-start | bytes 786440 | tf_op jit(solution)/shard_map/ppermute | solution.py:450
  5.3 0.4 %shard_map.51 = (f32[4,112,128]{2,1,0:T(8,128)S(1)}, f32[17,8,128]{2,1,0:T(8,128)S(1)}) custom-call(f32[17,8,128]{2,1,0:T(8,128)S(1)} %get-tuple-element.34.refs_0_, bf16[128,2560]{1,0:T(8,128)(2,1)S(1)} %copy-done.2, bf16[128,5120]{1,0:T(8,128)(2,1)S(1)} %copy-done, bf16[128,5120]{1,0:T(8,128)(2,1)S(1)} %copy-done.1), custom_call_target="tpu_custom_call" | custom-call | flops 1 | bytes 1 | tf_op jit(solution)/shard_map/pallas_call | solution.py:218
  5.7 1.6 %collective-permute-start.6 = (f32[4,112,128]{2,1,0:T(8,128)S(1)}, f32[4,112,128]{2,1,0:T(8,128)S(1)}, u32[]{:S(2)}, u32[]{:S(2)}) collective-permute-start(f32[4,112,128]{2,1,0:T(8,128)S(1)} %get-tuple-element.50), channel_id=1, source_target_pairs={{0,2},{1,3},{2,0},{3,1},{4,6},{5,7},{6,4},{7,5},{8,10},{9,11},{10,... | collective-permute-start | bytes 688136 | tf_op jit(solution)/shard_map/ppermute | solution.py:450
  7.3 0.8 %shard_map.52 = (f32[4,136,128]{2,1,0:T(8,128)S(1)}, f32[4,136,128]{2,1,0:T(8,128)S(1)}, f32[17,8,128]{2,1,0:T(8,128)S(1)}) custom-call(f32[17,8,128]{2,1,0:T(8,128)S(1)} %get-tuple-element.35.refs_0_, bf16[128,2560]{1,0:T(8,128)(2,1)S(1)} %copy-done.2, bf16[128,5120]{1,0:T(8,128)(2,1)S(1)} %copy-done, bf16[128,5120]{1,0:T(8,128)(2,1)S(1)} %copy-done.1), custom_call_target="tpu_custom_call" | custom-call | flops 1 | bytes 1 | tf_op jit(solution)/shard_map/pallas_call | solution.py:218
  8.1 0.6 %collective-permute-start = (f32[4,136,128]{2,1,0:T(8,128)S(1)}, f32[4,136,128]{2,1,0:T(8,128)S(1)}, u32[]{:S(2)}, u32[]{:S(2)}) collective-permute-start(f32[4,136,128]{2,1,0:T(8,128)S(1)} %get-tuple-element.40), channel_id=1, source_target_pairs={{0,2},{1,3},{2,0},{3,1},{4,6},{5,7},{6,4},{7,5},{8,10},{9,11},{10,... | collective-permute-start | bytes 835592 | tf_op jit(solution)/shard_map/ppermute | solution.py:450
  8.7 1.0 %collective-permute-start.1 = (f32[4,136,128]{2,1,0:T(8,128)S(1)}, f32[4,136,128]{2,1,0:T(8,128)S(1)}, u32[]{:S(2)}, u32[]{:S(2)}) collective-permute-start(f32[4,136,128]{2,1,0:T(8,128)S(1)} %get-tuple-element.41), channel_id=1, source_target_pairs={{0,4},{1,5},{2,6},{3,7},{4,0},{5,1},{6,2},{7,3},{8,12},{9,13},{10,... | collective-permute-start | bytes 835592 | tf_op jit(solution)/shard_map/ppermute | solution.py:450
  9.7 0.5 %shard_map.53 = (f32[4,128,128]{2,1,0:T(8,128)S(1)}, f32[4,112,128]{2,1,0:T(8,128)S(1)}, f32[17,8,128]{2,1,0:T(8,128)S(1)}) custom-call(f32[17,8,128]{2,1,0:T(8,128)S(1)} %get-tuple-element.36.refs_0_, bf16[128,2560]{1,0:T(8,128)(2,1)S(1)} %copy-done.2, bf16[128,5120]{1,0:T(8,128)(2,1)S(1)} %copy-done, bf16[128,5120]{1,0:T(8,128)(2,1)S(1)} %copy-done.1), custom_call_target="tpu_custom_call" | custom-call | flops 1 | bytes 1 | tf_op jit(solution)/shard_map/pallas_call | solution.py:218
  10.2 0.8 %shard_map.54 = (f32[4,136,128]{2,1,0:T(8,128)S(1)}, f32[4,136,128]{2,1,0:T(8,128)S(1)}, f32[17,8,128]{2,1,0:T(8,128)S(1)}) custom-call(f32[17,8,128]{2,1,0:T(8,128)S(1)} %get-tuple-element.37.refs_0_, bf16[128,2560]{1,0:T(8,128)(2,1)S(1)} %copy-done.2, bf16[128,5120]{1,0:T(8,128)(2,1)S(1)} %copy-done, bf16[128,5120]{1,0:T(8,128)(2,1)S(1)} %copy-done.1), custom_call_target="tpu_custom_call" | custom-call | flops 1 | bytes 1 | tf_op jit(solution)/shard_map/pallas_call | solution.py:218
  11.1 3.2 %collective-permute-done.6.refs_3_ = f32[4,112,128]{2,1,0:T(8,128)S(1)} collective-permute-done((f32[4,112,128]{2,1,0:T(8,128)S(1)}, f32[4,112,128]{2,1,0:T(8,128)S(1)}, u32[]{:S(2)}, u32[]{:S(2)}) %collective-permute-start.6) | collective-permute-done | bytes 229408 | tf_op jit(solution)/shard_map/ppermute | solution.py:450
  14.4 1.0 %collective-permute-start.8 = (f32[2,112,128]{2,1,0:T(8,128)S(1)}, f32[2,112,128]{2,1,0:T(8,128)S(1)}, u32[]{:S(2)}, u32[]{:S(2)}) collective-permute-start(f32[2,112,128]{2,1,0:T(8,128)S(1)} %get-tuple-element.54), channel_id=1, source_target_pairs={{0,4},{1,5},{2,6},{3,7},{4,0},{5,1},{6,2},{7,3},{8,12},{9,13},{10,... | collective-permute-start | bytes 344072 | tf_op jit(solution)/shard_map/ppermute | solution.py:450
  15.4 1.5 %collective-permute-start.7 = (f32[2,128,128]{2,1,0:T(8,128)S(1)}, f32[2,128,128]{2,1,0:T(8,128)S(1)}, u32[]{:S(2)}, u32[]{:S(2)}) collective-permute-start(f32[2,128,128]{2,1,0:T(8,128)S(1)} %get-tuple-element.53), channel_id=1, source_target_pairs={{0,2},{1,3},{2,0},{3,1},{4,6},{5,7},{6,4},{7,5},{8,10},{9,11},{10,... | collective-permute-start | bytes 393224 | tf_op jit(solution)/shard_map/ppermute | solution.py:450
  16.9 1.1 %collective-permute-start.9 = (f32[2,128]{1,0:T(2,128)S(1)}, f32[2,128]{1,0:T(2,128)S(1)}, u32[]{:S(2)}, u32[]{:S(2)}) collective-permute-start(f32[2,128]{1,0:T(2,128)S(1)} %fusion.refs_4_), channel_id=1, source_target_pairs={{0,6},{1,7},{2,4},{3,5},{4,2},{5,3},{6,0},{7,1},{8,14},{9,15},{10,... | collective-permute-start | bytes 3080 | tf_op jit(solution)/shard_map/ppermute | solution.py:450
  17.9 2.3 %collective-permute-done.refs_2_ = f32[4,136,128]{2,1,0:T(8,128)S(1)} collective-permute-done((f32[4,136,128]{2,1,0:T(8,128)S(1)}, f32[4,136,128]{2,1,0:T(8,128)S(1)}, u32[]{:S(2)}, u32[]{:S(2)}) %collective-permute-start) | collective-permute-done | bytes 278560 | tf_op jit(solution)/shard_map/ppermute | solution.py:450
  20.3 1.0 %collective-permute-start.3 = (f32[2,136,128]{2,1,0:T(8,128)S(1)}, f32[2,136,128]{2,1,0:T(8,128)S(1)}, u32[]{:S(2)}, u32[]{:S(2)}) collective-permute-start(f32[2,136,128]{2,1,0:T(8,128)S(1)} %get-tuple-element.45), channel_id=1, source_target_pairs={{0,4},{1,5},{2,6},{3,7},{4,0},{5,1},{6,2},{7,3},{8,12},{9,13},{10,... | collective-permute-start | bytes 417800 | tf_op jit(solution)/shard_map/ppermute | solution.py:450
  21.4 1.5 %collective-permute-start.4 = (f32[2,136,128]{2,1,0:T(8,128)S(1)}, f32[2,136,128]{2,1,0:T(8,128)S(1)}, u32[]{:S(2)}, u32[]{:S(2)}) collective-permute-start(f32[2,136,128]{2,1,0:T(8,128)S(1)} %get-tuple-element.46), channel_id=1, source_target_pairs={{0,2},{1,3},{2,0},{3,1},{4,6},{5,7},{6,4},{7,5},{8,10},{9,11},{10,... | collective-permute-start | bytes 417800 | tf_op jit(solution)/shard_map/ppermute | solution.py:450
  22.9 2.7 %collective-permute-start.11 = (f32[1,240,128]{2,1,0:T(8,128)S(1)}, f32[1,240,128]{2,1,0:T(8,128)S(1)}, u32[]{:S(2)}, u32[]{:S(2)}) collective-permute-start(f32[1,240,128]{2,1,0:T(8,128)S(1)} %get-tuple-element.61), channel_id=1, source_target_pairs={{0,8},{1,9},{2,10},{3,11},{4,12},{5,13},{6,14},{7,15},{8,0},{9,1},... | collective-permute-start | bytes 368648 | tf_op jit(solution)/shard_map/ppermute | solution.py:450
  25.6 2.0 %collective-permute-done.3.refs_2_ = f32[2,136,128]{2,1,0:T(8,128)S(1)} collective-permute-done((f32[2,136,128]{2,1,0:T(8,128)S(1)}, f32[2,136,128]{2,1,0:T(8,128)S(1)}, u32[]{:S(2)}, u32[]{:S(2)}) %collective-permute-start.3) | collective-permute-done | bytes 139296 | tf_op jit(solution)/shard_map/ppermute | solution.py:450
  27.6 1.5 %collective-permute-start.10 = (f32[1,272,128]{2,1,0:T(8,128)S(1)}, f32[1,272,128]{2,1,0:T(8,128)S(1)}, u32[]{:S(2)}, u32[]{:S(2)}) collective-permute-start(f32[1,272,128]{2,1,0:T(8,128)S(1)} %get-tuple-element.58), channel_id=1, source_target_pairs={{0,8},{1,9},{2,10},{3,11},{4,12},{5,13},{6,14},{7,15},{8,0},{9,1},... | collective-permute-start | bytes 417800 | tf_op jit(solution)/shard_map/ppermute | solution.py:450
  29.1 4.6 %collective-permute-done.11.refs_2_ = f32[1,240,128]{2,1,0:T(8,128)S(1)} collective-permute-done((f32[1,240,128]{2,1,0:T(8,128)S(1)}, f32[1,240,128]{2,1,0:T(8,128)S(1)}, u32[]{:S(2)}, u32[]{:S(2)}) %collective-permute-start.11) | collective-permute-done | bytes 122912 | tf_op jit(solution)/shard_map/ppermute | solution.py:450
  33.7 0.3 shard_map.59
  34.0 1.2 %collective-permute-done.10.refs_2_ = f32[1,272,128]{2,1,0:T(8,128)S(1)} collective-permute-done((f32[1,272,128]{2,1,0:T(8,128)S(1)}, f32[1,272,128]{2,1,0:T(8,128)S(1)}, u32[]{:S(2)}, u32[]{:S(2)}) %collective-permute-start.10) | collective-permute-done | bytes 139296 | tf_op jit(solution)/shard_map/ppermute | solution.py:450
  35.2 1.0 %shard_map.60 = (f32[320,128]{1,0:T(8,128)}, f32[640,128]{1,0:T(8,128)}) custom-call(f32[1,136,128]{2,1,0:T(8,128)S(1)} %get-tuple-element.56.refs_0_, f32[1,136,128]{2,1,0:T(8,128)S(1)} %get-tuple-element.57.refs_1_, f32[1,272,128]{2,1,0:T(8,128)S(1)} %collective-permute-done.10.refs_2_, f32[320,128]{1,0:T(8,128)S(1)} %get-tuple-element.62.refs_3_, ...), custom_call_target="tpu_custom_call" | custom-call | tf_op jit(solution)/shard_map/pallas_call | solution.py:426
  (19 shorter events, 0.3 us)
Async XLA Ops:
  0.6 4.6 %copy-start.1 = (bf16[128,5120]{1,0:T(8,128)(2,1)S(1)}, bf16[128,5120]{1,0:T(8,128)(2,1)}, u32[]{:S(2)}) copy-start(bf16[128,5120]{1,0:T(8,128)(2,1)} %refs_3_.7) | copy-start | bytes 3932164
  0.6 1.2 %copy-start.2 = (bf16[128,2560]{1,0:T(8,128)(2,1)S(1)}, bf16[128,2560]{1,0:T(8,128)(2,1)}, u32[]{:S(2)}) copy-start(bf16[128,2560]{1,0:T(8,128)(2,1)} %refs_1_.7) | copy-start | bytes 1966084
  1.8 3.4 %copy-start = (bf16[128,5120]{1,0:T(8,128)(2,1)S(1)}, bf16[128,5120]{1,0:T(8,128)(2,1)}, u32[]{:S(2)}) copy-start(bf16[128,5120]{1,0:T(8,128)(2,1)} %refs_2_.7) | copy-start | bytes 3932164
  2.2 12.1 %collective-permute-start.5 = (f32[4,128,128]{2,1,0:T(8,128)S(1)}, f32[4,128,128]{2,1,0:T(8,128)S(1)}, u32[]{:S(2)}, u32[]{:S(2)}) collective-permute-start(f32[4,128,128]{2,1,0:T(8,128)S(1)} %get-tuple-element.49), channel_id=1, source_target_pairs={{0,4},{1,5},{2,6},{3,7},{4,0},{5,1},{6,2},{7,3},{8,12},{9,13},{10,... | collective-permute-start | bytes 786440 | tf_op jit(solution)/shard_map/ppermute | solution.py:450
  5.7 8.6 %collective-permute-start.6 = (f32[4,112,128]{2,1,0:T(8,128)S(1)}, f32[4,112,128]{2,1,0:T(8,128)S(1)}, u32[]{:S(2)}, u32[]{:S(2)}) collective-permute-start(f32[4,112,128]{2,1,0:T(8,128)S(1)} %get-tuple-element.50), channel_id=1, source_target_pairs={{0,2},{1,3},{2,0},{3,1},{4,6},{5,7},{6,4},{7,5},{8,10},{9,11},{10,... | collective-permute-start | bytes 688136 | tf_op jit(solution)/shard_map/ppermute | solution.py:450
  8.1 12.2 %collective-permute-start = (f32[4,136,128]{2,1,0:T(8,128)S(1)}, f32[4,136,128]{2,1,0:T(8,128)S(1)}, u32[]{:S(2)}, u32[]{:S(2)}) collective-permute-start(f32[4,136,128]{2,1,0:T(8,128)S(1)} %get-tuple-element.40), channel_id=1, source_target_pairs={{0,2},{1,3},{2,0},{3,1},{4,6},{5,7},{6,4},{7,5},{8,10},{9,11},{10,... | collective-permute-start | bytes 835592 | tf_op jit(solution)/shard_map/ppermute | solution.py:450
  8.7 11.6 %collective-permute-start.1 = (f32[4,136,128]{2,1,0:T(8,128)S(1)}, f32[4,136,128]{2,1,0:T(8,128)S(1)}, u32[]{:S(2)}, u32[]{:S(2)}) collective-permute-start(f32[4,136,128]{2,1,0:T(8,128)S(1)} %get-tuple-element.41), channel_id=1, source_target_pairs={{0,4},{1,5},{2,6},{3,7},{4,0},{5,1},{6,2},{7,3},{8,12},{9,13},{10,... | collective-permute-start | bytes 835592 | tf_op jit(solution)/shard_map/ppermute | solution.py:450
  11.0 5.9 %collective-permute-start.2 = (f32[2,128]{1,0:T(2,128)S(1)}, f32[2,128]{1,0:T(2,128)S(1)}, u32[]{:S(2)}, u32[]{:S(2)}) collective-permute-start(f32[2,128]{1,0:T(2,128)S(1)} %slice_bitcast_fusion), channel_id=1, source_target_pairs={{0,1},{1,0},{2,3},{3,2},{4,5},{5,4},{6,7},{7,6},{8,9},{9,8},{10,11... | collective-permute-start | bytes 3080 | tf_op jit(solution)/shard_map/ppermute | solution.py:450
  14.4 8.5 %collective-permute-start.8 = (f32[2,112,128]{2,1,0:T(8,128)S(1)}, f32[2,112,128]{2,1,0:T(8,128)S(1)}, u32[]{:S(2)}, u32[]{:S(2)}) collective-permute-start(f32[2,112,128]{2,1,0:T(8,128)S(1)} %get-tuple-element.54), channel_id=1, source_target_pairs={{0,4},{1,5},{2,6},{3,7},{4,0},{5,1},{6,2},{7,3},{8,12},{9,13},{10,... | collective-permute-start | bytes 344072 | tf_op jit(solution)/shard_map/ppermute | solution.py:450
  15.4 7.5 %collective-permute-start.7 = (f32[2,128,128]{2,1,0:T(8,128)S(1)}, f32[2,128,128]{2,1,0:T(8,128)S(1)}, u32[]{:S(2)}, u32[]{:S(2)}) collective-permute-start(f32[2,128,128]{2,1,0:T(8,128)S(1)} %get-tuple-element.53), channel_id=1, source_target_pairs={{0,2},{1,3},{2,0},{3,1},{4,6},{5,7},{6,4},{7,5},{8,10},{9,11},{10,... | collective-permute-start | bytes 393224 | tf_op jit(solution)/shard_map/ppermute | solution.py:450
  16.9 6.0 %collective-permute-start.9 = (f32[2,128]{1,0:T(2,128)S(1)}, f32[2,128]{1,0:T(2,128)S(1)}, u32[]{:S(2)}, u32[]{:S(2)}) collective-permute-start(f32[2,128]{1,0:T(2,128)S(1)} %fusion.refs_4_), channel_id=1, source_target_pairs={{0,6},{1,7},{2,4},{3,5},{4,2},{5,3},{6,0},{7,1},{8,14},{9,15},{10,... | collective-permute-start | bytes 3080 | tf_op jit(solution)/shard_map/ppermute | solution.py:450
  20.3 7.3 %collective-permute-start.3 = (f32[2,136,128]{2,1,0:T(8,128)S(1)}, f32[2,136,128]{2,1,0:T(8,128)S(1)}, u32[]{:S(2)}, u32[]{:S(2)}) collective-permute-start(f32[2,136,128]{2,1,0:T(8,128)S(1)} %get-tuple-element.45), channel_id=1, source_target_pairs={{0,4},{1,5},{2,6},{3,7},{4,0},{5,1},{6,2},{7,3},{8,12},{9,13},{10,... | collective-permute-start | bytes 417800 | tf_op jit(solution)/shard_map/ppermute | solution.py:450
  21.4 6.2 %collective-permute-start.4 = (f32[2,136,128]{2,1,0:T(8,128)S(1)}, f32[2,136,128]{2,1,0:T(8,128)S(1)}, u32[]{:S(2)}, u32[]{:S(2)}) collective-permute-start(f32[2,136,128]{2,1,0:T(8,128)S(1)} %get-tuple-element.46), channel_id=1, source_target_pairs={{0,2},{1,3},{2,0},{3,1},{4,6},{5,7},{6,4},{7,5},{8,10},{9,11},{10,... | collective-permute-start | bytes 417800 | tf_op jit(solution)/shard_map/ppermute | solution.py:450
  22.9 10.8 %collective-permute-start.11 = (f32[1,240,128]{2,1,0:T(8,128)S(1)}, f32[1,240,128]{2,1,0:T(8,128)S(1)}, u32[]{:S(2)}, u32[]{:S(2)}) collective-permute-start(f32[1,240,128]{2,1,0:T(8,128)S(1)} %get-tuple-element.61), channel_id=1, source_target_pairs={{0,8},{1,9},{2,10},{3,11},{4,12},{5,13},{6,14},{7,15},{8,0},{9,1},... | collective-permute-start | bytes 368648 | tf_op jit(solution)/shard_map/ppermute | solution.py:450
  27.6 7.5 %collective-permute-start.10 = (f32[1,272,128]{2,1,0:T(8,128)S(1)}, f32[1,272,128]{2,1,0:T(8,128)S(1)}, u32[]{:S(2)}, u32[]{:S(2)}) collective-permute-start(f32[1,272,128]{2,1,0:T(8,128)S(1)} %get-tuple-element.58), channel_id=1, source_target_pairs={{0,8},{1,9},{2,10},{3,11},{4,12},{5,13},{6,14},{7,15},{8,0},{9,1},... | collective-permute-start | bytes 417800 | tf_op jit(solution)/shard_map/ppermute | solution.py:450
